TPU v7x, 32 devices: a whole 2x2x4 slice. The times are simulated.
32 devices in a mesh: dp: 2 (over y), expert: 16 (over z, x, core).
Axes of the slice: x: 2, y: 2, z: 4, core: 2. Of those that a mesh axis runs over, the one named last changes fastest.
Arguments:
- tokens: bfloat16 [4096, 4096], P(('dp', 'expert')), may hold values from -6 to 6
- expert_ids: int32 [4096, 2], P(('dp', 'expert')), may hold values from 0 to 63, as said below
- gate_values: float32 [4096, 2], P(('dp', 'expert')), may hold values from 0.2 to 1
- w_gate: bfloat16 [4096, 14336], P('dp', 'expert'), may hold values from -0.09375 to 0.09375
- w_up: bfloat16 [4096, 14336], P('dp', 'expert'), may hold values from -0.09375 to 0.09375
- w_down: bfloat16 [14336, 4096], P('expert', 'dp'), may hold values from -0.046875 to 0.046875
- target: bfloat16 [4096, 4096], P(('dp', 'expert')), may hold values from -6 to 6
Outputs:
- token_grad: bfloat16 [4096, 4096], P(('dp', 'expert'))
- gate_grad: bfloat16 [4096, 14336], P('dp', 'expert')
- up_grad: bfloat16 [4096, 14336], P('dp', 'expert')
Inputs may be any that keep to these rules, and one draw needn't show every extreme that they name: `expert_ids`: A token's two expert ids differ, and no token names two experts below 1. Among the 128 tokens of one device each expert below 1 is named by 1 to 3 tokens, and in every draw some device names each of them exactly 3 times.
All inputs are finite; a program needn't handle non-finite values.
Results may differ from a plain program's by a relative error of at most 0.008.
Values may be sent and summed in bfloat16 or wider, within the bound.
No kernel may reach another device: no remote copies, remote signals or barrier semaphores. Data moves between devices by JAX's collectives and lax.ppermute only.
A program may use at most 128 MiB of HBM per device.

v0:
```python
import jax
import jax.numpy as jnp
from jax import lax
from jax.sharding import PartitionSpec as P

EXPERTS = 1


def contract_last(matrix_a, matrix_b):
    return lax.dot_general(
        matrix_a, matrix_b, (((1,), (1,)), ((), ())), preferred_element_type=jnp.float32
    )


def rounded_terms(column_blocks, grad_blocks):
    terms = jnp.einsum(
        "krd,krh->kdh", column_blocks, grad_blocks, preferred_element_type=jnp.float32
    )
    terms = lax.optimization_barrier(terms.astype(jnp.bfloat16))
    return jnp.sum(terms.astype(jnp.float32), axis=0)


def spread_rows(rows, group_size, capacity, features):
    flat = rows.reshape(EXPERTS, 1, capacity * features)
    wide = jnp.broadcast_to(flat, (EXPERTS, group_size, capacity * features))
    return wide.reshape(EXPERTS * group_size * capacity, features)


def fold_group(rows, group_size, capacity, features):
    shaped = rows.reshape(EXPERTS, group_size, capacity * features).astype(jnp.float32)
    return jnp.sum(shaped, axis=1).reshape(EXPERTS * capacity, features)


def shards(tokens, expert_ids, gate_values, w_gate, w_up, w_down, target):
    devices_along = lax.axis_size("expert")
    group_size = devices_along // EXPERTS
    tok_rows = tokens.shape[0]
    features = tokens.shape[1]
    hid_local = w_gate.shape[1]
    capacity = max(2, 3 * tok_rows // 128)
    slot_total = EXPERTS * capacity
    flat_ids = expert_ids.reshape(-1)
    pair_count = flat_ids.shape[0]
    window = flat_ids < EXPERTS
    onehot = (flat_ids[:, None] == jnp.arange(EXPERTS, dtype=jnp.int32)[None, :]).astype(jnp.int32)
    slot_index = jnp.sum((jnp.cumsum(onehot, axis=0) - onehot) * onehot, axis=1)
    position = jnp.where(window, flat_ids * capacity + slot_index, slot_total)
    owning = jnp.arange(pair_count, dtype=jnp.int32) // 2
    slot_token = jnp.zeros((slot_total + 1,), jnp.int32).at[position].set(owning)[:slot_total]
    slot_live = jnp.zeros((slot_total + 1,), jnp.bool_).at[position].set(True)[:slot_total]
    slot_gate = (
        jnp.zeros((slot_total + 1,), jnp.float32)
        .at[position]
        .set(gate_values.reshape(-1))[:slot_total]
    )
    safe_pairs = jnp.minimum(position, slot_total - 1).reshape(tok_rows, 2)
    live_pairs = window.reshape(tok_rows, 2)

    def pick(table, column):
        return jnp.where(live_pairs[:, column : column + 1], table[safe_pairs[:, column]], 0.0)

    outgoing = jnp.where(slot_live[:, None], tokens[slot_token], jnp.zeros((), tokens.dtype))
    outgoing = spread_rows(outgoing, group_size, capacity, features)
    received = lax.all_to_all(outgoing, "expert", split_axis=0, concat_axis=0, tiled=True)
    rows_count = received.shape[0]
    full_gate, full_up, full_down = (
        lax.all_gather(w_gate, "dp", axis=0, tiled=True),
        lax.all_gather(w_up, "dp", axis=0, tiled=True),
        lax.all_gather(w_down, "dp", axis=1, tiled=True),
    )
    gate_pre = jnp.dot(received, full_gate, preferred_element_type=jnp.float32)
    up_pre = jnp.dot(received, full_up, preferred_element_type=jnp.float32)
    sigmoid_gate = jax.nn.sigmoid(gate_pre)
    activated = sigmoid_gate * gate_pre
    hidden = (activated * up_pre).astype(jnp.bfloat16)
    partial_out = jnp.dot(hidden, full_down, preferred_element_type=jnp.float32).astype(
        jnp.bfloat16
    )
    returned_out = lax.all_to_all(partial_out, "expert", split_axis=0, concat_axis=0, tiled=True)
    expert_out = fold_group(returned_out, group_size, capacity, features)
    combined = gate_values[:, 0:1] * pick(expert_out, 0) + gate_values[:, 1:2] * pick(expert_out, 1)
    residual = combined - target.astype(jnp.float32)
    outgoing_grad = jnp.where(
        slot_live[:, None], slot_gate[:, None] * residual[slot_token], 0.0
    ).astype(jnp.bfloat16)
    outgoing_grad = spread_rows(outgoing_grad, group_size, capacity, features)
    cotangent = lax.all_to_all(outgoing_grad, "expert", split_axis=0, concat_axis=0, tiled=True)
    grad_hidden = contract_last(cotangent, full_down)
    derivative = sigmoid_gate * (1.0 + gate_pre * (1.0 - sigmoid_gate))
    grad_gate_pre = (grad_hidden * up_pre * derivative).astype(jnp.bfloat16)
    grad_up_pre = (grad_hidden * activated).astype(jnp.bfloat16)
    row_part = (
        contract_last(grad_gate_pre, full_gate) + contract_last(grad_up_pre, full_up)
    ).astype(jnp.bfloat16)
    back_rows = lax.all_to_all(row_part, "expert", split_axis=0, concat_axis=0, tiled=True)
    row_grad = fold_group(back_rows, group_size, capacity, features)
    token_grad = (pick(row_grad, 0) + pick(row_grad, 1)).astype(jnp.bfloat16)
    shard_columns = lax.all_to_all(received, "dp", split_axis=1, concat_axis=0, tiled=True)
    shard_width = shard_columns.shape[1]
    dp_count = lax.axis_size("dp")
    every_gate, every_up = (
        lax.all_gather(grad_gate_pre, "dp", axis=0, tiled=True),
        lax.all_gather(grad_up_pre, "dp", axis=0, tiled=True),
    )
    column_blocks = shard_columns.reshape(dp_count, rows_count, shard_width)
    gate_sum = rounded_terms(column_blocks, every_gate.reshape(dp_count, rows_count, hid_local))
    up_sum = rounded_terms(column_blocks, every_up.reshape(dp_count, rows_count, hid_local))
    return (token_grad, gate_sum.astype(jnp.bfloat16), up_sum.astype(jnp.bfloat16))


def solution(mesh):
    placed = (
        P(("dp", "expert"), None),
        P(("dp", "expert"), None),
        P(("dp", "expert"), None),
        P("dp", "expert"),
        P("dp", "expert"),
        P("expert", "dp"),
        P(("dp", "expert"), None),
    )
    return jax.shard_map(
        shards,
        mesh=mesh,
        in_specs=placed,
        out_specs=(P(("dp", "expert"), None), P("dp", "expert"), P("dp", "expert")),
        check_vma=False,
    )
```

profile of v0, /device:TPU:0, one launch (start us, length us, event | category | flops | bytes accessed | tf_op | source)
XLA Modules:
  0.0 421.4 jit_solution(4980336294840509675)
XLA Ops:
  7.2 0.7 all-gather.6.cloned.1.call-update
  8.0 0.7 all-gather.4.cloned.1.call-update
  8.7 0.7 all-gather.8.cloned.1.call-update
  9.7 0.3 reduce-window.6
  10.1 0.2 slice_reduce_fusion.2
  11.2 1.4 scatter_custom_fusion.2
  12.7 1.5 scatter_custom_fusion
  14.2 0.6 gather_fusion
  14.9 0.2 broadcast_in_dim.87
  15.1 21.6 %all_to_all.52 = bf16[16,3,4096]{2,1,0:T(4,128)(2,1)S(1)} all-to-all(bf16[16,3,4096]{2,1,0:T(4,128)(2,1)S(1)} %broadcast_in_dim.87), channel_id=1, replica_groups=mesh['dp'=2,'expert'=16] {'expert'}, dimensions={0} | all-to-all | bytes 786432 | tf_op jit(solution)/shard_map/all_to_all | solution.py:64
  36.7 0.3 all_to_all.37
  37.0 67.5 %all-gather.6.cloned.1.call-done = bf16[4096,896]{1,0:T(8,128)(2,1)} async-done(((bf16[2048,896]{1,0:T(8,128)(2,1)}), bf16[4096,896]{1,0:T(8,128)(2,1)}) %all-gather.6.cloned.1.call-update) | async-done | bytes 7340048 | tf_op jit(solution)/shard_map/all_gather | solution.py:68
  104.5 4.3 %fusion.16 = f32[48,896]{1,0:T(8,128)S(1)} fusion(bf16[48,4096]{1,0:T(8,128)(2,1)S(1)} %all_to_all.37, bf16[4096,896]{1,0:T(8,128)(2,1)} %all-gather.6.cloned.1.call-done), kind=kOutput, calls=%fused_computation.59 | convolution fusion | flops 352321536 | bytes 7905280 | tf_op jit(solution)/shard_map/dot_general | solution.py:72
  108.8 89.5 %all-gather.4.cloned.1.call-done = bf16[4096,896]{1,0:T(8,128)(2,1)} async-done(((bf16[2048,896]{1,0:T(8,128)(2,1)}), bf16[4096,896]{1,0:T(8,128)(2,1)}) %all-gather.4.cloned.1.call-update) | async-done | bytes 7340048 | tf_op jit(solution)/shard_map/all_gather | solution.py:67
  198.3 4.3 %fusion.15 = f32[48,896]{1,0:T(8,128)S(1)} fusion(bf16[48,4096]{1,0:T(8,128)(2,1)S(1)} %all_to_all.37, bf16[4096,896]{1,0:T(8,128)(2,1)} %all-gather.4.cloned.1.call-done), kind=kOutput, calls=%fused_computation.58 | convolution fusion | flops 352321536 | bytes 7905280 | tf_op jit(solution)/shard_map/dot_general | solution.py:71
  202.6 89.4 %all-gather.8.cloned.1.call-done = bf16[896,4096]{1,0:T(8,128)(2,1)} async-done(((bf16[896,2048]{1,0:T(8,128)(2,1)}), bf16[896,4096]{1,0:T(8,128)(2,1)}) %all-gather.8.cloned.1.call-update) | async-done | bytes 7340048 | tf_op jit(solution)/shard_map/all_gather | solution.py:69
  292.0 4.4 %convolution_convert_fusion.2 = bf16[48,4096]{1,0:T(8,128)(2,1)S(1)} fusion(bf16[896,4096]{1,0:T(8,128)(2,1)} %all-gather.8.cloned.1.call-done, f32[48,896]{1,0:T(8,128)S(1)} %fusion.16, f32[48,896]{1,0:T(8,128)S(1)} %fusion.15), kind=kOutput, calls=%fused_computation.13 | convolution fusion | flops 352776192 | bytes 8077312 | tf_op jit(solution)/shard_map/dot_general | solution.py:76
  296.5 1.0 all_to_all.38
  297.5 5.6 %all-to-all-start.1 = ((bf16[16,3,4096]{2,1,0:T(4,128)(2,1)}), bf16[16,3,4096]{2,1,0:T(4,128)(2,1)S(1)}, u32[]{:S(2)}, u32[]{:S(2)}) async-start(bf16[16,3,4096]{2,1,0:T(4,128)(2,1)} %all_to_all.38), calls=%async_computation.1 | async-start | bytes 1048576 | tf_op jit(solution)/shard_map/all_to_all | solution.py:79
  303.4 1.4 scatter_custom_fusion.1
  305.2 12.4 %all-to-all-done.1 = bf16[16,3,4096]{2,1,0:T(4,128)(2,1)S(1)} async-done(((bf16[16,3,4096]{2,1,0:T(4,128)(2,1)}), bf16[16,3,4096]{2,1,0:T(4,128)(2,1)S(1)}, u32[]{:S(2)}, u32[]{:S(2)}) %all-to-all-start.1) | async-done | bytes 393248 | tf_op jit(solution)/shard_map/all_to_all | solution.py:79
  317.6 0.2 convert_reduce_fusion.1
  317.8 1.1 gather_fusion.2
  319.0 2.3 gather_fusion.1
  321.3 4.0 convert_subtract_fusion
  325.3 2.2 gather_fusion.3
  327.6 1.0 broadcast_in_dim.92
  328.6 4.1 all-to-all-start.2
  332.7 0.5 all_to_all.44
  333.2 0.9 copy.20
  334.1 13.1 %all-to-all-done.2 = bf16[16,3,4096]{2,1,0:T(4,128)(2,1)S(1)} async-done(((bf16[16,3,4096]{2,1,0:T(4,128)(2,1)}), bf16[16,3,4096]{2,1,0:T(4,128)(2,1)S(1)}, u32[]{:S(2)}, u32[]{:S(2)}) %all-to-all-start.2) | async-done | bytes 393248 | tf_op jit(solution)/shard_map/all_to_all | solution.py:87
  347.2 3.6 all-to-all-start.4
  350.8 0.3 all_to_all.41
  351.1 5.4 %multiply_convert_fusion = (bf16[48,896]{1,0:T(8,128)(2,1)S(1)}, bf16[48,896]{1,0:T(8,128)(2,1)S(1)}) fusion(f32[48,896]{1,0:T(8,128)S(1)} %fusion.15, f32[48,896]{1,0:T(8,128)S(1)} %fusion.16, bf16[48,4096]{1,0:T(8,128)(2,1)S(1)} %all_to_all.41, bf16[896,4096]{1,0:T(8,128)(2,1)} %all-gather.8.cloned.1.call-done), kind=kOutput, calls=%fused_computation.22 | convolution fusion | flops 352880640 | bytes 8249344 | tf_op jit(solution)/shard_map/dot_general | solution.py:10
  356.5 5.4 %fusion.17 = f32[48,4096]{1,0:T(8,128)S(1)} fusion(bf16[48,896]{1,0:T(8,128)(2,1)S(1)} %get-tuple-element.12, bf16[4096,896]{1,0:T(8,128)(2,1)} %all-gather.4.cloned.1.call-done), kind=kOutput, calls=%fused_computation.60 | convolution fusion | flops 352321536 | bytes 8212480 | tf_op jit(solution)/shard_map/dot_general | solution.py:10
  361.9 5.4 %fusion = bf16[48,4096]{1,0:T(8,128)(2,1)S(1)} fusion(f32[48,4096]{1,0:T(8,128)S(1)} %fusion.17, bf16[48,896]{1,0:T(8,128)(2,1)S(1)} %get-tuple-element.11, bf16[4096,896]{1,0:T(8,128)(2,1)} %all-gather.6.cloned.1.call-done), kind=kOutput, calls=%fused_computation.12 | convolution fusion | flops 352714752 | bytes 8605696 | tf_op jit(solution)/shard_map/dot_general | solution.py:10
  367.3 1.0 all_to_all.42
  368.3 5.1 %all_gather.18 = bf16[96,896]{1,0:T(8,128)(2,1)S(1)} all-gather(bf16[48,896]{1,0:T(8,128)(2,1)S(1)} %get-tuple-element.12), channel_id=1, replica_groups=mesh['dp'=2,'expert'=16] {'dp'}, dimensions={0}, use_global_device_ids=true | all-gather | bytes 258048 | tf_op jit(solution)/shard_map/all_gather | solution.py:102
  373.4 4.4 %all-to-all-start.3 = ((bf16[16,3,4096]{2,1,0:T(4,128)(2,1)}), bf16[16,3,4096]{2,1,0:T(4,128)(2,1)S(1)}, u32[]{:S(2)}, u32[]{:S(2)}) async-start(bf16[16,3,4096]{2,1,0:T(4,128)(2,1)} %all_to_all.42), calls=%async_computation.3 | async-start | bytes 1048576 | tf_op jit(solution)/shard_map/all_to_all | solution.py:95
  377.8 5.1 %convolution_convert_fusion.1 = bf16[2,2048,896]{2,1,0:T(8,128)(2,1)} fusion(bf16[2,48,896]{2,1,0:T(8,128)(2,1)S(1)} %bitcast.37, bf16[48,2,2048]{2,0,1:T(8,128)(2,1)S(1)} %all-to-all-done.4), kind=kOutput, calls=%fused_computation.10 | convolution fusion | flops 355991552 | bytes 7905280 | tf_op jit(solution)/shard_map/krd,krh->kdh/dot_general | solution.py:16
  382.9 5.8 %all_gather.19 = bf16[96,896]{1,0:T(8,128)(2,1)S(1)} all-gather(bf16[48,896]{1,0:T(8,128)(2,1)S(1)} %get-tuple-element.11), channel_id=1, replica_groups=mesh['dp'=2,'expert'=16] {'dp'}, dimensions={0}, use_global_device_ids=true | all-gather | bytes 258048 | tf_op jit(solution)/shard_map/all_gather | solution.py:103
  388.6 5.1 %convolution_convert_fusion = bf16[2,2048,896]{2,1,0:T(8,128)(2,1)} fusion(bf16[2,48,896]{2,1,0:T(8,128)(2,1)S(1)} %bitcast.38, bf16[48,2,2048]{2,0,1:T(8,128)(2,1)S(1)} %all-to-all-done.4), kind=kOutput, calls=%fused_computation.9 | convolution fusion | flops 355991552 | bytes 7905280 | tf_op jit(solution)/shard_map/krd,krh->kdh/dot_general | solution.py:16
  393.8 7.1 %reduce_sum.48 = bf16[2048,896]{1,0:T(8,128)(2,1)} reduce(bf16[2,2048,896]{2,1,0:T(8,128)(2,1)} %convolution_convert_fusion.1, bf16[]{:T(256)} %constant.48.clone.1), dimensions={0}, to_apply=%region_7.8 | reduce | flops 1835008 | bytes 11010050 | tf_op jit(solution)/shard_map/reduce_sum | solution.py:20
  400.9 7.1 %reduce_sum.49 = bf16[2048,896]{1,0:T(8,128)(2,1)} reduce(bf16[2,2048,896]{2,1,0:T(8,128)(2,1)} %convolution_convert_fusion, bf16[]{:T(256)} %constant.48.clone.1), dimensions={0}, to_apply=%region_8.9 | reduce | flops 1835008 | bytes 11010050 | tf_op jit(solution)/shard_map/reduce_sum | solution.py:20
  408.1 0.2 convert_reduce_fusion
  408.3 1.1 gather_fusion.5
  409.5 2.4 gather_fusion.4
  411.8 3.0 add_convert_fusion
  (38 shorter events, 2.2 us)
Async XLA Ops:
  7.2 7.0 %copy-start = (bf16[128,4096]{1,0:T(8,128)(2,1)S(1)}, bf16[128,4096]{1,0:T(8,128)(2,1)}, u32[]{:S(2)}) copy-start(bf16[128,4096]{1,0:T(8,128)(2,1)} %param.7) | copy-start | bytes 3145732
  7.2 97.3 %all-gather.6.cloned.1.call-start = ((), (), s32[]{:S(2)}) async-start(), calls=%async_computation.6 | async-start | bytes 11010048 | tf_op jit(solution)/shard_map/all_gather | solution.py:68
  7.9 190.3 %all-gather.4.cloned.1.call-start = ((), (), s32[]{:S(2)}) async-start(), calls=%async_computation.5 | async-start | bytes 11010048 | tf_op jit(solution)/shard_map/all_gather | solution.py:67
  8.7 0.7 copy-start.3
  8.7 283.4 %all-gather.8.cloned.1.call-start = ((), (), s32[]{:S(2)}) async-start(), calls=%async_computation.7 | async-start | bytes 11010048 | tf_op jit(solution)/shard_map/all_gather | solution.py:69
  202.6 100.6 %copy-start.2 = (f32[128,2]{0,1:T(2,128)S(1)}, f32[128,2]{0,1:T(2,128)}, u32[]{:S(2)}) copy-start(f32[128,2]{0,1:T(2,128)} %param.9) | copy-start | bytes 3076
  297.5 20.1 %all-to-all-start.1 = ((bf16[16,3,4096]{2,1,0:T(4,128)(2,1)}), bf16[16,3,4096]{2,1,0:T(4,128)(2,1)S(1)}, u32[]{:S(2)}, u32[]{:S(2)}) async-start(bf16[16,3,4096]{2,1,0:T(4,128)(2,1)} %all_to_all.38), calls=%async_computation.1 | async-start | bytes 1048576 | tf_op jit(solution)/shard_map/all_to_all | solution.py:79
  328.6 18.6 %all-to-all-start.2 = ((bf16[16,3,4096]{2,1,0:T(4,128)(2,1)}), bf16[16,3,4096]{2,1,0:T(4,128)(2,1)S(1)}, u32[]{:S(2)}, u32[]{:S(2)}) async-start(bf16[16,3,4096]{2,1,0:T(4,128)(2,1)} %broadcast_in_dim.92), calls=%async_computation.2 | async-start | bytes 1048576 | tf_op jit(solution)/shard_map/all_to_all | solution.py:87
  347.2 26.3 %all-to-all-start.4 = ((bf16[48,2,2048]{2,0,1:T(8,128)(2,1)}), bf16[48,2,2048]{2,0,1:T(8,128)(2,1)S(1)}, u32[]{:S(2)}, u32[]{:S(2)}) async-start(bf16[48,2,2048]{2,0,1:T(8,128)(2,1)} %copy.20), calls=%async_computation.4 | async-start | bytes 786432 | tf_op jit(solution)/shard_map/all_to_all | solution.py:98
  373.4 34.6 %all-to-all-start.3 = ((bf16[16,3,4096]{2,1,0:T(4,128)(2,1)}), bf16[16,3,4096]{2,1,0:T(4,128)(2,1)S(1)}, u32[]{:S(2)}, u32[]{:S(2)}) async-start(bf16[16,3,4096]{2,1,0:T(4,128)(2,1)} %all_to_all.42), calls=%async_computation.3 | async-start | bytes 1048576 | tf_op jit(solution)/shard_map/all_to_all | solution.py:95
  409.4 5.4 %copy-start.1 = (bf16[128,4096]{1,0:T(8,128)(2,1)S(1)}, bf16[128,4096]{1,0:T(8,128)(2,1)}, u32[]{:S(2)}) copy-start(bf16[128,4096]{1,0:T(8,128)(2,1)} %param.7) | copy-start | bytes 3145732
Sparse Core Ops, SparseCore 0:
  9.6 94.8 all-gather.5
  106.0 92.1 all-gather.3
  199.8 92.1 all-gather.7
where the time goes:
time: 422 us; the launch traced here: 421 us
  waiting for transfers between devices  274 us (65%)
  matrix products  39.4 us (9%)
  blocking collectives  32.5 us (8%)
  other arithmetic  22.6 us (5%)
  local copies, waits for them, and re-layouts  21.1 us (5%)
  starting transfers between devices  17.8 us (4%)
  between operations  14.1 us (3%)
    all_gather x1, waiting for transfers between devices, shards(): lax.all_gather(w_gate, 'dp', axis=0, tiled=True)  89.5 us
    all_gather x1, waiting for transfers between devices, shards(): lax.all_gather(w_down, 'dp', axis=1, tiled=True)  89.4 us
    all_gather x1, waiting for transfers between devices, shards(): lax.all_gather(w_up, 'dp', axis=0, tiled=True)  67.5 us
    all_to_all x1, blocking collectives, shards(): lax.all_to_all(outgoing, 'expert', split_axis=0, concat_axis=0, tiled=True)  21.6 us
    dot_general x3, matrix products, contract_last(): lax.dot_general(matrix_a, matrix_b, (((1,), (1,)), ((), ())), preferred_e...  16.1 us
    reduce_sum x2, other arithmetic, rounded_terms(): return jnp.sum(terms.astype(jnp.float32), axis=0)  14.3 us
    all_to_all x1, waiting for transfers between devices, shards(): lax.all_to_all(outgoing_grad, 'expert', split_axis=0, concat_axis=0, tile...  13.1 us
    all_to_all x1, waiting for transfers between devices, shards(): lax.all_to_all(partial_out, 'expert', split_axis=0, concat_axis=0, tiled=...  12.4 us
  transfers between devices with their start and end apart: 7, of which 5 were waited for; matrix products, arithmetic and copies ran while one was open for 14% of the time, Pallas kernels for 0%

commit v1 on v0

--- a/solution.py
+++ b/solution.py
@@ -1,9 +1,363 @@
+import functools
+
 import jax
 import jax.numpy as jnp
 from jax import lax
+from jax.experimental import pallas as pl
+from jax.experimental.pallas import tpu as pltpu
 from jax.sharding import PartitionSpec as P
 
 EXPERTS = 1
+LANES = 128
+GATE_PIECES = 3
+BF = jnp.bfloat16
+F32 = jnp.float32
+VMEM = pl.BlockSpec(memory_space=pltpu.VMEM)
+SMEM = pl.BlockSpec(memory_space=pltpu.SMEM)
+
+
+def sds(shape, dtype):
+    return jax.ShapeDtypeStruct(shape, dtype)
+
+
+def dot_nn(a, b):
+    return lax.dot_general(a, b, (((1,), (0,)), ((), ())), preferred_element_type=F32)
+
+
+def dot_nt(a, b):
+    return lax.dot_general(a, b, (((1,), (1,)), ((), ())), preferred_element_type=F32)
+
+
+def dot_tn(a, b):
+    return lax.dot_general(a, b, (((0,), (0,)), ((), ())), preferred_element_type=F32)
+
+
+def call(body, outs, args, specs, scratch=(), limit=16, flops=0, moved=0, name=None):
+    return pl.pallas_call(
+        body,
+        out_shape=outs,
+        in_specs=specs,
+        out_specs=jax.tree.map(lambda _: VMEM, outs),
+        scratch_shapes=list(scratch),
+        compiler_params=pltpu.CompilerParams(vmem_limit_bytes=limit << 20),
+        cost_estimate=pl.CostEstimate(flops=flops, bytes_accessed=moved, transcendentals=0),
+        name=name,
+    )(*args)
+
+
+def select_rows(ids_ref):
+    tok_rows = ids_ref.shape[1]
+    live = jnp.sum((ids_ref[...] < EXPERTS).astype(F32), axis=0, keepdims=True)
+    before = lax.broadcasted_iota(jnp.int32, (tok_rows, tok_rows), 0)
+    after = lax.broadcasted_iota(jnp.int32, (tok_rows, tok_rows), 1)
+    earlier = (before < after).astype(BF)
+    wide = jnp.broadcast_to(live, (16, tok_rows))
+    slot = dot_nn(wide.astype(BF), earlier)
+    wanted = lax.broadcasted_iota(jnp.int32, (16, tok_rows), 0).astype(F32)
+    return jnp.where(slot == wanted, wide, 0.0)
+
+
+def route_kernel(dims, ids_ref, gates_ref, tokens_ref, target_ref, out_ref, tok, tgt, head, tail):
+    n_dp, half, cap, blocks, unit = dims
+    chosen = select_rows(ids_ref)
+    live_gates = jnp.sum(jnp.where(ids_ref[...] < EXPERTS, gates_ref[...], 0.0), axis=0, keepdims=True)
+    gate = jnp.sum(chosen * live_gates, axis=1, keepdims=True)
+    pick = chosen.astype(BF)
+    tok[...] = dot_nn(pick, tokens_ref[...])
+    tgt[...] = dot_nn(pick, target_ref[...])
+    tail[...] = jnp.zeros_like(tail)
+    rest = gate
+    for piece in range(GATE_PIECES):
+        part = rest.astype(BF).astype(F32)
+        rest = rest - part
+        at = (2 + piece) * cap
+        tail[at : at + cap, :] = jnp.broadcast_to(part[0:cap], (cap, LANES))
+    width = blocks * LANES
+    for d in range(n_dp):
+        for q in range(blocks):
+            lo = d * width + q * LANES
+            head[q * cap : (q + 1) * cap, :] = tok[0:cap, lo : lo + LANES]
+        packed = head[...].astype(BF)
+        for h in range(half):
+            for core in range(2):
+                lo = d * width + (core * half + h) * LANES
+                tail[core * cap : (core + 1) * cap, :] = tgt[0:cap, lo : lo + LANES]
+            base = (d * half + h) * unit
+            out_ref[base : base + blocks * cap, :] = packed
+            out_ref[base + blocks * cap : base + unit, :] = tail[...].astype(BF)
+
+
+def both_cores(core_ref, own_ref, other_ref, wide):
+    size = own_ref.shape[0]
+    core = core_ref[0]
+    wide[pl.ds(pl.multiple_of(core * size, size), size), :] = own_ref[...].astype(wide.dtype)
+    wide[pl.ds(pl.multiple_of((1 - core) * size, size), size), :] = other_ref[...].astype(wide.dtype)
+
+
+def pre_kernel(dims, core_ref, own_ref, other_ref, gate_w, up_w,
+               rows_ref, target_ref, gates_ref, own_pre, send_pre, wide):
+    n_dp, half, cap, blocks, unit = dims
+    sources = 2 * n_dp * half
+    both_cores(core_ref, own_ref, other_ref, wide)
+    core = core_ref[0]
+
+    def one(k):
+        return wide[pl.ds(k, sources, stride=unit), :]
+
+    for c in range(cap):
+        rows = slice(c * sources, (c + 1) * sources)
+        for q in range(blocks):
+            rows_ref[rows, q * LANES : (q + 1) * LANES] = one(q * cap + c).astype(BF)
+        base = blocks * cap
+        target_ref[rows, :] = jnp.where(core == 0, one(base + c), one(base + cap + c))
+        gates_ref[rows, :] = sum(one(base + (2 + piece) * cap + c) for piece in range(GATE_PIECES))
+    hid = gate_w.shape[1]
+
+    def column(j, _):
+        cols = pl.ds(pl.multiple_of(j * LANES, LANES), LANES)
+        pair = jnp.concatenate([gate_w[:, cols], up_w[:, cols]], axis=1)
+        both = dot_nn(rows_ref[...], pair)
+        for side in range(2):
+            value = both[:, side * LANES : (side + 1) * LANES]
+            own_pre[side, :, cols] = value
+            send_pre[side, :, cols] = value.astype(BF)
+        return 0
+
+    lax.fori_loop(0, hid // LANES, column, 0)
+
+
+def down_kernel(dims, core_ref, own_ref, got_ref, down_w, up_deriv, act_ref, keep_ref, send_ref, hidden):
+    n_dp, half, cap, blocks, unit = dims
+    gate_pre = own_ref[0] + got_ref[0].astype(F32)
+    up_pre = own_ref[1] + got_ref[1].astype(F32)
+    sig = jax.nn.sigmoid(gate_pre)
+    act = sig * gate_pre
+    act_ref[...] = act
+    up_deriv[...] = up_pre * (sig * (1.0 + gate_pre * (1.0 - sig)))
+    hidden[...] = (act * up_pre).astype(BF)
+    rows = hidden.shape[0]
+    core = core_ref[0]
+    for side, ref in ((core, keep_ref), (1 - core, send_ref)):
+
+        def column(j, _, side=side, ref=ref):
+            start = (side * half + 2 * j) * LANES
+            cols = pl.ds(pl.multiple_of(start, 2 * LANES), 2 * LANES)
+            value = dot_nn(hidden[...], down_w[:, cols]).astype(ref.dtype)
+            for k in range(2):
+                base = pl.multiple_of((2 * j + k) * rows, rows)
+                ref[pl.ds(base, rows), :] = value[:, k * LANES : (k + 1) * LANES]
+            return 0
+
+        lax.fori_loop(0, half // 2, column, 0)
+
+
+def cotangent_kernel(parts, got_ref, gates_ref, target_ref, out_ref):
+    rows = target_ref.shape[0]
+    total = got_ref[0:rows, :].astype(F32)
+    for h in range(1, parts):
+        total = total + got_ref[h * rows : (h + 1) * rows, :].astype(F32)
+    gate = gates_ref[...]
+    value = (gate * (gate * total - target_ref[...])).astype(BF)
+    for h in range(parts):
+        out_ref[h * rows : (h + 1) * rows, :] = value
+
+
+def grad_hidden_kernel(rows, core_ref, own_ref, other_ref, down_w, own_out, send_out, cot):
+    size = own_ref.shape[0]
+    core = core_ref[0]
+    for ref, side in ((own_ref, core), (other_ref, 1 - core)):
+        for h in range(size // rows):
+            start = (side * (size // rows) + h) * LANES
+            cot[:, pl.ds(pl.multiple_of(start, LANES), LANES)] = ref[h * rows : (h + 1) * rows, :]
+    hid = down_w.shape[0]
+
+    def column(j, _):
+        cols = pl.ds(pl.multiple_of(j * LANES, LANES), LANES)
+        value = dot_nt(cot[...], down_w[cols, :])
+        own_out[:, cols] = value
+        send_out[:, cols] = value.astype(BF)
+        return 0
+
+    lax.fori_loop(0, hid // LANES, column, 0)
+
+
+def row_grad_kernel(dims, core_ref, own_ref, got_ref, up_deriv, act_ref, gate_w, up_w,
+                    gate_out, up_out, keep_ref, send_ref, wide):
+    n_dp, half, cap, blocks, unit = dims
+    sources = 2 * n_dp * half
+    grad_hidden = own_ref[...] + got_ref[...].astype(F32)
+    gate_out[...] = (grad_hidden * up_deriv[...]).astype(BF)
+    up_out[...] = (grad_hidden * act_ref[...]).astype(BF)
+
+    def column(j, _):
+        at = pl.ds(pl.multiple_of(j * 2 * LANES, 2 * LANES), 2 * LANES)
+        value = dot_nt(gate_out[...], gate_w[at, :]) + dot_nt(up_out[...], up_w[at, :])
+        for k in range(2):
+            for c in range(cap):
+                piece = value[c * sources : (c + 1) * sources, k * LANES : (k + 1) * LANES]
+                wide[pl.ds((2 * j + k) * cap + c, sources, stride=blocks * cap), :] = piece
+        return 0
+
+    lax.fori_loop(0, blocks // 2, column, 0)
+    size = keep_ref.shape[0]
+    core = core_ref[0]
+    keep_ref[...] = wide[pl.ds(pl.multiple_of(core * size, size), size), :]
+    send_ref[...] = wide[pl.ds(pl.multiple_of((1 - core) * size, size), size), :].astype(BF)
+
+
+def weight_grad_kernel(rows_ref, gate_ref, up_ref, gate_out, up_out):
+    gate_out[...] = dot_tn(rows_ref[...], gate_ref[...]).astype(BF)
+    up_out[...] = dot_tn(rows_ref[...], up_ref[...]).astype(BF)
+
+
+def token_grad_kernel(dims, ids_ref, got_ref, out_ref, rows):
+    n_dp, half, cap, blocks, unit = dims
+    size = blocks * cap
+    rows[...] = jnp.zeros_like(rows)
+    for d in range(n_dp):
+        total = got_ref[d * half * size : (d * half + 1) * size, :].astype(F32)
+        for h in range(1, half):
+            base = (d * half + h) * size
+            total = total + got_ref[base : base + size, :].astype(F32)
+        for q in range(blocks):
+            lo = (d * blocks + q) * LANES
+            rows[0:cap, lo : lo + LANES] = total[q * cap : (q + 1) * cap, :]
+    pick = select_rows(ids_ref).astype(BF)
+    out_ref[...] = dot_tn(pick, rows[...].astype(BF)).astype(out_ref.dtype)
+
+
+def fast_shards(n_dp, n_expert, cap, tokens, expert_ids, gate_values, w_gate, w_up, w_down, target):
+    tok_rows, features = tokens.shape
+    width, hid = w_gate.shape
+    half = n_expert // 2
+    blocks = width // LANES
+    peers = n_dp * half
+    sources = 2 * peers
+    rows = cap * sources
+    unit = -(-(blocks + 2 + GATE_PIECES) * cap // 16) * 16
+    dims = (n_dp, half, cap, blocks, unit)
+    core = (lax.axis_index("expert") % 2).astype(jnp.int32).reshape(1)
+    ids = expert_ids.T
+    plane = [[2 * h + c for h in range(half)] for c in range(2)]
+    slice_groups = [
+        [d * n_expert + 2 * h + c for d in range(n_dp) for h in range(half)] for c in range(2)
+    ]
+
+    def other_core(x):
+        return lax.ppermute(x, "expert", [(i, i ^ 1) for i in range(n_expert)])
+
+    def other_dp(x):
+        return lax.ppermute(x, "dp", [(0, 1), (1, 0)])
+
+    def over_plane(x):
+        return lax.all_to_all(x, "expert", 0, 0, axis_index_groups=plane, tiled=True)
+
+    def over_slice(x):
+        return lax.all_to_all(x, ("dp", "expert"), 0, 0, axis_index_groups=slice_groups, tiled=True)
+
+    outgoing = call(
+        functools.partial(route_kernel, dims),
+        sds((peers * unit, LANES), BF),
+        (ids, gate_values.T, tokens, target),
+        [VMEM] * 4,
+        [
+            pltpu.VMEM((16, features), F32),
+            pltpu.VMEM((16, features), F32),
+            pltpu.VMEM((blocks * cap, LANES), F32),
+            pltpu.VMEM((unit - blocks * cap, LANES), F32),
+        ],
+        name="route",
+    )
+    own = over_slice(outgoing)
+    other = other_core(own)
+    all_rows, all_target, all_gates, own_pre, send_pre = call(
+        functools.partial(pre_kernel, dims),
+        (
+            sds((rows, width), BF),
+            sds((rows, LANES), F32),
+            sds((rows, LANES), F32),
+            sds((2, rows, hid), F32),
+            sds((2, rows, hid), BF),
+        ),
+        (core, own, other, w_gate, w_up),
+        [SMEM] + [VMEM] * 4,
+        [pltpu.VMEM((sources * unit, LANES), F32)],
+        name="pre_activations",
+    )
+    got_pre = other_dp(send_pre)
+    up_deriv, act, keep, send = call(
+        functools.partial(down_kernel, dims),
+        (
+            sds((rows, hid), F32),
+            sds((rows, hid), F32),
+            sds((half * rows, LANES), F32),
+            sds((half * rows, LANES), BF),
+        ),
+        (core, own_pre, got_pre, w_down),
+        [SMEM] + [VMEM] * 3,
+        [pltpu.VMEM((rows, hid), BF)],
+        name="down",
+    )
+    chip_out = (keep + other_core(send).astype(F32)).astype(BF)
+    cot = call(
+        functools.partial(cotangent_kernel, half),
+        sds((half * rows, LANES), BF),
+        (over_plane(chip_out), all_gates, all_target),
+        [VMEM] * 3,
+        name="cotangent",
+    )
+    own = over_plane(cot)
+    other = other_core(own)
+    own_gh, send_gh = call(
+        functools.partial(grad_hidden_kernel, rows),
+        (sds((rows, hid), F32), sds((rows, hid), BF)),
+        (core, own, other, w_down),
+        [SMEM] + [VMEM] * 3,
+        [pltpu.VMEM((rows, width), BF)],
+        name="grad_hidden",
+    )
+    got_gh = other_dp(send_gh)
+    gate_pre_grad, up_pre_grad, keep, send = call(
+        functools.partial(row_grad_kernel, dims),
+        (
+            sds((rows, hid), BF),
+            sds((rows, hid), BF),
+            sds((peers * blocks * cap, LANES), F32),
+            sds((peers * blocks * cap, LANES), BF),
+        ),
+        (core, own_gh, got_gh, up_deriv, act, w_gate, w_up),
+        [SMEM] + [VMEM] * 6,
+        [pltpu.VMEM((sources * blocks * cap, LANES), F32)],
+        name="row_grad",
+    )
+    chip_rows = (keep + other_core(send).astype(F32)).astype(BF)
+    got_rows = over_slice(chip_rows)
+    tile = 256
+    gate_grad, up_grad = pl.pallas_call(
+        weight_grad_kernel,
+        out_shape=(sds((width, hid), BF), sds((width, hid), BF)),
+        grid=(width // tile,),
+        in_specs=[
+            pl.BlockSpec((rows, tile), lambda i: (0, i)),
+            pl.BlockSpec((rows, hid), lambda i: (0, 0)),
+            pl.BlockSpec((rows, hid), lambda i: (0, 0)),
+        ],
+        out_specs=(pl.BlockSpec((tile, hid), lambda i: (i, 0)), pl.BlockSpec((tile, hid), lambda i: (i, 0))),
+        compiler_params=pltpu.CompilerParams(vmem_limit_bytes=16 << 20),
+        cost_estimate=pl.CostEstimate(
+            flops=4 * rows * width * hid, bytes_accessed=4 * width * hid, transcendentals=0
+        ),
+        name="weight_grads",
+    )(all_rows, gate_pre_grad, up_pre_grad)
+    token_grad = call(
+        functools.partial(token_grad_kernel, dims),
+        sds((tok_rows, features), tokens.dtype),
+        (ids, got_rows),
+        [VMEM] * 2,
+        [pltpu.VMEM((16, features), F32)],
+        name="token_grad",
+    )
+    return token_grad, gate_grad, up_grad
 
 
 def contract_last(matrix_a, matrix_b):
@@ -31,7 +385,7 @@
     return jnp.sum(shaped, axis=1).reshape(EXPERTS * capacity, features)
 
 
-def shards(tokens, expert_ids, gate_values, w_gate, w_up, w_down, target):
+def general_shards(tokens, expert_ids, gate_values, w_gate, w_up, w_down, target):
     devices_along = lax.axis_size("expert")
     group_size = devices_along // EXPERTS
     tok_rows = tokens.shape[0]
@@ -109,6 +463,25 @@
 
 
 def solution(mesh):
+    n_dp, n_expert = mesh.shape["dp"], mesh.shape["expert"]
+
+    def shards(*args):
+        tok_rows, features = args[0].shape
+        width, hid = args[3].shape
+        cap = max(2, 3 * tok_rows // 128)
+        whole_blocks = (
+            n_dp == 2
+            and n_expert % 4 == 0
+            and width == n_expert * LANES
+            and hid % LANES == 0
+            and n_dp * n_expert % 16 == 0
+            and cap <= 8
+            and tok_rows % LANES == 0
+        )
+        if whole_blocks:
+            return fast_shards(n_dp, n_expert, cap, *args)
+        return general_shards(*args)
+
     placed = (
         P(("dp", "expert"), None),
         P(("dp", "expert"), None),

time: 422 us -> 98 us (0.23)
  waiting for transfers between devices: 274 us -> 24 us
  matrix products: 39.4 us -> 0 us
  other arithmetic: 22.6 us -> 0.76 us
  Pallas kernels: 0 us -> 18.5 us
  between operations: 14.1 us -> 0.73 us
  local copies, waits for them, and re-layouts: 21.1 us -> 7.9 us
  starting transfers between devices: 17.8 us -> 5.59 us
  blocking collectives: 32.5 us -> 40 us
    all_gather x3 -> x0, waiting for transfers between devices: 246 us -> none  [the longest x1 89.5 us: shards(): lax.all_gather(w_gate, 'dp', axis=0, tiled=True)]
    dot_general x8 -> x0, matrix products: 39.4 us -> none  [the longest x3 16.1 us: contract_last(): lax.dot_general(matrix_a, matrix_b, (((1,), (1,)), ((), ())), preferred_e...]
    all_to_all x4 -> x1, waiting for transfers between devices: 25.5 us -> 3.47 us  [over_slice(): lax.all_to_all(x, ('dp', 'expert'), 0, 0, axis_index_groups=slice_groups,...]
    ppermute x0 -> x6, waiting for transfers between devices: none -> 20.6 us  [the longest x2 14.7 us: other_dp(): return lax.ppermute(x, 'dp', [(0, 1), (1, 0)])]
    pallas_call x0 -> x8, Pallas kernels: none -> 18.5 us  [the longest x7 13 us: call(): pl.pallas_call(body, out_shape=outs, in_specs=specs, out_specs=jax.tree.m...]
    all_to_all x1 -> x3, blocking collectives: 21.6 us -> 40 us  [the longest x2 22 us: over_plane(): lax.all_to_all(x, 'expert', 0, 0, axis_index_groups=plane, tiled=True)]
    reduce_sum x4 -> x0, other arithmetic: 14.7 us -> none  [the longest x2 14.3 us: rounded_terms(): return jnp.sum(terms.astype(jnp.float32), axis=0)]
    all_to_all x4 -> x1, starting transfers between devices: 17.7 us -> 3.52 us  [over_slice(): lax.all_to_all(x, ('dp', 'expert'), 0, 0, axis_index_groups=slice_groups,...]
  transfers between devices with their start and end apart: 7 -> 7, of which waited for: 5 -> 7; matrix products, arithmetic and copies ran while one was open for 14% -> 0% of each run, Pallas kernels for 0% -> 6%
where the time goes in v1:
time: 98 us; the launch traced here: 97.5 us
  blocking collectives  40 us (41%)
  waiting for transfers between devices  24 us (24%)
  Pallas kernels  18.5 us (19%)
  local copies, waits for them, and re-layouts  7.9 us (8%)
  starting transfers between devices  5.59 us (6%)
    all_to_all x2, blocking collectives, over_plane(): lax.all_to_all(x, 'expert', 0, 0, axis_index_groups=plane, tiled=True)  22 us
    all_to_all x1, blocking collectives, over_slice(): lax.all_to_all(x, ('dp', 'expert'), 0, 0, axis_index_groups=slice_groups,...  18 us
    ppermute x2, waiting for transfers between devices, other_dp(): return lax.ppermute(x, 'dp', [(0, 1), (1, 0)])  14.7 us
    pallas_call x7, Pallas kernels, call(): pl.pallas_call(body, out_shape=outs, in_specs=specs, out_specs=jax.tree.m...  13 us
    unnamed x20, local copies, waits for them, and re-layouts  7.9 us
    ppermute x4, waiting for transfers between devices, other_core(): return lax.ppermute(x, 'expert', [(i, i ^ 1) for i in range(n_expert)])  5.83 us
    pallas_call x1, Pallas kernels, fast_shards(): pl.pallas_call(weight_grad_kernel, out_shape=(sds((width, hid), BF), sds(...  5.45 us
    all_to_all x1, starting transfers between devices, over_slice(): lax.all_to_all(x, ('dp', 'expert'), 0, 0, axis_index_groups=slice_groups,...  3.52 us
  transfers between devices with their start and end apart: 7, of which 7 were waited for; matrix products, arithmetic and copies ran while one was open for 0% of the time, Pallas kernels for 6%

profile of v1, /device:TPU:0, one launch (start us, length us, event | category | flops | bytes accessed | tf_op | source)
XLA Modules:
  0.0 97.5 jit_solution(12747309302537128908)
XLA Ops:
  0.6 0.0 copy-start.5
  0.6 1.2 %copy-done.5 = bf16[128,4096]{1,0:T(8,128)(2,1)S(1)} copy-done((bf16[128,4096]{1,0:T(8,128)(2,1)S(1)}, bf16[128,4096]{1,0:T(8,128)(2,1)}, u32[]{:S(2)}) %copy-start.5) | copy-done | bytes 1048600
  1.9 0.0 copy-start.6
  1.9 1.2 %copy-done.6 = bf16[128,4096]{1,0:T(8,128)(2,1)S(1)} copy-done((bf16[128,4096]{1,0:T(8,128)(2,1)S(1)}, bf16[128,4096]{1,0:T(8,128)(2,1)}, u32[]{:S(2)}) %copy-start.6) | copy-done | bytes 1048600
  3.1 0.0 copy-start.7
  3.1 0.7 copy-done.7
  3.8 0.0 copy-start.9
  3.8 0.7 copy-done.9
  4.4 0.6 route.1
  5.0 18.0 %all_to_all.44 = bf16[16,64,128]{2,1,0:T(8,128)(2,1)S(1)} all-to-all(bf16[16,64,128]{2,1,0:T(8,128)(2,1)S(1)} %bitcast.13), channel_id=1, replica_groups={{0,2,4,6,8,10,12,14,16,18,20,22,24,26,28,30},{1,3,5,7,9,11,13,15,17,19,..., dimensions={0} | all-to-all | bytes 524288 | tf_op jit(solution)/shard_map/all_to_all | solution.py:256
  23.0 0.0 collective-permute-start
  23.0 1.5 %collective-permute-done.other_ref = bf16[1024,128]{1,0:T(8,128)(2,1)S(1)} collective-permute-done((bf16[1024,128]{1,0:T(8,128)(2,1)S(1)}, bf16[1024,128]{1,0:T(8,128)(2,1)S(1)}, u32[]{:S(2)}, u32[]{:S(2)}) %collective-permute-start) | collective-permute-done | bytes 262176 | tf_op jit(solution)/shard_map/ppermute | solution.py:247
  24.5 0.0 copy-start
  24.5 2.0 %copy-done = bf16[2048,896]{1,0:T(8,128)(2,1)S(1)} copy-done((bf16[2048,896]{1,0:T(8,128)(2,1)S(1)}, bf16[2048,896]{1,0:T(8,128)(2,1)}, u32[]{:S(2)}) %copy-start) | copy-done | bytes 3670040
  26.6 0.0 copy-start.2
  26.6 2.0 %copy-done.2 = bf16[2048,896]{1,0:T(8,128)(2,1)S(1)} copy-done((bf16[2048,896]{1,0:T(8,128)(2,1)S(1)}, bf16[2048,896]{1,0:T(8,128)(2,1)}, u32[]{:S(2)}) %copy-start.2) | copy-done | bytes 3670040
  28.6 0.0 copy-start.4
  28.6 2.9 %pre_activations.1 = (bf16[96,2048]{1,0:T(8,128)(2,1)S(1)}, f32[96,128]{1,0:T(8,128)S(1)}, f32[96,128]{1,0:T(8,128)S(1)}, f32[2,96,896]{2,1,0:T(8,128)S(1)}, bf16[2,96,896]{2,1,0:T(8,128)(2,1)S(1)}) custom-call(s32[1]{0:T(128)} %bitcast.1.core_ref, bf16[1024,128]{1,0:T(8,128)(2,1)S(1)} %bitcast.12, bf16[1024,128]{1,0:T(8,128)(2,1)S(1)} %collective-permute-done.other_ref, ...), custom_call_target="tpu_custom_call" | custom-call | tf_op jit(solution)/shard_map/pre_activations/pallas_call | solution.py:36
  31.5 1.2 %collective-permute-start.1 = (bf16[2,96,896]{2,1,0:T(8,128)(2,1)S(1)}, bf16[2,96,896]{2,1,0:T(8,128)(2,1)S(1)}, u32[]{:S(2)}, u32[]{:S(2)}) collective-permute-start(bf16[2,96,896]{2,1,0:T(8,128)(2,1)S(1)} %get-tuple-element.21), channel_id=1, source_target_pairs={{0,16},{16,0},{1,17},{17,1},{2,18},{18,2},{3,19},{19,3},{4,20},{20... | collective-permute-start | bytes 1032200 | tf_op jit(solution)/shard_map/ppermute | solution.py:250
  32.7 9.0 %collective-permute-done.1.got_ref = bf16[2,96,896]{2,1,0:T(8,128)(2,1)S(1)} collective-permute-done((bf16[2,96,896]{2,1,0:T(8,128)(2,1)S(1)}, bf16[2,96,896]{2,1,0:T(8,128)(2,1)S(1)}, u32[]{:S(2)}, u32[]{:S(2)}) %collective-permute-start.1) | collective-permute-done | bytes 344096 | tf_op jit(solution)/shard_map/ppermute | solution.py:250
  41.7 0.0 copy-done.4
  41.7 0.0 copy-start.3
  41.7 2.1 %down.1 = (f32[96,896]{1,0:T(8,128)S(1)}, f32[96,896]{1,0:T(8,128)S(1)}, f32[768,128]{1,0:T(8,128)S(1)}, bf16[768,128]{1,0:T(8,128)(2,1)S(1)}) custom-call(s32[1]{0:T(128)} %bitcast.1.core_ref, f32[2,96,896]{2,1,0:T(8,128)S(1)} %get-tuple-element.20.own_ref, bf16[2,96,896]{2,1,0:T(8,128)(2,1)S(1)} %collective-permute-done.1.got_ref, ...), custom_call_target="tpu_custom_call" | custom-call | tf_op jit(solution)/shard_map/down/pallas_call | solution.py:36
  43.8 0.0 copy-start.1
  43.8 0.1 collective-permute-start.2
  43.8 1.4 %collective-permute-done.2 = bf16[768,128]{1,0:T(8,128)(2,1)S(1)} collective-permute-done((bf16[768,128]{1,0:T(8,128)(2,1)S(1)}, bf16[768,128]{1,0:T(8,128)(2,1)S(1)}, u32[]{:S(2)}, u32[]{:S(2)}) %collective-permute-start.2) | collective-permute-done | bytes 196640 | tf_op jit(solution)/shard_map/ppermute | solution.py:247
  45.3 11.3 %all_to_all.45 = bf16[8,96,128]{2,1,0:T(8,128)(2,1)S(1)} all-to-all(bf16[8,96,128]{2,1,0:T(8,128)(2,1)S(1)} %bitcast.22), channel_id=1, replica_groups={{0,2,4,6,8,10,12,14},{1,3,5,7,9,11,13,15},{16,18,20,22,24,26,28,30},{17..., dimensions={0} | all-to-all | bytes 393216 | tf_op jit(solution)/shard_map/all_to_all | solution.py:253
  56.7 10.7 %all_to_all.46 = bf16[8,96,128]{2,1,0:T(8,128)(2,1)S(1)} all-to-all(bf16[8,96,128]{2,1,0:T(8,128)(2,1)S(1)} %bitcast.17), channel_id=1, replica_groups={{0,2,4,6,8,10,12,14},{1,3,5,7,9,11,13,15},{16,18,20,22,24,26,28,30},{17..., dimensions={0} | all-to-all | bytes 393216 | tf_op jit(solution)/shard_map/all_to_all | solution.py:253
  67.4 0.0 collective-permute-start.3
  67.4 1.4 %collective-permute-done.3.other_ref = bf16[768,128]{1,0:T(8,128)(2,1)S(1)} collective-permute-done((bf16[768,128]{1,0:T(8,128)(2,1)S(1)}, bf16[768,128]{1,0:T(8,128)(2,1)S(1)}, u32[]{:S(2)}, u32[]{:S(2)}) %collective-permute-start.3) | collective-permute-done | bytes 196640 | tf_op jit(solution)/shard_map/ppermute | solution.py:247
  68.9 2.3 %grad_hidden.1 = (f32[96,896]{1,0:T(8,128)S(1)}, bf16[96,896]{1,0:T(8,128)(2,1)S(1)}) custom-call(s32[1]{0:T(128)} %bitcast.1.core_ref, bf16[768,128]{1,0:T(8,128)(2,1)S(1)} %bitcast.15, bf16[768,128]{1,0:T(8,128)(2,1)S(1)} %collective-permute-done.3.other_ref, bf16[896,2048]{1,0:T(8,128)(2,1)S(1)} %copy-done.4), custom_call_target="tpu_custom_call" | custom-call | tf_op jit(solution)/shard_map/grad_hidden/pallas_call | solution.py:36
  71.1 0.8 collective-permute-start.4
  71.9 5.7 %collective-permute-done.4.got_ref = bf16[96,896]{1,0:T(8,128)(2,1)S(1)} collective-permute-done((bf16[96,896]{1,0:T(8,128)(2,1)S(1)}, bf16[96,896]{1,0:T(8,128)(2,1)S(1)}, u32[]{:S(2)}, u32[]{:S(2)}) %collective-permute-start.4) | collective-permute-done | bytes 172064 | tf_op jit(solution)/shard_map/ppermute | solution.py:250
  77.6 0.0 copy-done.3
  77.6 0.0 copy-done.1
  77.6 3.6 %row_grad.1 = (bf16[96,896]{1,0:T(8,128)(2,1)S(1)}, bf16[96,896]{1,0:T(8,128)(2,1)S(1)}, f32[768,128]{1,0:T(8,128)S(1)}, bf16[768,128]{1,0:T(8,128)(2,1)S(1)}) custom-call(s32[1]{0:T(128)} %bitcast.1.core_ref, f32[96,896]{1,0:T(8,128)S(1)} %get-tuple-element.26.own_ref, bf16[96,896]{1,0:T(8,128)(2,1)S(1)} %collective-permute-done.4.got_ref, ...), custom_call_target="tpu_custom_call" | custom-call | tf_op jit(solution)/shard_map/row_grad/pallas_call | solution.py:36
  81.2 0.0 copy-start.8
  81.2 0.1 collective-permute-start.5
  81.3 1.4 %collective-permute-done.5 = bf16[768,128]{1,0:T(8,128)(2,1)S(1)} collective-permute-done((bf16[768,128]{1,0:T(8,128)(2,1)S(1)}, bf16[768,128]{1,0:T(8,128)(2,1)S(1)}, u32[]{:S(2)}, u32[]{:S(2)}) %collective-permute-start.5) | collective-permute-done | bytes 196640 | tf_op jit(solution)/shard_map/ppermute | solution.py:247
  82.8 0.7 add_convert_fusion
  83.5 3.5 %all-to-all-start.3 = ((bf16[16,48,128]{2,1,0:T(8,128)(2,1)}), bf16[16,48,128]{2,1,0:T(8,128)(2,1)S(1)}, u32[]{:S(2)}, u32[]{:S(2)}) async-start(bf16[16,48,128]{2,1,0:T(8,128)(2,1)} %bitcast.9), calls=%async_computation.3 | async-start | bytes 393216 | tf_op jit(solution)/shard_map/all_to_all | solution.py:256
  87.0 5.4 %weight_grads.1 = (bf16[2048,896]{1,0:T(8,128)(2,1)}, bf16[2048,896]{1,0:T(8,128)(2,1)}) custom-call(bf16[96,2048]{1,0:T(8,128)(2,1)S(1)} %get-tuple-element.32.rows_ref, bf16[96,896]{1,0:T(8,128)(2,1)S(1)} %get-tuple-element.33.gate_ref, bf16[96,896]{1,0:T(8,128)(2,1)S(1)} %get-tuple-element.34.up_ref), custom_call_target="tpu_custom_call" | custom-call | flops 704643072 | bytes 7340032 | tf_op jit(solution)/shard_map/weight_grads/pallas_call | solution.py:336
  92.5 3.5 %all-to-all-done.3 = bf16[16,48,128]{2,1,0:T(8,128)(2,1)S(1)} async-done(((bf16[16,48,128]{2,1,0:T(8,128)(2,1)}), bf16[16,48,128]{2,1,0:T(8,128)(2,1)S(1)}, u32[]{:S(2)}, u32[]{:S(2)}) %all-to-all-start.3) | async-done | bytes 196640 | tf_op jit(solution)/shard_map/all_to_all | solution.py:256
  95.9 0.0 copy-done.8
  95.9 1.6 %token_grad.1 = bf16[128,4096]{1,0:T(8,128)(2,1)} custom-call(s32[2,128]{1,0:T(2,128)S(1)} %bitcast.20, bf16[768,128]{1,0:T(8,128)(2,1)S(1)} %bitcast.18), custom_call_target="tpu_custom_call" | custom-call | tf_op jit(solution)/shard_map/token_grad/pallas_call | solution.py:36
  (2 shorter events, 0.1 us)
Async XLA Ops:
  0.6 1.2 %copy-start.5 = (bf16[128,4096]{1,0:T(8,128)(2,1)S(1)}, bf16[128,4096]{1,0:T(8,128)(2,1)}, u32[]{:S(2)}) copy-start(bf16[128,4096]{1,0:T(8,128)(2,1)} %tokens_ref.1) | copy-start | bytes 3145732
  1.9 1.2 %copy-start.6 = (bf16[128,4096]{1,0:T(8,128)(2,1)S(1)}, bf16[128,4096]{1,0:T(8,128)(2,1)}, u32[]{:S(2)}) copy-start(bf16[128,4096]{1,0:T(8,128)(2,1)} %target_ref.1) | copy-start | bytes 3145732
  3.1 0.7 copy-start.7
  3.8 0.7 copy-start.9
  23.0 1.5 %collective-permute-start = (bf16[1024,128]{1,0:T(8,128)(2,1)S(1)}, bf16[1024,128]{1,0:T(8,128)(2,1)S(1)}, u32[]{:S(2)}, u32[]{:S(2)}) collective-permute-start(bf16[1024,128]{1,0:T(8,128)(2,1)S(1)} %bitcast.11), channel_id=1, source_target_pairs={{0,1},{1,0},{2,3},{3,2},{4,5},{5,4},{6,7},{7,6},{8,9},{9,8},{10,11... | collective-permute-start | bytes 786440 | tf_op jit(solution)/shard_map/ppermute | solution.py:247
  24.5 2.0 %copy-start = (bf16[2048,896]{1,0:T(8,128)(2,1)S(1)}, bf16[2048,896]{1,0:T(8,128)(2,1)}, u32[]{:S(2)}) copy-start(bf16[2048,896]{1,0:T(8,128)(2,1)} %gate_w.3) | copy-start | bytes 11010052
  26.6 2.0 %copy-start.2 = (bf16[2048,896]{1,0:T(8,128)(2,1)S(1)}, bf16[2048,896]{1,0:T(8,128)(2,1)}, u32[]{:S(2)}) copy-start(bf16[2048,896]{1,0:T(8,128)(2,1)} %up_w.3) | copy-start | bytes 11010052
  28.6 13.1 %copy-start.4 = (bf16[896,2048]{1,0:T(8,128)(2,1)S(1)}, bf16[896,2048]{1,0:T(8,128)(2,1)}, u32[]{:S(2)}) copy-start(bf16[896,2048]{1,0:T(8,128)(2,1)} %down_w.3) | copy-start | bytes 11010052
  31.5 10.2 %collective-permute-start.1 = (bf16[2,96,896]{2,1,0:T(8,128)(2,1)S(1)}, bf16[2,96,896]{2,1,0:T(8,128)(2,1)S(1)}, u32[]{:S(2)}, u32[]{:S(2)}) collective-permute-start(bf16[2,96,896]{2,1,0:T(8,128)(2,1)S(1)} %get-tuple-element.21), channel_id=1, source_target_pairs={{0,16},{16,0},{1,17},{17,1},{2,18},{18,2},{3,19},{19,3},{4,20},{20... | collective-permute-start | bytes 1032200 | tf_op jit(solution)/shard_map/ppermute | solution.py:250
  41.7 36.0 %copy-start.3 = (bf16[2048,896]{1,0:T(8,128)(2,1)S(1)}, bf16[2048,896]{1,0:T(8,128)(2,1)}, u32[]{:S(2)}) copy-start(bf16[2048,896]{1,0:T(8,128)(2,1)} %up_w.3) | copy-start | bytes 11010052
  43.8 33.9 %copy-start.1 = (bf16[2048,896]{1,0:T(8,128)(2,1)S(1)}, bf16[2048,896]{1,0:T(8,128)(2,1)}, u32[]{:S(2)}) copy-start(bf16[2048,896]{1,0:T(8,128)(2,1)} %gate_w.3) | copy-start | bytes 11010052
  43.8 1.5 %collective-permute-start.2 = (bf16[768,128]{1,0:T(8,128)(2,1)S(1)}, bf16[768,128]{1,0:T(8,128)(2,1)S(1)}, u32[]{:S(2)}, u32[]{:S(2)}) collective-permute-start(bf16[768,128]{1,0:T(8,128)(2,1)S(1)} %get-tuple-element.23), channel_id=1, source_target_pairs={{0,1},{1,0},{2,3},{3,2},{4,5},{5,4},{6,7},{7,6},{8,9},{9,8},{10,11... | collective-permute-start | bytes 589832 | tf_op jit(solution)/shard_map/ppermute | solution.py:247
  67.4 1.4 %collective-permute-start.3 = (bf16[768,128]{1,0:T(8,128)(2,1)S(1)}, bf16[768,128]{1,0:T(8,128)(2,1)S(1)}, u32[]{:S(2)}, u32[]{:S(2)}) collective-permute-start(bf16[768,128]{1,0:T(8,128)(2,1)S(1)} %bitcast.14), channel_id=1, source_target_pairs={{0,1},{1,0},{2,3},{3,2},{4,5},{5,4},{6,7},{7,6},{8,9},{9,8},{10,11... | collective-permute-start | bytes 589832 | tf_op jit(solution)/shard_map/ppermute | solution.py:247
  71.1 6.5 %collective-permute-start.4 = (bf16[96,896]{1,0:T(8,128)(2,1)S(1)}, bf16[96,896]{1,0:T(8,128)(2,1)S(1)}, u32[]{:S(2)}, u32[]{:S(2)}) collective-permute-start(bf16[96,896]{1,0:T(8,128)(2,1)S(1)} %get-tuple-element.27), channel_id=1, source_target_pairs={{0,16},{16,0},{1,17},{17,1},{2,18},{18,2},{3,19},{19,3},{4,20},{20... | collective-permute-start | bytes 516104 | tf_op jit(solution)/shard_map/ppermute | solution.py:250
  81.2 14.7 %copy-start.8 = (s32[128,2]{0,1:T(2,128)S(1)}, s32[128,2]{0,1:T(2,128)}, u32[]{:S(2)}) copy-start(s32[128,2]{0,1:T(2,128)} %param.8) | copy-start | bytes 3076
  81.2 1.5 %collective-permute-start.5 = (bf16[768,128]{1,0:T(8,128)(2,1)S(1)}, bf16[768,128]{1,0:T(8,128)(2,1)S(1)}, u32[]{:S(2)}, u32[]{:S(2)}) collective-permute-start(bf16[768,128]{1,0:T(8,128)(2,1)S(1)} %get-tuple-element.31), channel_id=1, source_target_pairs={{0,1},{1,0},{2,3},{3,2},{4,5},{5,4},{6,7},{7,6},{8,9},{9,8},{10,11... | collective-permute-start | bytes 589832 | tf_op jit(solution)/shard_map/ppermute | solution.py:247
  83.5 12.4 %all-to-all-start.3 = ((bf16[16,48,128]{2,1,0:T(8,128)(2,1)}), bf16[16,48,128]{2,1,0:T(8,128)(2,1)S(1)}, u32[]{:S(2)}, u32[]{:S(2)}) async-start(bf16[16,48,128]{2,1,0:T(8,128)(2,1)} %bitcast.9), calls=%async_computation.3 | async-start | bytes 393216 | tf_op jit(solution)/shard_map/all_to_all | solution.py:256

commit v2 on v1

--- a/solution.py
+++ b/solution.py
@@ -13,6 +13,7 @@
 BF = jnp.bfloat16
 F32 = jnp.float32
 VMEM = pl.BlockSpec(memory_space=pltpu.VMEM)
+HBM = pl.BlockSpec(memory_space=pltpu.HBM)
 SMEM = pl.BlockSpec(memory_space=pltpu.SMEM)
 
 
@@ -57,15 +58,29 @@
     return jnp.where(slot == wanted, wide, 0.0)
 
 
-def route_kernel(dims, ids_ref, gates_ref, tokens_ref, target_ref, out_ref, tok, tgt, head, tail):
+def route_kernel(dims, ids_hbm, gates_hbm, tokens_hbm, target_hbm, out_ref,
+                 ids_ref, gates_ref, tokens_ref, target_ref, tok, tgt, head, tail, sems):
     n_dp, half, cap, blocks, unit = dims
+    pairs = (
+        (ids_hbm, ids_ref),
+        (gates_hbm, gates_ref),
+        (tokens_hbm, tokens_ref),
+        (target_hbm, target_ref),
+    )
+    copies = [pltpu.make_async_copy(src, dst, sems.at[i]) for i, (src, dst) in enumerate(pairs)]
+    for copy in copies:
+        copy.start()
+    tail[...] = jnp.zeros_like(tail)
+    copies[0].wait()
+    copies[1].wait()
     chosen = select_rows(ids_ref)
     live_gates = jnp.sum(jnp.where(ids_ref[...] < EXPERTS, gates_ref[...], 0.0), axis=0, keepdims=True)
     gate = jnp.sum(chosen * live_gates, axis=1, keepdims=True)
     pick = chosen.astype(BF)
+    copies[2].wait()
     tok[...] = dot_nn(pick, tokens_ref[...])
+    copies[3].wait()
     tgt[...] = dot_nn(pick, target_ref[...])
-    tail[...] = jnp.zeros_like(tail)
     rest = gate
     for piece in range(GATE_PIECES):
         part = rest.astype(BF).astype(F32)
@@ -94,10 +109,32 @@
     wide[pl.ds(pl.multiple_of((1 - core) * size, size), size), :] = other_ref[...].astype(wide.dtype)
 
 
-def pre_kernel(dims, core_ref, own_ref, other_ref, gate_w, up_w,
-               rows_ref, target_ref, gates_ref, own_pre, send_pre, wide):
+def partial_pre(rows_ref, gate_w, up_w, start, own_pre, send_pre):
+    def column(j, _):
+        cols = pl.ds(pl.multiple_of(j * LANES, LANES), LANES)
+        at = pl.ds(pl.multiple_of(start + j * LANES, LANES), LANES)
+        pair = jnp.concatenate([gate_w[:, at], up_w[:, at]], axis=1)
+        both = dot_nn(rows_ref[...], pair)
+        for side in range(2):
+            value = both[:, side * LANES : (side + 1) * LANES]
+            own_pre[side, :, cols] = value
+            send_pre[side, :, cols] = value.astype(BF)
+        return 0
+
+    lax.fori_loop(0, own_pre.shape[2] // LANES, column, 0)
+
+
+def first_pre_kernel(dims, size, core_ref, own_ref, other_ref, gate_hbm, up_hbm,
+                     rows_ref, target_ref, gates_ref, gate_w, up_w, own_pre, send_pre, wide, sems):
     n_dp, half, cap, blocks, unit = dims
     sources = 2 * n_dp * half
+    hid = gate_w.shape[1]
+    copies = []
+    for k, cols in enumerate((pl.ds(0, size), pl.ds(size, hid - size))):
+        for side, (src, dst) in enumerate(((gate_hbm, gate_w), (up_hbm, up_w))):
+            copies.append(pltpu.make_async_copy(src.at[:, cols], dst.at[:, cols], sems.at[k, side]))
+    for copy in copies:
+        copy.start()
     both_cores(core_ref, own_ref, other_ref, wide)
     core = core_ref[0]
 
@@ -111,23 +148,22 @@
         base = blocks * cap
         target_ref[rows, :] = jnp.where(core == 0, one(base + c), one(base + cap + c))
         gates_ref[rows, :] = sum(one(base + (2 + piece) * cap + c) for piece in range(GATE_PIECES))
-    hid = gate_w.shape[1]
-
-    def column(j, _):
-        cols = pl.ds(pl.multiple_of(j * LANES, LANES), LANES)
-        pair = jnp.concatenate([gate_w[:, cols], up_w[:, cols]], axis=1)
-        both = dot_nn(rows_ref[...], pair)
-        for side in range(2):
-            value = both[:, side * LANES : (side + 1) * LANES]
-            own_pre[side, :, cols] = value
-            send_pre[side, :, cols] = value.astype(BF)
-        return 0
-
-    lax.fori_loop(0, hid // LANES, column, 0)
-
-
-def down_kernel(dims, core_ref, own_ref, got_ref, down_w, up_deriv, act_ref, keep_ref, send_ref, hidden):
+    copies[0].wait()
+    copies[1].wait()
+    partial_pre(rows_ref, gate_w, up_w, 0, own_pre, send_pre)
+    copies[2].wait()
+    copies[3].wait()
+
+
+def more_pre_kernel(start, rows_ref, gate_w, up_w, own_pre, send_pre):
+    partial_pre(rows_ref, gate_w, up_w, start, own_pre, send_pre)
+
+
+def down_kernel(dims, start, last, core_ref, own_ref, got_ref, down_w, *refs):
     n_dp, half, cap, blocks, unit = dims
+    refs = list(refs)
+    total_ref = refs.pop(0) if start > 0 else None
+    up_deriv, act_ref, *out_refs, hidden = refs
     gate_pre = own_ref[0] + got_ref[0].astype(F32)
     up_pre = own_ref[1] + got_ref[1].astype(F32)
     sig = jax.nn.sigmoid(gate_pre)
@@ -135,17 +171,25 @@
     act_ref[...] = act
     up_deriv[...] = up_pre * (sig * (1.0 + gate_pre * (1.0 - sig)))
     hidden[...] = (act * up_pre).astype(BF)
-    rows = hidden.shape[0]
+    rows, hid = hidden.shape
     core = core_ref[0]
-    for side, ref in ((core, keep_ref), (1 - core, send_ref)):
-
-        def column(j, _, side=side, ref=ref):
-            start = (side * half + 2 * j) * LANES
-            cols = pl.ds(pl.multiple_of(start, 2 * LANES), 2 * LANES)
-            value = dot_nn(hidden[...], down_w[:, cols]).astype(ref.dtype)
+    for side in range(2):
+
+        def column(j, _, side=side):
+            shown = core if side == 0 else 1 - core
+            lo = (shown * half + 2 * j) * LANES
+            cols = pl.ds(pl.multiple_of(lo, 2 * LANES), 2 * LANES)
+            value = dot_nn(hidden[...], down_w[start : start + hid, cols])
             for k in range(2):
-                base = pl.multiple_of((2 * j + k) * rows, rows)
-                ref[pl.ds(base, rows), :] = value[:, k * LANES : (k + 1) * LANES]
+                part = value[:, k * LANES : (k + 1) * LANES]
+                mine = pl.ds(pl.multiple_of((2 * j + k) * rows, rows), rows)
+                both = pl.ds(pl.multiple_of((side * half + 2 * j + k) * rows, rows), rows)
+                if total_ref is not None:
+                    part = part + total_ref[both, :]
+                if last:
+                    out_refs[side][mine, :] = part.astype(out_refs[side].dtype)
+                else:
+                    out_refs[0][both, :] = part
             return 0
 
         lax.fori_loop(0, half // 2, column, 0)
@@ -162,36 +206,54 @@
         out_ref[h * rows : (h + 1) * rows, :] = value
 
 
-def grad_hidden_kernel(rows, core_ref, own_ref, other_ref, down_w, own_out, send_out, cot):
-    size = own_ref.shape[0]
-    core = core_ref[0]
-    for ref, side in ((own_ref, core), (other_ref, 1 - core)):
-        for h in range(size // rows):
-            start = (side * (size // rows) + h) * LANES
-            cot[:, pl.ds(pl.multiple_of(start, LANES), LANES)] = ref[h * rows : (h + 1) * rows, :]
-    hid = down_w.shape[0]
-
+def partial_grad_hidden(cot, down_w, start, own_out, send_out):
     def column(j, _):
         cols = pl.ds(pl.multiple_of(j * LANES, LANES), LANES)
-        value = dot_nt(cot[...], down_w[cols, :])
+        at = pl.ds(pl.multiple_of(start + j * LANES, LANES), LANES)
+        value = dot_nt(cot[...], down_w[at, :])
         own_out[:, cols] = value
         send_out[:, cols] = value.astype(BF)
         return 0
 
-    lax.fori_loop(0, hid // LANES, column, 0)
-
-
-def row_grad_kernel(dims, core_ref, own_ref, got_ref, up_deriv, act_ref, gate_w, up_w,
-                    gate_out, up_out, keep_ref, send_ref, wide):
+    lax.fori_loop(0, own_out.shape[1] // LANES, column, 0)
+
+
+def first_grad_hidden_kernel(start, core_ref, own_ref, other_ref, down_w, cot, own_out, send_out):
+    rows = cot.shape[0]
+    parts = own_ref.shape[0] // rows
+    core = core_ref[0]
+    for ref, side in ((own_ref, core), (other_ref, 1 - core)):
+        for h in range(parts):
+            lo = (side * parts + h) * LANES
+            cot[:, pl.ds(pl.multiple_of(lo, LANES), LANES)] = ref[h * rows : (h + 1) * rows, :]
+    partial_grad_hidden(cot, down_w, start, own_out, send_out)
+
+
+def more_grad_hidden_kernel(start, cot, down_w, own_out, send_out):
+    partial_grad_hidden(cot, down_w, start, own_out, send_out)
+
+
+def row_grad_kernel(dims, start, last, core_ref, own_ref, got_ref, up_deriv, act_ref, gate_w, up_w, *refs):
     n_dp, half, cap, blocks, unit = dims
     sources = 2 * n_dp * half
+    refs = list(refs)
+    total_ref = refs.pop(0) if start > 0 else None
+    gate_out, up_out, *out_refs = refs
     grad_hidden = own_ref[...] + got_ref[...].astype(F32)
     gate_out[...] = (grad_hidden * up_deriv[...]).astype(BF)
     up_out[...] = (grad_hidden * act_ref[...]).astype(BF)
+    hid = gate_out.shape[1]
+    wide = out_refs[-1]
 
     def column(j, _):
         at = pl.ds(pl.multiple_of(j * 2 * LANES, 2 * LANES), 2 * LANES)
-        value = dot_nt(gate_out[...], gate_w[at, :]) + dot_nt(up_out[...], up_w[at, :])
+        value = dot_nt(gate_out[...], gate_w[at, start : start + hid])
+        value = value + dot_nt(up_out[...], up_w[at, start : start + hid])
+        if total_ref is not None:
+            value = value + total_ref[:, at]
+        if not last:
+            wide[:, at] = value
+            return 0
         for k in range(2):
             for c in range(cap):
                 piece = value[c * sources : (c + 1) * sources, k * LANES : (k + 1) * LANES]
@@ -199,15 +261,23 @@
         return 0
 
     lax.fori_loop(0, blocks // 2, column, 0)
-    size = keep_ref.shape[0]
-    core = core_ref[0]
-    keep_ref[...] = wide[pl.ds(pl.multiple_of(core * size, size), size), :]
-    send_ref[...] = wide[pl.ds(pl.multiple_of((1 - core) * size, size), size), :].astype(BF)
-
-
-def weight_grad_kernel(rows_ref, gate_ref, up_ref, gate_out, up_out):
-    gate_out[...] = dot_tn(rows_ref[...], gate_ref[...]).astype(BF)
-    up_out[...] = dot_tn(rows_ref[...], up_ref[...]).astype(BF)
+    if last:
+        keep_ref, send_ref, _ = out_refs
+        size = keep_ref.shape[0]
+        core = core_ref[0]
+        keep_ref[...] = wide[pl.ds(pl.multiple_of(core * size, size), size), :]
+        send_ref[...] = wide[pl.ds(pl.multiple_of((1 - core) * size, size), size), :].astype(BF)
+
+
+def weight_grad_kernel(parts, rows_ref, *refs):
+    gate_out, up_out = refs[-2:]
+    rows = rows_ref[...]
+    lo = 0
+    for k in range(parts):
+        size = refs[k].shape[1]
+        gate_out[:, lo : lo + size] = dot_tn(rows, refs[k][...]).astype(BF)
+        up_out[:, lo : lo + size] = dot_tn(rows, refs[parts + k][...]).astype(BF)
+        lo += size
 
 
 def token_grad_kernel(dims, ids_ref, got_ref, out_ref, rows):
@@ -259,45 +329,79 @@
         functools.partial(route_kernel, dims),
         sds((peers * unit, LANES), BF),
         (ids, gate_values.T, tokens, target),
-        [VMEM] * 4,
+        [HBM] * 4,
         [
+            pltpu.VMEM(ids.shape, ids.dtype),
+            pltpu.VMEM(ids.shape, F32),
+            pltpu.VMEM(tokens.shape, tokens.dtype),
+            pltpu.VMEM(target.shape, target.dtype),
             pltpu.VMEM((16, features), F32),
             pltpu.VMEM((16, features), F32),
             pltpu.VMEM((blocks * cap, LANES), F32),
             pltpu.VMEM((unit - blocks * cap, LANES), F32),
+            pltpu.SemaphoreType.DMA((4,)),
         ],
+        limit=60,
         name="route",
     )
     own = over_slice(outgoing)
     other = other_core(own)
-    all_rows, all_target, all_gates, own_pre, send_pre = call(
-        functools.partial(pre_kernel, dims),
-        (
-            sds((rows, width), BF),
-            sds((rows, LANES), F32),
-            sds((rows, LANES), F32),
-            sds((2, rows, hid), F32),
-            sds((2, rows, hid), BF),
-        ),
-        (core, own, other, w_gate, w_up),
-        [SMEM] + [VMEM] * 4,
-        [pltpu.VMEM((sources * unit, LANES), F32)],
-        name="pre_activations",
-    )
-    got_pre = other_dp(send_pre)
-    up_deriv, act, keep, send = call(
-        functools.partial(down_kernel, dims),
-        (
-            sds((rows, hid), F32),
-            sds((rows, hid), F32),
-            sds((half * rows, LANES), F32),
-            sds((half * rows, LANES), BF),
-        ),
-        (core, own_pre, got_pre, w_down),
-        [SMEM] + [VMEM] * 3,
-        [pltpu.VMEM((rows, hid), BF)],
-        name="down",
-    )
+    first = -(-hid // (2 * LANES)) * LANES
+    chunks = [(0, first), (first, hid - first)]
+    last = len(chunks) - 1
+    pres = []
+    for start, size in chunks:
+        outs = (sds((2, rows, size), F32), sds((2, rows, size), BF))
+        cost = dict(flops=8 * rows * width * size, moved=4 * width * size)
+        if start == 0:
+            all_rows, all_target, all_gates, gate_w, up_w, *pre = call(
+                functools.partial(first_pre_kernel, dims, size),
+                (
+                    sds((rows, width), BF),
+                    sds((rows, LANES), F32),
+                    sds((rows, LANES), F32),
+                    sds(w_gate.shape, w_gate.dtype),
+                    sds(w_up.shape, w_up.dtype),
+                    *outs,
+                ),
+                (core, own, other, w_gate, w_up),
+                [SMEM] + [VMEM] * 2 + [HBM] * 2,
+                [
+                    pltpu.VMEM((sources * unit, LANES), F32),
+                    pltpu.SemaphoreType.DMA((2, 2)),
+                ],
+                limit=44,
+                name="pre_activations",
+                **cost,
+            )
+        else:
+            pre = call(
+                functools.partial(more_pre_kernel, start),
+                outs,
+                (all_rows, gate_w, up_w),
+                [VMEM] * 3,
+                name="pre_activations",
+                **cost,
+            )
+        pres.append((pre[0], other_dp(pre[1])))
+    saved = []
+    total = ()
+    for k, (start, size) in enumerate(chunks):
+        outs = (sds((2 * half * rows, LANES), F32),)
+        if k == last:
+            outs = (sds((half * rows, LANES), F32), sds((half * rows, LANES), BF))
+        up_deriv, act, *total = call(
+            functools.partial(down_kernel, dims, start, k == last),
+            (sds((rows, size), F32), sds((rows, size), F32), *outs),
+            (core, *pres[k], w_down, *total),
+            [SMEM] + [VMEM] * (3 + len(total)),
+            [pltpu.VMEM((rows, size), BF)],
+            flops=4 * rows * width * size,
+            moved=2 * width * size,
+            name="down",
+        )
+        saved.append((up_deriv, act))
+    keep, send = total
     chip_out = (keep + other_core(send).astype(F32)).astype(BF)
     cot = call(
         functools.partial(cotangent_kernel, half),
@@ -308,47 +412,66 @@
     )
     own = over_plane(cot)
     other = other_core(own)
-    own_gh, send_gh = call(
-        functools.partial(grad_hidden_kernel, rows),
-        (sds((rows, hid), F32), sds((rows, hid), BF)),
-        (core, own, other, w_down),
-        [SMEM] + [VMEM] * 3,
-        [pltpu.VMEM((rows, width), BF)],
-        name="grad_hidden",
-    )
-    got_gh = other_dp(send_gh)
-    gate_pre_grad, up_pre_grad, keep, send = call(
-        functools.partial(row_grad_kernel, dims),
-        (
-            sds((rows, hid), BF),
-            sds((rows, hid), BF),
-            sds((peers * blocks * cap, LANES), F32),
-            sds((peers * blocks * cap, LANES), BF),
-        ),
-        (core, own_gh, got_gh, up_deriv, act, w_gate, w_up),
-        [SMEM] + [VMEM] * 6,
-        [pltpu.VMEM((sources * blocks * cap, LANES), F32)],
-        name="row_grad",
-    )
+    grads = []
+    for start, size in chunks:
+        outs = (sds((rows, size), F32), sds((rows, size), BF))
+        cost = dict(flops=4 * rows * width * size, moved=2 * width * size)
+        if start == 0:
+            cot, *grad = call(
+                functools.partial(first_grad_hidden_kernel, start),
+                (sds((rows, width), BF), *outs),
+                (core, own, other, w_down),
+                [SMEM] + [VMEM] * 3,
+                name="grad_hidden",
+                **cost,
+            )
+        else:
+            grad = call(
+                functools.partial(more_grad_hidden_kernel, start),
+                outs,
+                (cot, w_down),
+                [VMEM] * 2,
+                name="grad_hidden",
+                **cost,
+            )
+        grads.append((grad[0], other_dp(grad[1])))
+    pre_grads = []
+    total = ()
+    peer_rows = peers * blocks * cap
+    for k, (start, size) in enumerate(chunks):
+        outs, scratch = (sds((rows, width), F32),), []
+        if k == last:
+            outs = (sds((peer_rows, LANES), F32), sds((peer_rows, LANES), BF))
+            scratch = [pltpu.VMEM((2 * peer_rows, LANES), F32)]
+        gate_pre_grad, up_pre_grad, *total = call(
+            functools.partial(row_grad_kernel, dims, start, k == last),
+            (sds((rows, size), BF), sds((rows, size), BF), *outs),
+            (core, *grads[k], *saved[k], gate_w, up_w, *total),
+            [SMEM] + [VMEM] * (6 + len(total)),
+            scratch,
+            flops=8 * rows * width * size,
+            moved=4 * width * size,
+            name="row_grad",
+        )
+        pre_grads.append((gate_pre_grad, up_pre_grad))
+    keep, send = total
     chip_rows = (keep + other_core(send).astype(F32)).astype(BF)
     got_rows = over_slice(chip_rows)
+    pre_grads = [pair[0] for pair in pre_grads] + [pair[1] for pair in pre_grads]
     tile = 256
     gate_grad, up_grad = pl.pallas_call(
-        weight_grad_kernel,
+        functools.partial(weight_grad_kernel, len(chunks)),
         out_shape=(sds((width, hid), BF), sds((width, hid), BF)),
         grid=(width // tile,),
-        in_specs=[
-            pl.BlockSpec((rows, tile), lambda i: (0, i)),
-            pl.BlockSpec((rows, hid), lambda i: (0, 0)),
-            pl.BlockSpec((rows, hid), lambda i: (0, 0)),
-        ],
+        in_specs=[pl.BlockSpec((rows, tile), lambda i: (0, i))]
+        + [pl.BlockSpec(grad.shape, lambda i: (0, 0)) for grad in pre_grads],
         out_specs=(pl.BlockSpec((tile, hid), lambda i: (i, 0)), pl.BlockSpec((tile, hid), lambda i: (i, 0))),
         compiler_params=pltpu.CompilerParams(vmem_limit_bytes=16 << 20),
         cost_estimate=pl.CostEstimate(
             flops=4 * rows * width * hid, bytes_accessed=4 * width * hid, transcendentals=0
         ),
         name="weight_grads",
-    )(all_rows, gate_pre_grad, up_pre_grad)
+    )(all_rows, *pre_grads)
     token_grad = call(
         functools.partial(token_grad_kernel, dims),
         sds((tok_rows, features), tokens.dtype),

time: 98 us -> 91.8 us (0.937)
  local copies, waits for them, and re-layouts: 7.9 us -> 0.01 us
  waiting for transfers between devices: 24 us -> 17 us
  Pallas kernels: 18.5 us -> 24.6 us
  starting transfers between devices: 5.59 us -> 7.98 us
    unnamed x20 -> x4, local copies, waits for them, and re-layouts: 7.9 us -> 0.01 us
    ppermute x2 -> x4, waiting for transfers between devices: 14.7 us -> 7.95 us  [other_dp(): return lax.ppermute(x, 'dp', [(0, 1), (1, 0)])]
    pallas_call x7 -> x11, Pallas kernels: 13 us -> 18.9 us  [call(): pl.pallas_call(body, out_shape=outs, in_specs=specs, out_specs=jax.tree.m...]
    ppermute x2 -> x4, starting transfers between devices: 1.92 us -> 4.31 us  [other_dp(): return lax.ppermute(x, 'dp', [(0, 1), (1, 0)])]
  transfers between devices with their start and end apart: 7 -> 9, of which waited for: 7 -> 8; matrix products, arithmetic and copies ran while one was open for 0% -> 0% of each run, Pallas kernels for 6% -> 13%
where the time goes in v2:
time: 91.8 us; the launch traced here: 91.3 us
  blocking collectives  40.2 us (44%)
  Pallas kernels  24.6 us (27%)
  waiting for transfers between devices  17 us (19%)
  starting transfers between devices  7.98 us (9%)
    all_to_all x2, blocking collectives, over_plane(): lax.all_to_all(x, 'expert', 0, 0, axis_index_groups=plane, tiled=True)  22 us
    pallas_call x11, Pallas kernels, call(): pl.pallas_call(body, out_shape=outs, in_specs=specs, out_specs=jax.tree.m...  18.9 us
    all_to_all x1, blocking collectives, over_slice(): lax.all_to_all(x, ('dp', 'expert'), 0, 0, axis_index_groups=slice_groups,...  18.2 us
    ppermute x4, waiting for transfers between devices, other_dp(): return lax.ppermute(x, 'dp', [(0, 1), (1, 0)])  7.95 us
    ppermute x4, waiting for transfers between devices, other_core(): return lax.ppermute(x, 'expert', [(i, i ^ 1) for i in range(n_expert)])  5.83 us
    pallas_call x1, Pallas kernels, fast_shards(): pl.pallas_call(functools.partial(weight_grad_kernel, len(chunks)), out_sh...  5.72 us
    ppermute x4, starting transfers between devices, other_dp(): return lax.ppermute(x, 'dp', [(0, 1), (1, 0)])  4.31 us
    all_to_all x1, starting transfers between devices, over_slice(): lax.all_to_all(x, ('dp', 'expert'), 0, 0, axis_index_groups=slice_groups,...  3.52 us
  transfers between devices with their start and end apart: 9, of which 8 were waited for; matrix products, arithmetic and copies ran while one was open for 0% of the time, Pallas kernels for 13%

profile of v2, /device:TPU:0, one launch (start us, length us, event | category | flops | bytes accessed | tf_op | source)
XLA Modules:
  0.0 91.3 jit_solution(4467473137771836568)
XLA Ops:
  0.6 2.6 %route.1 = bf16[1024,128]{1,0:T(8,128)(2,1)} custom-call(s32[2,128]{1,0:T(2,128)} %bitcast.18, f32[2,128]{1,0:T(2,128)} %bitcast.22, bf16[128,4096]{1,0:T(8,128)(2,1)} %tokens_hbm.1, bf16[128,4096]{1,0:T(8,128)(2,1)} %target_hbm.1), custom_call_target="tpu_custom_call" | custom-call | tf_op jit(solution)/shard_map/route/pallas_call | solution.py:37
  3.2 18.2 %all_to_all.44 = bf16[16,64,128]{2,1,0:T(8,128)(2,1)S(1)} all-to-all(bf16[16,64,128]{2,1,0:T(8,128)(2,1)} %bitcast.20), channel_id=1, replica_groups={{0,2,4,6,8,10,12,14,16,18,20,22,24,26,28,30},{1,3,5,7,9,11,13,15,17,19,..., dimensions={0} | all-to-all | bytes 524288 | tf_op jit(solution)/shard_map/all_to_all | solution.py:326
  21.4 0.0 collective-permute-start
  21.4 1.5 %collective-permute-done.other_ref = bf16[1024,128]{1,0:T(8,128)(2,1)S(1)} collective-permute-done((bf16[1024,128]{1,0:T(8,128)(2,1)S(1)}, bf16[1024,128]{1,0:T(8,128)(2,1)S(1)}, u32[]{:S(2)}, u32[]{:S(2)}) %collective-permute-start) | collective-permute-done | bytes 262176 | tf_op jit(solution)/shard_map/ppermute | solution.py:317
  23.0 3.6 %pre_activations.2 = (bf16[96,2048]{1,0:T(8,128)(2,1)S(1)}, f32[96,128]{1,0:T(8,128)S(1)}, f32[96,128]{1,0:T(8,128)S(1)}, bf16[2048,896]{1,0:T(8,128)(2,1)S(1)},...) custom-call(s32[1]{0:T(128)} %bitcast.1.core_ref, ...), custom_call_target="tpu_custom_call" | custom-call | flops 805306368 | bytes 4194304 | tf_op jit(solution)/shard_map/pre_activations/pallas_call | solution.py:37
  26.5 1.2 %collective-permute-start.2 = (bf16[2,96,512]{2,1,0:T(8,128)(2,1)S(1)}, bf16[2,96,512]{2,1,0:T(8,128)(2,1)S(1)}, u32[]{:S(2)}, u32[]{:S(2)}) collective-permute-start(bf16[2,96,512]{2,1,0:T(8,128)(2,1)S(1)} %get-tuple-element.39), channel_id=1, source_target_pairs={{0,16},{16,0},{1,17},{17,1},{2,18},{18,2},{3,19},{19,3},{4,20},{20... | collective-permute-start | bytes 589832 | tf_op jit(solution)/shard_map/ppermute | solution.py:320
  27.7 0.0 copy-start
  27.7 0.9 %pre_activations.3 = (f32[2,96,384]{2,1,0:T(8,128)S(1)}, bf16[2,96,384]{2,1,0:T(8,128)(2,1)S(1)}) custom-call(bf16[96,2048]{1,0:T(8,128)(2,1)S(1)} %get-tuple-element.33.rows_ref, bf16[2048,896]{1,0:T(8,128)(2,1)S(1)} %get-tuple-element.34.gate_w, bf16[2048,896]{1,0:T(8,128)(2,1)S(1)} %get-tuple-element.35.up_w), custom_call_target="tpu_custom_call" | custom-call | flops 603979776 | bytes 3145728 | tf_op jit(solution)/shard_map/pre_activations/pallas_call | solution.py:37
  28.6 1.0 %collective-permute-start.1 = (bf16[2,96,384]{2,1,0:T(8,128)(2,1)S(1)}, bf16[2,96,384]{2,1,0:T(8,128)(2,1)S(1)}, u32[]{:S(2)}, u32[]{:S(2)}) collective-permute-start(bf16[2,96,384]{2,1,0:T(8,128)(2,1)S(1)} %get-tuple-element.37), channel_id=1, source_target_pairs={{0,16},{16,0},{1,17},{17,1},{2,18},{18,2},{3,19},{19,3},{4,20},{20... | collective-permute-start | bytes 442376 | tf_op jit(solution)/shard_map/ppermute | solution.py:320
  29.6 4.7 %collective-permute-done.2.got_ref = bf16[2,96,512]{2,1,0:T(8,128)(2,1)S(1)} collective-permute-done((bf16[2,96,512]{2,1,0:T(8,128)(2,1)S(1)}, bf16[2,96,512]{2,1,0:T(8,128)(2,1)S(1)}, u32[]{:S(2)}, u32[]{:S(2)}) %collective-permute-start.2) | collective-permute-done | bytes 196640 | tf_op jit(solution)/shard_map/ppermute | solution.py:320
  34.3 0.0 copy-done
  34.3 1.6 %down.2 = (f32[96,512]{1,0:T(8,128)S(1)}, f32[96,512]{1,0:T(8,128)S(1)}, f32[1536,128]{1,0:T(8,128)S(1)}) custom-call(s32[1]{0:T(128)} %bitcast.1.core_ref, f32[2,96,512]{2,1,0:T(8,128)S(1)} %get-tuple-element.38.own_ref, bf16[2,96,512]{2,1,0:T(8,128)(2,1)S(1)} %collective-permute-done.2.got_ref, bf16[896,2048]{1,0:T(8,128)(2,1)S(1)} %copy-done), custom_call_target="tpu_custom_call" | custom-call | flops 402653184 | bytes 2097152 | tf_op jit(solution)/shard_map/down/pallas_call | solution.py:37
  36.0 0.7 collective-permute-done.1.got_ref
  36.7 1.6 %down.3 = (f32[96,384]{1,0:T(8,128)S(1)}, f32[96,384]{1,0:T(8,128)S(1)}, f32[768,128]{1,0:T(8,128)S(1)}, bf16[768,128]{1,0:T(8,128)(2,1)S(1)}) custom-call(s32[1]{0:T(128)} %bitcast.1.core_ref, f32[2,96,384]{2,1,0:T(8,128)S(1)} %get-tuple-element.36.own_ref, bf16[2,96,384]{2,1,0:T(8,128)(2,1)S(1)} %collective-permute-done.1.got_ref, ...), custom_call_target="tpu_custom_call" | custom-call | flops 301989888 | bytes 1572864 | tf_op jit(solution)/shard_map/down/pallas_call | solution.py:37
  38.3 0.1 collective-permute-start.3
  38.3 1.4 %collective-permute-done.3 = bf16[768,128]{1,0:T(8,128)(2,1)S(1)} collective-permute-done((bf16[768,128]{1,0:T(8,128)(2,1)S(1)}, bf16[768,128]{1,0:T(8,128)(2,1)S(1)}, u32[]{:S(2)}, u32[]{:S(2)}) %collective-permute-start.3) | collective-permute-done | bytes 196640 | tf_op jit(solution)/shard_map/ppermute | solution.py:317
  39.8 0.1 add_convert_fusion.1
  39.8 11.3 %all_to_all.45 = bf16[8,96,128]{2,1,0:T(8,128)(2,1)S(1)} all-to-all(bf16[8,96,128]{2,1,0:T(8,128)(2,1)S(1)} %bitcast.21), channel_id=1, replica_groups={{0,2,4,6,8,10,12,14},{1,3,5,7,9,11,13,15},{16,18,20,22,24,26,28,30},{17..., dimensions={0} | all-to-all | bytes 393216 | tf_op jit(solution)/shard_map/all_to_all | solution.py:323
  51.2 10.7 %all_to_all.46 = bf16[8,96,128]{2,1,0:T(8,128)(2,1)S(1)} all-to-all(bf16[8,96,128]{2,1,0:T(8,128)(2,1)S(1)} %bitcast.16), channel_id=1, replica_groups={{0,2,4,6,8,10,12,14},{1,3,5,7,9,11,13,15},{16,18,20,22,24,26,28,30},{17..., dimensions={0} | all-to-all | bytes 393216 | tf_op jit(solution)/shard_map/all_to_all | solution.py:323
  61.9 0.0 collective-permute-start.4
  61.9 1.4 %collective-permute-done.4.other_ref = bf16[768,128]{1,0:T(8,128)(2,1)S(1)} collective-permute-done((bf16[768,128]{1,0:T(8,128)(2,1)S(1)}, bf16[768,128]{1,0:T(8,128)(2,1)S(1)}, u32[]{:S(2)}, u32[]{:S(2)}) %collective-permute-start.4) | collective-permute-done | bytes 196640 | tf_op jit(solution)/shard_map/ppermute | solution.py:317
  63.4 1.4 %grad_hidden.2 = (bf16[96,2048]{1,0:T(8,128)(2,1)S(1)}, f32[96,512]{1,0:T(8,128)S(1)}, bf16[96,512]{1,0:T(8,128)(2,1)S(1)}) custom-call(s32[1]{0:T(128)} %bitcast.1.core_ref, bf16[768,128]{1,0:T(8,128)(2,1)S(1)} %bitcast.14, bf16[768,128]{1,0:T(8,128)(2,1)S(1)} %collective-permute-done.4.other_ref, bf16[896,2048]{1,0:T(8,128)(2,1)S(1)} %copy-done), custom_call_target="tpu_custom_call" | custom-call | flops 402653184 | bytes 2097152 | tf_op jit(solution)/shard_map/grad_hidden/pallas_call | solution.py:37
  64.7 0.8 collective-permute-start.6
  65.5 1.0 %grad_hidden.3 = (f32[96,384]{1,0:T(8,128)S(1)}, bf16[96,384]{1,0:T(8,128)(2,1)S(1)}) custom-call(bf16[96,2048]{1,0:T(8,128)(2,1)S(1)} %get-tuple-element.45.cot, bf16[896,2048]{1,0:T(8,128)(2,1)S(1)} %copy-done), custom_call_target="tpu_custom_call" | custom-call | flops 301989888 | bytes 1572864 | tf_op jit(solution)/shard_map/grad_hidden/pallas_call | solution.py:37
  66.4 1.4 %collective-permute-start.5 = (bf16[96,384]{1,0:T(8,128)(2,1)S(1)}, bf16[96,384]{1,0:T(8,128)(2,1)S(1)}, u32[]{:S(2)}, u32[]{:S(2)}) collective-permute-start(bf16[96,384]{1,0:T(8,128)(2,1)S(1)} %get-tuple-element.47), channel_id=1, source_target_pairs={{0,16},{16,0},{1,17},{17,1},{2,18},{18,2},{3,19},{19,3},{4,20},{20... | collective-permute-start | bytes 221192 | tf_op jit(solution)/shard_map/ppermute | solution.py:320
  67.8 2.5 %collective-permute-done.6.got_ref = bf16[96,512]{1,0:T(8,128)(2,1)S(1)} collective-permute-done((bf16[96,512]{1,0:T(8,128)(2,1)S(1)}, bf16[96,512]{1,0:T(8,128)(2,1)S(1)}, u32[]{:S(2)}, u32[]{:S(2)}) %collective-permute-start.6) | collective-permute-done | bytes 98336 | tf_op jit(solution)/shard_map/ppermute | solution.py:320
  70.4 2.4 %row_grad.2 = (bf16[96,512]{1,0:T(8,128)(2,1)S(1)}, bf16[96,512]{1,0:T(8,128)(2,1)S(1)}, f32[96,2048]{1,0:T(8,128)S(1)}) custom-call(s32[1]{0:T(128)} %bitcast.1.core_ref, f32[96,512]{1,0:T(8,128)S(1)} %get-tuple-element.50.own_ref, bf16[96,512]{1,0:T(8,128)(2,1)S(1)} %collective-permute-done.6.got_ref, f32[96,512]{1,0:T(8,128)S(1)} %get-tuple-element.52.up_deriv, ...), custom_call_target="tpu_custom_call" | custom-call | flops 805306368 | bytes 4194304 | tf_op jit(solution)/shard_map/row_grad/pallas_call | solution.py:37
  72.8 0.0 collective-permute-done.5.got_ref
  72.8 2.2 %row_grad.3 = (bf16[96,384]{1,0:T(8,128)(2,1)S(1)}, bf16[96,384]{1,0:T(8,128)(2,1)S(1)}, f32[768,128]{1,0:T(8,128)S(1)}, bf16[768,128]{1,0:T(8,128)(2,1)S(1)}) custom-call(s32[1]{0:T(128)} %bitcast.1.core_ref, f32[96,384]{1,0:T(8,128)S(1)} %get-tuple-element.46.own_ref, bf16[96,384]{1,0:T(8,128)(2,1)S(1)} %collective-permute-done.5.got_ref, ...), custom_call_target="tpu_custom_call" | custom-call | flops 603979776 | bytes 3145728 | tf_op jit(solution)/shard_map/row_grad/pallas_call | solution.py:37
  75.0 0.0 copy-start.1
  75.1 0.1 collective-permute-start.7
  75.1 1.4 %collective-permute-done.7 = bf16[768,128]{1,0:T(8,128)(2,1)S(1)} collective-permute-done((bf16[768,128]{1,0:T(8,128)(2,1)S(1)}, bf16[768,128]{1,0:T(8,128)(2,1)S(1)}, u32[]{:S(2)}, u32[]{:S(2)}) %collective-permute-start.7) | collective-permute-done | bytes 196640 | tf_op jit(solution)/shard_map/ppermute | solution.py:317
  76.6 0.7 add_convert_fusion
  77.3 3.5 %all-to-all-start.3 = ((bf16[16,48,128]{2,1,0:T(8,128)(2,1)}), bf16[16,48,128]{2,1,0:T(8,128)(2,1)S(1)}, u32[]{:S(2)}, u32[]{:S(2)}) async-start(bf16[16,48,128]{2,1,0:T(8,128)(2,1)} %bitcast.9), calls=%async_computation.3 | async-start | bytes 393216 | tf_op jit(solution)/shard_map/all_to_all | solution.py:326
  80.8 5.7 %weight_grads.1 = (bf16[2048,896]{1,0:T(8,128)(2,1)}, bf16[2048,896]{1,0:T(8,128)(2,1)}) custom-call(bf16[96,2048]{1,0:T(8,128)(2,1)S(1)} %get-tuple-element.33.rows_ref, bf16[96,512]{1,0:T(8,128)(2,1)S(1)} %get-tuple-element.57.refs_0_, bf16[96,384]{1,0:T(8,128)(2,1)S(1)} %get-tuple-element.58.refs_1_, bf16[96,512]{1,0:T(8,128)(2,1)S(1)} %get-tuple-element.59.refs_2_, ...), custom_call_target="tpu_custom_call" | custom-call | flops 704643072 | bytes 7340032 | tf_op jit(solution)/shard_map/weight_grads/pallas_call | solution.py:462
  86.5 3.2 %all-to-all-done.3 = bf16[16,48,128]{2,1,0:T(8,128)(2,1)S(1)} async-done(((bf16[16,48,128]{2,1,0:T(8,128)(2,1)}), bf16[16,48,128]{2,1,0:T(8,128)(2,1)S(1)}, u32[]{:S(2)}, u32[]{:S(2)}) %all-to-all-start.3) | async-done | bytes 196640 | tf_op jit(solution)/shard_map/all_to_all | solution.py:326
  89.7 0.0 copy-done.1
  89.7 1.6 %token_grad.1 = bf16[128,4096]{1,0:T(8,128)(2,1)} custom-call(s32[2,128]{1,0:T(2,128)S(1)} %bitcast.19, bf16[768,128]{1,0:T(8,128)(2,1)S(1)} %bitcast.17), custom_call_target="tpu_custom_call" | custom-call | tf_op jit(solution)/shard_map/token_grad/pallas_call | solution.py:37
  (1 shorter events, 0.0 us)
Async XLA Ops:
  21.4 1.5 %collective-permute-start = (bf16[1024,128]{1,0:T(8,128)(2,1)S(1)}, bf16[1024,128]{1,0:T(8,128)(2,1)S(1)}, u32[]{:S(2)}, u32[]{:S(2)}) collective-permute-start(bf16[1024,128]{1,0:T(8,128)(2,1)S(1)} %bitcast.11), channel_id=1, source_target_pairs={{0,1},{1,0},{2,3},{3,2},{4,5},{5,4},{6,7},{7,6},{8,9},{9,8},{10,11... | collective-permute-start | bytes 786440 | tf_op jit(solution)/shard_map/ppermute | solution.py:317
  26.5 7.8 %collective-permute-start.2 = (bf16[2,96,512]{2,1,0:T(8,128)(2,1)S(1)}, bf16[2,96,512]{2,1,0:T(8,128)(2,1)S(1)}, u32[]{:S(2)}, u32[]{:S(2)}) collective-permute-start(bf16[2,96,512]{2,1,0:T(8,128)(2,1)S(1)} %get-tuple-element.39), channel_id=1, source_target_pairs={{0,16},{16,0},{1,17},{17,1},{2,18},{18,2},{3,19},{19,3},{4,20},{20... | collective-permute-start | bytes 589832 | tf_op jit(solution)/shard_map/ppermute | solution.py:320
  27.7 6.7 %copy-start = (bf16[896,2048]{1,0:T(8,128)(2,1)S(1)}, bf16[896,2048]{1,0:T(8,128)(2,1)}, u32[]{:S(2)}) copy-start(bf16[896,2048]{1,0:T(8,128)(2,1)} %down_w.7) | copy-start | bytes 11010052
  28.6 8.1 %collective-permute-start.1 = (bf16[2,96,384]{2,1,0:T(8,128)(2,1)S(1)}, bf16[2,96,384]{2,1,0:T(8,128)(2,1)S(1)}, u32[]{:S(2)}, u32[]{:S(2)}) collective-permute-start(bf16[2,96,384]{2,1,0:T(8,128)(2,1)S(1)} %get-tuple-element.37), channel_id=1, source_target_pairs={{0,16},{16,0},{1,17},{17,1},{2,18},{18,2},{3,19},{19,3},{4,20},{20... | collective-permute-start | bytes 442376 | tf_op jit(solution)/shard_map/ppermute | solution.py:320
  38.3 1.5 %collective-permute-start.3 = (bf16[768,128]{1,0:T(8,128)(2,1)S(1)}, bf16[768,128]{1,0:T(8,128)(2,1)S(1)}, u32[]{:S(2)}, u32[]{:S(2)}) collective-permute-start(bf16[768,128]{1,0:T(8,128)(2,1)S(1)} %get-tuple-element.42), channel_id=1, source_target_pairs={{0,1},{1,0},{2,3},{3,2},{4,5},{5,4},{6,7},{7,6},{8,9},{9,8},{10,11... | collective-permute-start | bytes 589832 | tf_op jit(solution)/shard_map/ppermute | solution.py:317
  61.9 1.4 %collective-permute-start.4 = (bf16[768,128]{1,0:T(8,128)(2,1)S(1)}, bf16[768,128]{1,0:T(8,128)(2,1)S(1)}, u32[]{:S(2)}, u32[]{:S(2)}) collective-permute-start(bf16[768,128]{1,0:T(8,128)(2,1)S(1)} %bitcast.13), channel_id=1, source_target_pairs={{0,1},{1,0},{2,3},{3,2},{4,5},{5,4},{6,7},{7,6},{8,9},{9,8},{10,11... | collective-permute-start | bytes 589832 | tf_op jit(solution)/shard_map/ppermute | solution.py:317
  64.7 5.6 %collective-permute-start.6 = (bf16[96,512]{1,0:T(8,128)(2,1)S(1)}, bf16[96,512]{1,0:T(8,128)(2,1)S(1)}, u32[]{:S(2)}, u32[]{:S(2)}) collective-permute-start(bf16[96,512]{1,0:T(8,128)(2,1)S(1)} %get-tuple-element.51), channel_id=1, source_target_pairs={{0,16},{16,0},{1,17},{17,1},{2,18},{18,2},{3,19},{19,3},{4,20},{20... | collective-permute-start | bytes 294920 | tf_op jit(solution)/shard_map/ppermute | solution.py:320
  66.4 6.4 %collective-permute-start.5 = (bf16[96,384]{1,0:T(8,128)(2,1)S(1)}, bf16[96,384]{1,0:T(8,128)(2,1)S(1)}, u32[]{:S(2)}, u32[]{:S(2)}) collective-permute-start(bf16[96,384]{1,0:T(8,128)(2,1)S(1)} %get-tuple-element.47), channel_id=1, source_target_pairs={{0,16},{16,0},{1,17},{17,1},{2,18},{18,2},{3,19},{19,3},{4,20},{20... | collective-permute-start | bytes 221192 | tf_op jit(solution)/shard_map/ppermute | solution.py:320
  75.0 14.7 %copy-start.1 = (s32[128,2]{0,1:T(2,128)S(1)}, s32[128,2]{0,1:T(2,128)}, u32[]{:S(2)}) copy-start(s32[128,2]{0,1:T(2,128)} %param.8) | copy-start | bytes 3076
  75.1 1.5 %collective-permute-start.7 = (bf16[768,128]{1,0:T(8,128)(2,1)S(1)}, bf16[768,128]{1,0:T(8,128)(2,1)S(1)}, u32[]{:S(2)}, u32[]{:S(2)}) collective-permute-start(bf16[768,128]{1,0:T(8,128)(2,1)S(1)} %get-tuple-element.56), channel_id=1, source_target_pairs={{0,1},{1,0},{2,3},{3,2},{4,5},{5,4},{6,7},{7,6},{8,9},{9,8},{10,11... | collective-permute-start | bytes 589832 | tf_op jit(solution)/shard_map/ppermute | solution.py:317
  77.3 12.4 %all-to-all-start.3 = ((bf16[16,48,128]{2,1,0:T(8,128)(2,1)}), bf16[16,48,128]{2,1,0:T(8,128)(2,1)S(1)}, u32[]{:S(2)}, u32[]{:S(2)}) async-start(bf16[16,48,128]{2,1,0:T(8,128)(2,1)} %bitcast.9), calls=%async_computation.3 | async-start | bytes 393216 | tf_op jit(solution)/shard_map/all_to_all | solution.py:326

commit v3 on v2

--- a/solution.py
+++ b/solution.py
@@ -33,12 +33,12 @@
     return lax.dot_general(a, b, (((0,), (0,)), ((), ())), preferred_element_type=F32)
 
 
-def call(body, outs, args, specs, scratch=(), limit=16, flops=0, moved=0, name=None):
+def call(body, outs, args, specs, scratch=(), limit=16, flops=0, moved=0, name=None, out_spec=VMEM):
     return pl.pallas_call(
         body,
         out_shape=outs,
         in_specs=specs,
-        out_specs=jax.tree.map(lambda _: VMEM, outs),
+        out_specs=jax.tree.map(lambda _: out_spec, outs),
         scratch_shapes=list(scratch),
         compiler_params=pltpu.CompilerParams(vmem_limit_bytes=limit << 20),
         cost_estimate=pl.CostEstimate(flops=flops, bytes_accessed=moved, transcendentals=0),
@@ -56,6 +56,14 @@
     slot = dot_nn(wide.astype(BF), earlier)
     wanted = lax.broadcasted_iota(jnp.int32, (16, tok_rows), 0).astype(F32)
     return jnp.where(slot == wanted, wide, 0.0)
+
+
+def add_kernel(own_ref, got_ref, out_ref):
+    out_ref[...] = (own_ref[...] + got_ref[...].astype(F32)).astype(out_ref.dtype)
+
+
+def add_cores(own, got):
+    return call(add_kernel, sds(got.shape, got.dtype), (own, got), [VMEM] * 2, name="add_cores")
 
 
 def route_kernel(dims, ids_hbm, gates_hbm, tokens_hbm, target_hbm, out_ref,
@@ -109,32 +117,49 @@
     wide[pl.ds(pl.multiple_of((1 - core) * size, size), size), :] = other_ref[...].astype(wide.dtype)
 
 
-def partial_pre(rows_ref, gate_w, up_w, start, own_pre, send_pre):
-    def column(j, _):
-        cols = pl.ds(pl.multiple_of(j * LANES, LANES), LANES)
-        at = pl.ds(pl.multiple_of(start + j * LANES, LANES), LANES)
-        pair = jnp.concatenate([gate_w[:, at], up_w[:, at]], axis=1)
+def fetch_columns(starts, gate_hbm, up_hbm, gate_w, up_w, sems):
+    lo, hi = starts
+    copies = []
+    for k, at in enumerate(range(lo, hi, 2 * LANES)):
+        count = min(2 * LANES, hi - at)
+        pair = []
+        for side, (src, dst) in enumerate(((gate_hbm, gate_w), (up_hbm, up_w))):
+            part = src.at[:, pl.ds(at, count)]
+            pair.append(pltpu.make_async_copy(part, dst.at[:, pl.ds(at - lo, count)], sems.at[k, side]))
+            pair[-1].start()
+        copies.append(pair)
+    return copies
+
+
+def load_kernel(start, gate_hbm, up_hbm, *refs):
+    done_ref, gate_w, up_w, sems = refs[-4:]
+    stop = start + gate_w.shape[1]
+    copies = fetch_columns((start, stop), gate_hbm, up_hbm, gate_w, up_w, sems)
+    done_ref[...] = jnp.zeros_like(done_ref)
+    for pair in copies:
+        for copy in pair:
+            copy.wait()
+
+
+def partial_pre(rows_ref, gate_w, up_w, copies, first, own_pre, send_pre):
+    for j in range(gate_w.shape[1] // LANES):
+        if copies and j % 2 == 0:
+            for copy in copies[j // 2]:
+                copy.wait()
+        here = slice(j * LANES, (j + 1) * LANES)
+        cols = slice(first + j * LANES, first + (j + 1) * LANES)
+        pair = jnp.concatenate([gate_w[:, here], up_w[:, here]], axis=1)
         both = dot_nn(rows_ref[...], pair)
         for side in range(2):
             value = both[:, side * LANES : (side + 1) * LANES]
             own_pre[side, :, cols] = value
             send_pre[side, :, cols] = value.astype(BF)
-        return 0
-
-    lax.fori_loop(0, own_pre.shape[2] // LANES, column, 0)
-
-
-def first_pre_kernel(dims, size, core_ref, own_ref, other_ref, gate_hbm, up_hbm,
-                     rows_ref, target_ref, gates_ref, gate_w, up_w, own_pre, send_pre, wide, sems):
+
+
+def first_pre_kernel(dims, core_ref, loaded_ref, own_ref, other_ref, gate_head, up_head, gate_rest, up_rest,
+                     rows_ref, target_ref, gates_ref, own_pre, send_pre, wide):
     n_dp, half, cap, blocks, unit = dims
     sources = 2 * n_dp * half
-    hid = gate_w.shape[1]
-    copies = []
-    for k, cols in enumerate((pl.ds(0, size), pl.ds(size, hid - size))):
-        for side, (src, dst) in enumerate(((gate_hbm, gate_w), (up_hbm, up_w))):
-            copies.append(pltpu.make_async_copy(src.at[:, cols], dst.at[:, cols], sems.at[k, side]))
-    for copy in copies:
-        copy.start()
     both_cores(core_ref, own_ref, other_ref, wide)
     core = core_ref[0]
 
@@ -148,15 +173,13 @@
         base = blocks * cap
         target_ref[rows, :] = jnp.where(core == 0, one(base + c), one(base + cap + c))
         gates_ref[rows, :] = sum(one(base + (2 + piece) * cap + c) for piece in range(GATE_PIECES))
-    copies[0].wait()
-    copies[1].wait()
-    partial_pre(rows_ref, gate_w, up_w, 0, own_pre, send_pre)
-    copies[2].wait()
-    copies[3].wait()
-
-
-def more_pre_kernel(start, rows_ref, gate_w, up_w, own_pre, send_pre):
-    partial_pre(rows_ref, gate_w, up_w, start, own_pre, send_pre)
+    partial_pre(rows_ref, gate_head, up_head, (), 0, own_pre, send_pre)
+    partial_pre(rows_ref, gate_rest, up_rest, (), gate_head.shape[1], own_pre, send_pre)
+
+
+def more_pre_kernel(start, rows_ref, gate_hbm, up_hbm, own_pre, send_pre, gate_w, up_w, sems):
+    copies = fetch_columns((start, start + own_pre.shape[2]), gate_hbm, up_hbm, gate_w, up_w, sems)
+    partial_pre(rows_ref, gate_w, up_w, copies, 0, own_pre, send_pre)
 
 
 def down_kernel(dims, start, last, core_ref, own_ref, got_ref, down_w, *refs):
@@ -192,7 +215,7 @@
                     out_refs[0][both, :] = part
             return 0
 
-        lax.fori_loop(0, half // 2, column, 0)
+        lax.fori_loop(0, half // 2, column, 0, unroll=True)
 
 
 def cotangent_kernel(parts, got_ref, gates_ref, target_ref, out_ref):
@@ -215,7 +238,7 @@
         send_out[:, cols] = value.astype(BF)
         return 0
 
-    lax.fori_loop(0, own_out.shape[1] // LANES, column, 0)
+    lax.fori_loop(0, own_out.shape[1] // LANES, column, 0, unroll=True)
 
 
 def first_grad_hidden_kernel(start, core_ref, own_ref, other_ref, down_w, cot, own_out, send_out):
@@ -260,7 +283,7 @@
                 wide[pl.ds((2 * j + k) * cap + c, sources, stride=blocks * cap), :] = piece
         return 0
 
-    lax.fori_loop(0, blocks // 2, column, 0)
+    lax.fori_loop(0, blocks // 2, column, 0, unroll=True)
     if last:
         keep_ref, send_ref, _ = out_refs
         size = keep_ref.shape[0]
@@ -280,20 +303,26 @@
         lo += size
 
 
-def token_grad_kernel(dims, ids_ref, got_ref, out_ref, rows):
+def token_grad_kernel(dims, ids_ref, got_ref, out_hbm, rows, out, sems):
     n_dp, half, cap, blocks, unit = dims
     size = blocks * cap
+    width = blocks * LANES
+    pick = select_rows(ids_ref).astype(BF)
     rows[...] = jnp.zeros_like(rows)
+    copies = []
     for d in range(n_dp):
         total = got_ref[d * half * size : (d * half + 1) * size, :].astype(F32)
         for h in range(1, half):
             base = (d * half + h) * size
             total = total + got_ref[base : base + size, :].astype(F32)
         for q in range(blocks):
-            lo = (d * blocks + q) * LANES
-            rows[0:cap, lo : lo + LANES] = total[q * cap : (q + 1) * cap, :]
-    pick = select_rows(ids_ref).astype(BF)
-    out_ref[...] = dot_tn(pick, rows[...].astype(BF)).astype(out_ref.dtype)
+            rows[0:cap, q * LANES : (q + 1) * LANES] = total[q * cap : (q + 1) * cap, :]
+        cols = slice(d * width, (d + 1) * width)
+        out[:, cols] = dot_tn(pick, rows[...].astype(BF)).astype(out.dtype)
+        copies.append(pltpu.make_async_copy(out.at[:, cols], out_hbm.at[:, cols], sems.at[d]))
+        copies[-1].start()
+    for copy in copies:
+        copy.wait()
 
 
 def fast_shards(n_dp, n_expert, cap, tokens, expert_ids, gate_values, w_gate, w_up, w_down, target):
@@ -344,33 +373,45 @@
         limit=60,
         name="route",
     )
-    own = over_slice(outgoing)
+    first = -(-hid // (2 * LANES)) * LANES
+    head = 2 * LANES
+
+    def load(start, size, after=()):
+        return call(
+            functools.partial(load_kernel, start),
+            (sds((8, LANES), F32), sds((width, size), w_gate.dtype), sds((width, size), w_up.dtype)),
+            (w_gate, w_up, *after),
+            [HBM] * 2 + [VMEM] * len(after),
+            [pltpu.SemaphoreType.DMA((-(-size // (2 * LANES)), 2))],
+            limit=50,
+            flops=1_000_000_000,
+            moved=8 * width * size,
+            name="load_weights",
+        )
+
+    loaded, *weights = load(0, head)
+    own, loaded = lax.optimization_barrier((over_slice(outgoing), loaded))
+    loaded, *more = load(head, first - head, (loaded,))
+    weights += more
     other = other_core(own)
-    first = -(-hid // (2 * LANES)) * LANES
     chunks = [(0, first), (first, hid - first)]
     last = len(chunks) - 1
     pres = []
     for start, size in chunks:
         outs = (sds((2, rows, size), F32), sds((2, rows, size), BF))
         cost = dict(flops=8 * rows * width * size, moved=4 * width * size)
+        fetched = [
+            pltpu.VMEM((width, size), w_gate.dtype),
+            pltpu.VMEM((width, size), w_up.dtype),
+            pltpu.SemaphoreType.DMA((-(-size // (2 * LANES)), 2)),
+        ]
         if start == 0:
-            all_rows, all_target, all_gates, gate_w, up_w, *pre = call(
-                functools.partial(first_pre_kernel, dims, size),
-                (
-                    sds((rows, width), BF),
-                    sds((rows, LANES), F32),
-                    sds((rows, LANES), F32),
-                    sds(w_gate.shape, w_gate.dtype),
-                    sds(w_up.shape, w_up.dtype),
-                    *outs,
-                ),
-                (core, own, other, w_gate, w_up),
-                [SMEM] + [VMEM] * 2 + [HBM] * 2,
-                [
-                    pltpu.VMEM((sources * unit, LANES), F32),
-                    pltpu.SemaphoreType.DMA((2, 2)),
-                ],
-                limit=44,
+            all_rows, all_target, all_gates, *pre = call(
+                functools.partial(first_pre_kernel, dims),
+                (sds((rows, width), BF), sds((rows, LANES), F32), sds((rows, LANES), F32), *outs),
+                (core, loaded, own, other, *weights),
+                [SMEM] + [VMEM] * 7,
+                [pltpu.VMEM((sources * unit, LANES), F32)],
                 name="pre_activations",
                 **cost,
             )
@@ -378,8 +419,10 @@
             pre = call(
                 functools.partial(more_pre_kernel, start),
                 outs,
-                (all_rows, gate_w, up_w),
-                [VMEM] * 3,
+                (all_rows, w_gate, w_up),
+                [VMEM] + [HBM] * 2,
+                fetched,
+                limit=50,
                 name="pre_activations",
                 **cost,
             )
@@ -402,7 +445,7 @@
         )
         saved.append((up_deriv, act))
     keep, send = total
-    chip_out = (keep + other_core(send).astype(F32)).astype(BF)
+    chip_out = add_cores(keep, other_core(send))
     cot = call(
         functools.partial(cotangent_kernel, half),
         sds((half * rows, LANES), BF),
@@ -446,7 +489,7 @@
         gate_pre_grad, up_pre_grad, *total = call(
             functools.partial(row_grad_kernel, dims, start, k == last),
             (sds((rows, size), BF), sds((rows, size), BF), *outs),
-            (core, *grads[k], *saved[k], gate_w, up_w, *total),
+            (core, *grads[k], *saved[k], w_gate, w_up, *total),
             [SMEM] + [VMEM] * (6 + len(total)),
             scratch,
             flops=8 * rows * width * size,
@@ -455,7 +498,7 @@
         )
         pre_grads.append((gate_pre_grad, up_pre_grad))
     keep, send = total
-    chip_rows = (keep + other_core(send).astype(F32)).astype(BF)
+    chip_rows = add_cores(keep, other_core(send))
     got_rows = over_slice(chip_rows)
     pre_grads = [pair[0] for pair in pre_grads] + [pair[1] for pair in pre_grads]
     tile = 256
@@ -477,7 +520,12 @@
         sds((tok_rows, features), tokens.dtype),
         (ids, got_rows),
         [VMEM] * 2,
-        [pltpu.VMEM((16, features), F32)],
+        [
+            pltpu.VMEM((16, width), F32),
+            pltpu.VMEM((tok_rows, features), tokens.dtype),
+            pltpu.SemaphoreType.DMA((n_dp,)),
+        ],
+        out_spec=HBM,
         name="token_grad",
     )
     return token_grad, gate_grad, up_grad
@@ -597,6 +645,7 @@
             and n_expert % 4 == 0
             and width == n_expert * LANES
             and hid % LANES == 0
+            and hid > 4 * LANES
             and n_dp * n_expert % 16 == 0
             and cap <= 8
             and tok_rows % LANES == 0

time: 91.8 us -> 86.3 us (0.940)
  blocking collectives: 40.2 us -> 22 us
  starting transfers between devices: 7.98 us -> 16.3 us
  waiting for transfers between devices: 17 us -> 23.8 us
  Pallas kernels: 24.6 us -> 22.9 us
    all_to_all x1 -> x0, blocking collectives: 18.2 us -> none  [over_slice(): lax.all_to_all(x, ('dp', 'expert'), 0, 0, axis_index_groups=slice_groups,...]
    all_to_all x1 -> x2, starting transfers between devices: 3.52 us -> 11.8 us  [over_slice(): lax.all_to_all(x, ('dp', 'expert'), 0, 0, axis_index_groups=slice_groups,...]
    all_to_all x1 -> x2, waiting for transfers between devices: 3.19 us -> 11.5 us  [over_slice(): lax.all_to_all(x, ('dp', 'expert'), 0, 0, axis_index_groups=slice_groups,...]
    pallas_call x11 -> x15, Pallas kernels: 18.9 us -> 17.2 us  [call(): pl.pallas_call(body, out_shape=outs, in_specs=specs, out_specs=jax.tree.m...]
    ppermute x4, waiting for transfers between devices: 5.83 us -> 4.3 us  [other_core(): return lax.ppermute(x, 'expert', [(i, i ^ 1) for i in range(n_expert)])]
  transfers between devices with their start and end apart: 9 -> 10, of which waited for: 8 -> 8; matrix products, arithmetic and copies ran while one was open for 0% -> 0% of each run, Pallas kernels for 13% -> 16%
where the time goes in v3:
time: 86.3 us; the launch traced here: 85.8 us
  waiting for transfers between devices  23.8 us (28%)
  Pallas kernels  22.9 us (27%)
  blocking collectives  22 us (25%)
  starting transfers between devices  16.3 us (19%)
    all_to_all x2, blocking collectives, over_plane(): lax.all_to_all(x, 'expert', 0, 0, axis_index_groups=plane, tiled=True)  22 us
    pallas_call x15, Pallas kernels, call(): pl.pallas_call(body, out_shape=outs, in_specs=specs, out_specs=jax.tree.m...  17.2 us
    all_to_all x2, starting transfers between devices, over_slice(): lax.all_to_all(x, ('dp', 'expert'), 0, 0, axis_index_groups=slice_groups,...  11.8 us
    all_to_all x2, waiting for transfers between devices, over_slice(): lax.all_to_all(x, ('dp', 'expert'), 0, 0, axis_index_groups=slice_groups,...  11.5 us
    ppermute x4, waiting for transfers between devices, other_dp(): return lax.ppermute(x, 'dp', [(0, 1), (1, 0)])  8.01 us
    pallas_call x1, Pallas kernels, fast_shards(): pl.pallas_call(functools.partial(weight_grad_kernel, len(chunks)), out_sh...  5.72 us
    ppermute x4, starting transfers between devices, other_dp(): return lax.ppermute(x, 'dp', [(0, 1), (1, 0)])  4.31 us
    ppermute x4, waiting for transfers between devices, other_core(): return lax.ppermute(x, 'expert', [(i, i ^ 1) for i in range(n_expert)])  4.3 us
  transfers between devices with their start and end apart: 10, of which 8 were waited for; matrix products, arithmetic and copies ran while one was open for 0% of the time, Pallas kernels for 16%

profile of v3, /device:TPU:0, one launch (start us, length us, event | category | flops | bytes accessed | tf_op | source)
XLA Modules:
  0.0 85.8 jit_solution(4301894249080063321)
XLA Ops:
  0.6 2.6 %route.1 = bf16[1024,128]{1,0:T(8,128)(2,1)} custom-call(s32[2,128]{1,0:T(2,128)} %bitcast.19, f32[2,128]{1,0:T(2,128)} %bitcast.22, bf16[128,4096]{1,0:T(8,128)(2,1)} %tokens_hbm.1, bf16[128,4096]{1,0:T(8,128)(2,1)} %target_hbm.1), custom_call_target="tpu_custom_call" | custom-call | tf_op jit(solution)/shard_map/route/pallas_call | solution.py:37
  3.2 8.3 %all-to-all-start = ((bf16[16,64,128]{2,1,0:T(8,128)(2,1)}), bf16[16,64,128]{2,1,0:T(8,128)(2,1)S(1)}, u32[]{:S(2)}, u32[]{:S(2)}) async-start(bf16[16,64,128]{2,1,0:T(8,128)(2,1)} %bitcast.21), calls=%async_computation | async-start | bytes 524288 | tf_op jit(solution)/shard_map/all_to_all | solution.py:355
  11.6 1.6 %load_weights.2 = (f32[8,128]{1,0:T(8,128)S(1)}, bf16[2048,256]{1,0:T(8,128)(2,1)S(1)}, bf16[2048,256]{1,0:T(8,128)(2,1)S(1)}) custom-call(bf16[2048,896]{1,0:T(8,128)(2,1)} %gate_w.3, bf16[2048,896]{1,0:T(8,128)(2,1)} %up_w.3), custom_call_target="tpu_custom_call" | custom-call | flops 1000000000 | bytes 4194304 | tf_op jit(solution)/shard_map/load_weights/pallas_call | solution.py:37
  13.2 8.3 %all-to-all-done = bf16[16,64,128]{2,1,0:T(8,128)(2,1)S(1)} async-done(((bf16[16,64,128]{2,1,0:T(8,128)(2,1)}), bf16[16,64,128]{2,1,0:T(8,128)(2,1)S(1)}, u32[]{:S(2)}, u32[]{:S(2)}) %all-to-all-start) | async-done | bytes 262176 | tf_op jit(solution)/shard_map/all_to_all | solution.py:355
  21.4 0.0 collective-permute-start
  21.4 1.6 %load_weights.3 = (f32[8,128]{1,0:T(8,128)S(1)}, bf16[2048,256]{1,0:T(8,128)(2,1)S(1)}, bf16[2048,256]{1,0:T(8,128)(2,1)S(1)}) custom-call(bf16[2048,896]{1,0:T(8,128)(2,1)} %gate_w.3, bf16[2048,896]{1,0:T(8,128)(2,1)} %up_w.3, f32[8,128]{1,0:T(8,128)S(1)} %get-tuple-element.40.refs_0_), custom_call_target="tpu_custom_call" | custom-call | flops 1000000000 | bytes 4194304 | tf_op jit(solution)/shard_map/load_weights/pallas_call | solution.py:37
  23.0 0.0 collective-permute-done.other_ref
  23.0 1.3 %pre_activations.2 = (bf16[96,2048]{1,0:T(8,128)(2,1)S(1)}, f32[96,128]{1,0:T(8,128)S(1)}, f32[96,128]{1,0:T(8,128)S(1)}, f32[2,96,512]{2,1,0:T(8,128)S(1)}, bf16[2,96,512]{2,1,0:T(8,128)(2,1)S(1)}) custom-call(s32[1]{0:T(128)} %bitcast.1.core_ref, f32[8,128]{1,0:T(8,128)S(1)} %get-tuple-element.41.loaded_ref, bf16[1024,128]{1,0:T(8,128)(2,1)S(1)} %bitcast.12, ...), custom_call_target="tpu_custom_call" | custom-call | flops 805306368 | bytes 4194304 | tf_op jit(solution)/shard_map/pre_activations/pallas_call | solution.py:37
  24.4 1.2 %collective-permute-start.2 = (bf16[2,96,512]{2,1,0:T(8,128)(2,1)S(1)}, bf16[2,96,512]{2,1,0:T(8,128)(2,1)S(1)}, u32[]{:S(2)}, u32[]{:S(2)}) collective-permute-start(bf16[2,96,512]{2,1,0:T(8,128)(2,1)S(1)} %get-tuple-element.51), channel_id=1, source_target_pairs={{0,16},{16,0},{1,17},{17,1},{2,18},{18,2},{3,19},{19,3},{4,20},{20... | collective-permute-start | bytes 589832 | tf_op jit(solution)/shard_map/ppermute | solution.py:349
  25.5 0.0 copy-start.2
  25.5 2.7 %pre_activations.3 = (f32[2,96,384]{2,1,0:T(8,128)S(1)}, bf16[2,96,384]{2,1,0:T(8,128)(2,1)S(1)}) custom-call(bf16[96,2048]{1,0:T(8,128)(2,1)S(1)} %get-tuple-element.47.rows_ref, bf16[2048,896]{1,0:T(8,128)(2,1)} %gate_w.3, bf16[2048,896]{1,0:T(8,128)(2,1)} %up_w.3), custom_call_target="tpu_custom_call" | custom-call | flops 603979776 | bytes 3145728 | tf_op jit(solution)/shard_map/pre_activations/pallas_call | solution.py:37
  28.3 1.0 %collective-permute-start.1 = (bf16[2,96,384]{2,1,0:T(8,128)(2,1)S(1)}, bf16[2,96,384]{2,1,0:T(8,128)(2,1)S(1)}, u32[]{:S(2)}, u32[]{:S(2)}) collective-permute-start(bf16[2,96,384]{2,1,0:T(8,128)(2,1)S(1)} %get-tuple-element.49), channel_id=1, source_target_pairs={{0,16},{16,0},{1,17},{17,1},{2,18},{18,2},{3,19},{19,3},{4,20},{20... | collective-permute-start | bytes 442376 | tf_op jit(solution)/shard_map/ppermute | solution.py:349
  29.3 2.9 %collective-permute-done.2.got_ref = bf16[2,96,512]{2,1,0:T(8,128)(2,1)S(1)} collective-permute-done((bf16[2,96,512]{2,1,0:T(8,128)(2,1)S(1)}, bf16[2,96,512]{2,1,0:T(8,128)(2,1)S(1)}, u32[]{:S(2)}, u32[]{:S(2)}) %collective-permute-start.2) | collective-permute-done | bytes 196640 | tf_op jit(solution)/shard_map/ppermute | solution.py:349
  32.1 0.0 copy-done.2
  32.1 0.5 down.2
  32.7 2.2 %collective-permute-done.1.got_ref = bf16[2,96,384]{2,1,0:T(8,128)(2,1)S(1)} collective-permute-done((bf16[2,96,384]{2,1,0:T(8,128)(2,1)S(1)}, bf16[2,96,384]{2,1,0:T(8,128)(2,1)S(1)}, u32[]{:S(2)}, u32[]{:S(2)}) %collective-permute-start.1) | collective-permute-done | bytes 147488 | tf_op jit(solution)/shard_map/ppermute | solution.py:349
  34.9 0.5 down.3
  35.4 0.1 collective-permute-start.3
  35.5 1.4 %collective-permute-done.3.got_ref = bf16[768,128]{1,0:T(8,128)(2,1)S(1)} collective-permute-done((bf16[768,128]{1,0:T(8,128)(2,1)S(1)}, bf16[768,128]{1,0:T(8,128)(2,1)S(1)}, u32[]{:S(2)}, u32[]{:S(2)}) %collective-permute-start.3) | collective-permute-done | bytes 196640 | tf_op jit(solution)/shard_map/ppermute | solution.py:346
  36.9 11.3 %all_to_all.45 = bf16[8,96,128]{2,1,0:T(8,128)(2,1)S(1)} all-to-all(bf16[8,96,128]{2,1,0:T(8,128)(2,1)S(1)} %bitcast.17), channel_id=1, replica_groups={{0,2,4,6,8,10,12,14},{1,3,5,7,9,11,13,15},{16,18,20,22,24,26,28,30},{17..., dimensions={0} | all-to-all | bytes 393216 | tf_op jit(solution)/shard_map/all_to_all | solution.py:352
  48.3 10.7 %all_to_all.46 = bf16[8,96,128]{2,1,0:T(8,128)(2,1)S(1)} all-to-all(bf16[8,96,128]{2,1,0:T(8,128)(2,1)S(1)} %bitcast.16), channel_id=1, replica_groups={{0,2,4,6,8,10,12,14},{1,3,5,7,9,11,13,15},{16,18,20,22,24,26,28,30},{17..., dimensions={0} | all-to-all | bytes 393216 | tf_op jit(solution)/shard_map/all_to_all | solution.py:352
  59.0 0.0 copy-start
  59.0 0.0 copy-start.1
  59.0 0.0 collective-permute-start.4
  59.0 1.4 %collective-permute-done.4.other_ref = bf16[768,128]{1,0:T(8,128)(2,1)S(1)} collective-permute-done((bf16[768,128]{1,0:T(8,128)(2,1)S(1)}, bf16[768,128]{1,0:T(8,128)(2,1)S(1)}, u32[]{:S(2)}, u32[]{:S(2)}) %collective-permute-start.4) | collective-permute-done | bytes 196640 | tf_op jit(solution)/shard_map/ppermute | solution.py:346
  60.5 0.9 %grad_hidden.2 = (bf16[96,2048]{1,0:T(8,128)(2,1)S(1)}, f32[96,512]{1,0:T(8,128)S(1)}, bf16[96,512]{1,0:T(8,128)(2,1)S(1)}) custom-call(s32[1]{0:T(128)} %bitcast.1.core_ref, bf16[768,128]{1,0:T(8,128)(2,1)S(1)} %bitcast.14, bf16[768,128]{1,0:T(8,128)(2,1)S(1)} %collective-permute-done.4.other_ref, bf16[896,2048]{1,0:T(8,128)(2,1)S(1)} %copy-done.2), custom_call_target="tpu_custom_call" | custom-call | flops 402653184 | bytes 2097152 | tf_op jit(solution)/shard_map/grad_hidden/pallas_call | solution.py:37
  61.3 0.8 collective-permute-start.6
  62.1 0.6 grad_hidden.3
  62.7 1.4 %collective-permute-start.5 = (bf16[96,384]{1,0:T(8,128)(2,1)S(1)}, bf16[96,384]{1,0:T(8,128)(2,1)S(1)}, u32[]{:S(2)}, u32[]{:S(2)}) collective-permute-start(bf16[96,384]{1,0:T(8,128)(2,1)S(1)} %get-tuple-element.59), channel_id=1, source_target_pairs={{0,16},{16,0},{1,17},{17,1},{2,18},{18,2},{3,19},{19,3},{4,20},{20... | collective-permute-start | bytes 221192 | tf_op jit(solution)/shard_map/ppermute | solution.py:349
  64.1 2.9 %collective-permute-done.6.got_ref = bf16[96,512]{1,0:T(8,128)(2,1)S(1)} collective-permute-done((bf16[96,512]{1,0:T(8,128)(2,1)S(1)}, bf16[96,512]{1,0:T(8,128)(2,1)S(1)}, u32[]{:S(2)}, u32[]{:S(2)}) %collective-permute-start.6) | collective-permute-done | bytes 98336 | tf_op jit(solution)/shard_map/ppermute | solution.py:349
  67.0 0.0 copy-done
  67.0 0.0 copy-done.1
  67.0 1.4 %row_grad.2 = (bf16[96,512]{1,0:T(8,128)(2,1)S(1)}, bf16[96,512]{1,0:T(8,128)(2,1)S(1)}, f32[96,2048]{1,0:T(8,128)S(1)}) custom-call(s32[1]{0:T(128)} %bitcast.1.core_ref, f32[96,512]{1,0:T(8,128)S(1)} %get-tuple-element.62.own_ref, bf16[96,512]{1,0:T(8,128)(2,1)S(1)} %collective-permute-done.6.got_ref, f32[96,512]{1,0:T(8,128)S(1)} %get-tuple-element.64.up_deriv, ...), custom_call_target="tpu_custom_call" | custom-call | flops 805306368 | bytes 4194304 | tf_op jit(solution)/shard_map/row_grad/pallas_call | solution.py:37
  68.4 0.0 collective-permute-done.5.got_ref
  68.4 1.3 %row_grad.3 = (bf16[96,384]{1,0:T(8,128)(2,1)S(1)}, bf16[96,384]{1,0:T(8,128)(2,1)S(1)}, f32[768,128]{1,0:T(8,128)S(1)}, bf16[768,128]{1,0:T(8,128)(2,1)S(1)}) custom-call(s32[1]{0:T(128)} %bitcast.1.core_ref, f32[96,384]{1,0:T(8,128)S(1)} %get-tuple-element.58.own_ref, bf16[96,384]{1,0:T(8,128)(2,1)S(1)} %collective-permute-done.5.got_ref, ...), custom_call_target="tpu_custom_call" | custom-call | flops 603979776 | bytes 3145728 | tf_op jit(solution)/shard_map/row_grad/pallas_call | solution.py:37
  69.7 0.0 copy-start.3
  69.7 0.1 collective-permute-start.7
  69.8 1.4 %collective-permute-done.7.got_ref = bf16[768,128]{1,0:T(8,128)(2,1)S(1)} collective-permute-done((bf16[768,128]{1,0:T(8,128)(2,1)S(1)}, bf16[768,128]{1,0:T(8,128)(2,1)S(1)}, u32[]{:S(2)}, u32[]{:S(2)}) %collective-permute-start.7) | collective-permute-done | bytes 196640 | tf_op jit(solution)/shard_map/ppermute | solution.py:346
  71.2 0.7 add_cores.3
  71.9 3.5 %all-to-all-start.3 = ((bf16[16,48,128]{2,1,0:T(8,128)(2,1)}), bf16[16,48,128]{2,1,0:T(8,128)(2,1)S(1)}, u32[]{:S(2)}, u32[]{:S(2)}) async-start(bf16[16,48,128]{2,1,0:T(8,128)(2,1)} %bitcast.9), calls=%async_computation.3 | async-start | bytes 393216 | tf_op jit(solution)/shard_map/all_to_all | solution.py:355
  75.5 5.7 %weight_grads.1 = (bf16[2048,896]{1,0:T(8,128)(2,1)}, bf16[2048,896]{1,0:T(8,128)(2,1)}) custom-call(bf16[96,2048]{1,0:T(8,128)(2,1)S(1)} %get-tuple-element.47.rows_ref, bf16[96,512]{1,0:T(8,128)(2,1)S(1)} %get-tuple-element.69.refs_0_, bf16[96,384]{1,0:T(8,128)(2,1)S(1)} %get-tuple-element.70.refs_1_, bf16[96,512]{1,0:T(8,128)(2,1)S(1)} %get-tuple-element.71.refs_2_, ...), custom_call_target="tpu_custom_call" | custom-call | flops 704643072 | bytes 7340032 | tf_op jit(solution)/shard_map/weight_grads/pallas_call | solution.py:505
  81.2 3.2 %all-to-all-done.3 = bf16[16,48,128]{2,1,0:T(8,128)(2,1)S(1)} async-done(((bf16[16,48,128]{2,1,0:T(8,128)(2,1)}), bf16[16,48,128]{2,1,0:T(8,128)(2,1)S(1)}, u32[]{:S(2)}, u32[]{:S(2)}) %all-to-all-start.3) | async-done | bytes 196640 | tf_op jit(solution)/shard_map/all_to_all | solution.py:355
  84.4 0.0 copy-done.3
  84.4 1.4 %token_grad.1 = bf16[128,4096]{1,0:T(8,128)(2,1)} custom-call(s32[2,128]{1,0:T(2,128)S(1)} %bitcast.20, bf16[768,128]{1,0:T(8,128)(2,1)S(1)} %bitcast.18), custom_call_target="tpu_custom_call" | custom-call | tf_op jit(solution)/shard_map/token_grad/pallas_call | solution.py:37
  (2 shorter events, 0.1 us)
Async XLA Ops:
  3.2 18.2 %all-to-all-start = ((bf16[16,64,128]{2,1,0:T(8,128)(2,1)}), bf16[16,64,128]{2,1,0:T(8,128)(2,1)S(1)}, u32[]{:S(2)}, u32[]{:S(2)}) async-start(bf16[16,64,128]{2,1,0:T(8,128)(2,1)} %bitcast.21), calls=%async_computation | async-start | bytes 524288 | tf_op jit(solution)/shard_map/all_to_all | solution.py:355
  21.4 1.6 %collective-permute-start = (bf16[1024,128]{1,0:T(8,128)(2,1)S(1)}, bf16[1024,128]{1,0:T(8,128)(2,1)S(1)}, u32[]{:S(2)}, u32[]{:S(2)}) collective-permute-start(bf16[1024,128]{1,0:T(8,128)(2,1)S(1)} %bitcast.11), channel_id=1, source_target_pairs={{0,1},{1,0},{2,3},{3,2},{4,5},{5,4},{6,7},{7,6},{8,9},{9,8},{10,11... | collective-permute-start | bytes 786440 | tf_op jit(solution)/shard_map/ppermute | solution.py:346
  24.4 7.8 %collective-permute-start.2 = (bf16[2,96,512]{2,1,0:T(8,128)(2,1)S(1)}, bf16[2,96,512]{2,1,0:T(8,128)(2,1)S(1)}, u32[]{:S(2)}, u32[]{:S(2)}) collective-permute-start(bf16[2,96,512]{2,1,0:T(8,128)(2,1)S(1)} %get-tuple-element.51), channel_id=1, source_target_pairs={{0,16},{16,0},{1,17},{17,1},{2,18},{18,2},{3,19},{19,3},{4,20},{20... | collective-permute-start | bytes 589832 | tf_op jit(solution)/shard_map/ppermute | solution.py:349
  25.5 6.6 %copy-start.2 = (bf16[896,2048]{1,0:T(8,128)(2,1)S(1)}, bf16[896,2048]{1,0:T(8,128)(2,1)}, u32[]{:S(2)}) copy-start(bf16[896,2048]{1,0:T(8,128)(2,1)} %down_w.7) | copy-start | bytes 11010052
  28.3 6.6 %collective-permute-start.1 = (bf16[2,96,384]{2,1,0:T(8,128)(2,1)S(1)}, bf16[2,96,384]{2,1,0:T(8,128)(2,1)S(1)}, u32[]{:S(2)}, u32[]{:S(2)}) collective-permute-start(bf16[2,96,384]{2,1,0:T(8,128)(2,1)S(1)} %get-tuple-element.49), channel_id=1, source_target_pairs={{0,16},{16,0},{1,17},{17,1},{2,18},{18,2},{3,19},{19,3},{4,20},{20... | collective-permute-start | bytes 442376 | tf_op jit(solution)/shard_map/ppermute | solution.py:349
  35.4 1.5 %collective-permute-start.3 = (bf16[768,128]{1,0:T(8,128)(2,1)S(1)}, bf16[768,128]{1,0:T(8,128)(2,1)S(1)}, u32[]{:S(2)}, u32[]{:S(2)}) collective-permute-start(bf16[768,128]{1,0:T(8,128)(2,1)S(1)} %get-tuple-element.54), channel_id=1, source_target_pairs={{0,1},{1,0},{2,3},{3,2},{4,5},{5,4},{6,7},{7,6},{8,9},{9,8},{10,11... | collective-permute-start | bytes 589832 | tf_op jit(solution)/shard_map/ppermute | solution.py:346
  59.0 8.0 %copy-start = (bf16[2048,896]{1,0:T(8,128)(2,1)S(1)}, bf16[2048,896]{1,0:T(8,128)(2,1)}, u32[]{:S(2)}) copy-start(bf16[2048,896]{1,0:T(8,128)(2,1)} %gate_w.3) | copy-start | bytes 11010052
  59.0 8.0 %copy-start.1 = (bf16[2048,896]{1,0:T(8,128)(2,1)S(1)}, bf16[2048,896]{1,0:T(8,128)(2,1)}, u32[]{:S(2)}) copy-start(bf16[2048,896]{1,0:T(8,128)(2,1)} %up_w.3) | copy-start | bytes 11010052
  59.0 1.4 %collective-permute-start.4 = (bf16[768,128]{1,0:T(8,128)(2,1)S(1)}, bf16[768,128]{1,0:T(8,128)(2,1)S(1)}, u32[]{:S(2)}, u32[]{:S(2)}) collective-permute-start(bf16[768,128]{1,0:T(8,128)(2,1)S(1)} %bitcast.13), channel_id=1, source_target_pairs={{0,1},{1,0},{2,3},{3,2},{4,5},{5,4},{6,7},{7,6},{8,9},{9,8},{10,11... | collective-permute-start | bytes 589832 | tf_op jit(solution)/shard_map/ppermute | solution.py:346
  61.3 5.7 %collective-permute-start.6 = (bf16[96,512]{1,0:T(8,128)(2,1)S(1)}, bf16[96,512]{1,0:T(8,128)(2,1)S(1)}, u32[]{:S(2)}, u32[]{:S(2)}) collective-permute-start(bf16[96,512]{1,0:T(8,128)(2,1)S(1)} %get-tuple-element.63), channel_id=1, source_target_pairs={{0,16},{16,0},{1,17},{17,1},{2,18},{18,2},{3,19},{19,3},{4,20},{20... | collective-permute-start | bytes 294920 | tf_op jit(solution)/shard_map/ppermute | solution.py:349
  62.7 5.7 %collective-permute-start.5 = (bf16[96,384]{1,0:T(8,128)(2,1)S(1)}, bf16[96,384]{1,0:T(8,128)(2,1)S(1)}, u32[]{:S(2)}, u32[]{:S(2)}) collective-permute-start(bf16[96,384]{1,0:T(8,128)(2,1)S(1)} %get-tuple-element.59), channel_id=1, source_target_pairs={{0,16},{16,0},{1,17},{17,1},{2,18},{18,2},{3,19},{19,3},{4,20},{20... | collective-permute-start | bytes 221192 | tf_op jit(solution)/shard_map/ppermute | solution.py:349
  69.7 14.7 %copy-start.3 = (s32[128,2]{0,1:T(2,128)S(1)}, s32[128,2]{0,1:T(2,128)}, u32[]{:S(2)}) copy-start(s32[128,2]{0,1:T(2,128)} %param.8) | copy-start | bytes 3076
  69.7 1.5 %collective-permute-start.7 = (bf16[768,128]{1,0:T(8,128)(2,1)S(1)}, bf16[768,128]{1,0:T(8,128)(2,1)S(1)}, u32[]{:S(2)}, u32[]{:S(2)}) collective-permute-start(bf16[768,128]{1,0:T(8,128)(2,1)S(1)} %get-tuple-element.68), channel_id=1, source_target_pairs={{0,1},{1,0},{2,3},{3,2},{4,5},{5,4},{6,7},{7,6},{8,9},{9,8},{10,11... | collective-permute-start | bytes 589832 | tf_op jit(solution)/shard_map/ppermute | solution.py:346
  71.9 12.4 %all-to-all-start.3 = ((bf16[16,48,128]{2,1,0:T(8,128)(2,1)}), bf16[16,48,128]{2,1,0:T(8,128)(2,1)S(1)}, u32[]{:S(2)}, u32[]{:S(2)}) async-start(bf16[16,48,128]{2,1,0:T(8,128)(2,1)} %bitcast.9), calls=%async_computation.3 | async-start | bytes 393216 | tf_op jit(solution)/shard_map/all_to_all | solution.py:355

commit v4 on v3

--- a/solution.py
+++ b/solution.py
@@ -31,6 +31,10 @@
 
 def dot_tn(a, b):
     return lax.dot_general(a, b, (((0,), (0,)), ((), ())), preferred_element_type=F32)
+
+
+def in_hbm(*arrays):
+    return tuple(pltpu.with_memory_space_constraint(x, pltpu.HBM) for x in arrays)
 
 
 def call(body, outs, args, specs, scratch=(), limit=16, flops=0, moved=0, name=None, out_spec=VMEM):
@@ -69,12 +73,12 @@
 def route_kernel(dims, ids_hbm, gates_hbm, tokens_hbm, target_hbm, out_ref,
                  ids_ref, gates_ref, tokens_ref, target_ref, tok, tgt, head, tail, sems):
     n_dp, half, cap, blocks, unit = dims
-    pairs = (
-        (ids_hbm, ids_ref),
-        (gates_hbm, gates_ref),
-        (tokens_hbm, tokens_ref),
-        (target_hbm, target_ref),
-    )
+    width = blocks * LANES
+    pairs = [(ids_hbm, ids_ref), (gates_hbm, gates_ref)]
+    for hbm, ref in ((tokens_hbm, tokens_ref), (target_hbm, target_ref)):
+        for d in range(n_dp):
+            cols = slice(d * width, (d + 1) * width)
+            pairs.append((hbm.at[:, cols], ref.at[:, cols]))
     copies = [pltpu.make_async_copy(src, dst, sems.at[i]) for i, (src, dst) in enumerate(pairs)]
     for copy in copies:
         copy.start()
@@ -85,29 +89,33 @@
     live_gates = jnp.sum(jnp.where(ids_ref[...] < EXPERTS, gates_ref[...], 0.0), axis=0, keepdims=True)
     gate = jnp.sum(chosen * live_gates, axis=1, keepdims=True)
     pick = chosen.astype(BF)
-    copies[2].wait()
-    tok[...] = dot_nn(pick, tokens_ref[...])
-    copies[3].wait()
-    tgt[...] = dot_nn(pick, target_ref[...])
     rest = gate
     for piece in range(GATE_PIECES):
         part = rest.astype(BF).astype(F32)
         rest = rest - part
         at = (2 + piece) * cap
         tail[at : at + cap, :] = jnp.broadcast_to(part[0:cap], (cap, LANES))
-    width = blocks * LANES
+    lead = blocks * cap
     for d in range(n_dp):
+        cols = slice(d * width, (d + 1) * width)
+        copies[2 + d].wait()
+        tok[...] = dot_nn(pick, tokens_ref[:, cols])
         for q in range(blocks):
-            lo = d * width + q * LANES
-            head[q * cap : (q + 1) * cap, :] = tok[0:cap, lo : lo + LANES]
+            head[q * cap : (q + 1) * cap, :] = tok[0:cap, q * LANES : (q + 1) * LANES]
         packed = head[...].astype(BF)
         for h in range(half):
+            base = (d * half + h) * unit
+            out_ref[base : base + lead, :] = packed
+    for d in range(n_dp):
+        cols = slice(d * width, (d + 1) * width)
+        copies[2 + n_dp + d].wait()
+        tgt[...] = dot_nn(pick, target_ref[:, cols])
+        for h in range(half):
             for core in range(2):
-                lo = d * width + (core * half + h) * LANES
+                lo = (core * half + h) * LANES
                 tail[core * cap : (core + 1) * cap, :] = tgt[0:cap, lo : lo + LANES]
             base = (d * half + h) * unit
-            out_ref[base : base + blocks * cap, :] = packed
-            out_ref[base + blocks * cap : base + unit, :] = tail[...].astype(BF)
+            out_ref[base + lead : base + unit, :] = tail[...].astype(BF)
 
 
 def both_cores(core_ref, own_ref, other_ref, wide):
@@ -177,16 +185,28 @@
     partial_pre(rows_ref, gate_rest, up_rest, (), gate_head.shape[1], own_pre, send_pre)
 
 
-def more_pre_kernel(start, rows_ref, gate_hbm, up_hbm, own_pre, send_pre, gate_w, up_w, sems):
+def more_pre_kernel(start, rows_ref, gate_hbm, up_hbm, turned_ref, own_pre, send_pre, gate_w, up_w, sems):
     copies = fetch_columns((start, start + own_pre.shape[2]), gate_hbm, up_hbm, gate_w, up_w, sems)
+    turned_ref[...] = rows_ref[...].T
     partial_pre(rows_ref, gate_w, up_w, copies, 0, own_pre, send_pre)
 
 
-def down_kernel(dims, start, last, core_ref, own_ref, got_ref, down_w, *refs):
+def down_side(dims, start, lo, hidden, down_w, total_ref, side, out_ref):
     n_dp, half, cap, blocks, unit = dims
-    refs = list(refs)
-    total_ref = refs.pop(0) if start > 0 else None
-    up_deriv, act_ref, *out_refs, hidden = refs
+    rows, hid = hidden.shape
+    for j in range(half // 2):
+        cols = pl.ds(pl.multiple_of((lo + 2 * j) * LANES, 2 * LANES), 2 * LANES)
+        value = dot_nn(hidden[...], down_w[start : start + hid, cols])
+        for k in range(2):
+            part = value[:, k * LANES : (k + 1) * LANES]
+            block = 2 * j + k
+            if total_ref is not None:
+                both = side * half + block
+                part = part + total_ref[both * rows : (both + 1) * rows, :]
+            out_ref[block * rows : (block + 1) * rows, :] = part.astype(out_ref.dtype)
+
+
+def activate(own_ref, got_ref, up_deriv, act_ref, hidden):
     gate_pre = own_ref[0] + got_ref[0].astype(F32)
     up_pre = own_ref[1] + got_ref[1].astype(F32)
     sig = jax.nn.sigmoid(gate_pre)
@@ -194,28 +214,24 @@
     act_ref[...] = act
     up_deriv[...] = up_pre * (sig * (1.0 + gate_pre * (1.0 - sig)))
     hidden[...] = (act * up_pre).astype(BF)
-    rows, hid = hidden.shape
-    core = core_ref[0]
-    for side in range(2):
-
-        def column(j, _, side=side):
-            shown = core if side == 0 else 1 - core
-            lo = (shown * half + 2 * j) * LANES
-            cols = pl.ds(pl.multiple_of(lo, 2 * LANES), 2 * LANES)
-            value = dot_nn(hidden[...], down_w[start : start + hid, cols])
-            for k in range(2):
-                part = value[:, k * LANES : (k + 1) * LANES]
-                mine = pl.ds(pl.multiple_of((2 * j + k) * rows, rows), rows)
-                both = pl.ds(pl.multiple_of((side * half + 2 * j + k) * rows, rows), rows)
-                if total_ref is not None:
-                    part = part + total_ref[both, :]
-                if last:
-                    out_refs[side][mine, :] = part.astype(out_refs[side].dtype)
-                else:
-                    out_refs[0][both, :] = part
-            return 0
-
-        lax.fori_loop(0, half // 2, column, 0, unroll=True)
+
+
+def first_down_kernel(dims, start, core_ref, own_ref, got_ref, down_w, up_deriv, act_ref, total_ref, hidden):
+    half = dims[1]
+    activate(own_ref, got_ref, up_deriv, act_ref, hidden)
+    size = half * hidden.shape[0]
+    for side, core in enumerate((core_ref[0], 1 - core_ref[0])):
+        part = total_ref.at[side * size : (side + 1) * size]
+        down_side(dims, start, core * half, hidden, down_w, None, side, part)
+
+
+def send_down_kernel(dims, start, core_ref, own_ref, got_ref, down_w, total_ref, up_deriv, act_ref, hidden, send_ref):
+    activate(own_ref, got_ref, up_deriv, act_ref, hidden)
+    down_side(dims, start, (1 - core_ref[0]) * dims[1], hidden, down_w, total_ref, 1, send_ref)
+
+
+def keep_down_kernel(dims, start, core_ref, hidden, down_w, total_ref, keep_ref):
+    down_side(dims, start, core_ref[0] * dims[1], hidden, down_w, total_ref, 0, keep_ref)
 
 
 def cotangent_kernel(parts, got_ref, gates_ref, target_ref, out_ref):
@@ -229,31 +245,38 @@
         out_ref[h * rows : (h + 1) * rows, :] = value
 
 
-def partial_grad_hidden(cot, down_w, start, own_out, send_out):
-    def column(j, _):
-        cols = pl.ds(pl.multiple_of(j * LANES, LANES), LANES)
-        at = pl.ds(pl.multiple_of(start + j * LANES, LANES), LANES)
-        value = dot_nt(cot[...], down_w[at, :])
-        own_out[:, cols] = value
-        send_out[:, cols] = value.astype(BF)
-        return 0
-
-    lax.fori_loop(0, own_out.shape[1] // LANES, column, 0, unroll=True)
-
-
-def first_grad_hidden_kernel(start, core_ref, own_ref, other_ref, down_w, cot, own_out, send_out):
-    rows = cot.shape[0]
-    parts = own_ref.shape[0] // rows
-    core = core_ref[0]
-    for ref, side in ((own_ref, core), (other_ref, 1 - core)):
-        for h in range(parts):
-            lo = (side * parts + h) * LANES
-            cot[:, pl.ds(pl.multiple_of(lo, LANES), LANES)] = ref[h * rows : (h + 1) * rows, :]
-    partial_grad_hidden(cot, down_w, start, own_out, send_out)
-
-
-def more_grad_hidden_kernel(start, cot, down_w, own_out, send_out):
-    partial_grad_hidden(cot, down_w, start, own_out, send_out)
+def gather_blocks(ref, out):
+    rows = out.shape[0]
+    for h in range(out.shape[1] // LANES):
+        out[:, h * LANES : (h + 1) * LANES] = ref[h * rows : (h + 1) * rows, :]
+
+
+def half_grad_hidden(cot, core, down_w, start, total_ref, outs):
+    width = cot.shape[1]
+    cols = pl.ds(pl.multiple_of(core * width, width), width)
+    size = outs[0].shape[1]
+    for lo in range(0, size, 2 * LANES):
+        here = slice(lo, min(lo + 2 * LANES, size))
+        there = slice(start + here.start, start + here.stop)
+        value = dot_nt(cot[...], down_w[there, cols])
+        if total_ref is not None:
+            value = value + total_ref[:, there]
+        for out in outs:
+            out[:, here] = value.astype(out.dtype)
+
+
+def own_grad_hidden_kernel(core_ref, own_ref, down_w, total_ref, cot):
+    gather_blocks(own_ref, cot)
+    half_grad_hidden(cot, core_ref[0], down_w, 0, None, (total_ref,))
+
+
+def first_grad_hidden_kernel(start, core_ref, other_ref, down_w, total_ref, cot, own_out, send_out):
+    gather_blocks(other_ref, cot)
+    half_grad_hidden(cot, 1 - core_ref[0], down_w, start, total_ref, (own_out, send_out))
+
+
+def more_grad_hidden_kernel(start, core_ref, cot, down_w, total_ref, own_out, send_out):
+    half_grad_hidden(cot, 1 - core_ref[0], down_w, start, total_ref, (own_out, send_out))
 
 
 def row_grad_kernel(dims, start, last, core_ref, own_ref, got_ref, up_deriv, act_ref, gate_w, up_w, *refs):
@@ -292,15 +315,22 @@
         send_ref[...] = wide[pl.ds(pl.multiple_of((1 - core) * size, size), size), :].astype(BF)
 
 
-def weight_grad_kernel(parts, rows_ref, *refs):
-    gate_out, up_out = refs[-2:]
-    rows = rows_ref[...]
-    lo = 0
-    for k in range(parts):
-        size = refs[k].shape[1]
-        gate_out[:, lo : lo + size] = dot_tn(rows, refs[k][...]).astype(BF)
-        up_out[:, lo : lo + size] = dot_tn(rows, refs[parts + k][...]).astype(BF)
-        lo += size
+def weight_grad_kernel(parts, tile, turned_ref, *refs):
+    grads = (refs[:parts], refs[parts : 2 * parts])
+    outs, values, sems = refs[2 * parts : 2 * parts + 2], refs[2 * parts + 2 : 2 * parts + 4], refs[-1]
+    copies = []
+    for t in range(turned_ref.shape[0] // tile):
+        at = slice(t * tile, (t + 1) * tile)
+        for side in range(2):
+            lo = 0
+            for ref in grads[side]:
+                size = ref.shape[1]
+                values[side][at, lo : lo + size] = dot_nn(turned_ref[at, :], ref[...]).astype(BF)
+                lo += size
+            copies.append(pltpu.make_async_copy(values[side].at[at, :], outs[side].at[at, :], sems.at[t, side]))
+            copies[-1].start()
+    for copy in copies:
+        copy.wait()
 
 
 def token_grad_kernel(dims, ids_ref, got_ref, out_hbm, rows, out, sems):
@@ -357,20 +387,19 @@
     outgoing = call(
         functools.partial(route_kernel, dims),
         sds((peers * unit, LANES), BF),
-        (ids, gate_values.T, tokens, target),
+        in_hbm(ids, gate_values.T, tokens, target),
         [HBM] * 4,
         [
             pltpu.VMEM(ids.shape, ids.dtype),
             pltpu.VMEM(ids.shape, F32),
             pltpu.VMEM(tokens.shape, tokens.dtype),
             pltpu.VMEM(target.shape, target.dtype),
-            pltpu.VMEM((16, features), F32),
-            pltpu.VMEM((16, features), F32),
+            pltpu.VMEM((16, width), F32),
+            pltpu.VMEM((16, width), F32),
             pltpu.VMEM((blocks * cap, LANES), F32),
             pltpu.VMEM((unit - blocks * cap, LANES), F32),
-            pltpu.SemaphoreType.DMA((4,)),
+            pltpu.SemaphoreType.DMA((2 + 2 * n_dp,)),
         ],
-        limit=60,
         name="route",
     )
     first = -(-hid // (2 * LANES)) * LANES
@@ -380,10 +409,9 @@
         return call(
             functools.partial(load_kernel, start),
             (sds((8, LANES), F32), sds((width, size), w_gate.dtype), sds((width, size), w_up.dtype)),
-            (w_gate, w_up, *after),
+            (*in_hbm(w_gate, w_up), *after),
             [HBM] * 2 + [VMEM] * len(after),
             [pltpu.SemaphoreType.DMA((-(-size // (2 * LANES)), 2))],
-            limit=50,
             flops=1_000_000_000,
             moved=8 * width * size,
             name="load_weights",
@@ -416,36 +444,52 @@
                 **cost,
             )
         else:
-            pre = call(
+            turned, *pre = call(
                 functools.partial(more_pre_kernel, start),
-                outs,
-                (all_rows, w_gate, w_up),
+                (sds((width, rows), BF), *outs),
+                (all_rows, *in_hbm(w_gate, w_up)),
                 [VMEM] + [HBM] * 2,
                 fetched,
-                limit=50,
                 name="pre_activations",
                 **cost,
             )
         pres.append((pre[0], other_dp(pre[1])))
-    saved = []
-    total = ()
-    for k, (start, size) in enumerate(chunks):
-        outs = (sds((2 * half * rows, LANES), F32),)
-        if k == last:
-            outs = (sds((half * rows, LANES), F32), sds((half * rows, LANES), BF))
-        up_deriv, act, *total = call(
-            functools.partial(down_kernel, dims, start, k == last),
-            (sds((rows, size), F32), sds((rows, size), F32), *outs),
-            (core, *pres[k], w_down, *total),
-            [SMEM] + [VMEM] * (3 + len(total)),
-            [pltpu.VMEM((rows, size), BF)],
-            flops=4 * rows * width * size,
-            moved=2 * width * size,
-            name="down",
-        )
-        saved.append((up_deriv, act))
-    keep, send = total
-    chip_out = add_cores(keep, other_core(send))
+    (start, size), (start_b, size_b) = chunks
+    half_rows = half * rows
+    cost = dict(flops=4 * rows * width * size, moved=2 * width * size)
+    up_deriv, act, total = call(
+        functools.partial(first_down_kernel, dims, start),
+        (sds((rows, size), F32), sds((rows, size), F32), sds((2 * half_rows, LANES), F32)),
+        (core, *pres[0], w_down),
+        [SMEM] + [VMEM] * 3,
+        [pltpu.VMEM((rows, size), BF)],
+        name="down",
+        **cost,
+    )
+    up_deriv_b, act_b, hidden_b, send = call(
+        functools.partial(send_down_kernel, dims, start_b),
+        (
+            sds((rows, size_b), F32),
+            sds((rows, size_b), F32),
+            sds((rows, size_b), BF),
+            sds((half_rows, LANES), BF),
+        ),
+        (core, *pres[1], w_down, total),
+        [SMEM] + [VMEM] * 4,
+        name="down_send",
+        **cost,
+    )
+    sent = other_core(send)
+    keep = call(
+        functools.partial(keep_down_kernel, dims, start_b),
+        sds((half_rows, LANES), F32),
+        (core, hidden_b, w_down, total),
+        [SMEM] + [VMEM] * 3,
+        name="down_keep",
+        **cost,
+    )
+    saved = [(up_deriv, act), (up_deriv_b, act_b)]
+    chip_out = add_cores(keep, sent)
     cot = call(
         functools.partial(cotangent_kernel, half),
         sds((half * rows, LANES), BF),
@@ -455,15 +499,25 @@
     )
     own = over_plane(cot)
     other = other_core(own)
+    own_total = call(
+        own_grad_hidden_kernel,
+        sds((rows, hid), F32),
+        (core, own, w_down),
+        [SMEM] + [VMEM] * 2,
+        [pltpu.VMEM((rows, width // 2), BF)],
+        flops=2 * rows * width * hid,
+        moved=2 * width * hid,
+        name="grad_hidden_own",
+    )
     grads = []
     for start, size in chunks:
         outs = (sds((rows, size), F32), sds((rows, size), BF))
-        cost = dict(flops=4 * rows * width * size, moved=2 * width * size)
+        cost = dict(flops=2 * rows * width * size, moved=2 * width * size)
         if start == 0:
             cot, *grad = call(
                 functools.partial(first_grad_hidden_kernel, start),
-                (sds((rows, width), BF), *outs),
-                (core, own, other, w_down),
+                (sds((rows, width // 2), BF), *outs),
+                (core, other, w_down, own_total),
                 [SMEM] + [VMEM] * 3,
                 name="grad_hidden",
                 **cost,
@@ -472,8 +526,8 @@
             grad = call(
                 functools.partial(more_grad_hidden_kernel, start),
                 outs,
-                (cot, w_down),
-                [VMEM] * 2,
+                (core, cot, w_down, own_total),
+                [SMEM] + [VMEM] * 3,
                 name="grad_hidden",
                 **cost,
             )
@@ -502,19 +556,21 @@
     got_rows = over_slice(chip_rows)
     pre_grads = [pair[0] for pair in pre_grads] + [pair[1] for pair in pre_grads]
     tile = 256
-    gate_grad, up_grad = pl.pallas_call(
-        functools.partial(weight_grad_kernel, len(chunks)),
-        out_shape=(sds((width, hid), BF), sds((width, hid), BF)),
-        grid=(width // tile,),
-        in_specs=[pl.BlockSpec((rows, tile), lambda i: (0, i))]
-        + [pl.BlockSpec(grad.shape, lambda i: (0, 0)) for grad in pre_grads],
-        out_specs=(pl.BlockSpec((tile, hid), lambda i: (i, 0)), pl.BlockSpec((tile, hid), lambda i: (i, 0))),
-        compiler_params=pltpu.CompilerParams(vmem_limit_bytes=16 << 20),
-        cost_estimate=pl.CostEstimate(
-            flops=4 * rows * width * hid, bytes_accessed=4 * width * hid, transcendentals=0
-        ),
+    gate_grad, up_grad = call(
+        functools.partial(weight_grad_kernel, len(chunks), tile),
+        (sds((width, hid), BF), sds((width, hid), BF)),
+        (turned, *pre_grads),
+        [VMEM] * (1 + len(pre_grads)),
+        [
+            pltpu.VMEM((width, hid), BF),
+            pltpu.VMEM((width, hid), BF),
+            pltpu.SemaphoreType.DMA((width // tile, 2)),
+        ],
+        flops=4 * rows * width * hid,
+        moved=4 * width * hid,
+        out_spec=HBM,
         name="weight_grads",
-    )(all_rows, *pre_grads)
+    )
     token_grad = call(
         functools.partial(token_grad_kernel, dims),
         sds((tok_rows, features), tokens.dtype),

time: 86.3 us -> 85.9 us (level)
  Pallas kernels: 22.9 us -> 20.9 us
  waiting for transfers between devices: 23.8 us -> 25.3 us
    pallas_call x1 -> x0, Pallas kernels: 5.72 us -> none  [fast_shards(): pl.pallas_call(functools.partial(weight_grad_kernel, len(chunks)), out_sh...]
    pallas_call x15 -> x18, Pallas kernels: 17.2 us -> 20.9 us  [call(): pl.pallas_call(body, out_shape=outs, in_specs=specs, out_specs=jax.tree.m...]
    all_to_all x2, waiting for transfers between devices: 11.5 us -> 13.8 us  [over_slice(): lax.all_to_all(x, ('dp', 'expert'), 0, 0, axis_index_groups=slice_groups,...]
    ppermute x4, waiting for transfers between devices: 4.3 us -> 3.28 us  [other_core(): return lax.ppermute(x, 'expert', [(i, i ^ 1) for i in range(n_expert)])]
  transfers between devices with their start and end apart: 10 -> 10, of which waited for: 8 -> 8; matrix products, arithmetic and copies ran while one was open for 0% -> 0% of each run, Pallas kernels for 16% -> 15%
where the time goes in v4:
time: 85.9 us; the launch traced here: 85.4 us
  waiting for transfers between devices  25.3 us (29%)
  blocking collectives  22 us (26%)
  Pallas kernels  20.9 us (24%)
  starting transfers between devices  16.3 us (19%)
    all_to_all x2, blocking collectives, over_plane(): lax.all_to_all(x, 'expert', 0, 0, axis_index_groups=plane, tiled=True)  22 us
    pallas_call x18, Pallas kernels, call(): pl.pallas_call(body, out_shape=outs, in_specs=specs, out_specs=jax.tree.m...  20.9 us
    all_to_all x2, waiting for transfers between devices, over_slice(): lax.all_to_all(x, ('dp', 'expert'), 0, 0, axis_index_groups=slice_groups,...  13.8 us
    all_to_all x2, starting transfers between devices, over_slice(): lax.all_to_all(x, ('dp', 'expert'), 0, 0, axis_index_groups=slice_groups,...  11.8 us
    ppermute x4, waiting for transfers between devices, other_dp(): return lax.ppermute(x, 'dp', [(0, 1), (1, 0)])  8.25 us
    ppermute x4, starting transfers between devices, other_dp(): return lax.ppermute(x, 'dp', [(0, 1), (1, 0)])  4.31 us
    ppermute x4, waiting for transfers between devices, other_core(): return lax.ppermute(x, 'expert', [(i, i ^ 1) for i in range(n_expert)])  3.28 us
  transfers between devices with their start and end apart: 10, of which 8 were waited for; matrix products, arithmetic and copies ran while one was open for 0% of the time, Pallas kernels for 15%

profile of v4, /device:TPU:0, one launch (start us, length us, event | category | flops | bytes accessed | tf_op | source)
XLA Modules:
  0.0 85.4 jit_solution(355705584778372607)
XLA Ops:
  0.6 2.7 %route.1 = bf16[1024,128]{1,0:T(8,128)(2,1)} custom-call(s32[2,128]{1,0:T(2,128)} %bitcast.19, f32[2,128]{1,0:T(2,128)} %bitcast.21, bf16[128,4096]{1,0:T(8,128)(2,1)} %tokens_hbm.1, bf16[128,4096]{1,0:T(8,128)(2,1)} %target_hbm.1), custom_call_target="tpu_custom_call" | custom-call | tf_op jit(solution)/shard_map/route/pallas_call | solution.py:41
  3.3 8.3 %all-to-all-start = ((bf16[16,64,128]{2,1,0:T(8,128)(2,1)}), bf16[16,64,128]{2,1,0:T(8,128)(2,1)S(1)}, u32[]{:S(2)}, u32[]{:S(2)}) async-start(bf16[16,64,128]{2,1,0:T(8,128)(2,1)} %bitcast.3), calls=%async_computation | async-start | bytes 524288 | tf_op jit(solution)/shard_map/all_to_all | solution.py:385
  11.6 1.6 %load_weights.2 = (f32[8,128]{1,0:T(8,128)S(1)}, bf16[2048,256]{1,0:T(8,128)(2,1)S(1)}, bf16[2048,256]{1,0:T(8,128)(2,1)S(1)}) custom-call(bf16[2048,896]{1,0:T(8,128)(2,1)} %gate_w.3, bf16[2048,896]{1,0:T(8,128)(2,1)} %up_w.3), custom_call_target="tpu_custom_call" | custom-call | flops 1000000000 | bytes 4194304 | tf_op jit(solution)/shard_map/load_weights/pallas_call | solution.py:41
  13.2 8.3 %all-to-all-done = bf16[16,64,128]{2,1,0:T(8,128)(2,1)S(1)} async-done(((bf16[16,64,128]{2,1,0:T(8,128)(2,1)}), bf16[16,64,128]{2,1,0:T(8,128)(2,1)S(1)}, u32[]{:S(2)}, u32[]{:S(2)}) %all-to-all-start) | async-done | bytes 262176 | tf_op jit(solution)/shard_map/all_to_all | solution.py:385
  21.5 0.0 collective-permute-start
  21.5 1.6 %load_weights.3 = (f32[8,128]{1,0:T(8,128)S(1)}, bf16[2048,256]{1,0:T(8,128)(2,1)S(1)}, bf16[2048,256]{1,0:T(8,128)(2,1)S(1)}) custom-call(bf16[2048,896]{1,0:T(8,128)(2,1)} %gate_w.3, bf16[2048,896]{1,0:T(8,128)(2,1)} %up_w.3, f32[8,128]{1,0:T(8,128)S(1)} %get-tuple-element.41.refs_0_), custom_call_target="tpu_custom_call" | custom-call | flops 1000000000 | bytes 4194304 | tf_op jit(solution)/shard_map/load_weights/pallas_call | solution.py:41
  23.1 0.0 collective-permute-done.other_ref
  23.1 1.4 %pre_activations.2 = (bf16[96,2048]{1,0:T(8,128)(2,1)S(1)}, f32[96,128]{1,0:T(8,128)S(1)}, f32[96,128]{1,0:T(8,128)S(1)}, f32[2,96,512]{2,1,0:T(8,128)S(1)}, bf16[2,96,512]{2,1,0:T(8,128)(2,1)S(1)}) custom-call(s32[1]{0:T(128)} %bitcast.1.core_ref, f32[8,128]{1,0:T(8,128)S(1)} %get-tuple-element.42.loaded_ref, bf16[1024,128]{1,0:T(8,128)(2,1)S(1)} %bitcast.12, ...), custom_call_target="tpu_custom_call" | custom-call | flops 805306368 | bytes 4194304 | tf_op jit(solution)/shard_map/pre_activations/pallas_call | solution.py:41
  24.5 1.2 %collective-permute-start.2 = (bf16[2,96,512]{2,1,0:T(8,128)(2,1)S(1)}, bf16[2,96,512]{2,1,0:T(8,128)(2,1)S(1)}, u32[]{:S(2)}, u32[]{:S(2)}) collective-permute-start(bf16[2,96,512]{2,1,0:T(8,128)(2,1)S(1)} %get-tuple-element.52), channel_id=1, source_target_pairs={{0,16},{16,0},{1,17},{17,1},{2,18},{18,2},{3,19},{19,3},{4,20},{20... | collective-permute-start | bytes 589832 | tf_op jit(solution)/shard_map/ppermute | solution.py:379
  25.6 0.0 copy-start
  25.6 2.8 %pre_activations.3 = (bf16[2048,96]{1,0:T(8,128)(2,1)S(1)}, f32[2,96,384]{2,1,0:T(8,128)S(1)}, bf16[2,96,384]{2,1,0:T(8,128)(2,1)S(1)}) custom-call(bf16[96,2048]{1,0:T(8,128)(2,1)S(1)} %get-tuple-element.48.rows_ref, bf16[2048,896]{1,0:T(8,128)(2,1)} %gate_w.3, bf16[2048,896]{1,0:T(8,128)(2,1)} %up_w.3), custom_call_target="tpu_custom_call" | custom-call | flops 603979776 | bytes 3145728 | tf_op jit(solution)/shard_map/pre_activations/pallas_call | solution.py:41
  28.4 1.0 %collective-permute-start.1 = (bf16[2,96,384]{2,1,0:T(8,128)(2,1)S(1)}, bf16[2,96,384]{2,1,0:T(8,128)(2,1)S(1)}, u32[]{:S(2)}, u32[]{:S(2)}) collective-permute-start(bf16[2,96,384]{2,1,0:T(8,128)(2,1)S(1)} %get-tuple-element.50), channel_id=1, source_target_pairs={{0,16},{16,0},{1,17},{17,1},{2,18},{18,2},{3,19},{19,3},{4,20},{20... | collective-permute-start | bytes 442376 | tf_op jit(solution)/shard_map/ppermute | solution.py:379
  29.4 2.8 %collective-permute-done.2.got_ref = bf16[2,96,512]{2,1,0:T(8,128)(2,1)S(1)} collective-permute-done((bf16[2,96,512]{2,1,0:T(8,128)(2,1)S(1)}, bf16[2,96,512]{2,1,0:T(8,128)(2,1)S(1)}, u32[]{:S(2)}, u32[]{:S(2)}) %collective-permute-start.2) | collective-permute-done | bytes 196640 | tf_op jit(solution)/shard_map/ppermute | solution.py:379
  32.3 0.0 copy-done
  32.3 0.5 down.1
  32.8 2.2 %collective-permute-done.1.got_ref = bf16[2,96,384]{2,1,0:T(8,128)(2,1)S(1)} collective-permute-done((bf16[2,96,384]{2,1,0:T(8,128)(2,1)S(1)}, bf16[2,96,384]{2,1,0:T(8,128)(2,1)S(1)}, u32[]{:S(2)}, u32[]{:S(2)}) %collective-permute-start.1) | collective-permute-done | bytes 147488 | tf_op jit(solution)/shard_map/ppermute | solution.py:379
  35.0 0.3 down_send.1
  35.4 0.1 collective-permute-start.3
  35.4 0.3 down_keep.1.own_ref
  35.7 1.1 %collective-permute-done.3.got_ref = bf16[768,128]{1,0:T(8,128)(2,1)S(1)} collective-permute-done((bf16[768,128]{1,0:T(8,128)(2,1)S(1)}, bf16[768,128]{1,0:T(8,128)(2,1)S(1)}, u32[]{:S(2)}, u32[]{:S(2)}) %collective-permute-start.3) | collective-permute-done | bytes 196640 | tf_op jit(solution)/shard_map/ppermute | solution.py:376
  36.9 11.3 %all_to_all.45 = bf16[8,96,128]{2,1,0:T(8,128)(2,1)S(1)} all-to-all(bf16[8,96,128]{2,1,0:T(8,128)(2,1)S(1)} %bitcast.17), channel_id=1, replica_groups={{0,2,4,6,8,10,12,14},{1,3,5,7,9,11,13,15},{16,18,20,22,24,26,28,30},{17..., dimensions={0} | all-to-all | bytes 393216 | tf_op jit(solution)/shard_map/all_to_all | solution.py:382
  48.3 10.7 %all_to_all.46 = bf16[8,96,128]{2,1,0:T(8,128)(2,1)S(1)} all-to-all(bf16[8,96,128]{2,1,0:T(8,128)(2,1)S(1)} %bitcast.16), channel_id=1, replica_groups={{0,2,4,6,8,10,12,14},{1,3,5,7,9,11,13,15},{16,18,20,22,24,26,28,30},{17..., dimensions={0} | all-to-all | bytes 393216 | tf_op jit(solution)/shard_map/all_to_all | solution.py:382
  59.0 0.0 collective-permute-start.4
  59.0 0.7 grad_hidden_own.1.total_ref
  59.7 0.0 copy-start.1
  59.7 0.0 copy-start.2
  59.7 0.7 collective-permute-done.4.other_ref
  60.4 0.5 grad_hidden.2
  60.9 0.8 collective-permute-start.6
  61.7 0.4 grad_hidden.3
  62.0 1.4 %collective-permute-start.5 = (bf16[96,384]{1,0:T(8,128)(2,1)S(1)}, bf16[96,384]{1,0:T(8,128)(2,1)S(1)}, u32[]{:S(2)}, u32[]{:S(2)}) collective-permute-start(bf16[96,384]{1,0:T(8,128)(2,1)S(1)} %get-tuple-element.60), channel_id=1, source_target_pairs={{0,16},{16,0},{1,17},{17,1},{2,18},{18,2},{3,19},{19,3},{4,20},{20... | collective-permute-start | bytes 221192 | tf_op jit(solution)/shard_map/ppermute | solution.py:379
  63.4 3.2 %collective-permute-done.6.got_ref = bf16[96,512]{1,0:T(8,128)(2,1)S(1)} collective-permute-done((bf16[96,512]{1,0:T(8,128)(2,1)S(1)}, bf16[96,512]{1,0:T(8,128)(2,1)S(1)}, u32[]{:S(2)}, u32[]{:S(2)}) %collective-permute-start.6) | collective-permute-done | bytes 98336 | tf_op jit(solution)/shard_map/ppermute | solution.py:379
  66.6 0.0 copy-done.1
  66.6 0.0 copy-done.2
  66.6 1.4 %row_grad.2 = (bf16[96,512]{1,0:T(8,128)(2,1)S(1)}, bf16[96,512]{1,0:T(8,128)(2,1)S(1)}, f32[96,2048]{1,0:T(8,128)S(1)}) custom-call(s32[1]{0:T(128)} %bitcast.1.core_ref, f32[96,512]{1,0:T(8,128)S(1)} %get-tuple-element.63.own_ref, bf16[96,512]{1,0:T(8,128)(2,1)S(1)} %collective-permute-done.6.got_ref, f32[96,512]{1,0:T(8,128)S(1)} %get-tuple-element.65.up_deriv, ...), custom_call_target="tpu_custom_call" | custom-call | flops 805306368 | bytes 4194304 | tf_op jit(solution)/shard_map/row_grad/pallas_call | solution.py:41
  68.0 0.0 collective-permute-done.5.got_ref
  68.0 1.3 %row_grad.3 = (bf16[96,384]{1,0:T(8,128)(2,1)S(1)}, bf16[96,384]{1,0:T(8,128)(2,1)S(1)}, f32[768,128]{1,0:T(8,128)S(1)}, bf16[768,128]{1,0:T(8,128)(2,1)S(1)}) custom-call(s32[1]{0:T(128)} %bitcast.1.core_ref, f32[96,384]{1,0:T(8,128)S(1)} %get-tuple-element.59.own_ref, bf16[96,384]{1,0:T(8,128)(2,1)S(1)} %collective-permute-done.5.got_ref, ...), custom_call_target="tpu_custom_call" | custom-call | flops 603979776 | bytes 3145728 | tf_op jit(solution)/shard_map/row_grad/pallas_call | solution.py:41
  69.3 0.0 copy-start.3
  69.3 0.1 collective-permute-start.7
  69.4 1.4 %collective-permute-done.7.got_ref = bf16[768,128]{1,0:T(8,128)(2,1)S(1)} collective-permute-done((bf16[768,128]{1,0:T(8,128)(2,1)S(1)}, bf16[768,128]{1,0:T(8,128)(2,1)S(1)}, u32[]{:S(2)}, u32[]{:S(2)}) %collective-permute-start.7) | collective-permute-done | bytes 196640 | tf_op jit(solution)/shard_map/ppermute | solution.py:376
  70.8 0.7 add_cores.3
  71.6 3.5 %all-to-all-start.3 = ((bf16[16,48,128]{2,1,0:T(8,128)(2,1)}), bf16[16,48,128]{2,1,0:T(8,128)(2,1)S(1)}, u32[]{:S(2)}, u32[]{:S(2)}) async-start(bf16[16,48,128]{2,1,0:T(8,128)(2,1)} %bitcast.9), calls=%async_computation.3 | async-start | bytes 393216 | tf_op jit(solution)/shard_map/all_to_all | solution.py:385
  75.1 3.4 %weight_grads.1 = (bf16[2048,896]{1,0:T(8,128)(2,1)}, bf16[2048,896]{1,0:T(8,128)(2,1)}) custom-call(bf16[2048,96]{1,0:T(8,128)(2,1)S(1)} %get-tuple-element.70.turned_ref, bf16[96,512]{1,0:T(8,128)(2,1)S(1)} %get-tuple-element.71.refs_0_, bf16[96,384]{1,0:T(8,128)(2,1)S(1)} %get-tuple-element.72.refs_1_, bf16[96,512]{1,0:T(8,128)(2,1)S(1)} %get-tuple-element.73.refs_2_, ...), custom_call_target="tpu_custom_call" | custom-call | flops 704643072 | bytes 7340032 | tf_op jit(solution)/shard_map/weight_grads/pallas_call | solution.py:41
  78.5 5.5 %all-to-all-done.3 = bf16[16,48,128]{2,1,0:T(8,128)(2,1)S(1)} async-done(((bf16[16,48,128]{2,1,0:T(8,128)(2,1)}), bf16[16,48,128]{2,1,0:T(8,128)(2,1)S(1)}, u32[]{:S(2)}, u32[]{:S(2)}) %all-to-all-start.3) | async-done | bytes 196640 | tf_op jit(solution)/shard_map/all_to_all | solution.py:385
  84.0 0.0 copy-done.3
  84.0 1.4 %token_grad.1 = bf16[128,4096]{1,0:T(8,128)(2,1)} custom-call(s32[2,128]{1,0:T(2,128)S(1)} %bitcast.20, bf16[768,128]{1,0:T(8,128)(2,1)S(1)} %bitcast.18), custom_call_target="tpu_custom_call" | custom-call | tf_op jit(solution)/shard_map/token_grad/pallas_call | solution.py:41
  (2 shorter events, 0.1 us)
Async XLA Ops:
  3.3 18.2 %all-to-all-start = ((bf16[16,64,128]{2,1,0:T(8,128)(2,1)}), bf16[16,64,128]{2,1,0:T(8,128)(2,1)S(1)}, u32[]{:S(2)}, u32[]{:S(2)}) async-start(bf16[16,64,128]{2,1,0:T(8,128)(2,1)} %bitcast.3), calls=%async_computation | async-start | bytes 524288 | tf_op jit(solution)/shard_map/all_to_all | solution.py:385
  21.5 1.6 %collective-permute-start = (bf16[1024,128]{1,0:T(8,128)(2,1)S(1)}, bf16[1024,128]{1,0:T(8,128)(2,1)S(1)}, u32[]{:S(2)}, u32[]{:S(2)}) collective-permute-start(bf16[1024,128]{1,0:T(8,128)(2,1)S(1)} %bitcast.11), channel_id=1, source_target_pairs={{0,1},{1,0},{2,3},{3,2},{4,5},{5,4},{6,7},{7,6},{8,9},{9,8},{10,11... | collective-permute-start | bytes 786440 | tf_op jit(solution)/shard_map/ppermute | solution.py:376
  24.5 7.8 %collective-permute-start.2 = (bf16[2,96,512]{2,1,0:T(8,128)(2,1)S(1)}, bf16[2,96,512]{2,1,0:T(8,128)(2,1)S(1)}, u32[]{:S(2)}, u32[]{:S(2)}) collective-permute-start(bf16[2,96,512]{2,1,0:T(8,128)(2,1)S(1)} %get-tuple-element.52), channel_id=1, source_target_pairs={{0,16},{16,0},{1,17},{17,1},{2,18},{18,2},{3,19},{19,3},{4,20},{20... | collective-permute-start | bytes 589832 | tf_op jit(solution)/shard_map/ppermute | solution.py:379
  25.6 6.6 %copy-start = (bf16[896,2048]{1,0:T(8,128)(2,1)S(1)}, bf16[896,2048]{1,0:T(8,128)(2,1)}, u32[]{:S(2)}) copy-start(bf16[896,2048]{1,0:T(8,128)(2,1)} %down_w.11) | copy-start | bytes 11010052
  28.4 6.6 %collective-permute-start.1 = (bf16[2,96,384]{2,1,0:T(8,128)(2,1)S(1)}, bf16[2,96,384]{2,1,0:T(8,128)(2,1)S(1)}, u32[]{:S(2)}, u32[]{:S(2)}) collective-permute-start(bf16[2,96,384]{2,1,0:T(8,128)(2,1)S(1)} %get-tuple-element.50), channel_id=1, source_target_pairs={{0,16},{16,0},{1,17},{17,1},{2,18},{18,2},{3,19},{19,3},{4,20},{20... | collective-permute-start | bytes 442376 | tf_op jit(solution)/shard_map/ppermute | solution.py:379
  35.4 1.5 %collective-permute-start.3 = (bf16[768,128]{1,0:T(8,128)(2,1)S(1)}, bf16[768,128]{1,0:T(8,128)(2,1)S(1)}, u32[]{:S(2)}, u32[]{:S(2)}) collective-permute-start(bf16[768,128]{1,0:T(8,128)(2,1)S(1)} %get-tuple-element.55), channel_id=1, source_target_pairs={{0,1},{1,0},{2,3},{3,2},{4,5},{5,4},{6,7},{7,6},{8,9},{9,8},{10,11... | collective-permute-start | bytes 589832 | tf_op jit(solution)/shard_map/ppermute | solution.py:376
  59.0 1.4 %collective-permute-start.4 = (bf16[768,128]{1,0:T(8,128)(2,1)S(1)}, bf16[768,128]{1,0:T(8,128)(2,1)S(1)}, u32[]{:S(2)}, u32[]{:S(2)}) collective-permute-start(bf16[768,128]{1,0:T(8,128)(2,1)S(1)} %bitcast.13), channel_id=1, source_target_pairs={{0,1},{1,0},{2,3},{3,2},{4,5},{5,4},{6,7},{7,6},{8,9},{9,8},{10,11... | collective-permute-start | bytes 589832 | tf_op jit(solution)/shard_map/ppermute | solution.py:376
  59.7 6.9 %copy-start.1 = (bf16[2048,896]{1,0:T(8,128)(2,1)S(1)}, bf16[2048,896]{1,0:T(8,128)(2,1)}, u32[]{:S(2)}) copy-start(bf16[2048,896]{1,0:T(8,128)(2,1)} %gate_w.3) | copy-start | bytes 11010052
  59.7 6.9 %copy-start.2 = (bf16[2048,896]{1,0:T(8,128)(2,1)S(1)}, bf16[2048,896]{1,0:T(8,128)(2,1)}, u32[]{:S(2)}) copy-start(bf16[2048,896]{1,0:T(8,128)(2,1)} %up_w.3) | copy-start | bytes 11010052
  60.9 5.7 %collective-permute-start.6 = (bf16[96,512]{1,0:T(8,128)(2,1)S(1)}, bf16[96,512]{1,0:T(8,128)(2,1)S(1)}, u32[]{:S(2)}, u32[]{:S(2)}) collective-permute-start(bf16[96,512]{1,0:T(8,128)(2,1)S(1)} %get-tuple-element.64), channel_id=1, source_target_pairs={{0,16},{16,0},{1,17},{17,1},{2,18},{18,2},{3,19},{19,3},{4,20},{20... | collective-permute-start | bytes 294920 | tf_op jit(solution)/shard_map/ppermute | solution.py:379
  62.0 6.0 %collective-permute-start.5 = (bf16[96,384]{1,0:T(8,128)(2,1)S(1)}, bf16[96,384]{1,0:T(8,128)(2,1)S(1)}, u32[]{:S(2)}, u32[]{:S(2)}) collective-permute-start(bf16[96,384]{1,0:T(8,128)(2,1)S(1)} %get-tuple-element.60), channel_id=1, source_target_pairs={{0,16},{16,0},{1,17},{17,1},{2,18},{18,2},{3,19},{19,3},{4,20},{20... | collective-permute-start | bytes 221192 | tf_op jit(solution)/shard_map/ppermute | solution.py:379
  69.3 14.7 %copy-start.3 = (s32[128,2]{0,1:T(2,128)S(1)}, s32[128,2]{0,1:T(2,128)}, u32[]{:S(2)}) copy-start(s32[128,2]{0,1:T(2,128)} %param.8) | copy-start | bytes 3076
  69.3 1.5 %collective-permute-start.7 = (bf16[768,128]{1,0:T(8,128)(2,1)S(1)}, bf16[768,128]{1,0:T(8,128)(2,1)S(1)}, u32[]{:S(2)}, u32[]{:S(2)}) collective-permute-start(bf16[768,128]{1,0:T(8,128)(2,1)S(1)} %get-tuple-element.69), channel_id=1, source_target_pairs={{0,1},{1,0},{2,3},{3,2},{4,5},{5,4},{6,7},{7,6},{8,9},{9,8},{10,11... | collective-permute-start | bytes 589832 | tf_op jit(solution)/shard_map/ppermute | solution.py:376
  71.6 12.4 %all-to-all-start.3 = ((bf16[16,48,128]{2,1,0:T(8,128)(2,1)}), bf16[16,48,128]{2,1,0:T(8,128)(2,1)S(1)}, u32[]{:S(2)}, u32[]{:S(2)}) async-start(bf16[16,48,128]{2,1,0:T(8,128)(2,1)} %bitcast.9), calls=%async_computation.3 | async-start | bytes 393216 | tf_op jit(solution)/shard_map/all_to_all | solution.py:385

commit v5 on v4

--- a/solution.py
+++ b/solution.py
@@ -35,6 +35,18 @@
 
 def in_hbm(*arrays):
     return tuple(pltpu.with_memory_space_constraint(x, pltpu.HBM) for x in arrays)
+
+
+def core_of(place_ref):
+    return place_ref[0] & 1
+
+
+def x_of(place_ref):
+    return (place_ref[0] >> 1) & 1
+
+
+def z_of(place_ref):
+    return place_ref[0] >> 2
 
 
 def call(body, outs, args, specs, scratch=(), limit=16, flops=0, moved=0, name=None, out_spec=VMEM):
@@ -70,7 +82,7 @@
     return call(add_kernel, sds(got.shape, got.dtype), (own, got), [VMEM] * 2, name="add_cores")
 
 
-def route_kernel(dims, ids_hbm, gates_hbm, tokens_hbm, target_hbm, out_ref,
+def route_kernel(dims, ids_hbm, gates_hbm, tokens_hbm, target_hbm, out_ref, pick_ref,
                  ids_ref, gates_ref, tokens_ref, target_ref, tok, tgt, head, tail, sems):
     n_dp, half, cap, blocks, unit = dims
     width = blocks * LANES
@@ -89,6 +101,7 @@
     live_gates = jnp.sum(jnp.where(ids_ref[...] < EXPERTS, gates_ref[...], 0.0), axis=0, keepdims=True)
     gate = jnp.sum(chosen * live_gates, axis=1, keepdims=True)
     pick = chosen.astype(BF)
+    pick_ref[...] = pick
     rest = gate
     for piece in range(GATE_PIECES):
         part = rest.astype(BF).astype(F32)
@@ -112,15 +125,15 @@
         tgt[...] = dot_nn(pick, target_ref[:, cols])
         for h in range(half):
             for core in range(2):
-                lo = (core * half + h) * LANES
+                lo = (core * half + h % 2 * (half // 2) + h // 2) * LANES
                 tail[core * cap : (core + 1) * cap, :] = tgt[0:cap, lo : lo + LANES]
             base = (d * half + h) * unit
             out_ref[base + lead : base + unit, :] = tail[...].astype(BF)
 
 
-def both_cores(core_ref, own_ref, other_ref, wide):
+def both_cores(place_ref, own_ref, other_ref, wide):
     size = own_ref.shape[0]
-    core = core_ref[0]
+    core = core_of(place_ref)
     wide[pl.ds(pl.multiple_of(core * size, size), size), :] = own_ref[...].astype(wide.dtype)
     wide[pl.ds(pl.multiple_of((1 - core) * size, size), size), :] = other_ref[...].astype(wide.dtype)
 
@@ -164,12 +177,12 @@
             send_pre[side, :, cols] = value.astype(BF)
 
 
-def first_pre_kernel(dims, core_ref, loaded_ref, own_ref, other_ref, gate_head, up_head, gate_rest, up_rest,
+def first_pre_kernel(dims, place_ref, loaded_ref, own_ref, other_ref, gate_head, up_head, gate_rest, up_rest,
                      rows_ref, target_ref, gates_ref, own_pre, send_pre, wide):
     n_dp, half, cap, blocks, unit = dims
     sources = 2 * n_dp * half
-    both_cores(core_ref, own_ref, other_ref, wide)
-    core = core_ref[0]
+    both_cores(place_ref, own_ref, other_ref, wide)
+    core = core_of(place_ref)
 
     def one(k):
         return wide[pl.ds(k, sources, stride=unit), :]
@@ -191,19 +204,24 @@
     partial_pre(rows_ref, gate_w, up_w, copies, 0, own_pre, send_pre)
 
 
-def down_side(dims, start, lo, hidden, down_w, total_ref, side, out_ref):
+def down_side(dims, start, place_ref, hidden, down_w, total_ref, side, out_ref):
     n_dp, half, cap, blocks, unit = dims
     rows, hid = hidden.shape
-    for j in range(half // 2):
-        cols = pl.ds(pl.multiple_of((lo + 2 * j) * LANES, 2 * LANES), 2 * LANES)
-        value = dot_nn(hidden[...], down_w[start : start + hid, cols])
-        for k in range(2):
-            part = value[:, k * LANES : (k + 1) * LANES]
-            block = 2 * j + k
-            if total_ref is not None:
-                both = side * half + block
-                part = part + total_ref[both * rows : (both + 1) * rows, :]
-            out_ref[block * rows : (block + 1) * rows, :] = part.astype(out_ref.dtype)
+    quarter = half // 2
+    core = jnp.where(side == 0, core_of(place_ref), 1 - core_of(place_ref))
+    for k in range(2):
+        x = x_of(place_ref) if k == 0 else 1 - x_of(place_ref)
+        for j in range(0, quarter, 2):
+            lo = (core * half + x * quarter + j) * LANES
+            cols = pl.ds(pl.multiple_of(lo, 2 * LANES), 2 * LANES)
+            value = dot_nn(hidden[...], down_w[start : start + hid, cols])
+            for n in range(2):
+                part = value[:, n * LANES : (n + 1) * LANES]
+                block = k * quarter + j + n
+                if total_ref is not None:
+                    both = side * half + block
+                    part = part + total_ref[both * rows : (both + 1) * rows, :]
+                out_ref[block * rows : (block + 1) * rows, :] = part.astype(out_ref.dtype)
 
 
 def activate(own_ref, got_ref, up_deriv, act_ref, hidden):
@@ -216,33 +234,50 @@
     hidden[...] = (act * up_pre).astype(BF)
 
 
-def first_down_kernel(dims, start, core_ref, own_ref, got_ref, down_w, up_deriv, act_ref, total_ref, hidden):
-    half = dims[1]
+def first_down_kernel(dims, start, place_ref, own_ref, got_ref, down_w, up_deriv, act_ref, total_ref, hidden):
     activate(own_ref, got_ref, up_deriv, act_ref, hidden)
-    size = half * hidden.shape[0]
-    for side, core in enumerate((core_ref[0], 1 - core_ref[0])):
+    size = dims[1] * hidden.shape[0]
+    for side in range(2):
         part = total_ref.at[side * size : (side + 1) * size]
-        down_side(dims, start, core * half, hidden, down_w, None, side, part)
-
-
-def send_down_kernel(dims, start, core_ref, own_ref, got_ref, down_w, total_ref, up_deriv, act_ref, hidden, send_ref):
+        down_side(dims, start, place_ref, hidden, down_w, None, side, part)
+
+
+def send_down_kernel(dims, start, place_ref, own_ref, got_ref, down_w, total_ref, up_deriv, act_ref, hidden, send_ref):
     activate(own_ref, got_ref, up_deriv, act_ref, hidden)
-    down_side(dims, start, (1 - core_ref[0]) * dims[1], hidden, down_w, total_ref, 1, send_ref)
-
-
-def keep_down_kernel(dims, start, core_ref, hidden, down_w, total_ref, keep_ref):
-    down_side(dims, start, core_ref[0] * dims[1], hidden, down_w, total_ref, 0, keep_ref)
-
-
-def cotangent_kernel(parts, got_ref, gates_ref, target_ref, out_ref):
+    down_side(dims, start, place_ref, hidden, down_w, total_ref, 1, send_ref)
+
+
+def keep_down_kernel(dims, start, place_ref, hidden, down_w, total_ref, keep_ref):
+    down_side(dims, start, place_ref, hidden, down_w, total_ref, 0, keep_ref)
+
+
+def chip_sum_kernel(own_ref, got_ref, keep_ref, send_ref):
+    size = keep_ref.shape[0]
+    keep_ref[...] = own_ref[0:size, :] + got_ref[0:size, :].astype(F32)
+    send_ref[...] = (own_ref[size : 2 * size, :] + got_ref[size : 2 * size, :].astype(F32)).astype(BF)
+
+
+def residual_kernel(place_ref, own_ref, got_ref, gates_ref, target_ref, keep_ref, send_ref):
     rows = target_ref.shape[0]
-    total = got_ref[0:rows, :].astype(F32)
-    for h in range(1, parts):
-        total = total + got_ref[h * rows : (h + 1) * rows, :].astype(F32)
-    gate = gates_ref[...]
-    value = (gate * (gate * total - target_ref[...])).astype(BF)
-    for h in range(parts):
-        out_ref[h * rows : (h + 1) * rows, :] = value
+    for z in range(own_ref.shape[0] // rows):
+        at = slice(z * rows, (z + 1) * rows)
+        value = gates_ref[...] * (own_ref[at, :] + got_ref[at, :].astype(F32))
+        value = jnp.where(z_of(place_ref) == z, value - target_ref[...], value)
+        keep_ref[at, :] = value
+        send_ref[at, :] = value.astype(BF)
+
+
+def line_sum_kernel(own_ref, got_ref, keep_ref, send_ref):
+    value = own_ref[...] + got_ref[...].astype(F32)
+    keep_ref[...] = value
+    send_ref[...] = value.astype(BF)
+
+
+def cotangent_kernel(own_ref, got_ref, gates_ref, out_ref):
+    rows = gates_ref.shape[0]
+    for z in range(own_ref.shape[0] // rows):
+        at = slice(z * rows, (z + 1) * rows)
+        out_ref[at, :] = (gates_ref[...] * (own_ref[at, :] + got_ref[at, :].astype(F32))).astype(BF)
 
 
 def gather_blocks(ref, out):
@@ -251,9 +286,9 @@
         out[:, h * LANES : (h + 1) * LANES] = ref[h * rows : (h + 1) * rows, :]
 
 
-def half_grad_hidden(cot, core, down_w, start, total_ref, outs):
+def quarter_grad_hidden(cot, core, x, down_w, start, total_ref, outs):
     width = cot.shape[1]
-    cols = pl.ds(pl.multiple_of(core * width, width), width)
+    cols = pl.ds(pl.multiple_of((2 * core + x) * width, width), width)
     size = outs[0].shape[1]
     for lo in range(0, size, 2 * LANES):
         here = slice(lo, min(lo + 2 * LANES, size))
@@ -265,21 +300,24 @@
             out[:, here] = value.astype(out.dtype)
 
 
-def own_grad_hidden_kernel(core_ref, own_ref, down_w, total_ref, cot):
-    gather_blocks(own_ref, cot)
-    half_grad_hidden(cot, core_ref[0], down_w, 0, None, (total_ref,))
-
-
-def first_grad_hidden_kernel(start, core_ref, other_ref, down_w, total_ref, cot, own_out, send_out):
-    gather_blocks(other_ref, cot)
-    half_grad_hidden(cot, 1 - core_ref[0], down_w, start, total_ref, (own_out, send_out))
-
-
-def more_grad_hidden_kernel(start, core_ref, cot, down_w, total_ref, own_out, send_out):
-    half_grad_hidden(cot, 1 - core_ref[0], down_w, start, total_ref, (own_out, send_out))
-
-
-def row_grad_kernel(dims, start, last, core_ref, own_ref, got_ref, up_deriv, act_ref, gate_w, up_w, *refs):
+def near_grad_hidden_kernel(flips, place_ref, got_ref, down_w, *refs):
+    *total_ref, out_ref, cot = refs
+    core = 1 - core_of(place_ref) if flips[0] else core_of(place_ref)
+    x = 1 - x_of(place_ref) if flips[1] else x_of(place_ref)
+    gather_blocks(got_ref, cot)
+    quarter_grad_hidden(cot, core, x, down_w, 0, total_ref[0] if total_ref else None, (out_ref,))
+
+
+def first_grad_hidden_kernel(start, place_ref, got_ref, down_w, total_ref, cot, own_out, send_out):
+    gather_blocks(got_ref, cot)
+    quarter_grad_hidden(cot, 1 - core_of(place_ref), 1 - x_of(place_ref), down_w, start, total_ref, (own_out, send_out))
+
+
+def more_grad_hidden_kernel(start, place_ref, cot, down_w, total_ref, own_out, send_out):
+    quarter_grad_hidden(cot, 1 - core_of(place_ref), 1 - x_of(place_ref), down_w, start, total_ref, (own_out, send_out))
+
+
+def row_grad_kernel(dims, start, last, place_ref, own_ref, got_ref, up_deriv, act_ref, gate_w, up_w, *refs):
     n_dp, half, cap, blocks, unit = dims
     sources = 2 * n_dp * half
     refs = list(refs)
@@ -310,7 +348,7 @@
     if last:
         keep_ref, send_ref, _ = out_refs
         size = keep_ref.shape[0]
-        core = core_ref[0]
+        core = core_of(place_ref)
         keep_ref[...] = wide[pl.ds(pl.multiple_of(core * size, size), size), :]
         send_ref[...] = wide[pl.ds(pl.multiple_of((1 - core) * size, size), size), :].astype(BF)
 
@@ -333,11 +371,11 @@
         copy.wait()
 
 
-def token_grad_kernel(dims, ids_ref, got_ref, out_hbm, rows, out, sems):
+def token_grad_kernel(dims, pick_ref, got_ref, out_hbm, rows, out, sems):
     n_dp, half, cap, blocks, unit = dims
     size = blocks * cap
     width = blocks * LANES
-    pick = select_rows(ids_ref).astype(BF)
+    pick = pick_ref[...]
     rows[...] = jnp.zeros_like(rows)
     copies = []
     for d in range(n_dp):
@@ -365,28 +403,27 @@
     rows = cap * sources
     unit = -(-(blocks + 2 + GATE_PIECES) * cap // 16) * 16
     dims = (n_dp, half, cap, blocks, unit)
-    core = (lax.axis_index("expert") % 2).astype(jnp.int32).reshape(1)
+    place = lax.axis_index("expert").astype(jnp.int32).reshape(1)
     ids = expert_ids.T
-    plane = [[2 * h + c for h in range(half)] for c in range(2)]
     slice_groups = [
         [d * n_expert + 2 * h + c for d in range(n_dp) for h in range(half)] for c in range(2)
     ]
 
+    def other(x, mask):
+        return lax.ppermute(x, "expert", [(i, i ^ mask) for i in range(n_expert)])
+
     def other_core(x):
-        return lax.ppermute(x, "expert", [(i, i ^ 1) for i in range(n_expert)])
+        return other(x, 1)
 
     def other_dp(x):
         return lax.ppermute(x, "dp", [(0, 1), (1, 0)])
 
-    def over_plane(x):
-        return lax.all_to_all(x, "expert", 0, 0, axis_index_groups=plane, tiled=True)
-
     def over_slice(x):
         return lax.all_to_all(x, ("dp", "expert"), 0, 0, axis_index_groups=slice_groups, tiled=True)
 
-    outgoing = call(
+    outgoing, pick = call(
         functools.partial(route_kernel, dims),
-        sds((peers * unit, LANES), BF),
+        (sds((peers * unit, LANES), BF), sds((16, tok_rows), BF)),
         in_hbm(ids, gate_values.T, tokens, target),
         [HBM] * 4,
         [
@@ -421,7 +458,7 @@
     own, loaded = lax.optimization_barrier((over_slice(outgoing), loaded))
     loaded, *more = load(head, first - head, (loaded,))
     weights += more
-    other = other_core(own)
+    near = other_core(own)
     chunks = [(0, first), (first, hid - first)]
     last = len(chunks) - 1
     pres = []
@@ -437,7 +474,7 @@
             all_rows, all_target, all_gates, *pre = call(
                 functools.partial(first_pre_kernel, dims),
                 (sds((rows, width), BF), sds((rows, LANES), F32), sds((rows, LANES), F32), *outs),
-                (core, loaded, own, other, *weights),
+                (place, loaded, own, near, *weights),
                 [SMEM] + [VMEM] * 7,
                 [pltpu.VMEM((sources * unit, LANES), F32)],
                 name="pre_activations",
@@ -460,7 +497,7 @@
     up_deriv, act, total = call(
         functools.partial(first_down_kernel, dims, start),
         (sds((rows, size), F32), sds((rows, size), F32), sds((2 * half_rows, LANES), F32)),
-        (core, *pres[0], w_down),
+        (place, *pres[0], w_down),
         [SMEM] + [VMEM] * 3,
         [pltpu.VMEM((rows, size), BF)],
         name="down",
@@ -474,7 +511,7 @@
             sds((rows, size_b), BF),
             sds((half_rows, LANES), BF),
         ),
-        (core, *pres[1], w_down, total),
+        (place, *pres[1], w_down, total),
         [SMEM] + [VMEM] * 4,
         name="down_send",
         **cost,
@@ -483,32 +520,54 @@
     keep = call(
         functools.partial(keep_down_kernel, dims, start_b),
         sds((half_rows, LANES), F32),
-        (core, hidden_b, w_down, total),
+        (place, hidden_b, w_down, total),
         [SMEM] + [VMEM] * 3,
         name="down_keep",
         **cost,
     )
     saved = [(up_deriv, act), (up_deriv_b, act_b)]
-    chip_out = add_cores(keep, sent)
+    quarter_rows = half_rows // 2
+    pair = (sds((quarter_rows, LANES), F32), sds((quarter_rows, LANES), BF))
+    keep, send = call(chip_sum_kernel, pair, (keep, sent), [VMEM] * 2, name="chip_sum")
+    keep, send = call(
+        residual_kernel,
+        pair,
+        (place, keep, other(send, 2), all_gates, all_target),
+        [SMEM] + [VMEM] * 4,
+        name="residual",
+    )
+    step = 4
+    while 2 * step < n_expert:
+        keep, send = call(line_sum_kernel, pair, (keep, other(send, step)), [VMEM] * 2, name="line_sum")
+        step *= 2
     cot = call(
-        functools.partial(cotangent_kernel, half),
-        sds((half * rows, LANES), BF),
-        (over_plane(chip_out), all_gates, all_target),
+        cotangent_kernel,
+        pair[1],
+        (keep, other(send, step), all_gates),
         [VMEM] * 3,
         name="cotangent",
     )
-    own = over_plane(cot)
-    other = other_core(own)
-    own_total = call(
-        own_grad_hidden_kernel,
-        sds((rows, hid), F32),
-        (core, own, w_down),
-        [SMEM] + [VMEM] * 2,
-        [pltpu.VMEM((rows, width // 2), BF)],
-        flops=2 * rows * width * hid,
-        moved=2 * width * hid,
-        name="grad_hidden_own",
-    )
+    from_x = other(cot, 2)
+    from_core = other_core(cot)
+    own_total = ()
+    for flips in ((0, 0), (1, 0), (0, 1)):
+        got = from_x if flips[1] else from_core if flips[0] else cot
+        own_total = (
+            call(
+                functools.partial(near_grad_hidden_kernel, flips),
+                sds((rows, hid), F32),
+                (place, got, w_down, *own_total),
+                [SMEM] + [VMEM] * (2 + len(own_total)),
+                [pltpu.VMEM((rows, width // 4), BF)],
+                flops=rows * width * hid,
+                moved=width * hid,
+                name="grad_hidden_near",
+            ),
+        )
+        if flips[0]:
+            from_x, own_total = lax.optimization_barrier((from_x, own_total))
+            from_both = other_core(from_x)
+    own_total = own_total[0]
     grads = []
     for start, size in chunks:
         outs = (sds((rows, size), F32), sds((rows, size), BF))
@@ -516,8 +575,8 @@
         if start == 0:
             cot, *grad = call(
                 functools.partial(first_grad_hidden_kernel, start),
-                (sds((rows, width // 2), BF), *outs),
-                (core, other, w_down, own_total),
+                (sds((rows, width // 4), BF), *outs),
+                (place, from_both, w_down, own_total),
                 [SMEM] + [VMEM] * 3,
                 name="grad_hidden",
                 **cost,
@@ -526,7 +585,7 @@
             grad = call(
                 functools.partial(more_grad_hidden_kernel, start),
                 outs,
-                (core, cot, w_down, own_total),
+                (place, cot, w_down, own_total),
                 [SMEM] + [VMEM] * 3,
                 name="grad_hidden",
                 **cost,
@@ -543,7 +602,7 @@
         gate_pre_grad, up_pre_grad, *total = call(
             functools.partial(row_grad_kernel, dims, start, k == last),
             (sds((rows, size), BF), sds((rows, size), BF), *outs),
-            (core, *grads[k], *saved[k], w_gate, w_up, *total),
+            (place, *grads[k], *saved[k], w_gate, w_up, *total),
             [SMEM] + [VMEM] * (6 + len(total)),
             scratch,
             flops=8 * rows * width * size,
@@ -574,7 +633,7 @@
     token_grad = call(
         functools.partial(token_grad_kernel, dims),
         sds((tok_rows, features), tokens.dtype),
-        (ids, got_rows),
+        (pick, got_rows),
         [VMEM] * 2,
         [
             pltpu.VMEM((16, width), F32),
@@ -698,11 +757,11 @@
         cap = max(2, 3 * tok_rows // 128)
         whole_blocks = (
             n_dp == 2
-            and n_expert % 4 == 0
+            and n_expert % 16 == 0
+            and n_expert & (n_expert - 1) == 0
             and width == n_expert * LANES
             and hid % LANES == 0
             and hid > 4 * LANES
-            and n_dp * n_expert % 16 == 0
             and cap <= 8
             and tok_rows % LANES == 0
         )

time: 85.9 us -> 85 us (0.990)
  blocking collectives: 22 us -> 0 us
  waiting for transfers between devices: 25.3 us -> 42.5 us
  starting transfers between devices: 16.3 us -> 20 us
    all_to_all x2 -> x0, blocking collectives: 22 us -> none  [over_plane(): lax.all_to_all(x, 'expert', 0, 0, axis_index_groups=plane, tiled=True)]
    ppermute x4 -> x9, waiting for transfers between devices: 3.28 us -> 20.3 us  [other(): return lax.ppermute(x, 'expert', [(i, i ^ mask) for i in range(n_expert)])]
    ppermute x4 -> x9, starting transfers between devices: 0.15 us -> 3.85 us  [other(): return lax.ppermute(x, 'expert', [(i, i ^ mask) for i in range(n_expert)])]
    pallas_call x18 -> x22, Pallas kernels: 20.9 us -> 21.3 us  [call(): pl.pallas_call(body, out_shape=outs, in_specs=specs, out_specs=jax.tree.m...]
  transfers between devices with their start and end apart: 10 -> 15, of which waited for: 8 -> 12; matrix products, arithmetic and copies ran while one was open for 0% -> 0% of each run, Pallas kernels for 15% -> 16%
where the time goes in v5:
time: 85 us; the launch traced here: 84.7 us
  waiting for transfers between devices  42.5 us (50%)
  Pallas kernels  21.3 us (25%)
  starting transfers between devices  20 us (24%)
    pallas_call x22, Pallas kernels, call(): pl.pallas_call(body, out_shape=outs, in_specs=specs, out_specs=jax.tree.m...  21.3 us
    ppermute x9, waiting for transfers between devices, other(): return lax.ppermute(x, 'expert', [(i, i ^ mask) for i in range(n_expert)])  20.3 us
    all_to_all x2, waiting for transfers between devices, over_slice(): lax.all_to_all(x, ('dp', 'expert'), 0, 0, axis_index_groups=slice_groups,...  13.8 us
    all_to_all x2, starting transfers between devices, over_slice(): lax.all_to_all(x, ('dp', 'expert'), 0, 0, axis_index_groups=slice_groups,...  11.8 us
    ppermute x4, waiting for transfers between devices, other_dp(): return lax.ppermute(x, 'dp', [(0, 1), (1, 0)])  8.35 us
    ppermute x4, starting transfers between devices, other_dp(): return lax.ppermute(x, 'dp', [(0, 1), (1, 0)])  4.31 us
    ppermute x9, starting transfers between devices, other(): return lax.ppermute(x, 'expert', [(i, i ^ mask) for i in range(n_expert)])  3.85 us
  transfers between devices with their start and end apart: 15, of which 12 were waited for; matrix products, arithmetic and copies ran while one was open for 0% of the time, Pallas kernels for 16%

profile of v5, /device:TPU:0, one launch (start us, length us, event | category | flops | bytes accessed | tf_op | source)
XLA Modules:
  0.0 84.7 jit_solution(17420932464859617156)
XLA Ops:
  0.6 2.7 %route.1 = (bf16[1024,128]{1,0:T(8,128)(2,1)}, bf16[16,128]{1,0:T(8,128)(2,1)S(1)}) custom-call(s32[2,128]{1,0:T(2,128)} %bitcast.10, f32[2,128]{1,0:T(2,128)} %bitcast.11, bf16[128,4096]{1,0:T(8,128)(2,1)} %tokens_hbm.1, bf16[128,4096]{1,0:T(8,128)(2,1)} %target_hbm.1), custom_call_target="tpu_custom_call" | custom-call | tf_op jit(solution)/shard_map/route/pallas_call | solution.py:53
  3.3 8.3 %all-to-all-start = ((bf16[16,64,128]{2,1,0:T(8,128)(2,1)}), bf16[16,64,128]{2,1,0:T(8,128)(2,1)S(1)}, u32[]{:S(2)}, u32[]{:S(2)}) async-start(bf16[16,64,128]{2,1,0:T(8,128)(2,1)} %bitcast.3), calls=%async_computation | async-start | bytes 524288 | tf_op jit(solution)/shard_map/all_to_all | solution.py:422
  11.7 1.6 %load_weights.2 = (f32[8,128]{1,0:T(8,128)S(1)}, bf16[2048,256]{1,0:T(8,128)(2,1)S(1)}, bf16[2048,256]{1,0:T(8,128)(2,1)S(1)}) custom-call(bf16[2048,896]{1,0:T(8,128)(2,1)} %gate_w.3, bf16[2048,896]{1,0:T(8,128)(2,1)} %up_w.3), custom_call_target="tpu_custom_call" | custom-call | flops 1000000000 | bytes 4194304 | tf_op jit(solution)/shard_map/load_weights/pallas_call | solution.py:53
  13.2 8.3 %all-to-all-done = bf16[16,64,128]{2,1,0:T(8,128)(2,1)S(1)} async-done(((bf16[16,64,128]{2,1,0:T(8,128)(2,1)}), bf16[16,64,128]{2,1,0:T(8,128)(2,1)S(1)}, u32[]{:S(2)}, u32[]{:S(2)}) %all-to-all-start) | async-done | bytes 262176 | tf_op jit(solution)/shard_map/all_to_all | solution.py:422
  21.5 0.0 collective-permute-start
  21.5 1.6 %load_weights.3 = (f32[8,128]{1,0:T(8,128)S(1)}, bf16[2048,256]{1,0:T(8,128)(2,1)S(1)}, bf16[2048,256]{1,0:T(8,128)(2,1)S(1)}) custom-call(bf16[2048,896]{1,0:T(8,128)(2,1)} %gate_w.3, bf16[2048,896]{1,0:T(8,128)(2,1)} %up_w.3, f32[8,128]{1,0:T(8,128)S(1)} %get-tuple-element.53.refs_0_), custom_call_target="tpu_custom_call" | custom-call | flops 1000000000 | bytes 4194304 | tf_op jit(solution)/shard_map/load_weights/pallas_call | solution.py:53
  23.1 1.4 %pre_activations.2 = (bf16[96,2048]{1,0:T(8,128)(2,1)S(1)}, f32[96,128]{1,0:T(8,128)S(1)}, f32[96,128]{1,0:T(8,128)S(1)}, f32[2,96,512]{2,1,0:T(8,128)S(1)}, bf16[2,96,512]{2,1,0:T(8,128)(2,1)S(1)}) custom-call(s32[1]{0:T(128)} %bitcast.2.place_ref, f32[8,128]{1,0:T(8,128)S(1)} %get-tuple-element.54.loaded_ref, bf16[1024,128]{1,0:T(8,128)(2,1)S(1)} %bitcast.8, ...), custom_call_target="tpu_custom_call" | custom-call | flops 805306368 | bytes 4194304 | tf_op jit(solution)/shard_map/pre_activations/pallas_call | solution.py:53
  24.6 1.2 %collective-permute-start.2 = (bf16[2,96,512]{2,1,0:T(8,128)(2,1)S(1)}, bf16[2,96,512]{2,1,0:T(8,128)(2,1)S(1)}, u32[]{:S(2)}, u32[]{:S(2)}) collective-permute-start(bf16[2,96,512]{2,1,0:T(8,128)(2,1)S(1)} %get-tuple-element.64), channel_id=1, source_target_pairs={{0,16},{16,0},{1,17},{17,1},{2,18},{18,2},{3,19},{19,3},{4,20},{20... | collective-permute-start | bytes 589832 | tf_op jit(solution)/shard_map/ppermute | solution.py:419
  25.7 2.8 %pre_activations.3 = (bf16[2048,96]{1,0:T(8,128)(2,1)S(1)}, f32[2,96,384]{2,1,0:T(8,128)S(1)}, bf16[2,96,384]{2,1,0:T(8,128)(2,1)S(1)}) custom-call(bf16[96,2048]{1,0:T(8,128)(2,1)S(1)} %get-tuple-element.60.rows_ref, bf16[2048,896]{1,0:T(8,128)(2,1)} %gate_w.3, bf16[2048,896]{1,0:T(8,128)(2,1)} %up_w.3), custom_call_target="tpu_custom_call" | custom-call | flops 603979776 | bytes 3145728 | tf_op jit(solution)/shard_map/pre_activations/pallas_call | solution.py:53
  28.5 1.0 %collective-permute-start.1 = (bf16[2,96,384]{2,1,0:T(8,128)(2,1)S(1)}, bf16[2,96,384]{2,1,0:T(8,128)(2,1)S(1)}, u32[]{:S(2)}, u32[]{:S(2)}) collective-permute-start(bf16[2,96,384]{2,1,0:T(8,128)(2,1)S(1)} %get-tuple-element.62), channel_id=1, source_target_pairs={{0,16},{16,0},{1,17},{17,1},{2,18},{18,2},{3,19},{19,3},{4,20},{20... | collective-permute-start | bytes 442376 | tf_op jit(solution)/shard_map/ppermute | solution.py:419
  29.5 2.8 %collective-permute-done.2.got_ref = bf16[2,96,512]{2,1,0:T(8,128)(2,1)S(1)} collective-permute-done((bf16[2,96,512]{2,1,0:T(8,128)(2,1)S(1)}, bf16[2,96,512]{2,1,0:T(8,128)(2,1)S(1)}, u32[]{:S(2)}, u32[]{:S(2)}) %collective-permute-start.2) | collective-permute-done | bytes 196640 | tf_op jit(solution)/shard_map/ppermute | solution.py:419
  32.3 0.5 down.1
  32.9 2.3 %collective-permute-done.1.got_ref = bf16[2,96,384]{2,1,0:T(8,128)(2,1)S(1)} collective-permute-done((bf16[2,96,384]{2,1,0:T(8,128)(2,1)S(1)}, bf16[2,96,384]{2,1,0:T(8,128)(2,1)S(1)}, u32[]{:S(2)}, u32[]{:S(2)}) %collective-permute-start.1) | collective-permute-done | bytes 147488 | tf_op jit(solution)/shard_map/ppermute | solution.py:419
  35.1 0.3 down_send.1
  35.5 0.1 collective-permute-start.3
  35.5 0.3 down_keep.1.own_ref
  35.8 1.1 %collective-permute-done.3.got_ref = bf16[768,128]{1,0:T(8,128)(2,1)S(1)} collective-permute-done((bf16[768,128]{1,0:T(8,128)(2,1)S(1)}, bf16[768,128]{1,0:T(8,128)(2,1)S(1)}, u32[]{:S(2)}, u32[]{:S(2)}) %collective-permute-start.3) | collective-permute-done | bytes 196640 | tf_op jit(solution)/shard_map/ppermute | solution.py:413
  37.0 0.8 collective-permute-start.4
  37.9 4.1 %collective-permute-done.4.got_ref = bf16[384,128]{1,0:T(8,128)(2,1)S(1)} collective-permute-done((bf16[384,128]{1,0:T(8,128)(2,1)S(1)}, bf16[384,128]{1,0:T(8,128)(2,1)S(1)}, u32[]{:S(2)}, u32[]{:S(2)}) %collective-permute-start.4) | collective-permute-done | bytes 98336 | tf_op jit(solution)/shard_map/ppermute | solution.py:413
  42.0 1.0 %collective-permute-start.5 = (bf16[384,128]{1,0:T(8,128)(2,1)S(1)}, bf16[384,128]{1,0:T(8,128)(2,1)S(1)}, u32[]{:S(2)}, u32[]{:S(2)}) collective-permute-start(bf16[384,128]{1,0:T(8,128)(2,1)S(1)} %get-tuple-element.73), channel_id=1, source_target_pairs={{0,4},{1,5},{2,6},{3,7},{4,0},{5,1},{6,2},{7,3},{8,12},{9,13},{10,... | collective-permute-start | bytes 294920 | tf_op jit(solution)/shard_map/ppermute | solution.py:413
  43.0 3.7 %collective-permute-done.5.got_ref = bf16[384,128]{1,0:T(8,128)(2,1)S(1)} collective-permute-done((bf16[384,128]{1,0:T(8,128)(2,1)S(1)}, bf16[384,128]{1,0:T(8,128)(2,1)S(1)}, u32[]{:S(2)}, u32[]{:S(2)}) %collective-permute-start.5) | collective-permute-done | bytes 98336 | tf_op jit(solution)/shard_map/ppermute | solution.py:413
  46.7 1.0 %collective-permute-start.6 = (bf16[384,128]{1,0:T(8,128)(2,1)S(1)}, bf16[384,128]{1,0:T(8,128)(2,1)S(1)}, u32[]{:S(2)}, u32[]{:S(2)}) collective-permute-start(bf16[384,128]{1,0:T(8,128)(2,1)S(1)} %get-tuple-element.75), channel_id=1, source_target_pairs={{0,8},{1,9},{2,10},{3,11},{4,12},{5,13},{6,14},{7,15},{8,0},{9,1},... | collective-permute-start | bytes 294920 | tf_op jit(solution)/shard_map/ppermute | solution.py:413
  47.7 5.7 %collective-permute-done.6.got_ref = bf16[384,128]{1,0:T(8,128)(2,1)S(1)} collective-permute-done((bf16[384,128]{1,0:T(8,128)(2,1)S(1)}, bf16[384,128]{1,0:T(8,128)(2,1)S(1)}, u32[]{:S(2)}, u32[]{:S(2)}) %collective-permute-start.6) | collective-permute-done | bytes 98336 | tf_op jit(solution)/shard_map/ppermute | solution.py:413
  53.4 0.1 collective-permute-start.8
  53.4 0.8 collective-permute-start.7
  54.3 0.4 grad_hidden_near.3.refs_0_
  54.7 0.0 collective-permute-done.8.got_ref
  54.7 0.4 grad_hidden_near.4.refs_0_
  55.2 3.5 %collective-permute-done.7.got_ref = bf16[384,128]{1,0:T(8,128)(2,1)S(1)} collective-permute-done((bf16[384,128]{1,0:T(8,128)(2,1)S(1)}, bf16[384,128]{1,0:T(8,128)(2,1)S(1)}, u32[]{:S(2)}, u32[]{:S(2)}) %collective-permute-start.7) | collective-permute-done | bytes 98336 | tf_op jit(solution)/shard_map/ppermute | solution.py:413
  58.7 0.4 grad_hidden_near.5.total_ref
  59.1 0.0 copy-start.1
  59.1 0.0 copy-start.2
  59.1 0.8 collective-permute-done.9.got_ref
  60.0 0.3 grad_hidden.2
  60.3 1.2 %collective-permute-start.11 = (bf16[96,512]{1,0:T(8,128)(2,1)S(1)}, bf16[96,512]{1,0:T(8,128)(2,1)S(1)}, u32[]{:S(2)}, u32[]{:S(2)}) collective-permute-start(bf16[96,512]{1,0:T(8,128)(2,1)S(1)} %get-tuple-element.84), channel_id=1, source_target_pairs={{0,16},{16,0},{1,17},{17,1},{2,18},{18,2},{3,19},{19,3},{4,20},{20... | collective-permute-start | bytes 294920 | tf_op jit(solution)/shard_map/ppermute | solution.py:419
  61.4 0.3 grad_hidden.3
  61.7 1.0 %collective-permute-start.10 = (bf16[96,384]{1,0:T(8,128)(2,1)S(1)}, bf16[96,384]{1,0:T(8,128)(2,1)S(1)}, u32[]{:S(2)}, u32[]{:S(2)}) collective-permute-start(bf16[96,384]{1,0:T(8,128)(2,1)S(1)} %get-tuple-element.80), channel_id=1, source_target_pairs={{0,16},{16,0},{1,17},{17,1},{2,18},{18,2},{3,19},{19,3},{4,20},{20... | collective-permute-start | bytes 221192 | tf_op jit(solution)/shard_map/ppermute | solution.py:419
  62.7 3.3 %collective-permute-done.11.got_ref = bf16[96,512]{1,0:T(8,128)(2,1)S(1)} collective-permute-done((bf16[96,512]{1,0:T(8,128)(2,1)S(1)}, bf16[96,512]{1,0:T(8,128)(2,1)S(1)}, u32[]{:S(2)}, u32[]{:S(2)}) %collective-permute-start.11) | collective-permute-done | bytes 98336 | tf_op jit(solution)/shard_map/ppermute | solution.py:419
  66.0 1.4 %row_grad.2 = (bf16[96,512]{1,0:T(8,128)(2,1)S(1)}, bf16[96,512]{1,0:T(8,128)(2,1)S(1)}, f32[96,2048]{1,0:T(8,128)S(1)}) custom-call(s32[1]{0:T(128)} %bitcast.2.place_ref, f32[96,512]{1,0:T(8,128)S(1)} %get-tuple-element.83.own_ref, bf16[96,512]{1,0:T(8,128)(2,1)S(1)} %collective-permute-done.11.got_ref, f32[96,512]{1,0:T(8,128)S(1)} %get-tuple-element.85.up_deriv, ...), custom_call_target="tpu_custom_call" | custom-call | flops 805306368 | bytes 4194304 | tf_op jit(solution)/shard_map/row_grad/pallas_call | solution.py:53
  67.4 0.0 collective-permute-done.10.got_ref
  67.4 1.3 %row_grad.3 = (bf16[96,384]{1,0:T(8,128)(2,1)S(1)}, bf16[96,384]{1,0:T(8,128)(2,1)S(1)}, f32[768,128]{1,0:T(8,128)S(1)}, bf16[768,128]{1,0:T(8,128)(2,1)S(1)}) custom-call(s32[1]{0:T(128)} %bitcast.2.place_ref, f32[96,384]{1,0:T(8,128)S(1)} %get-tuple-element.79.own_ref, bf16[96,384]{1,0:T(8,128)(2,1)S(1)} %collective-permute-done.10.got_ref, ...), custom_call_target="tpu_custom_call" | custom-call | flops 603979776 | bytes 3145728 | tf_op jit(solution)/shard_map/row_grad/pallas_call | solution.py:53
  68.7 0.1 collective-permute-start.12
  68.8 1.4 %collective-permute-done.12.got_ref = bf16[768,128]{1,0:T(8,128)(2,1)S(1)} collective-permute-done((bf16[768,128]{1,0:T(8,128)(2,1)S(1)}, bf16[768,128]{1,0:T(8,128)(2,1)S(1)}, u32[]{:S(2)}, u32[]{:S(2)}) %collective-permute-start.12) | collective-permute-done | bytes 196640 | tf_op jit(solution)/shard_map/ppermute | solution.py:413
  70.2 0.7 add_cores.1
  70.9 3.5 %all-to-all-start.1 = ((bf16[16,48,128]{2,1,0:T(8,128)(2,1)}), bf16[16,48,128]{2,1,0:T(8,128)(2,1)S(1)}, u32[]{:S(2)}, u32[]{:S(2)}) async-start(bf16[16,48,128]{2,1,0:T(8,128)(2,1)} %bitcast.5), calls=%async_computation.1 | async-start | bytes 393216 | tf_op jit(solution)/shard_map/all_to_all | solution.py:422
  74.4 3.4 %weight_grads.1 = (bf16[2048,896]{1,0:T(8,128)(2,1)}, bf16[2048,896]{1,0:T(8,128)(2,1)}) custom-call(bf16[2048,96]{1,0:T(8,128)(2,1)S(1)} %get-tuple-element.90.turned_ref, bf16[96,512]{1,0:T(8,128)(2,1)S(1)} %get-tuple-element.91.refs_0_, bf16[96,384]{1,0:T(8,128)(2,1)S(1)} %get-tuple-element.92.refs_1_, bf16[96,512]{1,0:T(8,128)(2,1)S(1)} %get-tuple-element.93.refs_2_, ...), custom_call_target="tpu_custom_call" | custom-call | flops 704643072 | bytes 7340032 | tf_op jit(solution)/shard_map/weight_grads/pallas_call | solution.py:53
  77.8 5.5 %all-to-all-done.1 = bf16[16,48,128]{2,1,0:T(8,128)(2,1)S(1)} async-done(((bf16[16,48,128]{2,1,0:T(8,128)(2,1)}), bf16[16,48,128]{2,1,0:T(8,128)(2,1)S(1)}, u32[]{:S(2)}, u32[]{:S(2)}) %all-to-all-start.1) | async-done | bytes 196640 | tf_op jit(solution)/shard_map/all_to_all | solution.py:422
  83.4 1.3 %token_grad.1 = bf16[128,4096]{1,0:T(8,128)(2,1)} custom-call(bf16[16,128]{1,0:T(8,128)(2,1)S(1)} %get-tuple-element.50.pick_ref, bf16[768,128]{1,0:T(8,128)(2,1)S(1)} %bitcast.9), custom_call_target="tpu_custom_call" | custom-call | tf_op jit(solution)/shard_map/token_grad/pallas_call | solution.py:53
  (10 shorter events, 0.2 us)
Async XLA Ops:
  3.3 18.2 %all-to-all-start = ((bf16[16,64,128]{2,1,0:T(8,128)(2,1)}), bf16[16,64,128]{2,1,0:T(8,128)(2,1)S(1)}, u32[]{:S(2)}, u32[]{:S(2)}) async-start(bf16[16,64,128]{2,1,0:T(8,128)(2,1)} %bitcast.3), calls=%async_computation | async-start | bytes 524288 | tf_op jit(solution)/shard_map/all_to_all | solution.py:422
  21.5 1.6 %collective-permute-start = (bf16[1024,128]{1,0:T(8,128)(2,1)S(1)}, bf16[1024,128]{1,0:T(8,128)(2,1)S(1)}, u32[]{:S(2)}, u32[]{:S(2)}) collective-permute-start(bf16[1024,128]{1,0:T(8,128)(2,1)S(1)} %bitcast.7), channel_id=1, source_target_pairs={{0,1},{1,0},{2,3},{3,2},{4,5},{5,4},{6,7},{7,6},{8,9},{9,8},{10,11... | collective-permute-start | bytes 786440 | tf_op jit(solution)/shard_map/ppermute | solution.py:413
  24.6 7.8 %collective-permute-start.2 = (bf16[2,96,512]{2,1,0:T(8,128)(2,1)S(1)}, bf16[2,96,512]{2,1,0:T(8,128)(2,1)S(1)}, u32[]{:S(2)}, u32[]{:S(2)}) collective-permute-start(bf16[2,96,512]{2,1,0:T(8,128)(2,1)S(1)} %get-tuple-element.64), channel_id=1, source_target_pairs={{0,16},{16,0},{1,17},{17,1},{2,18},{18,2},{3,19},{19,3},{4,20},{20... | collective-permute-start | bytes 589832 | tf_op jit(solution)/shard_map/ppermute | solution.py:419
  25.7 6.6 %copy-start = (bf16[896,2048]{1,0:T(8,128)(2,1)S(1)}, bf16[896,2048]{1,0:T(8,128)(2,1)}, u32[]{:S(2)}) copy-start(bf16[896,2048]{1,0:T(8,128)(2,1)} %down_w.15) | copy-start | bytes 11010052
  28.5 6.6 %collective-permute-start.1 = (bf16[2,96,384]{2,1,0:T(8,128)(2,1)S(1)}, bf16[2,96,384]{2,1,0:T(8,128)(2,1)S(1)}, u32[]{:S(2)}, u32[]{:S(2)}) collective-permute-start(bf16[2,96,384]{2,1,0:T(8,128)(2,1)S(1)} %get-tuple-element.62), channel_id=1, source_target_pairs={{0,16},{16,0},{1,17},{17,1},{2,18},{18,2},{3,19},{19,3},{4,20},{20... | collective-permute-start | bytes 442376 | tf_op jit(solution)/shard_map/ppermute | solution.py:419
  35.5 1.5 %collective-permute-start.3 = (bf16[768,128]{1,0:T(8,128)(2,1)S(1)}, bf16[768,128]{1,0:T(8,128)(2,1)S(1)}, u32[]{:S(2)}, u32[]{:S(2)}) collective-permute-start(bf16[768,128]{1,0:T(8,128)(2,1)S(1)} %get-tuple-element.67), channel_id=1, source_target_pairs={{0,1},{1,0},{2,3},{3,2},{4,5},{5,4},{6,7},{7,6},{8,9},{9,8},{10,11... | collective-permute-start | bytes 589832 | tf_op jit(solution)/shard_map/ppermute | solution.py:413
  37.0 4.9 %collective-permute-start.4 = (bf16[384,128]{1,0:T(8,128)(2,1)S(1)}, bf16[384,128]{1,0:T(8,128)(2,1)S(1)}, u32[]{:S(2)}, u32[]{:S(2)}) collective-permute-start(bf16[384,128]{1,0:T(8,128)(2,1)S(1)} %get-tuple-element.69), channel_id=1, source_target_pairs={{0,2},{1,3},{2,0},{3,1},{4,6},{5,7},{6,4},{7,5},{8,10},{9,11},{10,... | collective-permute-start | bytes 294920 | tf_op jit(solution)/shard_map/ppermute | solution.py:413
  42.0 4.7 %collective-permute-start.5 = (bf16[384,128]{1,0:T(8,128)(2,1)S(1)}, bf16[384,128]{1,0:T(8,128)(2,1)S(1)}, u32[]{:S(2)}, u32[]{:S(2)}) collective-permute-start(bf16[384,128]{1,0:T(8,128)(2,1)S(1)} %get-tuple-element.73), channel_id=1, source_target_pairs={{0,4},{1,5},{2,6},{3,7},{4,0},{5,1},{6,2},{7,3},{8,12},{9,13},{10,... | collective-permute-start | bytes 294920 | tf_op jit(solution)/shard_map/ppermute | solution.py:413
  46.7 6.6 %collective-permute-start.6 = (bf16[384,128]{1,0:T(8,128)(2,1)S(1)}, bf16[384,128]{1,0:T(8,128)(2,1)S(1)}, u32[]{:S(2)}, u32[]{:S(2)}) collective-permute-start(bf16[384,128]{1,0:T(8,128)(2,1)S(1)} %get-tuple-element.75), channel_id=1, source_target_pairs={{0,8},{1,9},{2,10},{3,11},{4,12},{5,13},{6,14},{7,15},{8,0},{9,1},... | collective-permute-start | bytes 294920 | tf_op jit(solution)/shard_map/ppermute | solution.py:413
  53.4 1.4 %collective-permute-start.8 = (bf16[384,128]{1,0:T(8,128)(2,1)S(1)}, bf16[384,128]{1,0:T(8,128)(2,1)S(1)}, u32[]{:S(2)}, u32[]{:S(2)}) collective-permute-start(bf16[384,128]{1,0:T(8,128)(2,1)S(1)} %cotangent.1.got_ref), channel_id=1, source_target_pairs={{0,1},{1,0},{2,3},{3,2},{4,5},{5,4},{6,7},{7,6},{8,9},{9,8},{10,11... | collective-permute-start | bytes 294920 | tf_op jit(solution)/shard_map/ppermute | solution.py:413
  53.4 5.2 %collective-permute-start.7 = (bf16[384,128]{1,0:T(8,128)(2,1)S(1)}, bf16[384,128]{1,0:T(8,128)(2,1)S(1)}, u32[]{:S(2)}, u32[]{:S(2)}) collective-permute-start(bf16[384,128]{1,0:T(8,128)(2,1)S(1)} %cotangent.1.got_ref), channel_id=1, source_target_pairs={{0,2},{1,3},{2,0},{3,1},{4,6},{5,7},{6,4},{7,5},{8,10},{9,11},{10,... | collective-permute-start | bytes 294920 | tf_op jit(solution)/shard_map/ppermute | solution.py:413
  58.6 1.3 %collective-permute-start.9 = (bf16[384,128]{1,0:T(8,128)(2,1)S(1)}, bf16[384,128]{1,0:T(8,128)(2,1)S(1)}, u32[]{:S(2)}, u32[]{:S(2)}) collective-permute-start(bf16[384,128]{1,0:T(8,128)(2,1)S(1)} %collective-permute-done.7.got_ref), channel_id=1, source_target_pairs={{0,1},{1,0},{2,3},{3,2},{4,5},{5,4},{6,7},{7,6},{8,9},{9,8},{10,11... | collective-permute-start | bytes 294920 | tf_op jit(solution)/shard_map/ppermute | solution.py:413
  59.1 6.9 %copy-start.1 = (bf16[2048,896]{1,0:T(8,128)(2,1)S(1)}, bf16[2048,896]{1,0:T(8,128)(2,1)}, u32[]{:S(2)}) copy-start(bf16[2048,896]{1,0:T(8,128)(2,1)} %gate_w.3) | copy-start | bytes 11010052
  59.1 6.9 %copy-start.2 = (bf16[2048,896]{1,0:T(8,128)(2,1)S(1)}, bf16[2048,896]{1,0:T(8,128)(2,1)}, u32[]{:S(2)}) copy-start(bf16[2048,896]{1,0:T(8,128)(2,1)} %up_w.3) | copy-start | bytes 11010052
  60.3 5.7 %collective-permute-start.11 = (bf16[96,512]{1,0:T(8,128)(2,1)S(1)}, bf16[96,512]{1,0:T(8,128)(2,1)S(1)}, u32[]{:S(2)}, u32[]{:S(2)}) collective-permute-start(bf16[96,512]{1,0:T(8,128)(2,1)S(1)} %get-tuple-element.84), channel_id=1, source_target_pairs={{0,16},{16,0},{1,17},{17,1},{2,18},{18,2},{3,19},{19,3},{4,20},{20... | collective-permute-start | bytes 294920 | tf_op jit(solution)/shard_map/ppermute | solution.py:419
  61.7 5.7 %collective-permute-start.10 = (bf16[96,384]{1,0:T(8,128)(2,1)S(1)}, bf16[96,384]{1,0:T(8,128)(2,1)S(1)}, u32[]{:S(2)}, u32[]{:S(2)}) collective-permute-start(bf16[96,384]{1,0:T(8,128)(2,1)S(1)} %get-tuple-element.80), channel_id=1, source_target_pairs={{0,16},{16,0},{1,17},{17,1},{2,18},{18,2},{3,19},{19,3},{4,20},{20... | collective-permute-start | bytes 221192 | tf_op jit(solution)/shard_map/ppermute | solution.py:419
  68.7 1.5 %collective-permute-start.12 = (bf16[768,128]{1,0:T(8,128)(2,1)S(1)}, bf16[768,128]{1,0:T(8,128)(2,1)S(1)}, u32[]{:S(2)}, u32[]{:S(2)}) collective-permute-start(bf16[768,128]{1,0:T(8,128)(2,1)S(1)} %get-tuple-element.89), channel_id=1, source_target_pairs={{0,1},{1,0},{2,3},{3,2},{4,5},{5,4},{6,7},{7,6},{8,9},{9,8},{10,11... | collective-permute-start | bytes 589832 | tf_op jit(solution)/shard_map/ppermute | solution.py:413
  70.9 12.4 %all-to-all-start.1 = ((bf16[16,48,128]{2,1,0:T(8,128)(2,1)}), bf16[16,48,128]{2,1,0:T(8,128)(2,1)S(1)}, u32[]{:S(2)}, u32[]{:S(2)}) async-start(bf16[16,48,128]{2,1,0:T(8,128)(2,1)} %bitcast.5), calls=%async_computation.1 | async-start | bytes 393216 | tf_op jit(solution)/shard_map/all_to_all | solution.py:422

commit v6 on v5

--- a/solution.py
+++ b/solution.py
@@ -41,12 +41,13 @@
     return place_ref[0] & 1
 
 
-def x_of(place_ref):
-    return (place_ref[0] >> 1) & 1
-
-
-def z_of(place_ref):
-    return place_ref[0] >> 2
+def quad_of(place_ref, k=0):
+    x, low = (place_ref[0] >> 1) & 1, (place_ref[0] >> 2) & 1
+    return (1 - x if k & 1 else x) + 2 * (1 - low if k & 2 else low)
+
+
+def rest_of(place_ref):
+    return place_ref[0] >> 3
 
 
 def call(body, outs, args, specs, scratch=(), limit=16, flops=0, moved=0, name=None, out_spec=VMEM):
@@ -125,7 +126,7 @@
         tgt[...] = dot_nn(pick, target_ref[:, cols])
         for h in range(half):
             for core in range(2):
-                lo = (core * half + h % 2 * (half // 2) + h // 2) * LANES
+                lo = (core * half + h % 4 * (half // 4) + h // 4) * LANES
                 tail[core * cap : (core + 1) * cap, :] = tgt[0:cap, lo : lo + LANES]
             base = (d * half + h) * unit
             out_ref[base + lead : base + unit, :] = tail[...].astype(BF)
@@ -207,12 +208,12 @@
 def down_side(dims, start, place_ref, hidden, down_w, total_ref, side, out_ref):
     n_dp, half, cap, blocks, unit = dims
     rows, hid = hidden.shape
-    quarter = half // 2
-    core = jnp.where(side == 0, core_of(place_ref), 1 - core_of(place_ref))
-    for k in range(2):
-        x = x_of(place_ref) if k == 0 else 1 - x_of(place_ref)
+    quarter = half // 4
+    core = core_of(place_ref) if side == 0 else 1 - core_of(place_ref)
+    for k in range(4):
+        quad = quad_of(place_ref, k)
         for j in range(0, quarter, 2):
-            lo = (core * half + x * quarter + j) * LANES
+            lo = (core * half + quad * quarter + j) * LANES
             cols = pl.ds(pl.multiple_of(lo, 2 * LANES), 2 * LANES)
             value = dot_nn(hidden[...], down_w[start : start + hid, cols])
             for n in range(2):
@@ -251,18 +252,21 @@
     down_side(dims, start, place_ref, hidden, down_w, total_ref, 0, keep_ref)
 
 
-def chip_sum_kernel(own_ref, got_ref, keep_ref, send_ref):
+def chip_sum_kernel(own_ref, got_ref, keep_ref, *send_refs):
     size = keep_ref.shape[0]
-    keep_ref[...] = own_ref[0:size, :] + got_ref[0:size, :].astype(F32)
-    send_ref[...] = (own_ref[size : 2 * size, :] + got_ref[size : 2 * size, :].astype(F32)).astype(BF)
-
-
-def residual_kernel(place_ref, own_ref, got_ref, gates_ref, target_ref, keep_ref, send_ref):
+    for k, ref in enumerate((keep_ref, *send_refs)):
+        at = slice(k * size, (k + 1) * size)
+        ref[...] = (own_ref[at, :] + got_ref[at, :].astype(F32)).astype(ref.dtype)
+
+
+def residual_kernel(place_ref, own_ref, first_ref, second_ref, third_ref, gates_ref, target_ref, keep_ref, send_ref):
     rows = target_ref.shape[0]
     for z in range(own_ref.shape[0] // rows):
         at = slice(z * rows, (z + 1) * rows)
-        value = gates_ref[...] * (own_ref[at, :] + got_ref[at, :].astype(F32))
-        value = jnp.where(z_of(place_ref) == z, value - target_ref[...], value)
+        value = own_ref[at, :] + first_ref[at, :].astype(F32)
+        value = value + (second_ref[at, :].astype(F32) + third_ref[at, :].astype(F32))
+        value = gates_ref[...] * value
+        value = jnp.where(rest_of(place_ref) == z, value - target_ref[...], value)
         keep_ref[at, :] = value
         send_ref[at, :] = value.astype(BF)
 
@@ -280,41 +284,48 @@
         out_ref[at, :] = (gates_ref[...] * (own_ref[at, :] + got_ref[at, :].astype(F32))).astype(BF)
 
 
-def gather_blocks(ref, out):
+def gather_blocks(refs, out):
     rows = out.shape[0]
-    for h in range(out.shape[1] // LANES):
-        out[:, h * LANES : (h + 1) * LANES] = ref[h * rows : (h + 1) * rows, :]
-
-
-def quarter_grad_hidden(cot, core, x, down_w, start, total_ref, outs):
-    width = cot.shape[1]
-    cols = pl.ds(pl.multiple_of((2 * core + x) * width, width), width)
+    parts = refs[0].shape[0] // rows
+    for k, ref in enumerate(refs):
+        for h in range(parts):
+            lo = (k * parts + h) * LANES
+            out[:, lo : lo + LANES] = ref[h * rows : (h + 1) * rows, :]
+
+
+def quad_grad_hidden(cot, core, quads, down_w, start, total_ref, outs):
+    width = cot.shape[1] // len(quads)
     size = outs[0].shape[1]
     for lo in range(0, size, 2 * LANES):
         here = slice(lo, min(lo + 2 * LANES, size))
         there = slice(start + here.start, start + here.stop)
-        value = dot_nt(cot[...], down_w[there, cols])
-        if total_ref is not None:
-            value = value + total_ref[:, there]
+        value = total_ref[:, there] if total_ref is not None else None
+        for k, quad in enumerate(quads):
+            cols = pl.ds(pl.multiple_of((4 * core + quad) * width, width), width)
+            part = dot_nt(cot[:, k * width : (k + 1) * width], down_w[there, cols])
+            value = part if value is None else value + part
         for out in outs:
             out[:, here] = value.astype(out.dtype)
 
 
-def near_grad_hidden_kernel(flips, place_ref, got_ref, down_w, *refs):
-    *total_ref, out_ref, cot = refs
-    core = 1 - core_of(place_ref) if flips[0] else core_of(place_ref)
-    x = 1 - x_of(place_ref) if flips[1] else x_of(place_ref)
-    gather_blocks(got_ref, cot)
-    quarter_grad_hidden(cot, core, x, down_w, 0, total_ref[0] if total_ref else None, (out_ref,))
-
-
-def first_grad_hidden_kernel(start, place_ref, got_ref, down_w, total_ref, cot, own_out, send_out):
-    gather_blocks(got_ref, cot)
-    quarter_grad_hidden(cot, 1 - core_of(place_ref), 1 - x_of(place_ref), down_w, start, total_ref, (own_out, send_out))
+def near_grad_hidden_kernel(flip, flips, place_ref, down_w, *refs):
+    got_refs, rest = refs[: len(flips)], refs[len(flips) :]
+    *total_ref, out_ref, cot = rest
+    core = 1 - core_of(place_ref) if flip else core_of(place_ref)
+    quads = [quad_of(place_ref, k) for k in flips]
+    gather_blocks(got_refs, cot)
+    quad_grad_hidden(cot, core, quads, down_w, 0, total_ref[0] if total_ref else None, (out_ref,))
+
+
+def first_grad_hidden_kernel(start, place_ref, first_ref, second_ref, third_ref, down_w, total_ref, cot, own_out, send_out):
+    gather_blocks((first_ref, second_ref, third_ref), cot)
+    quads = [quad_of(place_ref, k) for k in (1, 2, 3)]
+    quad_grad_hidden(cot, 1 - core_of(place_ref), quads, down_w, start, total_ref, (own_out, send_out))
 
 
 def more_grad_hidden_kernel(start, place_ref, cot, down_w, total_ref, own_out, send_out):
-    quarter_grad_hidden(cot, 1 - core_of(place_ref), 1 - x_of(place_ref), down_w, start, total_ref, (own_out, send_out))
+    quads = [quad_of(place_ref, k) for k in (1, 2, 3)]
+    quad_grad_hidden(cot, 1 - core_of(place_ref), quads, down_w, start, total_ref, (own_out, send_out))
 
 
 def row_grad_kernel(dims, start, last, place_ref, own_ref, got_ref, up_deriv, act_ref, gate_w, up_w, *refs):
@@ -458,7 +469,7 @@
     own, loaded = lax.optimization_barrier((over_slice(outgoing), loaded))
     loaded, *more = load(head, first - head, (loaded,))
     weights += more
-    near = other_core(own)
+    neighbour = other_core(own)
     chunks = [(0, first), (first, hid - first)]
     last = len(chunks) - 1
     pres = []
@@ -474,7 +485,7 @@
             all_rows, all_target, all_gates, *pre = call(
                 functools.partial(first_pre_kernel, dims),
                 (sds((rows, width), BF), sds((rows, LANES), F32), sds((rows, LANES), F32), *outs),
-                (place, loaded, own, near, *weights),
+                (place, loaded, own, neighbour, *weights),
                 [SMEM] + [VMEM] * 7,
                 [pltpu.VMEM((sources * unit, LANES), F32)],
                 name="pre_activations",
@@ -526,48 +537,47 @@
         **cost,
     )
     saved = [(up_deriv, act), (up_deriv_b, act_b)]
-    quarter_rows = half_rows // 2
-    pair = (sds((quarter_rows, LANES), F32), sds((quarter_rows, LANES), BF))
-    keep, send = call(chip_sum_kernel, pair, (keep, sent), [VMEM] * 2, name="chip_sum")
+    quad_rows = half_rows // 4
+    kept, sent_on = sds((quad_rows, LANES), F32), sds((quad_rows, LANES), BF)
+    keep, *sends = call(chip_sum_kernel, (kept, *[sent_on] * 3), (keep, sent), [VMEM] * 2, name="chip_sum")
     keep, send = call(
         residual_kernel,
-        pair,
-        (place, keep, other(send, 2), all_gates, all_target),
-        [SMEM] + [VMEM] * 4,
+        (kept, sent_on),
+        (place, keep, *[other(x, 2 * (k + 1)) for k, x in enumerate(sends)], all_gates, all_target),
+        [SMEM] + [VMEM] * 6,
         name="residual",
     )
-    step = 4
+    step = 8
     while 2 * step < n_expert:
-        keep, send = call(line_sum_kernel, pair, (keep, other(send, step)), [VMEM] * 2, name="line_sum")
+        keep, send = call(line_sum_kernel, (kept, sent_on), (keep, other(send, step)), [VMEM] * 2, name="line_sum")
         step *= 2
     cot = call(
         cotangent_kernel,
-        pair[1],
+        sent_on,
         (keep, other(send, step), all_gates),
         [VMEM] * 3,
         name="cotangent",
     )
-    from_x = other(cot, 2)
+    from_quad = [other(cot, 2 * k) for k in (1, 2, 3)]
     from_core = other_core(cot)
-    own_total = ()
-    for flips in ((0, 0), (1, 0), (0, 1)):
-        got = from_x if flips[1] else from_core if flips[0] else cot
-        own_total = (
-            call(
-                functools.partial(near_grad_hidden_kernel, flips),
-                sds((rows, hid), F32),
-                (place, got, w_down, *own_total),
-                [SMEM] + [VMEM] * (2 + len(own_total)),
-                [pltpu.VMEM((rows, width // 4), BF)],
-                flops=rows * width * hid,
-                moved=width * hid,
-                name="grad_hidden_near",
-            ),
+
+    def near(flip, flips, got, *total):
+        return call(
+            functools.partial(near_grad_hidden_kernel, flip, flips),
+            sds((rows, hid), F32),
+            (place, w_down, *got, *total),
+            [SMEM] + [VMEM] * (1 + len(got) + len(total)),
+            [pltpu.VMEM((rows, len(got) * quad_rows // rows * LANES), BF)],
+            flops=len(got) * rows * width * hid // 4,
+            moved=len(got) * width * hid // 4,
+            name="grad_hidden_near",
         )
-        if flips[0]:
-            from_x, own_total = lax.optimization_barrier((from_x, own_total))
-            from_both = other_core(from_x)
-    own_total = own_total[0]
+
+    own_total = near(0, (0,), (cot,))
+    own_total = near(1, (0,), (from_core,), own_total)
+    from_quad, own_total = lax.optimization_barrier((from_quad, own_total))
+    from_both = [other_core(x) for x in from_quad]
+    own_total = near(0, (1, 2, 3), from_quad, own_total)
     grads = []
     for start, size in chunks:
         outs = (sds((rows, size), F32), sds((rows, size), BF))
@@ -575,9 +585,9 @@
         if start == 0:
             cot, *grad = call(
                 functools.partial(first_grad_hidden_kernel, start),
-                (sds((rows, width // 4), BF), *outs),
-                (place, from_both, w_down, own_total),
-                [SMEM] + [VMEM] * 3,
+                (sds((rows, 3 * width // 8), BF), *outs),
+                (place, *from_both, w_down, own_total),
+                [SMEM] + [VMEM] * 5,
                 name="grad_hidden",
                 **cost,
             )

time: 85 us -> 82.9 us (0.975)
  waiting for transfers between devices: 42.5 us -> 34.2 us
  starting transfers between devices: 20 us -> 26.2 us
    ppermute x9 -> x14, waiting for transfers between devices: 20.3 us -> 12.3 us  [other(): return lax.ppermute(x, 'expert', [(i, i ^ mask) for i in range(n_expert)])]
    ppermute x9 -> x14, starting transfers between devices: 3.85 us -> 9.54 us  [other(): return lax.ppermute(x, 'expert', [(i, i ^ mask) for i in range(n_expert)])]
    pallas_call x22 -> x21, Pallas kernels: 21.3 us -> 21.3 us  [call(): pl.pallas_call(body, out_shape=outs, in_specs=specs, out_specs=jax.tree.m...]
  transfers between devices with their start and end apart: 15 -> 20, of which waited for: 12 -> 17; matrix products, arithmetic and copies ran while one was open for 0% -> 0% of each run, Pallas kernels for 16% -> 16%
where the time goes in v6:
time: 82.9 us; the launch traced here: 82.5 us
  waiting for transfers between devices  34.2 us (41%)
  starting transfers between devices  26.2 us (32%)
  Pallas kernels  21.3 us (26%)
  between operations  0.84 us (1%)
    pallas_call x21, Pallas kernels, call(): pl.pallas_call(body, out_shape=outs, in_specs=specs, out_specs=jax.tree.m...  21.3 us
    all_to_all x2, waiting for transfers between devices, over_slice(): lax.all_to_all(x, ('dp', 'expert'), 0, 0, axis_index_groups=slice_groups,...  13.6 us
    all_to_all x2, starting transfers between devices, over_slice(): lax.all_to_all(x, ('dp', 'expert'), 0, 0, axis_index_groups=slice_groups,...  12.4 us
    ppermute x14, waiting for transfers between devices, other(): return lax.ppermute(x, 'expert', [(i, i ^ mask) for i in range(n_expert)])  12.3 us
    ppermute x14, starting transfers between devices, other(): return lax.ppermute(x, 'expert', [(i, i ^ mask) for i in range(n_expert)])  9.54 us
    ppermute x4, waiting for transfers between devices, other_dp(): return lax.ppermute(x, 'dp', [(0, 1), (1, 0)])  8.32 us
    ppermute x4, starting transfers between devices, other_dp(): return lax.ppermute(x, 'dp', [(0, 1), (1, 0)])  4.31 us
  transfers between devices with their start and end apart: 20, of which 17 were waited for; matrix products, arithmetic and copies ran while one was open for 0% of the time, Pallas kernels for 16%

profile of v6, /device:TPU:0, one launch (start us, length us, event | category | flops | bytes accessed | tf_op | source)
XLA Modules:
  0.0 82.5 jit_solution(10050127642255628007)
XLA Ops:
  0.6 2.7 %route.1 = (bf16[1024,128]{1,0:T(8,128)(2,1)}, bf16[16,128]{1,0:T(8,128)(2,1)S(1)}) custom-call(s32[2,128]{1,0:T(2,128)} %bitcast.10, f32[2,128]{1,0:T(2,128)} %bitcast.11, bf16[128,4096]{1,0:T(8,128)(2,1)} %tokens_hbm.1, bf16[128,4096]{1,0:T(8,128)(2,1)} %target_hbm.1), custom_call_target="tpu_custom_call" | custom-call | tf_op jit(solution)/shard_map/route/pallas_call | solution.py:54
  3.3 8.3 %all-to-all-start = ((bf16[16,64,128]{2,1,0:T(8,128)(2,1)}), bf16[16,64,128]{2,1,0:T(8,128)(2,1)S(1)}, u32[]{:S(2)}, u32[]{:S(2)}) async-start(bf16[16,64,128]{2,1,0:T(8,128)(2,1)} %bitcast.3), calls=%async_computation | async-start | bytes 524288 | tf_op jit(solution)/shard_map/all_to_all | solution.py:433
  11.7 1.6 %load_weights.2 = (f32[8,128]{1,0:T(8,128)S(1)}, bf16[2048,256]{1,0:T(8,128)(2,1)S(1)}, bf16[2048,256]{1,0:T(8,128)(2,1)S(1)}) custom-call(bf16[2048,896]{1,0:T(8,128)(2,1)} %gate_w.3, bf16[2048,896]{1,0:T(8,128)(2,1)} %up_w.3), custom_call_target="tpu_custom_call" | custom-call | flops 1000000000 | bytes 4194304 | tf_op jit(solution)/shard_map/load_weights/pallas_call | solution.py:54
  13.2 8.3 %all-to-all-done = bf16[16,64,128]{2,1,0:T(8,128)(2,1)S(1)} async-done(((bf16[16,64,128]{2,1,0:T(8,128)(2,1)}), bf16[16,64,128]{2,1,0:T(8,128)(2,1)S(1)}, u32[]{:S(2)}, u32[]{:S(2)}) %all-to-all-start) | async-done | bytes 262176 | tf_op jit(solution)/shard_map/all_to_all | solution.py:433
  21.5 1.6 %load_weights.3 = (f32[8,128]{1,0:T(8,128)S(1)}, bf16[2048,256]{1,0:T(8,128)(2,1)S(1)}, bf16[2048,256]{1,0:T(8,128)(2,1)S(1)}) custom-call(bf16[2048,896]{1,0:T(8,128)(2,1)} %gate_w.3, bf16[2048,896]{1,0:T(8,128)(2,1)} %up_w.3, f32[8,128]{1,0:T(8,128)S(1)} %get-tuple-element.55.refs_0_), custom_call_target="tpu_custom_call" | custom-call | flops 1000000000 | bytes 4194304 | tf_op jit(solution)/shard_map/load_weights/pallas_call | solution.py:54
  23.1 1.4 %pre_activations.2 = (bf16[96,2048]{1,0:T(8,128)(2,1)S(1)}, f32[96,128]{1,0:T(8,128)S(1)}, f32[96,128]{1,0:T(8,128)S(1)}, f32[2,96,512]{2,1,0:T(8,128)S(1)}, bf16[2,96,512]{2,1,0:T(8,128)(2,1)S(1)}) custom-call(s32[1]{0:T(128)} %bitcast.2.place_ref, f32[8,128]{1,0:T(8,128)S(1)} %get-tuple-element.56.loaded_ref, bf16[1024,128]{1,0:T(8,128)(2,1)S(1)} %bitcast.8, ...), custom_call_target="tpu_custom_call" | custom-call | flops 805306368 | bytes 4194304 | tf_op jit(solution)/shard_map/pre_activations/pallas_call | solution.py:54
  24.6 1.2 %collective-permute-start.2 = (bf16[2,96,512]{2,1,0:T(8,128)(2,1)S(1)}, bf16[2,96,512]{2,1,0:T(8,128)(2,1)S(1)}, u32[]{:S(2)}, u32[]{:S(2)}) collective-permute-start(bf16[2,96,512]{2,1,0:T(8,128)(2,1)S(1)} %get-tuple-element.66), channel_id=1, source_target_pairs={{0,16},{16,0},{1,17},{17,1},{2,18},{18,2},{3,19},{19,3},{4,20},{20... | collective-permute-start | bytes 589832 | tf_op jit(solution)/shard_map/ppermute | solution.py:430
  25.7 2.8 %pre_activations.3 = (bf16[2048,96]{1,0:T(8,128)(2,1)S(1)}, f32[2,96,384]{2,1,0:T(8,128)S(1)}, bf16[2,96,384]{2,1,0:T(8,128)(2,1)S(1)}) custom-call(bf16[96,2048]{1,0:T(8,128)(2,1)S(1)} %get-tuple-element.62.rows_ref, bf16[2048,896]{1,0:T(8,128)(2,1)} %gate_w.3, bf16[2048,896]{1,0:T(8,128)(2,1)} %up_w.3), custom_call_target="tpu_custom_call" | custom-call | flops 603979776 | bytes 3145728 | tf_op jit(solution)/shard_map/pre_activations/pallas_call | solution.py:54
  28.5 1.0 %collective-permute-start.1 = (bf16[2,96,384]{2,1,0:T(8,128)(2,1)S(1)}, bf16[2,96,384]{2,1,0:T(8,128)(2,1)S(1)}, u32[]{:S(2)}, u32[]{:S(2)}) collective-permute-start(bf16[2,96,384]{2,1,0:T(8,128)(2,1)S(1)} %get-tuple-element.64), channel_id=1, source_target_pairs={{0,16},{16,0},{1,17},{17,1},{2,18},{18,2},{3,19},{19,3},{4,20},{20... | collective-permute-start | bytes 442376 | tf_op jit(solution)/shard_map/ppermute | solution.py:430
  29.5 2.8 %collective-permute-done.2.got_ref = bf16[2,96,512]{2,1,0:T(8,128)(2,1)S(1)} collective-permute-done((bf16[2,96,512]{2,1,0:T(8,128)(2,1)S(1)}, bf16[2,96,512]{2,1,0:T(8,128)(2,1)S(1)}, u32[]{:S(2)}, u32[]{:S(2)}) %collective-permute-start.2) | collective-permute-done | bytes 196640 | tf_op jit(solution)/shard_map/ppermute | solution.py:430
  32.3 0.5 down.1
  32.9 2.3 %collective-permute-done.1.got_ref = bf16[2,96,384]{2,1,0:T(8,128)(2,1)S(1)} collective-permute-done((bf16[2,96,384]{2,1,0:T(8,128)(2,1)S(1)}, bf16[2,96,384]{2,1,0:T(8,128)(2,1)S(1)}, u32[]{:S(2)}, u32[]{:S(2)}) %collective-permute-start.1) | collective-permute-done | bytes 147488 | tf_op jit(solution)/shard_map/ppermute | solution.py:430
  35.1 0.3 down_send.1
  35.5 0.3 down_keep.1.own_ref
  35.8 1.1 %collective-permute-done.3.got_ref = bf16[768,128]{1,0:T(8,128)(2,1)S(1)} collective-permute-done((bf16[768,128]{1,0:T(8,128)(2,1)S(1)}, bf16[768,128]{1,0:T(8,128)(2,1)S(1)}, u32[]{:S(2)}, u32[]{:S(2)}) %collective-permute-start.3) | collective-permute-done | bytes 196640 | tf_op jit(solution)/shard_map/ppermute | solution.py:424
  37.0 0.8 %collective-permute-start.4 = (bf16[192,128]{1,0:T(8,128)(2,1)S(1)}, bf16[192,128]{1,0:T(8,128)(2,1)S(1)}, u32[]{:S(2)}, u32[]{:S(2)}) collective-permute-start(bf16[192,128]{1,0:T(8,128)(2,1)S(1)} %get-tuple-element.71), channel_id=1, source_target_pairs={{0,2},{1,3},{2,0},{3,1},{4,6},{5,7},{6,4},{7,5},{8,10},{9,11},{10,... | collective-permute-start | bytes 147464 | tf_op jit(solution)/shard_map/ppermute | solution.py:424
  37.9 0.7 collective-permute-start.5
  38.6 2.0 %collective-permute-start.6 = (bf16[192,128]{1,0:T(8,128)(2,1)S(1)}, bf16[192,128]{1,0:T(8,128)(2,1)S(1)}, u32[]{:S(2)}, u32[]{:S(2)}) collective-permute-start(bf16[192,128]{1,0:T(8,128)(2,1)S(1)} %get-tuple-element.73), channel_id=1, source_target_pairs={{0,6},{1,7},{2,4},{3,5},{4,2},{5,3},{6,0},{7,1},{8,14},{9,15},{10,... | collective-permute-start | bytes 147464 | tf_op jit(solution)/shard_map/ppermute | solution.py:424
  40.6 0.6 collective-permute-done.4.first_ref
  41.2 1.1 %collective-permute-done.5.second_ref = bf16[192,128]{1,0:T(8,128)(2,1)S(1)} collective-permute-done((bf16[192,128]{1,0:T(8,128)(2,1)S(1)}, bf16[192,128]{1,0:T(8,128)(2,1)S(1)}, u32[]{:S(2)}, u32[]{:S(2)}) %collective-permute-start.5) | collective-permute-done | bytes 49184 | tf_op jit(solution)/shard_map/ppermute | solution.py:424
  42.2 1.3 %collective-permute-done.6.third_ref = bf16[192,128]{1,0:T(8,128)(2,1)S(1)} collective-permute-done((bf16[192,128]{1,0:T(8,128)(2,1)S(1)}, bf16[192,128]{1,0:T(8,128)(2,1)S(1)}, u32[]{:S(2)}, u32[]{:S(2)}) %collective-permute-start.6) | collective-permute-done | bytes 49184 | tf_op jit(solution)/shard_map/ppermute | solution.py:424
  43.6 1.7 %collective-permute-start.7 = (bf16[192,128]{1,0:T(8,128)(2,1)S(1)}, bf16[192,128]{1,0:T(8,128)(2,1)S(1)}, u32[]{:S(2)}, u32[]{:S(2)}) collective-permute-start(bf16[192,128]{1,0:T(8,128)(2,1)S(1)} %get-tuple-element.77), channel_id=1, source_target_pairs={{0,8},{1,9},{2,10},{3,11},{4,12},{5,13},{6,14},{7,15},{8,0},{9,1},... | collective-permute-start | bytes 147464 | tf_op jit(solution)/shard_map/ppermute | solution.py:424
  45.3 3.4 %collective-permute-done.7.got_ref = bf16[192,128]{1,0:T(8,128)(2,1)S(1)} collective-permute-done((bf16[192,128]{1,0:T(8,128)(2,1)S(1)}, bf16[192,128]{1,0:T(8,128)(2,1)S(1)}, u32[]{:S(2)}, u32[]{:S(2)}) %collective-permute-start.7) | collective-permute-done | bytes 49184 | tf_op jit(solution)/shard_map/ppermute | solution.py:424
  48.8 2.1 %collective-permute-start.10 = (bf16[192,128]{1,0:T(8,128)(2,1)S(1)}, bf16[192,128]{1,0:T(8,128)(2,1)S(1)}, u32[]{:S(2)}, u32[]{:S(2)}) collective-permute-start(bf16[192,128]{1,0:T(8,128)(2,1)S(1)} %cotangent.1.refs_0_), channel_id=1, source_target_pairs={{0,6},{1,7},{2,4},{3,5},{4,2},{5,3},{6,0},{7,1},{8,14},{9,15},{10,... | collective-permute-start | bytes 147464 | tf_op jit(solution)/shard_map/ppermute | solution.py:424
  50.8 0.8 collective-permute-start.8
  51.6 0.7 collective-permute-start.9
  52.3 0.3 grad_hidden_near.3.refs_1_
  52.6 0.3 grad_hidden_near.4.refs_3_
  52.9 0.9 %collective-permute-done.10.refs_2_ = bf16[192,128]{1,0:T(8,128)(2,1)S(1)} collective-permute-done((bf16[192,128]{1,0:T(8,128)(2,1)S(1)}, bf16[192,128]{1,0:T(8,128)(2,1)S(1)}, u32[]{:S(2)}, u32[]{:S(2)}) %collective-permute-start.10) | collective-permute-done | bytes 49184 | tf_op jit(solution)/shard_map/ppermute | solution.py:424
  53.8 1.1 %collective-permute-done.8.refs_0_ = bf16[192,128]{1,0:T(8,128)(2,1)S(1)} collective-permute-done((bf16[192,128]{1,0:T(8,128)(2,1)S(1)}, bf16[192,128]{1,0:T(8,128)(2,1)S(1)}, u32[]{:S(2)}, u32[]{:S(2)}) %collective-permute-start.8) | collective-permute-done | bytes 49184 | tf_op jit(solution)/shard_map/ppermute | solution.py:424
  54.9 0.8 collective-permute-done.9.refs_1_
  55.7 0.5 collective-permute-start.13
  56.2 0.6 grad_hidden_near.5.total_ref
  56.9 0.2 collective-permute-done.13.second_ref
  57.1 0.3 collective-permute-done.14.third_ref
  57.4 0.4 grad_hidden.2
  57.8 1.0 %collective-permute-start.16 = (bf16[96,512]{1,0:T(8,128)(2,1)S(1)}, bf16[96,512]{1,0:T(8,128)(2,1)S(1)}, u32[]{:S(2)}, u32[]{:S(2)}) collective-permute-start(bf16[96,512]{1,0:T(8,128)(2,1)S(1)} %get-tuple-element.88), channel_id=1, source_target_pairs={{0,16},{16,0},{1,17},{17,1},{2,18},{18,2},{3,19},{19,3},{4,20},{20... | collective-permute-start | bytes 294920 | tf_op jit(solution)/shard_map/ppermute | solution.py:430
  58.8 0.3 grad_hidden.3
  59.1 1.2 %collective-permute-start.15 = (bf16[96,384]{1,0:T(8,128)(2,1)S(1)}, bf16[96,384]{1,0:T(8,128)(2,1)S(1)}, u32[]{:S(2)}, u32[]{:S(2)}) collective-permute-start(bf16[96,384]{1,0:T(8,128)(2,1)S(1)} %get-tuple-element.84), channel_id=1, source_target_pairs={{0,16},{16,0},{1,17},{17,1},{2,18},{18,2},{3,19},{19,3},{4,20},{20... | collective-permute-start | bytes 221192 | tf_op jit(solution)/shard_map/ppermute | solution.py:430
  60.3 3.2 %collective-permute-done.16.got_ref = bf16[96,512]{1,0:T(8,128)(2,1)S(1)} collective-permute-done((bf16[96,512]{1,0:T(8,128)(2,1)S(1)}, bf16[96,512]{1,0:T(8,128)(2,1)S(1)}, u32[]{:S(2)}, u32[]{:S(2)}) %collective-permute-start.16) | collective-permute-done | bytes 98336 | tf_op jit(solution)/shard_map/ppermute | solution.py:430
  63.5 1.4 %row_grad.2 = (bf16[96,512]{1,0:T(8,128)(2,1)S(1)}, bf16[96,512]{1,0:T(8,128)(2,1)S(1)}, f32[96,2048]{1,0:T(8,128)S(1)}) custom-call(s32[1]{0:T(128)} %bitcast.2.place_ref, f32[96,512]{1,0:T(8,128)S(1)} %get-tuple-element.87.own_ref, bf16[96,512]{1,0:T(8,128)(2,1)S(1)} %collective-permute-done.16.got_ref, f32[96,512]{1,0:T(8,128)S(1)} %get-tuple-element.89.up_deriv, ...), custom_call_target="tpu_custom_call" | custom-call | flops 805306368 | bytes 4194304 | tf_op jit(solution)/shard_map/row_grad/pallas_call | solution.py:54
  65.0 1.3 %row_grad.3 = (bf16[96,384]{1,0:T(8,128)(2,1)S(1)}, bf16[96,384]{1,0:T(8,128)(2,1)S(1)}, f32[768,128]{1,0:T(8,128)S(1)}, bf16[768,128]{1,0:T(8,128)(2,1)S(1)}) custom-call(s32[1]{0:T(128)} %bitcast.2.place_ref, f32[96,384]{1,0:T(8,128)S(1)} %get-tuple-element.83.own_ref, bf16[96,384]{1,0:T(8,128)(2,1)S(1)} %collective-permute-done.15.got_ref, ...), custom_call_target="tpu_custom_call" | custom-call | flops 603979776 | bytes 3145728 | tf_op jit(solution)/shard_map/row_grad/pallas_call | solution.py:54
  66.3 1.4 %collective-permute-done.17.got_ref = bf16[768,128]{1,0:T(8,128)(2,1)S(1)} collective-permute-done((bf16[768,128]{1,0:T(8,128)(2,1)S(1)}, bf16[768,128]{1,0:T(8,128)(2,1)S(1)}, u32[]{:S(2)}, u32[]{:S(2)}) %collective-permute-start.17) | collective-permute-done | bytes 196640 | tf_op jit(solution)/shard_map/ppermute | solution.py:424
  67.8 0.7 add_cores.1
  68.5 4.1 %all-to-all-start.1 = ((bf16[16,48,128]{2,1,0:T(8,128)(2,1)}), bf16[16,48,128]{2,1,0:T(8,128)(2,1)S(1)}, u32[]{:S(2)}, u32[]{:S(2)}) async-start(bf16[16,48,128]{2,1,0:T(8,128)(2,1)} %bitcast.5), calls=%async_computation.1 | async-start | bytes 393216 | tf_op jit(solution)/shard_map/all_to_all | solution.py:433
  72.6 3.4 %weight_grads.1 = (bf16[2048,896]{1,0:T(8,128)(2,1)}, bf16[2048,896]{1,0:T(8,128)(2,1)}) custom-call(bf16[2048,96]{1,0:T(8,128)(2,1)S(1)} %get-tuple-element.94.turned_ref, bf16[96,512]{1,0:T(8,128)(2,1)S(1)} %get-tuple-element.95.refs_0_, bf16[96,384]{1,0:T(8,128)(2,1)S(1)} %get-tuple-element.96.refs_1_, bf16[96,512]{1,0:T(8,128)(2,1)S(1)} %get-tuple-element.97.refs_2_, ...), custom_call_target="tpu_custom_call" | custom-call | flops 704643072 | bytes 7340032 | tf_op jit(solution)/shard_map/weight_grads/pallas_call | solution.py:54
  76.0 5.3 %all-to-all-done.1 = bf16[16,48,128]{2,1,0:T(8,128)(2,1)S(1)} async-done(((bf16[16,48,128]{2,1,0:T(8,128)(2,1)}), bf16[16,48,128]{2,1,0:T(8,128)(2,1)S(1)}, u32[]{:S(2)}, u32[]{:S(2)}) %all-to-all-start.1) | async-done | bytes 196640 | tf_op jit(solution)/shard_map/all_to_all | solution.py:433
  81.2 1.3 %token_grad.1 = bf16[128,4096]{1,0:T(8,128)(2,1)} custom-call(bf16[16,128]{1,0:T(8,128)(2,1)S(1)} %get-tuple-element.52.pick_ref, bf16[768,128]{1,0:T(8,128)(2,1)S(1)} %bitcast.9), custom_call_target="tpu_custom_call" | custom-call | tf_op jit(solution)/shard_map/token_grad/pallas_call | solution.py:54
  (19 shorter events, 0.5 us)
Async XLA Ops:
  3.3 18.2 %all-to-all-start = ((bf16[16,64,128]{2,1,0:T(8,128)(2,1)}), bf16[16,64,128]{2,1,0:T(8,128)(2,1)S(1)}, u32[]{:S(2)}, u32[]{:S(2)}) async-start(bf16[16,64,128]{2,1,0:T(8,128)(2,1)} %bitcast.3), calls=%async_computation | async-start | bytes 524288 | tf_op jit(solution)/shard_map/all_to_all | solution.py:433
  21.5 1.6 %collective-permute-start = (bf16[1024,128]{1,0:T(8,128)(2,1)S(1)}, bf16[1024,128]{1,0:T(8,128)(2,1)S(1)}, u32[]{:S(2)}, u32[]{:S(2)}) collective-permute-start(bf16[1024,128]{1,0:T(8,128)(2,1)S(1)} %bitcast.7), channel_id=1, source_target_pairs={{0,1},{1,0},{2,3},{3,2},{4,5},{5,4},{6,7},{7,6},{8,9},{9,8},{10,11... | collective-permute-start | bytes 786440 | tf_op jit(solution)/shard_map/ppermute | solution.py:424
  24.6 7.8 %collective-permute-start.2 = (bf16[2,96,512]{2,1,0:T(8,128)(2,1)S(1)}, bf16[2,96,512]{2,1,0:T(8,128)(2,1)S(1)}, u32[]{:S(2)}, u32[]{:S(2)}) collective-permute-start(bf16[2,96,512]{2,1,0:T(8,128)(2,1)S(1)} %get-tuple-element.66), channel_id=1, source_target_pairs={{0,16},{16,0},{1,17},{17,1},{2,18},{18,2},{3,19},{19,3},{4,20},{20... | collective-permute-start | bytes 589832 | tf_op jit(solution)/shard_map/ppermute | solution.py:430
  25.7 6.6 %copy-start = (bf16[896,2048]{1,0:T(8,128)(2,1)S(1)}, bf16[896,2048]{1,0:T(8,128)(2,1)}, u32[]{:S(2)}) copy-start(bf16[896,2048]{1,0:T(8,128)(2,1)} %down_w.15) | copy-start | bytes 11010052
  28.5 6.6 %collective-permute-start.1 = (bf16[2,96,384]{2,1,0:T(8,128)(2,1)S(1)}, bf16[2,96,384]{2,1,0:T(8,128)(2,1)S(1)}, u32[]{:S(2)}, u32[]{:S(2)}) collective-permute-start(bf16[2,96,384]{2,1,0:T(8,128)(2,1)S(1)} %get-tuple-element.64), channel_id=1, source_target_pairs={{0,16},{16,0},{1,17},{17,1},{2,18},{18,2},{3,19},{19,3},{4,20},{20... | collective-permute-start | bytes 442376 | tf_op jit(solution)/shard_map/ppermute | solution.py:430
  35.5 1.5 %collective-permute-start.3 = (bf16[768,128]{1,0:T(8,128)(2,1)S(1)}, bf16[768,128]{1,0:T(8,128)(2,1)S(1)}, u32[]{:S(2)}, u32[]{:S(2)}) collective-permute-start(bf16[768,128]{1,0:T(8,128)(2,1)S(1)} %get-tuple-element.69), channel_id=1, source_target_pairs={{0,1},{1,0},{2,3},{3,2},{4,5},{5,4},{6,7},{7,6},{8,9},{9,8},{10,11... | collective-permute-start | bytes 589832 | tf_op jit(solution)/shard_map/ppermute | solution.py:424
  37.0 4.2 %collective-permute-start.4 = (bf16[192,128]{1,0:T(8,128)(2,1)S(1)}, bf16[192,128]{1,0:T(8,128)(2,1)S(1)}, u32[]{:S(2)}, u32[]{:S(2)}) collective-permute-start(bf16[192,128]{1,0:T(8,128)(2,1)S(1)} %get-tuple-element.71), channel_id=1, source_target_pairs={{0,2},{1,3},{2,0},{3,1},{4,6},{5,7},{6,4},{7,5},{8,10},{9,11},{10,... | collective-permute-start | bytes 147464 | tf_op jit(solution)/shard_map/ppermute | solution.py:424
  37.9 4.4 %collective-permute-start.5 = (bf16[192,128]{1,0:T(8,128)(2,1)S(1)}, bf16[192,128]{1,0:T(8,128)(2,1)S(1)}, u32[]{:S(2)}, u32[]{:S(2)}) collective-permute-start(bf16[192,128]{1,0:T(8,128)(2,1)S(1)} %get-tuple-element.72), channel_id=1, source_target_pairs={{0,4},{1,5},{2,6},{3,7},{4,0},{5,1},{6,2},{7,3},{8,12},{9,13},{10,... | collective-permute-start | bytes 147464 | tf_op jit(solution)/shard_map/ppermute | solution.py:424
  38.6 5.0 %collective-permute-start.6 = (bf16[192,128]{1,0:T(8,128)(2,1)S(1)}, bf16[192,128]{1,0:T(8,128)(2,1)S(1)}, u32[]{:S(2)}, u32[]{:S(2)}) collective-permute-start(bf16[192,128]{1,0:T(8,128)(2,1)S(1)} %get-tuple-element.73), channel_id=1, source_target_pairs={{0,6},{1,7},{2,4},{3,5},{4,2},{5,3},{6,0},{7,1},{8,14},{9,15},{10,... | collective-permute-start | bytes 147464 | tf_op jit(solution)/shard_map/ppermute | solution.py:424
  43.6 5.1 %collective-permute-start.7 = (bf16[192,128]{1,0:T(8,128)(2,1)S(1)}, bf16[192,128]{1,0:T(8,128)(2,1)S(1)}, u32[]{:S(2)}, u32[]{:S(2)}) collective-permute-start(bf16[192,128]{1,0:T(8,128)(2,1)S(1)} %get-tuple-element.77), channel_id=1, source_target_pairs={{0,8},{1,9},{2,10},{3,11},{4,12},{5,13},{6,14},{7,15},{8,0},{9,1},... | collective-permute-start | bytes 147464 | tf_op jit(solution)/shard_map/ppermute | solution.py:424
  48.7 3.9 %collective-permute-start.11 = (bf16[192,128]{1,0:T(8,128)(2,1)S(1)}, bf16[192,128]{1,0:T(8,128)(2,1)S(1)}, u32[]{:S(2)}, u32[]{:S(2)}) collective-permute-start(bf16[192,128]{1,0:T(8,128)(2,1)S(1)} %cotangent.1.refs_0_), channel_id=1, source_target_pairs={{0,1},{1,0},{2,3},{3,2},{4,5},{5,4},{6,7},{7,6},{8,9},{9,8},{10,11... | collective-permute-start | bytes 147464 | tf_op jit(solution)/shard_map/ppermute | solution.py:424
  48.8 5.1 %collective-permute-start.10 = (bf16[192,128]{1,0:T(8,128)(2,1)S(1)}, bf16[192,128]{1,0:T(8,128)(2,1)S(1)}, u32[]{:S(2)}, u32[]{:S(2)}) collective-permute-start(bf16[192,128]{1,0:T(8,128)(2,1)S(1)} %cotangent.1.refs_0_), channel_id=1, source_target_pairs={{0,6},{1,7},{2,4},{3,5},{4,2},{5,3},{6,0},{7,1},{8,14},{9,15},{10,... | collective-permute-start | bytes 147464 | tf_op jit(solution)/shard_map/ppermute | solution.py:424
  50.8 4.1 %collective-permute-start.8 = (bf16[192,128]{1,0:T(8,128)(2,1)S(1)}, bf16[192,128]{1,0:T(8,128)(2,1)S(1)}, u32[]{:S(2)}, u32[]{:S(2)}) collective-permute-start(bf16[192,128]{1,0:T(8,128)(2,1)S(1)} %cotangent.1.refs_0_), channel_id=1, source_target_pairs={{0,2},{1,3},{2,0},{3,1},{4,6},{5,7},{6,4},{7,5},{8,10},{9,11},{10,... | collective-permute-start | bytes 147464 | tf_op jit(solution)/shard_map/ppermute | solution.py:424
  51.6 4.1 %collective-permute-start.9 = (bf16[192,128]{1,0:T(8,128)(2,1)S(1)}, bf16[192,128]{1,0:T(8,128)(2,1)S(1)}, u32[]{:S(2)}, u32[]{:S(2)}) collective-permute-start(bf16[192,128]{1,0:T(8,128)(2,1)S(1)} %cotangent.1.refs_0_), channel_id=1, source_target_pairs={{0,4},{1,5},{2,6},{3,7},{4,0},{5,1},{6,2},{7,3},{8,12},{9,13},{10,... | collective-permute-start | bytes 147464 | tf_op jit(solution)/shard_map/ppermute | solution.py:424
  55.7 1.2 %collective-permute-start.12 = (bf16[192,128]{1,0:T(8,128)(2,1)S(1)}, bf16[192,128]{1,0:T(8,128)(2,1)S(1)}, u32[]{:S(2)}, u32[]{:S(2)}) collective-permute-start(bf16[192,128]{1,0:T(8,128)(2,1)S(1)} %collective-permute-done.8.refs_0_), channel_id=1, source_target_pairs={{0,1},{1,0},{2,3},{3,2},{4,5},{5,4},{6,7},{7,6},{8,9},{9,8},{10,11... | collective-permute-start | bytes 147464 | tf_op jit(solution)/shard_map/ppermute | solution.py:424
  55.7 1.4 %collective-permute-start.13 = (bf16[192,128]{1,0:T(8,128)(2,1)S(1)}, bf16[192,128]{1,0:T(8,128)(2,1)S(1)}, u32[]{:S(2)}, u32[]{:S(2)}) collective-permute-start(bf16[192,128]{1,0:T(8,128)(2,1)S(1)} %collective-permute-done.9.refs_1_), channel_id=1, source_target_pairs={{0,1},{1,0},{2,3},{3,2},{4,5},{5,4},{6,7},{7,6},{8,9},{9,8},{10,11... | collective-permute-start | bytes 147464 | tf_op jit(solution)/shard_map/ppermute | solution.py:424
  56.2 1.2 %collective-permute-start.14 = (bf16[192,128]{1,0:T(8,128)(2,1)S(1)}, bf16[192,128]{1,0:T(8,128)(2,1)S(1)}, u32[]{:S(2)}, u32[]{:S(2)}) collective-permute-start(bf16[192,128]{1,0:T(8,128)(2,1)S(1)} %collective-permute-done.10.refs_2_), channel_id=1, source_target_pairs={{0,1},{1,0},{2,3},{3,2},{4,5},{5,4},{6,7},{7,6},{8,9},{9,8},{10,11... | collective-permute-start | bytes 147464 | tf_op jit(solution)/shard_map/ppermute | solution.py:424
  56.8 6.8 %copy-start.1 = (bf16[2048,896]{1,0:T(8,128)(2,1)S(1)}, bf16[2048,896]{1,0:T(8,128)(2,1)}, u32[]{:S(2)}) copy-start(bf16[2048,896]{1,0:T(8,128)(2,1)} %gate_w.3) | copy-start | bytes 11010052
  56.8 6.8 %copy-start.2 = (bf16[2048,896]{1,0:T(8,128)(2,1)S(1)}, bf16[2048,896]{1,0:T(8,128)(2,1)}, u32[]{:S(2)}) copy-start(bf16[2048,896]{1,0:T(8,128)(2,1)} %up_w.3) | copy-start | bytes 11010052
  57.8 5.7 %collective-permute-start.16 = (bf16[96,512]{1,0:T(8,128)(2,1)S(1)}, bf16[96,512]{1,0:T(8,128)(2,1)S(1)}, u32[]{:S(2)}, u32[]{:S(2)}) collective-permute-start(bf16[96,512]{1,0:T(8,128)(2,1)S(1)} %get-tuple-element.88), channel_id=1, source_target_pairs={{0,16},{16,0},{1,17},{17,1},{2,18},{18,2},{3,19},{19,3},{4,20},{20... | collective-permute-start | bytes 294920 | tf_op jit(solution)/shard_map/ppermute | solution.py:430
  59.1 5.9 %collective-permute-start.15 = (bf16[96,384]{1,0:T(8,128)(2,1)S(1)}, bf16[96,384]{1,0:T(8,128)(2,1)S(1)}, u32[]{:S(2)}, u32[]{:S(2)}) collective-permute-start(bf16[96,384]{1,0:T(8,128)(2,1)S(1)} %get-tuple-element.84), channel_id=1, source_target_pairs={{0,16},{16,0},{1,17},{17,1},{2,18},{18,2},{3,19},{19,3},{4,20},{20... | collective-permute-start | bytes 221192 | tf_op jit(solution)/shard_map/ppermute | solution.py:430
  66.3 1.5 %collective-permute-start.17 = (bf16[768,128]{1,0:T(8,128)(2,1)S(1)}, bf16[768,128]{1,0:T(8,128)(2,1)S(1)}, u32[]{:S(2)}, u32[]{:S(2)}) collective-permute-start(bf16[768,128]{1,0:T(8,128)(2,1)S(1)} %get-tuple-element.93), channel_id=1, source_target_pairs={{0,1},{1,0},{2,3},{3,2},{4,5},{5,4},{6,7},{7,6},{8,9},{9,8},{10,11... | collective-permute-start | bytes 589832 | tf_op jit(solution)/shard_map/ppermute | solution.py:424
  68.5 12.8 %all-to-all-start.1 = ((bf16[16,48,128]{2,1,0:T(8,128)(2,1)}), bf16[16,48,128]{2,1,0:T(8,128)(2,1)S(1)}, u32[]{:S(2)}, u32[]{:S(2)}) async-start(bf16[16,48,128]{2,1,0:T(8,128)(2,1)} %bitcast.5), calls=%async_computation.1 | async-start | bytes 393216 | tf_op jit(solution)/shard_map/all_to_all | solution.py:433

commit v7 on v6

--- a/solution.py
+++ b/solution.py
@@ -132,11 +132,21 @@
             out_ref[base + lead : base + unit, :] = tail[...].astype(BF)
 
 
-def both_cores(place_ref, own_ref, other_ref, wide):
-    size = own_ref.shape[0]
-    core = core_of(place_ref)
-    wide[pl.ds(pl.multiple_of(core * size, size), size), :] = own_ref[...].astype(wide.dtype)
-    wide[pl.ds(pl.multiple_of((1 - core) * size, size), size), :] = other_ref[...].astype(wide.dtype)
+def lay_out(dims, place_ref, src_ref, wide, begin, rows_ref, target_ref, gates_ref):
+    n_dp, half, cap, blocks, unit = dims
+    peers = n_dp * half
+    wide[...] = src_ref[...].astype(F32)
+
+    def one(k):
+        return wide[pl.ds(k, peers, stride=unit), :]
+
+    for c in range(cap):
+        at = begin(c)
+        for q in range(blocks):
+            rows_ref[at, q * LANES : (q + 1) * LANES] = one(q * cap + c).astype(BF)
+        base = blocks * cap
+        target_ref[at, :] = jnp.where(core_of(place_ref) == 0, one(base + c), one(base + cap + c))
+        gates_ref[at, :] = sum(one(base + (2 + piece) * cap + c) for piece in range(GATE_PIECES))
 
 
 def fetch_columns(starts, gate_hbm, up_hbm, gate_w, up_w, sems):
@@ -153,11 +163,20 @@
     return copies
 
 
-def load_kernel(start, gate_hbm, up_hbm, *refs):
-    done_ref, gate_w, up_w, sems = refs[-4:]
-    stop = start + gate_w.shape[1]
-    copies = fetch_columns((start, stop), gate_hbm, up_hbm, gate_w, up_w, sems)
+def load_kernel(gate_hbm, up_hbm, done_ref, gate_w, up_w, sems):
+    copies = fetch_columns((0, gate_w.shape[1]), gate_hbm, up_hbm, gate_w, up_w, sems)
     done_ref[...] = jnp.zeros_like(done_ref)
+    for pair in copies:
+        for copy in pair:
+            copy.wait()
+
+
+def load_more_kernel(dims, start, place_ref, own_ref, gate_hbm, up_hbm, gate_w, up_w,
+                     rows_ref, target_ref, gates_ref, wide, sems):
+    peers = dims[0] * dims[1]
+    copies = fetch_columns((start, start + gate_w.shape[1]), gate_hbm, up_hbm, gate_w, up_w, sems)
+    begin = lambda c: slice(c * peers, (c + 1) * peers)
+    lay_out(dims, place_ref, own_ref, wide, begin, rows_ref, target_ref, gates_ref)
     for pair in copies:
         for copy in pair:
             copy.wait()
@@ -178,23 +197,22 @@
             send_pre[side, :, cols] = value.astype(BF)
 
 
-def first_pre_kernel(dims, place_ref, loaded_ref, own_ref, other_ref, gate_head, up_head, gate_rest, up_rest,
+def first_pre_kernel(dims, place_ref, loaded_ref, own_rows, own_target, own_gates, other_ref,
+                     gate_head, up_head, gate_rest, up_rest,
                      rows_ref, target_ref, gates_ref, own_pre, send_pre, wide):
     n_dp, half, cap, blocks, unit = dims
-    sources = 2 * n_dp * half
-    both_cores(place_ref, own_ref, other_ref, wide)
+    peers = n_dp * half
     core = core_of(place_ref)
 
-    def one(k):
-        return wide[pl.ds(k, sources, stride=unit), :]
+    def begin(c, side):
+        return pl.ds(pl.multiple_of((2 * c + side) * peers, peers), peers)
 
     for c in range(cap):
-        rows = slice(c * sources, (c + 1) * sources)
-        for q in range(blocks):
-            rows_ref[rows, q * LANES : (q + 1) * LANES] = one(q * cap + c).astype(BF)
-        base = blocks * cap
-        target_ref[rows, :] = jnp.where(core == 0, one(base + c), one(base + cap + c))
-        gates_ref[rows, :] = sum(one(base + (2 + piece) * cap + c) for piece in range(GATE_PIECES))
+        here = slice(c * peers, (c + 1) * peers)
+        for own, full in ((own_rows, rows_ref), (own_target, target_ref), (own_gates, gates_ref)):
+            full[begin(c, core), :] = own[here, :]
+    there = lambda c: begin(c, 1 - core)
+    lay_out(dims, place_ref, other_ref, wide, there, rows_ref, target_ref, gates_ref)
     partial_pre(rows_ref, gate_head, up_head, (), 0, own_pre, send_pre)
     partial_pre(rows_ref, gate_rest, up_rest, (), gate_head.shape[1], own_pre, send_pre)
 
@@ -332,7 +350,7 @@
     n_dp, half, cap, blocks, unit = dims
     sources = 2 * n_dp * half
     refs = list(refs)
-    total_ref = refs.pop(0) if start > 0 else None
+    total_ref = refs.pop(0) if last else None
     gate_out, up_out, *out_refs = refs
     grad_hidden = own_ref[...] + got_ref[...].astype(F32)
     gate_out[...] = (grad_hidden * up_deriv[...]).astype(BF)
@@ -453,25 +471,41 @@
     first = -(-hid // (2 * LANES)) * LANES
     head = 2 * LANES
 
-    def load(start, size, after=()):
-        return call(
-            functools.partial(load_kernel, start),
-            (sds((8, LANES), F32), sds((width, size), w_gate.dtype), sds((width, size), w_up.dtype)),
-            (*in_hbm(w_gate, w_up), *after),
-            [HBM] * 2 + [VMEM] * len(after),
-            [pltpu.SemaphoreType.DMA((-(-size // (2 * LANES)), 2))],
-            flops=1_000_000_000,
-            moved=8 * width * size,
-            name="load_weights",
-        )
-
-    loaded, *weights = load(0, head)
+    def columns(size):
+        return sds((width, size), w_gate.dtype), sds((width, size), w_up.dtype)
+
+    def column_sems(size):
+        return pltpu.SemaphoreType.DMA((-(-size // (2 * LANES)), 2))
+
+    loaded, *weights = call(
+        load_kernel,
+        (sds((8, LANES), F32), *columns(head)),
+        in_hbm(w_gate, w_up),
+        [HBM] * 2,
+        [column_sems(head)],
+        flops=1_000_000_000,
+        moved=8 * width * head,
+        name="load_weights",
+    )
     own, loaded = lax.optimization_barrier((over_slice(outgoing), loaded))
-    loaded, *more = load(head, first - head, (loaded,))
+    *more, own_rows, own_target, own_gates = call(
+        functools.partial(load_more_kernel, dims, head),
+        (
+            *columns(first - head),
+            sds((cap * peers, width), BF),
+            sds((cap * peers, LANES), F32),
+            sds((cap * peers, LANES), F32),
+        ),
+        (place, own, *in_hbm(w_gate, w_up)),
+        [SMEM, VMEM] + [HBM] * 2,
+        [pltpu.VMEM((peers * unit, LANES), F32), column_sems(first - head)],
+        flops=1_000_000_000,
+        moved=8 * width * head,
+        name="load_weights",
+    )
     weights += more
     neighbour = other_core(own)
     chunks = [(0, first), (first, hid - first)]
-    last = len(chunks) - 1
     pres = []
     for start, size in chunks:
         outs = (sds((2, rows, size), F32), sds((2, rows, size), BF))
@@ -479,15 +513,15 @@
         fetched = [
             pltpu.VMEM((width, size), w_gate.dtype),
             pltpu.VMEM((width, size), w_up.dtype),
-            pltpu.SemaphoreType.DMA((-(-size // (2 * LANES)), 2)),
+            column_sems(size),
         ]
         if start == 0:
             all_rows, all_target, all_gates, *pre = call(
                 functools.partial(first_pre_kernel, dims),
                 (sds((rows, width), BF), sds((rows, LANES), F32), sds((rows, LANES), F32), *outs),
-                (place, loaded, own, neighbour, *weights),
-                [SMEM] + [VMEM] * 7,
-                [pltpu.VMEM((sources * unit, LANES), F32)],
+                (place, loaded, own_rows, own_target, own_gates, neighbour, *weights),
+                [SMEM] + [VMEM] * 9,
+                [pltpu.VMEM((peers * unit, LANES), F32)],
                 name="pre_activations",
                 **cost,
             )
@@ -579,10 +613,12 @@
     from_both = [other_core(x) for x in from_quad]
     own_total = near(0, (1, 2, 3), from_quad, own_total)
     grads = []
-    for start, size in chunks:
+    order = [1, 0]
+    for k in order:
+        start, size = chunks[k]
         outs = (sds((rows, size), F32), sds((rows, size), BF))
         cost = dict(flops=2 * rows * width * size, moved=2 * width * size)
-        if start == 0:
+        if k == order[0]:
             cot, *grad = call(
                 functools.partial(first_grad_hidden_kernel, start),
                 (sds((rows, 3 * width // 8), BF), *outs),
@@ -601,25 +637,26 @@
                 **cost,
             )
         grads.append((grad[0], other_dp(grad[1])))
-    pre_grads = []
+    pre_grads = [None] * len(chunks)
     total = ()
     peer_rows = peers * blocks * cap
-    for k, (start, size) in enumerate(chunks):
+    for k, grad in zip(order, grads):
+        start, size = chunks[k]
         outs, scratch = (sds((rows, width), F32),), []
-        if k == last:
+        if k == order[-1]:
             outs = (sds((peer_rows, LANES), F32), sds((peer_rows, LANES), BF))
             scratch = [pltpu.VMEM((2 * peer_rows, LANES), F32)]
         gate_pre_grad, up_pre_grad, *total = call(
-            functools.partial(row_grad_kernel, dims, start, k == last),
+            functools.partial(row_grad_kernel, dims, start, k == order[-1]),
             (sds((rows, size), BF), sds((rows, size), BF), *outs),
-            (place, *grads[k], *saved[k], w_gate, w_up, *total),
+            (place, *grad, *saved[k], w_gate, w_up, *total),
             [SMEM] + [VMEM] * (6 + len(total)),
             scratch,
             flops=8 * rows * width * size,
             moved=4 * width * size,
             name="row_grad",
         )
-        pre_grads.append((gate_pre_grad, up_pre_grad))
+        pre_grads[k] = (gate_pre_grad, up_pre_grad)
     keep, send = total
     chip_rows = add_cores(keep, other_core(send))
     got_rows = over_slice(chip_rows)

time: 82.9 us -> 82.2 us (level)
  transfers between devices with their start and end apart: 20 -> 20, of which waited for: 17 -> 18; matrix products, arithmetic and copies ran while one was open for 0% -> 0% of each run, Pallas kernels for 16% -> 16%
where the time goes in v7:
time: 82.2 us; the launch traced here: 81.8 us
  waiting for transfers between devices  33.8 us (41%)
  starting transfers between devices  26.3 us (32%)
  Pallas kernels  20.9 us (25%)
  between operations  0.84 us (1%)
    pallas_call x21, Pallas kernels, call(): pl.pallas_call(body, out_shape=outs, in_specs=specs, out_specs=jax.tree.m...  20.9 us
    all_to_all x2, waiting for transfers between devices, over_slice(): lax.all_to_all(x, ('dp', 'expert'), 0, 0, axis_index_groups=slice_groups,...  13.6 us
    all_to_all x2, starting transfers between devices, over_slice(): lax.all_to_all(x, ('dp', 'expert'), 0, 0, axis_index_groups=slice_groups,...  12.4 us
    ppermute x14, waiting for transfers between devices, other(): return lax.ppermute(x, 'expert', [(i, i ^ mask) for i in range(n_expert)])  12.3 us
    ppermute x14, starting transfers between devices, other(): return lax.ppermute(x, 'expert', [(i, i ^ mask) for i in range(n_expert)])  9.56 us
    ppermute x4, waiting for transfers between devices, other_dp(): return lax.ppermute(x, 'dp', [(0, 1), (1, 0)])  7.94 us
    ppermute x4, starting transfers between devices, other_dp(): return lax.ppermute(x, 'dp', [(0, 1), (1, 0)])  4.31 us
  transfers between devices with their start and end apart: 20, of which 18 were waited for; matrix products, arithmetic and copies ran while one was open for 0% of the time, Pallas kernels for 16%

profile of v7, /device:TPU:0, one launch (start us, length us, event | category | flops | bytes accessed | tf_op | source)
XLA Modules:
  0.0 81.8 jit_solution(151791146820363481)
XLA Ops:
  0.6 2.7 %route.1 = (bf16[1024,128]{1,0:T(8,128)(2,1)}, bf16[16,128]{1,0:T(8,128)(2,1)S(1)}) custom-call(s32[2,128]{1,0:T(2,128)} %bitcast.10, f32[2,128]{1,0:T(2,128)} %bitcast.11, bf16[128,4096]{1,0:T(8,128)(2,1)} %tokens_hbm.1, bf16[128,4096]{1,0:T(8,128)(2,1)} %target_hbm.1), custom_call_target="tpu_custom_call" | custom-call | tf_op jit(solution)/shard_map/route/pallas_call | solution.py:54
  3.3 8.3 %all-to-all-start = ((bf16[16,64,128]{2,1,0:T(8,128)(2,1)}), bf16[16,64,128]{2,1,0:T(8,128)(2,1)S(1)}, u32[]{:S(2)}, u32[]{:S(2)}) async-start(bf16[16,64,128]{2,1,0:T(8,128)(2,1)} %bitcast.3), calls=%async_computation | async-start | bytes 524288 | tf_op jit(solution)/shard_map/all_to_all | solution.py:451
  11.7 1.6 %load_weights.2 = (f32[8,128]{1,0:T(8,128)S(1)}, bf16[2048,256]{1,0:T(8,128)(2,1)S(1)}, bf16[2048,256]{1,0:T(8,128)(2,1)S(1)}) custom-call(bf16[2048,896]{1,0:T(8,128)(2,1)} %gate_w.3, bf16[2048,896]{1,0:T(8,128)(2,1)} %up_w.3), custom_call_target="tpu_custom_call" | custom-call | flops 1000000000 | bytes 4194304 | tf_op jit(solution)/shard_map/load_weights/pallas_call | solution.py:54
  13.2 8.3 %all-to-all-done = bf16[16,64,128]{2,1,0:T(8,128)(2,1)S(1)} async-done(((bf16[16,64,128]{2,1,0:T(8,128)(2,1)}), bf16[16,64,128]{2,1,0:T(8,128)(2,1)S(1)}, u32[]{:S(2)}, u32[]{:S(2)}) %all-to-all-start) | async-done | bytes 262176 | tf_op jit(solution)/shard_map/all_to_all | solution.py:451
  21.5 1.6 %load_weights.3 = (bf16[2048,256]{1,0:T(8,128)(2,1)S(1)}, bf16[2048,256]{1,0:T(8,128)(2,1)S(1)}, bf16[48,2048]{1,0:T(8,128)(2,1)S(1)}, f32[48,128]{1,0:T(8,128)S(1)}, f32[48,128]{1,0:T(8,128)S(1)}) custom-call(s32[1]{0:T(128)} %bitcast.2.place_ref, bf16[1024,128]{1,0:T(8,128)(2,1)S(1)} %bitcast.8, bf16[2048,896]{1,0:T(8,128)(2,1)} %gate_w.3, ...), custom_call_target="tpu_custom_call" | custom-call | flops 1000000000 | bytes 4194304 | tf_op jit(solution)/shard_map/load_weights/pallas_call | solution.py:54
  23.1 1.1 %pre_activations.2 = (bf16[96,2048]{1,0:T(8,128)(2,1)S(1)}, f32[96,128]{1,0:T(8,128)S(1)}, f32[96,128]{1,0:T(8,128)S(1)}, f32[2,96,512]{2,1,0:T(8,128)S(1)}, bf16[2,96,512]{2,1,0:T(8,128)(2,1)S(1)}) custom-call(s32[1]{0:T(128)} %bitcast.2.place_ref, f32[8,128]{1,0:T(8,128)S(1)} %get-tuple-element.57.loaded_ref, ...), custom_call_target="tpu_custom_call" | custom-call | flops 805306368 | bytes 4194304 | tf_op jit(solution)/shard_map/pre_activations/pallas_call | solution.py:54
  24.2 1.2 %collective-permute-start.2 = (bf16[2,96,512]{2,1,0:T(8,128)(2,1)S(1)}, bf16[2,96,512]{2,1,0:T(8,128)(2,1)S(1)}, u32[]{:S(2)}, u32[]{:S(2)}) collective-permute-start(bf16[2,96,512]{2,1,0:T(8,128)(2,1)S(1)} %get-tuple-element.70), channel_id=1, source_target_pairs={{0,16},{16,0},{1,17},{17,1},{2,18},{18,2},{3,19},{19,3},{4,20},{20... | collective-permute-start | bytes 589832 | tf_op jit(solution)/shard_map/ppermute | solution.py:448
  25.4 2.8 %pre_activations.3 = (bf16[2048,96]{1,0:T(8,128)(2,1)S(1)}, f32[2,96,384]{2,1,0:T(8,128)S(1)}, bf16[2,96,384]{2,1,0:T(8,128)(2,1)S(1)}) custom-call(bf16[96,2048]{1,0:T(8,128)(2,1)S(1)} %get-tuple-element.66.rows_ref, bf16[2048,896]{1,0:T(8,128)(2,1)} %gate_w.3, bf16[2048,896]{1,0:T(8,128)(2,1)} %up_w.3), custom_call_target="tpu_custom_call" | custom-call | flops 603979776 | bytes 3145728 | tf_op jit(solution)/shard_map/pre_activations/pallas_call | solution.py:54
  28.1 1.0 %collective-permute-start.1 = (bf16[2,96,384]{2,1,0:T(8,128)(2,1)S(1)}, bf16[2,96,384]{2,1,0:T(8,128)(2,1)S(1)}, u32[]{:S(2)}, u32[]{:S(2)}) collective-permute-start(bf16[2,96,384]{2,1,0:T(8,128)(2,1)S(1)} %get-tuple-element.68), channel_id=1, source_target_pairs={{0,16},{16,0},{1,17},{17,1},{2,18},{18,2},{3,19},{19,3},{4,20},{20... | collective-permute-start | bytes 442376 | tf_op jit(solution)/shard_map/ppermute | solution.py:448
  29.1 2.8 %collective-permute-done.2.got_ref = bf16[2,96,512]{2,1,0:T(8,128)(2,1)S(1)} collective-permute-done((bf16[2,96,512]{2,1,0:T(8,128)(2,1)S(1)}, bf16[2,96,512]{2,1,0:T(8,128)(2,1)S(1)}, u32[]{:S(2)}, u32[]{:S(2)}) %collective-permute-start.2) | collective-permute-done | bytes 196640 | tf_op jit(solution)/shard_map/ppermute | solution.py:448
  32.0 0.5 down.1
  32.5 2.2 %collective-permute-done.1.got_ref = bf16[2,96,384]{2,1,0:T(8,128)(2,1)S(1)} collective-permute-done((bf16[2,96,384]{2,1,0:T(8,128)(2,1)S(1)}, bf16[2,96,384]{2,1,0:T(8,128)(2,1)S(1)}, u32[]{:S(2)}, u32[]{:S(2)}) %collective-permute-start.1) | collective-permute-done | bytes 147488 | tf_op jit(solution)/shard_map/ppermute | solution.py:448
  34.7 0.3 down_send.1
  35.2 0.3 down_keep.1.own_ref
  35.5 1.1 %collective-permute-done.3.got_ref = bf16[768,128]{1,0:T(8,128)(2,1)S(1)} collective-permute-done((bf16[768,128]{1,0:T(8,128)(2,1)S(1)}, bf16[768,128]{1,0:T(8,128)(2,1)S(1)}, u32[]{:S(2)}, u32[]{:S(2)}) %collective-permute-start.3) | collective-permute-done | bytes 196640 | tf_op jit(solution)/shard_map/ppermute | solution.py:442
  36.7 0.8 %collective-permute-start.4 = (bf16[192,128]{1,0:T(8,128)(2,1)S(1)}, bf16[192,128]{1,0:T(8,128)(2,1)S(1)}, u32[]{:S(2)}, u32[]{:S(2)}) collective-permute-start(bf16[192,128]{1,0:T(8,128)(2,1)S(1)} %get-tuple-element.75), channel_id=1, source_target_pairs={{0,2},{1,3},{2,0},{3,1},{4,6},{5,7},{6,4},{7,5},{8,10},{9,11},{10,... | collective-permute-start | bytes 147464 | tf_op jit(solution)/shard_map/ppermute | solution.py:442
  37.5 0.7 collective-permute-start.5
  38.2 2.0 %collective-permute-start.6 = (bf16[192,128]{1,0:T(8,128)(2,1)S(1)}, bf16[192,128]{1,0:T(8,128)(2,1)S(1)}, u32[]{:S(2)}, u32[]{:S(2)}) collective-permute-start(bf16[192,128]{1,0:T(8,128)(2,1)S(1)} %get-tuple-element.77), channel_id=1, source_target_pairs={{0,6},{1,7},{2,4},{3,5},{4,2},{5,3},{6,0},{7,1},{8,14},{9,15},{10,... | collective-permute-start | bytes 147464 | tf_op jit(solution)/shard_map/ppermute | solution.py:442
  40.2 0.6 collective-permute-done.4.first_ref
  40.8 1.1 %collective-permute-done.5.second_ref = bf16[192,128]{1,0:T(8,128)(2,1)S(1)} collective-permute-done((bf16[192,128]{1,0:T(8,128)(2,1)S(1)}, bf16[192,128]{1,0:T(8,128)(2,1)S(1)}, u32[]{:S(2)}, u32[]{:S(2)}) %collective-permute-start.5) | collective-permute-done | bytes 49184 | tf_op jit(solution)/shard_map/ppermute | solution.py:442
  41.9 1.2 %collective-permute-done.6.third_ref = bf16[192,128]{1,0:T(8,128)(2,1)S(1)} collective-permute-done((bf16[192,128]{1,0:T(8,128)(2,1)S(1)}, bf16[192,128]{1,0:T(8,128)(2,1)S(1)}, u32[]{:S(2)}, u32[]{:S(2)}) %collective-permute-start.6) | collective-permute-done | bytes 49184 | tf_op jit(solution)/shard_map/ppermute | solution.py:442
  43.2 1.7 %collective-permute-start.7 = (bf16[192,128]{1,0:T(8,128)(2,1)S(1)}, bf16[192,128]{1,0:T(8,128)(2,1)S(1)}, u32[]{:S(2)}, u32[]{:S(2)}) collective-permute-start(bf16[192,128]{1,0:T(8,128)(2,1)S(1)} %get-tuple-element.81), channel_id=1, source_target_pairs={{0,8},{1,9},{2,10},{3,11},{4,12},{5,13},{6,14},{7,15},{8,0},{9,1},... | collective-permute-start | bytes 147464 | tf_op jit(solution)/shard_map/ppermute | solution.py:442
  44.9 3.3 %collective-permute-done.7.got_ref = bf16[192,128]{1,0:T(8,128)(2,1)S(1)} collective-permute-done((bf16[192,128]{1,0:T(8,128)(2,1)S(1)}, bf16[192,128]{1,0:T(8,128)(2,1)S(1)}, u32[]{:S(2)}, u32[]{:S(2)}) %collective-permute-start.7) | collective-permute-done | bytes 49184 | tf_op jit(solution)/shard_map/ppermute | solution.py:442
  48.4 2.1 %collective-permute-start.10 = (bf16[192,128]{1,0:T(8,128)(2,1)S(1)}, bf16[192,128]{1,0:T(8,128)(2,1)S(1)}, u32[]{:S(2)}, u32[]{:S(2)}) collective-permute-start(bf16[192,128]{1,0:T(8,128)(2,1)S(1)} %cotangent.1.refs_0_), channel_id=1, source_target_pairs={{0,6},{1,7},{2,4},{3,5},{4,2},{5,3},{6,0},{7,1},{8,14},{9,15},{10,... | collective-permute-start | bytes 147464 | tf_op jit(solution)/shard_map/ppermute | solution.py:442
  50.5 0.8 collective-permute-start.8
  51.2 0.7 collective-permute-start.9
  51.9 0.3 grad_hidden_near.3.refs_1_
  52.2 0.3 grad_hidden_near.4.refs_3_
  52.5 0.9 %collective-permute-done.10.refs_2_ = bf16[192,128]{1,0:T(8,128)(2,1)S(1)} collective-permute-done((bf16[192,128]{1,0:T(8,128)(2,1)S(1)}, bf16[192,128]{1,0:T(8,128)(2,1)S(1)}, u32[]{:S(2)}, u32[]{:S(2)}) %collective-permute-start.10) | collective-permute-done | bytes 49184 | tf_op jit(solution)/shard_map/ppermute | solution.py:442
  53.4 1.1 %collective-permute-done.8.refs_0_ = bf16[192,128]{1,0:T(8,128)(2,1)S(1)} collective-permute-done((bf16[192,128]{1,0:T(8,128)(2,1)S(1)}, bf16[192,128]{1,0:T(8,128)(2,1)S(1)}, u32[]{:S(2)}, u32[]{:S(2)}) %collective-permute-start.8) | collective-permute-done | bytes 49184 | tf_op jit(solution)/shard_map/ppermute | solution.py:442
  54.5 0.8 collective-permute-done.9.refs_1_
  55.3 0.5 collective-permute-start.13
  55.8 0.6 grad_hidden_near.5.total_ref
  56.7 0.3 collective-permute-done.14.third_ref
  57.1 0.3 grad_hidden.2
  57.4 1.0 %collective-permute-start.16 = (bf16[96,384]{1,0:T(8,128)(2,1)S(1)}, bf16[96,384]{1,0:T(8,128)(2,1)S(1)}, u32[]{:S(2)}, u32[]{:S(2)}) collective-permute-start(bf16[96,384]{1,0:T(8,128)(2,1)S(1)} %get-tuple-element.92), channel_id=1, source_target_pairs={{0,16},{16,0},{1,17},{17,1},{2,18},{18,2},{3,19},{19,3},{4,20},{20... | collective-permute-start | bytes 221192 | tf_op jit(solution)/shard_map/ppermute | solution.py:448
  58.4 0.4 grad_hidden.3
  58.8 1.2 %collective-permute-start.15 = (bf16[96,512]{1,0:T(8,128)(2,1)S(1)}, bf16[96,512]{1,0:T(8,128)(2,1)S(1)}, u32[]{:S(2)}, u32[]{:S(2)}) collective-permute-start(bf16[96,512]{1,0:T(8,128)(2,1)S(1)} %get-tuple-element.88), channel_id=1, source_target_pairs={{0,16},{16,0},{1,17},{17,1},{2,18},{18,2},{3,19},{19,3},{4,20},{20... | collective-permute-start | bytes 294920 | tf_op jit(solution)/shard_map/ppermute | solution.py:448
  60.0 2.4 %collective-permute-done.16.got_ref = bf16[96,384]{1,0:T(8,128)(2,1)S(1)} collective-permute-done((bf16[96,384]{1,0:T(8,128)(2,1)S(1)}, bf16[96,384]{1,0:T(8,128)(2,1)S(1)}, u32[]{:S(2)}, u32[]{:S(2)}) %collective-permute-start.16) | collective-permute-done | bytes 73760 | tf_op jit(solution)/shard_map/ppermute | solution.py:448
  62.4 1.1 %row_grad.2 = (bf16[96,384]{1,0:T(8,128)(2,1)S(1)}, bf16[96,384]{1,0:T(8,128)(2,1)S(1)}, f32[96,2048]{1,0:T(8,128)S(1)}) custom-call(s32[1]{0:T(128)} %bitcast.2.place_ref, f32[96,384]{1,0:T(8,128)S(1)} %get-tuple-element.91.own_ref, bf16[96,384]{1,0:T(8,128)(2,1)S(1)} %collective-permute-done.16.got_ref, f32[96,384]{1,0:T(8,128)S(1)} %get-tuple-element.93.up_deriv, ...), custom_call_target="tpu_custom_call" | custom-call | flops 603979776 | bytes 3145728 | tf_op jit(solution)/shard_map/row_grad/pallas_call | solution.py:54
  63.5 0.5 collective-permute-done.15.got_ref
  63.9 1.6 %row_grad.3 = (bf16[96,512]{1,0:T(8,128)(2,1)S(1)}, bf16[96,512]{1,0:T(8,128)(2,1)S(1)}, f32[768,128]{1,0:T(8,128)S(1)}, bf16[768,128]{1,0:T(8,128)(2,1)S(1)}) custom-call(s32[1]{0:T(128)} %bitcast.2.place_ref, f32[96,512]{1,0:T(8,128)S(1)} %get-tuple-element.87.own_ref, bf16[96,512]{1,0:T(8,128)(2,1)S(1)} %collective-permute-done.15.got_ref, ...), custom_call_target="tpu_custom_call" | custom-call | flops 805306368 | bytes 4194304 | tf_op jit(solution)/shard_map/row_grad/pallas_call | solution.py:54
  65.6 1.4 %collective-permute-done.17.got_ref = bf16[768,128]{1,0:T(8,128)(2,1)S(1)} collective-permute-done((bf16[768,128]{1,0:T(8,128)(2,1)S(1)}, bf16[768,128]{1,0:T(8,128)(2,1)S(1)}, u32[]{:S(2)}, u32[]{:S(2)}) %collective-permute-start.17) | collective-permute-done | bytes 196640 | tf_op jit(solution)/shard_map/ppermute | solution.py:442
  67.0 0.7 add_cores.1
  67.7 4.1 %all-to-all-start.1 = ((bf16[16,48,128]{2,1,0:T(8,128)(2,1)}), bf16[16,48,128]{2,1,0:T(8,128)(2,1)S(1)}, u32[]{:S(2)}, u32[]{:S(2)}) async-start(bf16[16,48,128]{2,1,0:T(8,128)(2,1)} %bitcast.5), calls=%async_computation.1 | async-start | bytes 393216 | tf_op jit(solution)/shard_map/all_to_all | solution.py:451
  71.9 3.4 %weight_grads.1 = (bf16[2048,896]{1,0:T(8,128)(2,1)}, bf16[2048,896]{1,0:T(8,128)(2,1)}) custom-call(bf16[2048,96]{1,0:T(8,128)(2,1)S(1)} %get-tuple-element.98.turned_ref, bf16[96,512]{1,0:T(8,128)(2,1)S(1)} %get-tuple-element.99.refs_0_, bf16[96,384]{1,0:T(8,128)(2,1)S(1)} %get-tuple-element.100.refs_1_, bf16[96,512]{1,0:T(8,128)(2,1)S(1)} %get-tuple-element.101.refs_2_, ...), custom_call_target="tpu_custom_call" | custom-call | flops 704643072 | bytes 7340032 | tf_op jit(solution)/shard_map/weight_grads/pallas_call | solution.py:54
  75.2 5.3 %all-to-all-done.1 = bf16[16,48,128]{2,1,0:T(8,128)(2,1)S(1)} async-done(((bf16[16,48,128]{2,1,0:T(8,128)(2,1)}), bf16[16,48,128]{2,1,0:T(8,128)(2,1)S(1)}, u32[]{:S(2)}, u32[]{:S(2)}) %all-to-all-start.1) | async-done | bytes 196640 | tf_op jit(solution)/shard_map/all_to_all | solution.py:451
  80.5 1.3 %token_grad.1 = bf16[128,4096]{1,0:T(8,128)(2,1)} custom-call(bf16[16,128]{1,0:T(8,128)(2,1)S(1)} %get-tuple-element.54.pick_ref, bf16[768,128]{1,0:T(8,128)(2,1)S(1)} %bitcast.9), custom_call_target="tpu_custom_call" | custom-call | tf_op jit(solution)/shard_map/token_grad/pallas_call | solution.py:54
  (19 shorter events, 0.6 us)
Async XLA Ops:
  3.3 18.2 %all-to-all-start = ((bf16[16,64,128]{2,1,0:T(8,128)(2,1)}), bf16[16,64,128]{2,1,0:T(8,128)(2,1)S(1)}, u32[]{:S(2)}, u32[]{:S(2)}) async-start(bf16[16,64,128]{2,1,0:T(8,128)(2,1)} %bitcast.3), calls=%async_computation | async-start | bytes 524288 | tf_op jit(solution)/shard_map/all_to_all | solution.py:451
  21.5 1.6 %collective-permute-start = (bf16[1024,128]{1,0:T(8,128)(2,1)S(1)}, bf16[1024,128]{1,0:T(8,128)(2,1)S(1)}, u32[]{:S(2)}, u32[]{:S(2)}) collective-permute-start(bf16[1024,128]{1,0:T(8,128)(2,1)S(1)} %bitcast.7), channel_id=1, source_target_pairs={{0,1},{1,0},{2,3},{3,2},{4,5},{5,4},{6,7},{7,6},{8,9},{9,8},{10,11... | collective-permute-start | bytes 786440 | tf_op jit(solution)/shard_map/ppermute | solution.py:442
  24.2 7.8 %collective-permute-start.2 = (bf16[2,96,512]{2,1,0:T(8,128)(2,1)S(1)}, bf16[2,96,512]{2,1,0:T(8,128)(2,1)S(1)}, u32[]{:S(2)}, u32[]{:S(2)}) collective-permute-start(bf16[2,96,512]{2,1,0:T(8,128)(2,1)S(1)} %get-tuple-element.70), channel_id=1, source_target_pairs={{0,16},{16,0},{1,17},{17,1},{2,18},{18,2},{3,19},{19,3},{4,20},{20... | collective-permute-start | bytes 589832 | tf_op jit(solution)/shard_map/ppermute | solution.py:448
  25.4 6.6 %copy-start = (bf16[896,2048]{1,0:T(8,128)(2,1)S(1)}, bf16[896,2048]{1,0:T(8,128)(2,1)}, u32[]{:S(2)}) copy-start(bf16[896,2048]{1,0:T(8,128)(2,1)} %down_w.15) | copy-start | bytes 11010052
  28.1 6.6 %collective-permute-start.1 = (bf16[2,96,384]{2,1,0:T(8,128)(2,1)S(1)}, bf16[2,96,384]{2,1,0:T(8,128)(2,1)S(1)}, u32[]{:S(2)}, u32[]{:S(2)}) collective-permute-start(bf16[2,96,384]{2,1,0:T(8,128)(2,1)S(1)} %get-tuple-element.68), channel_id=1, source_target_pairs={{0,16},{16,0},{1,17},{17,1},{2,18},{18,2},{3,19},{19,3},{4,20},{20... | collective-permute-start | bytes 442376 | tf_op jit(solution)/shard_map/ppermute | solution.py:448
  35.1 1.5 %collective-permute-start.3 = (bf16[768,128]{1,0:T(8,128)(2,1)S(1)}, bf16[768,128]{1,0:T(8,128)(2,1)S(1)}, u32[]{:S(2)}, u32[]{:S(2)}) collective-permute-start(bf16[768,128]{1,0:T(8,128)(2,1)S(1)} %get-tuple-element.73), channel_id=1, source_target_pairs={{0,1},{1,0},{2,3},{3,2},{4,5},{5,4},{6,7},{7,6},{8,9},{9,8},{10,11... | collective-permute-start | bytes 589832 | tf_op jit(solution)/shard_map/ppermute | solution.py:442
  36.7 4.2 %collective-permute-start.4 = (bf16[192,128]{1,0:T(8,128)(2,1)S(1)}, bf16[192,128]{1,0:T(8,128)(2,1)S(1)}, u32[]{:S(2)}, u32[]{:S(2)}) collective-permute-start(bf16[192,128]{1,0:T(8,128)(2,1)S(1)} %get-tuple-element.75), channel_id=1, source_target_pairs={{0,2},{1,3},{2,0},{3,1},{4,6},{5,7},{6,4},{7,5},{8,10},{9,11},{10,... | collective-permute-start | bytes 147464 | tf_op jit(solution)/shard_map/ppermute | solution.py:442
  37.5 4.4 %collective-permute-start.5 = (bf16[192,128]{1,0:T(8,128)(2,1)S(1)}, bf16[192,128]{1,0:T(8,128)(2,1)S(1)}, u32[]{:S(2)}, u32[]{:S(2)}) collective-permute-start(bf16[192,128]{1,0:T(8,128)(2,1)S(1)} %get-tuple-element.76), channel_id=1, source_target_pairs={{0,4},{1,5},{2,6},{3,7},{4,0},{5,1},{6,2},{7,3},{8,12},{9,13},{10,... | collective-permute-start | bytes 147464 | tf_op jit(solution)/shard_map/ppermute | solution.py:442
  38.2 5.0 %collective-permute-start.6 = (bf16[192,128]{1,0:T(8,128)(2,1)S(1)}, bf16[192,128]{1,0:T(8,128)(2,1)S(1)}, u32[]{:S(2)}, u32[]{:S(2)}) collective-permute-start(bf16[192,128]{1,0:T(8,128)(2,1)S(1)} %get-tuple-element.77), channel_id=1, source_target_pairs={{0,6},{1,7},{2,4},{3,5},{4,2},{5,3},{6,0},{7,1},{8,14},{9,15},{10,... | collective-permute-start | bytes 147464 | tf_op jit(solution)/shard_map/ppermute | solution.py:442
  43.2 5.1 %collective-permute-start.7 = (bf16[192,128]{1,0:T(8,128)(2,1)S(1)}, bf16[192,128]{1,0:T(8,128)(2,1)S(1)}, u32[]{:S(2)}, u32[]{:S(2)}) collective-permute-start(bf16[192,128]{1,0:T(8,128)(2,1)S(1)} %get-tuple-element.81), channel_id=1, source_target_pairs={{0,8},{1,9},{2,10},{3,11},{4,12},{5,13},{6,14},{7,15},{8,0},{9,1},... | collective-permute-start | bytes 147464 | tf_op jit(solution)/shard_map/ppermute | solution.py:442
  48.3 3.9 %collective-permute-start.11 = (bf16[192,128]{1,0:T(8,128)(2,1)S(1)}, bf16[192,128]{1,0:T(8,128)(2,1)S(1)}, u32[]{:S(2)}, u32[]{:S(2)}) collective-permute-start(bf16[192,128]{1,0:T(8,128)(2,1)S(1)} %cotangent.1.refs_0_), channel_id=1, source_target_pairs={{0,1},{1,0},{2,3},{3,2},{4,5},{5,4},{6,7},{7,6},{8,9},{9,8},{10,11... | collective-permute-start | bytes 147464 | tf_op jit(solution)/shard_map/ppermute | solution.py:442
  48.4 5.1 %collective-permute-start.10 = (bf16[192,128]{1,0:T(8,128)(2,1)S(1)}, bf16[192,128]{1,0:T(8,128)(2,1)S(1)}, u32[]{:S(2)}, u32[]{:S(2)}) collective-permute-start(bf16[192,128]{1,0:T(8,128)(2,1)S(1)} %cotangent.1.refs_0_), channel_id=1, source_target_pairs={{0,6},{1,7},{2,4},{3,5},{4,2},{5,3},{6,0},{7,1},{8,14},{9,15},{10,... | collective-permute-start | bytes 147464 | tf_op jit(solution)/shard_map/ppermute | solution.py:442
  50.5 4.1 %collective-permute-start.8 = (bf16[192,128]{1,0:T(8,128)(2,1)S(1)}, bf16[192,128]{1,0:T(8,128)(2,1)S(1)}, u32[]{:S(2)}, u32[]{:S(2)}) collective-permute-start(bf16[192,128]{1,0:T(8,128)(2,1)S(1)} %cotangent.1.refs_0_), channel_id=1, source_target_pairs={{0,2},{1,3},{2,0},{3,1},{4,6},{5,7},{6,4},{7,5},{8,10},{9,11},{10,... | collective-permute-start | bytes 147464 | tf_op jit(solution)/shard_map/ppermute | solution.py:442
  51.2 4.1 %collective-permute-start.9 = (bf16[192,128]{1,0:T(8,128)(2,1)S(1)}, bf16[192,128]{1,0:T(8,128)(2,1)S(1)}, u32[]{:S(2)}, u32[]{:S(2)}) collective-permute-start(bf16[192,128]{1,0:T(8,128)(2,1)S(1)} %cotangent.1.refs_0_), channel_id=1, source_target_pairs={{0,4},{1,5},{2,6},{3,7},{4,0},{5,1},{6,2},{7,3},{8,12},{9,13},{10,... | collective-permute-start | bytes 147464 | tf_op jit(solution)/shard_map/ppermute | solution.py:442
  55.3 1.2 %collective-permute-start.12 = (bf16[192,128]{1,0:T(8,128)(2,1)S(1)}, bf16[192,128]{1,0:T(8,128)(2,1)S(1)}, u32[]{:S(2)}, u32[]{:S(2)}) collective-permute-start(bf16[192,128]{1,0:T(8,128)(2,1)S(1)} %collective-permute-done.8.refs_0_), channel_id=1, source_target_pairs={{0,1},{1,0},{2,3},{3,2},{4,5},{5,4},{6,7},{7,6},{8,9},{9,8},{10,11... | collective-permute-start | bytes 147464 | tf_op jit(solution)/shard_map/ppermute | solution.py:442
  55.3 1.4 %collective-permute-start.13 = (bf16[192,128]{1,0:T(8,128)(2,1)S(1)}, bf16[192,128]{1,0:T(8,128)(2,1)S(1)}, u32[]{:S(2)}, u32[]{:S(2)}) collective-permute-start(bf16[192,128]{1,0:T(8,128)(2,1)S(1)} %collective-permute-done.9.refs_1_), channel_id=1, source_target_pairs={{0,1},{1,0},{2,3},{3,2},{4,5},{5,4},{6,7},{7,6},{8,9},{9,8},{10,11... | collective-permute-start | bytes 147464 | tf_op jit(solution)/shard_map/ppermute | solution.py:442
  55.8 1.2 %collective-permute-start.14 = (bf16[192,128]{1,0:T(8,128)(2,1)S(1)}, bf16[192,128]{1,0:T(8,128)(2,1)S(1)}, u32[]{:S(2)}, u32[]{:S(2)}) collective-permute-start(bf16[192,128]{1,0:T(8,128)(2,1)S(1)} %collective-permute-done.10.refs_2_), channel_id=1, source_target_pairs={{0,1},{1,0},{2,3},{3,2},{4,5},{5,4},{6,7},{7,6},{8,9},{9,8},{10,11... | collective-permute-start | bytes 147464 | tf_op jit(solution)/shard_map/ppermute | solution.py:442
  56.4 5.9 %copy-start.1 = (bf16[2048,896]{1,0:T(8,128)(2,1)S(1)}, bf16[2048,896]{1,0:T(8,128)(2,1)}, u32[]{:S(2)}) copy-start(bf16[2048,896]{1,0:T(8,128)(2,1)} %gate_w.3) | copy-start | bytes 11010052
  56.4 5.9 %copy-start.2 = (bf16[2048,896]{1,0:T(8,128)(2,1)S(1)}, bf16[2048,896]{1,0:T(8,128)(2,1)}, u32[]{:S(2)}) copy-start(bf16[2048,896]{1,0:T(8,128)(2,1)} %up_w.3) | copy-start | bytes 11010052
  57.4 5.0 %collective-permute-start.16 = (bf16[96,384]{1,0:T(8,128)(2,1)S(1)}, bf16[96,384]{1,0:T(8,128)(2,1)S(1)}, u32[]{:S(2)}, u32[]{:S(2)}) collective-permute-start(bf16[96,384]{1,0:T(8,128)(2,1)S(1)} %get-tuple-element.92), channel_id=1, source_target_pairs={{0,16},{16,0},{1,17},{17,1},{2,18},{18,2},{3,19},{19,3},{4,20},{20... | collective-permute-start | bytes 221192 | tf_op jit(solution)/shard_map/ppermute | solution.py:448
  58.8 5.2 %collective-permute-start.15 = (bf16[96,512]{1,0:T(8,128)(2,1)S(1)}, bf16[96,512]{1,0:T(8,128)(2,1)S(1)}, u32[]{:S(2)}, u32[]{:S(2)}) collective-permute-start(bf16[96,512]{1,0:T(8,128)(2,1)S(1)} %get-tuple-element.88), channel_id=1, source_target_pairs={{0,16},{16,0},{1,17},{17,1},{2,18},{18,2},{3,19},{19,3},{4,20},{20... | collective-permute-start | bytes 294920 | tf_op jit(solution)/shard_map/ppermute | solution.py:448
  65.5 1.5 %collective-permute-start.17 = (bf16[768,128]{1,0:T(8,128)(2,1)S(1)}, bf16[768,128]{1,0:T(8,128)(2,1)S(1)}, u32[]{:S(2)}, u32[]{:S(2)}) collective-permute-start(bf16[768,128]{1,0:T(8,128)(2,1)S(1)} %get-tuple-element.97), channel_id=1, source_target_pairs={{0,1},{1,0},{2,3},{3,2},{4,5},{5,4},{6,7},{7,6},{8,9},{9,8},{10,11... | collective-permute-start | bytes 589832 | tf_op jit(solution)/shard_map/ppermute | solution.py:442
  67.7 12.8 %all-to-all-start.1 = ((bf16[16,48,128]{2,1,0:T(8,128)(2,1)}), bf16[16,48,128]{2,1,0:T(8,128)(2,1)S(1)}, u32[]{:S(2)}, u32[]{:S(2)}) async-start(bf16[16,48,128]{2,1,0:T(8,128)(2,1)} %bitcast.5), calls=%async_computation.1 | async-start | bytes 393216 | tf_op jit(solution)/shard_map/all_to_all | solution.py:451

commit v8 on v7

--- a/solution.py
+++ b/solution.py
@@ -609,7 +609,7 @@
 
     own_total = near(0, (0,), (cot,))
     own_total = near(1, (0,), (from_core,), own_total)
-    from_quad, own_total = lax.optimization_barrier((from_quad, own_total))
+    from_quad[2], own_total = lax.optimization_barrier((from_quad[2], own_total))
     from_both = [other_core(x) for x in from_quad]
     own_total = near(0, (1, 2, 3), from_quad, own_total)
     grads = []

time: 82.2 us -> 81.5 us (level)
  starting transfers between devices: 26.3 us -> 25.2 us
  transfers between devices with their start and end apart: 20 -> 20, of which waited for: 18 -> 16; matrix products, arithmetic and copies ran while one was open for 0% -> 0% of each run, Pallas kernels for 16% -> 16%
where the time goes in v8:
time: 81.5 us; the launch traced here: 81.1 us
  waiting for transfers between devices  34.1 us (42%)
  starting transfers between devices  25.2 us (31%)
  Pallas kernels  20.9 us (26%)
  between operations  0.85 us (1%)
    pallas_call x21, Pallas kernels, call(): pl.pallas_call(body, out_shape=outs, in_specs=specs, out_specs=jax.tree.m...  20.9 us
    all_to_all x2, waiting for transfers between devices, over_slice(): lax.all_to_all(x, ('dp', 'expert'), 0, 0, axis_index_groups=slice_groups,...  13.8 us
    ppermute x14, waiting for transfers between devices, other(): return lax.ppermute(x, 'expert', [(i, i ^ mask) for i in range(n_expert)])  12.4 us
    all_to_all x2, starting transfers between devices, over_slice(): lax.all_to_all(x, ('dp', 'expert'), 0, 0, axis_index_groups=slice_groups,...  11.8 us
    ppermute x14, starting transfers between devices, other(): return lax.ppermute(x, 'expert', [(i, i ^ mask) for i in range(n_expert)])  9.05 us
    ppermute x4, waiting for transfers between devices, other_dp(): return lax.ppermute(x, 'dp', [(0, 1), (1, 0)])  7.94 us
    ppermute x4, starting transfers between devices, other_dp(): return lax.ppermute(x, 'dp', [(0, 1), (1, 0)])  4.31 us
  transfers between devices with their start and end apart: 20, of which 16 were waited for; matrix products, arithmetic and copies ran while one was open for 0% of the time, Pallas kernels for 16%

profile of v8, /device:TPU:0, one launch (start us, length us, event | category | flops | bytes accessed | tf_op | source)
XLA Modules:
  0.0 81.1 jit_solution(1021087830089245188)
XLA Ops:
  0.6 2.7 %route.1 = (bf16[1024,128]{1,0:T(8,128)(2,1)}, bf16[16,128]{1,0:T(8,128)(2,1)S(1)}) custom-call(s32[2,128]{1,0:T(2,128)} %bitcast.10, f32[2,128]{1,0:T(2,128)} %bitcast.11, bf16[128,4096]{1,0:T(8,128)(2,1)} %tokens_hbm.1, bf16[128,4096]{1,0:T(8,128)(2,1)} %target_hbm.1), custom_call_target="tpu_custom_call" | custom-call | tf_op jit(solution)/shard_map/route/pallas_call | solution.py:54
  3.3 8.3 %all-to-all-start = ((bf16[16,64,128]{2,1,0:T(8,128)(2,1)}), bf16[16,64,128]{2,1,0:T(8,128)(2,1)S(1)}, u32[]{:S(2)}, u32[]{:S(2)}) async-start(bf16[16,64,128]{2,1,0:T(8,128)(2,1)} %bitcast.3), calls=%async_computation | async-start | bytes 524288 | tf_op jit(solution)/shard_map/all_to_all | solution.py:451
  11.7 1.6 %load_weights.2 = (f32[8,128]{1,0:T(8,128)S(1)}, bf16[2048,256]{1,0:T(8,128)(2,1)S(1)}, bf16[2048,256]{1,0:T(8,128)(2,1)S(1)}) custom-call(bf16[2048,896]{1,0:T(8,128)(2,1)} %gate_w.3, bf16[2048,896]{1,0:T(8,128)(2,1)} %up_w.3), custom_call_target="tpu_custom_call" | custom-call | flops 1000000000 | bytes 4194304 | tf_op jit(solution)/shard_map/load_weights/pallas_call | solution.py:54
  13.2 8.3 %all-to-all-done = bf16[16,64,128]{2,1,0:T(8,128)(2,1)S(1)} async-done(((bf16[16,64,128]{2,1,0:T(8,128)(2,1)}), bf16[16,64,128]{2,1,0:T(8,128)(2,1)S(1)}, u32[]{:S(2)}, u32[]{:S(2)}) %all-to-all-start) | async-done | bytes 262176 | tf_op jit(solution)/shard_map/all_to_all | solution.py:451
  21.5 1.6 %load_weights.3 = (bf16[2048,256]{1,0:T(8,128)(2,1)S(1)}, bf16[2048,256]{1,0:T(8,128)(2,1)S(1)}, bf16[48,2048]{1,0:T(8,128)(2,1)S(1)}, f32[48,128]{1,0:T(8,128)S(1)}, f32[48,128]{1,0:T(8,128)S(1)}) custom-call(s32[1]{0:T(128)} %bitcast.2.place_ref, bf16[1024,128]{1,0:T(8,128)(2,1)S(1)} %bitcast.8, bf16[2048,896]{1,0:T(8,128)(2,1)} %gate_w.3, ...), custom_call_target="tpu_custom_call" | custom-call | flops 1000000000 | bytes 4194304 | tf_op jit(solution)/shard_map/load_weights/pallas_call | solution.py:54
  23.1 1.1 %pre_activations.2 = (bf16[96,2048]{1,0:T(8,128)(2,1)S(1)}, f32[96,128]{1,0:T(8,128)S(1)}, f32[96,128]{1,0:T(8,128)S(1)}, f32[2,96,512]{2,1,0:T(8,128)S(1)}, bf16[2,96,512]{2,1,0:T(8,128)(2,1)S(1)}) custom-call(s32[1]{0:T(128)} %bitcast.2.place_ref, f32[8,128]{1,0:T(8,128)S(1)} %get-tuple-element.55.loaded_ref, ...), custom_call_target="tpu_custom_call" | custom-call | flops 805306368 | bytes 4194304 | tf_op jit(solution)/shard_map/pre_activations/pallas_call | solution.py:54
  24.2 1.2 %collective-permute-start.2 = (bf16[2,96,512]{2,1,0:T(8,128)(2,1)S(1)}, bf16[2,96,512]{2,1,0:T(8,128)(2,1)S(1)}, u32[]{:S(2)}, u32[]{:S(2)}) collective-permute-start(bf16[2,96,512]{2,1,0:T(8,128)(2,1)S(1)} %get-tuple-element.68), channel_id=1, source_target_pairs={{0,16},{16,0},{1,17},{17,1},{2,18},{18,2},{3,19},{19,3},{4,20},{20... | collective-permute-start | bytes 589832 | tf_op jit(solution)/shard_map/ppermute | solution.py:448
  25.4 2.8 %pre_activations.3 = (bf16[2048,96]{1,0:T(8,128)(2,1)S(1)}, f32[2,96,384]{2,1,0:T(8,128)S(1)}, bf16[2,96,384]{2,1,0:T(8,128)(2,1)S(1)}) custom-call(bf16[96,2048]{1,0:T(8,128)(2,1)S(1)} %get-tuple-element.64.rows_ref, bf16[2048,896]{1,0:T(8,128)(2,1)} %gate_w.3, bf16[2048,896]{1,0:T(8,128)(2,1)} %up_w.3), custom_call_target="tpu_custom_call" | custom-call | flops 603979776 | bytes 3145728 | tf_op jit(solution)/shard_map/pre_activations/pallas_call | solution.py:54
  28.1 1.0 %collective-permute-start.1 = (bf16[2,96,384]{2,1,0:T(8,128)(2,1)S(1)}, bf16[2,96,384]{2,1,0:T(8,128)(2,1)S(1)}, u32[]{:S(2)}, u32[]{:S(2)}) collective-permute-start(bf16[2,96,384]{2,1,0:T(8,128)(2,1)S(1)} %get-tuple-element.66), channel_id=1, source_target_pairs={{0,16},{16,0},{1,17},{17,1},{2,18},{18,2},{3,19},{19,3},{4,20},{20... | collective-permute-start | bytes 442376 | tf_op jit(solution)/shard_map/ppermute | solution.py:448
  29.1 2.8 %collective-permute-done.2.got_ref = bf16[2,96,512]{2,1,0:T(8,128)(2,1)S(1)} collective-permute-done((bf16[2,96,512]{2,1,0:T(8,128)(2,1)S(1)}, bf16[2,96,512]{2,1,0:T(8,128)(2,1)S(1)}, u32[]{:S(2)}, u32[]{:S(2)}) %collective-permute-start.2) | collective-permute-done | bytes 196640 | tf_op jit(solution)/shard_map/ppermute | solution.py:448
  32.0 0.5 down.1
  32.5 2.2 %collective-permute-done.1.got_ref = bf16[2,96,384]{2,1,0:T(8,128)(2,1)S(1)} collective-permute-done((bf16[2,96,384]{2,1,0:T(8,128)(2,1)S(1)}, bf16[2,96,384]{2,1,0:T(8,128)(2,1)S(1)}, u32[]{:S(2)}, u32[]{:S(2)}) %collective-permute-start.1) | collective-permute-done | bytes 147488 | tf_op jit(solution)/shard_map/ppermute | solution.py:448
  34.7 0.3 down_send.1
  35.1 0.1 collective-permute-start.3
  35.2 0.3 down_keep.1.own_ref
  35.5 1.1 %collective-permute-done.3.got_ref = bf16[768,128]{1,0:T(8,128)(2,1)S(1)} collective-permute-done((bf16[768,128]{1,0:T(8,128)(2,1)S(1)}, bf16[768,128]{1,0:T(8,128)(2,1)S(1)}, u32[]{:S(2)}, u32[]{:S(2)}) %collective-permute-start.3) | collective-permute-done | bytes 196640 | tf_op jit(solution)/shard_map/ppermute | solution.py:442
  36.7 0.8 %collective-permute-start.4 = (bf16[192,128]{1,0:T(8,128)(2,1)S(1)}, bf16[192,128]{1,0:T(8,128)(2,1)S(1)}, u32[]{:S(2)}, u32[]{:S(2)}) collective-permute-start(bf16[192,128]{1,0:T(8,128)(2,1)S(1)} %get-tuple-element.73), channel_id=1, source_target_pairs={{0,2},{1,3},{2,0},{3,1},{4,6},{5,7},{6,4},{7,5},{8,10},{9,11},{10,... | collective-permute-start | bytes 147464 | tf_op jit(solution)/shard_map/ppermute | solution.py:442
  37.5 0.7 collective-permute-start.5
  38.2 2.0 %collective-permute-start.6 = (bf16[192,128]{1,0:T(8,128)(2,1)S(1)}, bf16[192,128]{1,0:T(8,128)(2,1)S(1)}, u32[]{:S(2)}, u32[]{:S(2)}) collective-permute-start(bf16[192,128]{1,0:T(8,128)(2,1)S(1)} %get-tuple-element.75), channel_id=1, source_target_pairs={{0,6},{1,7},{2,4},{3,5},{4,2},{5,3},{6,0},{7,1},{8,14},{9,15},{10,... | collective-permute-start | bytes 147464 | tf_op jit(solution)/shard_map/ppermute | solution.py:442
  40.2 0.6 collective-permute-done.4.first_ref
  40.8 1.1 %collective-permute-done.5.second_ref = bf16[192,128]{1,0:T(8,128)(2,1)S(1)} collective-permute-done((bf16[192,128]{1,0:T(8,128)(2,1)S(1)}, bf16[192,128]{1,0:T(8,128)(2,1)S(1)}, u32[]{:S(2)}, u32[]{:S(2)}) %collective-permute-start.5) | collective-permute-done | bytes 49184 | tf_op jit(solution)/shard_map/ppermute | solution.py:442
  41.9 1.2 %collective-permute-done.6.third_ref = bf16[192,128]{1,0:T(8,128)(2,1)S(1)} collective-permute-done((bf16[192,128]{1,0:T(8,128)(2,1)S(1)}, bf16[192,128]{1,0:T(8,128)(2,1)S(1)}, u32[]{:S(2)}, u32[]{:S(2)}) %collective-permute-start.6) | collective-permute-done | bytes 49184 | tf_op jit(solution)/shard_map/ppermute | solution.py:442
  43.2 1.7 %collective-permute-start.7 = (bf16[192,128]{1,0:T(8,128)(2,1)S(1)}, bf16[192,128]{1,0:T(8,128)(2,1)S(1)}, u32[]{:S(2)}, u32[]{:S(2)}) collective-permute-start(bf16[192,128]{1,0:T(8,128)(2,1)S(1)} %get-tuple-element.79), channel_id=1, source_target_pairs={{0,8},{1,9},{2,10},{3,11},{4,12},{5,13},{6,14},{7,15},{8,0},{9,1},... | collective-permute-start | bytes 147464 | tf_op jit(solution)/shard_map/ppermute | solution.py:442
  44.9 3.3 %collective-permute-done.7.got_ref = bf16[192,128]{1,0:T(8,128)(2,1)S(1)} collective-permute-done((bf16[192,128]{1,0:T(8,128)(2,1)S(1)}, bf16[192,128]{1,0:T(8,128)(2,1)S(1)}, u32[]{:S(2)}, u32[]{:S(2)}) %collective-permute-start.7) | collective-permute-done | bytes 49184 | tf_op jit(solution)/shard_map/ppermute | solution.py:442
  48.4 2.1 %collective-permute-start.12 = (bf16[192,128]{1,0:T(8,128)(2,1)S(1)}, bf16[192,128]{1,0:T(8,128)(2,1)S(1)}, u32[]{:S(2)}, u32[]{:S(2)}) collective-permute-start(bf16[192,128]{1,0:T(8,128)(2,1)S(1)} %cotangent.1.refs_0_), channel_id=1, source_target_pairs={{0,6},{1,7},{2,4},{3,5},{4,2},{5,3},{6,0},{7,1},{8,14},{9,15},{10,... | collective-permute-start | bytes 147464 | tf_op jit(solution)/shard_map/ppermute | solution.py:442
  50.5 0.9 %collective-permute-start.10 = (bf16[192,128]{1,0:T(8,128)(2,1)S(1)}, bf16[192,128]{1,0:T(8,128)(2,1)S(1)}, u32[]{:S(2)}, u32[]{:S(2)}) collective-permute-start(bf16[192,128]{1,0:T(8,128)(2,1)S(1)} %cotangent.1.refs_0_), channel_id=1, source_target_pairs={{0,4},{1,5},{2,6},{3,7},{4,0},{5,1},{6,2},{7,3},{8,12},{9,13},{10,... | collective-permute-start | bytes 147464 | tf_op jit(solution)/shard_map/ppermute | solution.py:442
  51.4 0.6 collective-permute-start.8
  51.9 0.3 grad_hidden_near.3.refs_1_
  52.2 0.3 grad_hidden_near.4.refs_3_
  52.5 0.9 %collective-permute-done.12.refs_2_ = bf16[192,128]{1,0:T(8,128)(2,1)S(1)} collective-permute-done((bf16[192,128]{1,0:T(8,128)(2,1)S(1)}, bf16[192,128]{1,0:T(8,128)(2,1)S(1)}, u32[]{:S(2)}, u32[]{:S(2)}) %collective-permute-start.12) | collective-permute-done | bytes 49184 | tf_op jit(solution)/shard_map/ppermute | solution.py:442
  53.4 1.1 %collective-permute-done.10.refs_1_ = bf16[192,128]{1,0:T(8,128)(2,1)S(1)} collective-permute-done((bf16[192,128]{1,0:T(8,128)(2,1)S(1)}, bf16[192,128]{1,0:T(8,128)(2,1)S(1)}, u32[]{:S(2)}, u32[]{:S(2)}) %collective-permute-start.10) | collective-permute-done | bytes 49184 | tf_op jit(solution)/shard_map/ppermute | solution.py:442
  54.5 0.9 %collective-permute-done.8.refs_0_ = bf16[192,128]{1,0:T(8,128)(2,1)S(1)} collective-permute-done((bf16[192,128]{1,0:T(8,128)(2,1)S(1)}, bf16[192,128]{1,0:T(8,128)(2,1)S(1)}, u32[]{:S(2)}, u32[]{:S(2)}) %collective-permute-start.8) | collective-permute-done | bytes 49184 | tf_op jit(solution)/shard_map/ppermute | solution.py:442
  55.5 0.6 grad_hidden_near.5.total_ref
  56.1 0.6 collective-permute-done.9.first_ref
  56.7 0.3 grad_hidden.2
  57.0 1.0 %collective-permute-start.16 = (bf16[96,384]{1,0:T(8,128)(2,1)S(1)}, bf16[96,384]{1,0:T(8,128)(2,1)S(1)}, u32[]{:S(2)}, u32[]{:S(2)}) collective-permute-start(bf16[96,384]{1,0:T(8,128)(2,1)S(1)} %get-tuple-element.88), channel_id=1, source_target_pairs={{0,16},{16,0},{1,17},{17,1},{2,18},{18,2},{3,19},{19,3},{4,20},{20... | collective-permute-start | bytes 221192 | tf_op jit(solution)/shard_map/ppermute | solution.py:448
  58.0 0.4 grad_hidden.3
  58.4 1.2 %collective-permute-start.15 = (bf16[96,512]{1,0:T(8,128)(2,1)S(1)}, bf16[96,512]{1,0:T(8,128)(2,1)S(1)}, u32[]{:S(2)}, u32[]{:S(2)}) collective-permute-start(bf16[96,512]{1,0:T(8,128)(2,1)S(1)} %get-tuple-element.84), channel_id=1, source_target_pairs={{0,16},{16,0},{1,17},{17,1},{2,18},{18,2},{3,19},{19,3},{4,20},{20... | collective-permute-start | bytes 294920 | tf_op jit(solution)/shard_map/ppermute | solution.py:448
  59.6 2.4 %collective-permute-done.16.got_ref = bf16[96,384]{1,0:T(8,128)(2,1)S(1)} collective-permute-done((bf16[96,384]{1,0:T(8,128)(2,1)S(1)}, bf16[96,384]{1,0:T(8,128)(2,1)S(1)}, u32[]{:S(2)}, u32[]{:S(2)}) %collective-permute-start.16) | collective-permute-done | bytes 73760 | tf_op jit(solution)/shard_map/ppermute | solution.py:448
  61.9 1.1 %row_grad.2 = (bf16[96,384]{1,0:T(8,128)(2,1)S(1)}, bf16[96,384]{1,0:T(8,128)(2,1)S(1)}, f32[96,2048]{1,0:T(8,128)S(1)}) custom-call(s32[1]{0:T(128)} %bitcast.2.place_ref, f32[96,384]{1,0:T(8,128)S(1)} %get-tuple-element.87.own_ref, bf16[96,384]{1,0:T(8,128)(2,1)S(1)} %collective-permute-done.16.got_ref, f32[96,384]{1,0:T(8,128)S(1)} %get-tuple-element.89.up_deriv, ...), custom_call_target="tpu_custom_call" | custom-call | flops 603979776 | bytes 3145728 | tf_op jit(solution)/shard_map/row_grad/pallas_call | solution.py:54
  63.0 0.5 collective-permute-done.15.got_ref
  63.5 1.6 %row_grad.3 = (bf16[96,512]{1,0:T(8,128)(2,1)S(1)}, bf16[96,512]{1,0:T(8,128)(2,1)S(1)}, f32[768,128]{1,0:T(8,128)S(1)}, bf16[768,128]{1,0:T(8,128)(2,1)S(1)}) custom-call(s32[1]{0:T(128)} %bitcast.2.place_ref, f32[96,512]{1,0:T(8,128)S(1)} %get-tuple-element.83.own_ref, bf16[96,512]{1,0:T(8,128)(2,1)S(1)} %collective-permute-done.15.got_ref, ...), custom_call_target="tpu_custom_call" | custom-call | flops 805306368 | bytes 4194304 | tf_op jit(solution)/shard_map/row_grad/pallas_call | solution.py:54
  65.2 1.4 %collective-permute-done.17.got_ref = bf16[768,128]{1,0:T(8,128)(2,1)S(1)} collective-permute-done((bf16[768,128]{1,0:T(8,128)(2,1)S(1)}, bf16[768,128]{1,0:T(8,128)(2,1)S(1)}, u32[]{:S(2)}, u32[]{:S(2)}) %collective-permute-start.17) | collective-permute-done | bytes 196640 | tf_op jit(solution)/shard_map/ppermute | solution.py:442
  66.6 0.7 add_cores.1
  67.4 3.5 %all-to-all-start.1 = ((bf16[16,48,128]{2,1,0:T(8,128)(2,1)}), bf16[16,48,128]{2,1,0:T(8,128)(2,1)S(1)}, u32[]{:S(2)}, u32[]{:S(2)}) async-start(bf16[16,48,128]{2,1,0:T(8,128)(2,1)} %bitcast.5), calls=%async_computation.1 | async-start | bytes 393216 | tf_op jit(solution)/shard_map/all_to_all | solution.py:451
  70.9 3.4 %weight_grads.1 = (bf16[2048,896]{1,0:T(8,128)(2,1)}, bf16[2048,896]{1,0:T(8,128)(2,1)}) custom-call(bf16[2048,96]{1,0:T(8,128)(2,1)S(1)} %get-tuple-element.94.turned_ref, bf16[96,512]{1,0:T(8,128)(2,1)S(1)} %get-tuple-element.95.refs_0_, bf16[96,384]{1,0:T(8,128)(2,1)S(1)} %get-tuple-element.96.refs_1_, bf16[96,512]{1,0:T(8,128)(2,1)S(1)} %get-tuple-element.97.refs_2_, ...), custom_call_target="tpu_custom_call" | custom-call | flops 704643072 | bytes 7340032 | tf_op jit(solution)/shard_map/weight_grads/pallas_call | solution.py:54
  74.3 5.5 %all-to-all-done.1 = bf16[16,48,128]{2,1,0:T(8,128)(2,1)S(1)} async-done(((bf16[16,48,128]{2,1,0:T(8,128)(2,1)}), bf16[16,48,128]{2,1,0:T(8,128)(2,1)S(1)}, u32[]{:S(2)}, u32[]{:S(2)}) %all-to-all-start.1) | async-done | bytes 196640 | tf_op jit(solution)/shard_map/all_to_all | solution.py:451
  79.8 1.3 %token_grad.1 = bf16[128,4096]{1,0:T(8,128)(2,1)} custom-call(bf16[16,128]{1,0:T(8,128)(2,1)S(1)} %get-tuple-element.52.pick_ref, bf16[768,128]{1,0:T(8,128)(2,1)S(1)} %bitcast.9), custom_call_target="tpu_custom_call" | custom-call | tf_op jit(solution)/shard_map/token_grad/pallas_call | solution.py:54
  (19 shorter events, 0.3 us)
Async XLA Ops:
  3.3 18.2 %all-to-all-start = ((bf16[16,64,128]{2,1,0:T(8,128)(2,1)}), bf16[16,64,128]{2,1,0:T(8,128)(2,1)S(1)}, u32[]{:S(2)}, u32[]{:S(2)}) async-start(bf16[16,64,128]{2,1,0:T(8,128)(2,1)} %bitcast.3), calls=%async_computation | async-start | bytes 524288 | tf_op jit(solution)/shard_map/all_to_all | solution.py:451
  21.5 1.6 %collective-permute-start = (bf16[1024,128]{1,0:T(8,128)(2,1)S(1)}, bf16[1024,128]{1,0:T(8,128)(2,1)S(1)}, u32[]{:S(2)}, u32[]{:S(2)}) collective-permute-start(bf16[1024,128]{1,0:T(8,128)(2,1)S(1)} %bitcast.7), channel_id=1, source_target_pairs={{0,1},{1,0},{2,3},{3,2},{4,5},{5,4},{6,7},{7,6},{8,9},{9,8},{10,11... | collective-permute-start | bytes 786440 | tf_op jit(solution)/shard_map/ppermute | solution.py:442
  24.2 7.8 %collective-permute-start.2 = (bf16[2,96,512]{2,1,0:T(8,128)(2,1)S(1)}, bf16[2,96,512]{2,1,0:T(8,128)(2,1)S(1)}, u32[]{:S(2)}, u32[]{:S(2)}) collective-permute-start(bf16[2,96,512]{2,1,0:T(8,128)(2,1)S(1)} %get-tuple-element.68), channel_id=1, source_target_pairs={{0,16},{16,0},{1,17},{17,1},{2,18},{18,2},{3,19},{19,3},{4,20},{20... | collective-permute-start | bytes 589832 | tf_op jit(solution)/shard_map/ppermute | solution.py:448
  25.4 6.6 %copy-start = (bf16[896,2048]{1,0:T(8,128)(2,1)S(1)}, bf16[896,2048]{1,0:T(8,128)(2,1)}, u32[]{:S(2)}) copy-start(bf16[896,2048]{1,0:T(8,128)(2,1)} %down_w.15) | copy-start | bytes 11010052
  28.1 6.6 %collective-permute-start.1 = (bf16[2,96,384]{2,1,0:T(8,128)(2,1)S(1)}, bf16[2,96,384]{2,1,0:T(8,128)(2,1)S(1)}, u32[]{:S(2)}, u32[]{:S(2)}) collective-permute-start(bf16[2,96,384]{2,1,0:T(8,128)(2,1)S(1)} %get-tuple-element.66), channel_id=1, source_target_pairs={{0,16},{16,0},{1,17},{17,1},{2,18},{18,2},{3,19},{19,3},{4,20},{20... | collective-permute-start | bytes 442376 | tf_op jit(solution)/shard_map/ppermute | solution.py:448
  35.1 1.5 %collective-permute-start.3 = (bf16[768,128]{1,0:T(8,128)(2,1)S(1)}, bf16[768,128]{1,0:T(8,128)(2,1)S(1)}, u32[]{:S(2)}, u32[]{:S(2)}) collective-permute-start(bf16[768,128]{1,0:T(8,128)(2,1)S(1)} %get-tuple-element.71), channel_id=1, source_target_pairs={{0,1},{1,0},{2,3},{3,2},{4,5},{5,4},{6,7},{7,6},{8,9},{9,8},{10,11... | collective-permute-start | bytes 589832 | tf_op jit(solution)/shard_map/ppermute | solution.py:442
  36.7 4.2 %collective-permute-start.4 = (bf16[192,128]{1,0:T(8,128)(2,1)S(1)}, bf16[192,128]{1,0:T(8,128)(2,1)S(1)}, u32[]{:S(2)}, u32[]{:S(2)}) collective-permute-start(bf16[192,128]{1,0:T(8,128)(2,1)S(1)} %get-tuple-element.73), channel_id=1, source_target_pairs={{0,2},{1,3},{2,0},{3,1},{4,6},{5,7},{6,4},{7,5},{8,10},{9,11},{10,... | collective-permute-start | bytes 147464 | tf_op jit(solution)/shard_map/ppermute | solution.py:442
  37.5 4.4 %collective-permute-start.5 = (bf16[192,128]{1,0:T(8,128)(2,1)S(1)}, bf16[192,128]{1,0:T(8,128)(2,1)S(1)}, u32[]{:S(2)}, u32[]{:S(2)}) collective-permute-start(bf16[192,128]{1,0:T(8,128)(2,1)S(1)} %get-tuple-element.74), channel_id=1, source_target_pairs={{0,4},{1,5},{2,6},{3,7},{4,0},{5,1},{6,2},{7,3},{8,12},{9,13},{10,... | collective-permute-start | bytes 147464 | tf_op jit(solution)/shard_map/ppermute | solution.py:442
  38.2 5.0 %collective-permute-start.6 = (bf16[192,128]{1,0:T(8,128)(2,1)S(1)}, bf16[192,128]{1,0:T(8,128)(2,1)S(1)}, u32[]{:S(2)}, u32[]{:S(2)}) collective-permute-start(bf16[192,128]{1,0:T(8,128)(2,1)S(1)} %get-tuple-element.75), channel_id=1, source_target_pairs={{0,6},{1,7},{2,4},{3,5},{4,2},{5,3},{6,0},{7,1},{8,14},{9,15},{10,... | collective-permute-start | bytes 147464 | tf_op jit(solution)/shard_map/ppermute | solution.py:442
  43.2 5.1 %collective-permute-start.7 = (bf16[192,128]{1,0:T(8,128)(2,1)S(1)}, bf16[192,128]{1,0:T(8,128)(2,1)S(1)}, u32[]{:S(2)}, u32[]{:S(2)}) collective-permute-start(bf16[192,128]{1,0:T(8,128)(2,1)S(1)} %get-tuple-element.79), channel_id=1, source_target_pairs={{0,8},{1,9},{2,10},{3,11},{4,12},{5,13},{6,14},{7,15},{8,0},{9,1},... | collective-permute-start | bytes 147464 | tf_op jit(solution)/shard_map/ppermute | solution.py:442
  48.3 3.9 %collective-permute-start.13 = (bf16[192,128]{1,0:T(8,128)(2,1)S(1)}, bf16[192,128]{1,0:T(8,128)(2,1)S(1)}, u32[]{:S(2)}, u32[]{:S(2)}) collective-permute-start(bf16[192,128]{1,0:T(8,128)(2,1)S(1)} %cotangent.1.refs_0_), channel_id=1, source_target_pairs={{0,1},{1,0},{2,3},{3,2},{4,5},{5,4},{6,7},{7,6},{8,9},{9,8},{10,11... | collective-permute-start | bytes 147464 | tf_op jit(solution)/shard_map/ppermute | solution.py:442
  48.4 5.1 %collective-permute-start.12 = (bf16[192,128]{1,0:T(8,128)(2,1)S(1)}, bf16[192,128]{1,0:T(8,128)(2,1)S(1)}, u32[]{:S(2)}, u32[]{:S(2)}) collective-permute-start(bf16[192,128]{1,0:T(8,128)(2,1)S(1)} %cotangent.1.refs_0_), channel_id=1, source_target_pairs={{0,6},{1,7},{2,4},{3,5},{4,2},{5,3},{6,0},{7,1},{8,14},{9,15},{10,... | collective-permute-start | bytes 147464 | tf_op jit(solution)/shard_map/ppermute | solution.py:442
  50.5 4.1 %collective-permute-start.10 = (bf16[192,128]{1,0:T(8,128)(2,1)S(1)}, bf16[192,128]{1,0:T(8,128)(2,1)S(1)}, u32[]{:S(2)}, u32[]{:S(2)}) collective-permute-start(bf16[192,128]{1,0:T(8,128)(2,1)S(1)} %cotangent.1.refs_0_), channel_id=1, source_target_pairs={{0,4},{1,5},{2,6},{3,7},{4,0},{5,1},{6,2},{7,3},{8,12},{9,13},{10,... | collective-permute-start | bytes 147464 | tf_op jit(solution)/shard_map/ppermute | solution.py:442
  51.4 4.1 %collective-permute-start.8 = (bf16[192,128]{1,0:T(8,128)(2,1)S(1)}, bf16[192,128]{1,0:T(8,128)(2,1)S(1)}, u32[]{:S(2)}, u32[]{:S(2)}) collective-permute-start(bf16[192,128]{1,0:T(8,128)(2,1)S(1)} %cotangent.1.refs_0_), channel_id=1, source_target_pairs={{0,2},{1,3},{2,0},{3,1},{4,6},{5,7},{6,4},{7,5},{8,10},{9,11},{10,... | collective-permute-start | bytes 147464 | tf_op jit(solution)/shard_map/ppermute | solution.py:442
  53.4 2.6 %collective-permute-start.14 = (bf16[192,128]{1,0:T(8,128)(2,1)S(1)}, bf16[192,128]{1,0:T(8,128)(2,1)S(1)}, u32[]{:S(2)}, u32[]{:S(2)}) collective-permute-start(bf16[192,128]{1,0:T(8,128)(2,1)S(1)} %collective-permute-done.12.refs_2_), channel_id=1, source_target_pairs={{0,1},{1,0},{2,3},{3,2},{4,5},{5,4},{6,7},{7,6},{8,9},{9,8},{10,11... | collective-permute-start | bytes 147464 | tf_op jit(solution)/shard_map/ppermute | solution.py:442
  54.5 1.5 %collective-permute-start.11 = (bf16[192,128]{1,0:T(8,128)(2,1)S(1)}, bf16[192,128]{1,0:T(8,128)(2,1)S(1)}, u32[]{:S(2)}, u32[]{:S(2)}) collective-permute-start(bf16[192,128]{1,0:T(8,128)(2,1)S(1)} %collective-permute-done.10.refs_1_), channel_id=1, source_target_pairs={{0,1},{1,0},{2,3},{3,2},{4,5},{5,4},{6,7},{7,6},{8,9},{9,8},{10,11... | collective-permute-start | bytes 147464 | tf_op jit(solution)/shard_map/ppermute | solution.py:442
  55.5 1.2 %collective-permute-start.9 = (bf16[192,128]{1,0:T(8,128)(2,1)S(1)}, bf16[192,128]{1,0:T(8,128)(2,1)S(1)}, u32[]{:S(2)}, u32[]{:S(2)}) collective-permute-start(bf16[192,128]{1,0:T(8,128)(2,1)S(1)} %collective-permute-done.8.refs_0_), channel_id=1, source_target_pairs={{0,1},{1,0},{2,3},{3,2},{4,5},{5,4},{6,7},{7,6},{8,9},{9,8},{10,11... | collective-permute-start | bytes 147464 | tf_op jit(solution)/shard_map/ppermute | solution.py:442
  56.0 5.9 %copy-start.1 = (bf16[2048,896]{1,0:T(8,128)(2,1)S(1)}, bf16[2048,896]{1,0:T(8,128)(2,1)}, u32[]{:S(2)}) copy-start(bf16[2048,896]{1,0:T(8,128)(2,1)} %gate_w.3) | copy-start | bytes 11010052
  56.1 5.9 %copy-start.2 = (bf16[2048,896]{1,0:T(8,128)(2,1)S(1)}, bf16[2048,896]{1,0:T(8,128)(2,1)}, u32[]{:S(2)}) copy-start(bf16[2048,896]{1,0:T(8,128)(2,1)} %up_w.3) | copy-start | bytes 11010052
  57.0 4.9 %collective-permute-start.16 = (bf16[96,384]{1,0:T(8,128)(2,1)S(1)}, bf16[96,384]{1,0:T(8,128)(2,1)S(1)}, u32[]{:S(2)}, u32[]{:S(2)}) collective-permute-start(bf16[96,384]{1,0:T(8,128)(2,1)S(1)} %get-tuple-element.88), channel_id=1, source_target_pairs={{0,16},{16,0},{1,17},{17,1},{2,18},{18,2},{3,19},{19,3},{4,20},{20... | collective-permute-start | bytes 221192 | tf_op jit(solution)/shard_map/ppermute | solution.py:448
  58.4 5.1 %collective-permute-start.15 = (bf16[96,512]{1,0:T(8,128)(2,1)S(1)}, bf16[96,512]{1,0:T(8,128)(2,1)S(1)}, u32[]{:S(2)}, u32[]{:S(2)}) collective-permute-start(bf16[96,512]{1,0:T(8,128)(2,1)S(1)} %get-tuple-element.84), channel_id=1, source_target_pairs={{0,16},{16,0},{1,17},{17,1},{2,18},{18,2},{3,19},{19,3},{4,20},{20... | collective-permute-start | bytes 294920 | tf_op jit(solution)/shard_map/ppermute | solution.py:448
  65.1 1.5 %collective-permute-start.17 = (bf16[768,128]{1,0:T(8,128)(2,1)S(1)}, bf16[768,128]{1,0:T(8,128)(2,1)S(1)}, u32[]{:S(2)}, u32[]{:S(2)}) collective-permute-start(bf16[768,128]{1,0:T(8,128)(2,1)S(1)} %get-tuple-element.93), channel_id=1, source_target_pairs={{0,1},{1,0},{2,3},{3,2},{4,5},{5,4},{6,7},{7,6},{8,9},{9,8},{10,11... | collective-permute-start | bytes 589832 | tf_op jit(solution)/shard_map/ppermute | solution.py:442
  67.4 12.4 %all-to-all-start.1 = ((bf16[16,48,128]{2,1,0:T(8,128)(2,1)}), bf16[16,48,128]{2,1,0:T(8,128)(2,1)S(1)}, u32[]{:S(2)}, u32[]{:S(2)}) async-start(bf16[16,48,128]{2,1,0:T(8,128)(2,1)} %bitcast.5), calls=%async_computation.1 | async-start | bytes 393216 | tf_op jit(solution)/shard_map/all_to_all | solution.py:451

commit v9 on v8

--- a/solution.py
+++ b/solution.py
@@ -577,7 +577,7 @@
     keep, send = call(
         residual_kernel,
         (kept, sent_on),
-        (place, keep, *[other(x, 2 * (k + 1)) for k, x in enumerate(sends)], all_gates, all_target),
+        (place, keep, *[other(sends[k], 2 * (k + 1)) for k in (2, 0, 1)], all_gates, all_target),
         [SMEM] + [VMEM] * 6,
         name="residual",
     )

time: 81.5 us -> 80.8 us (level)
  waiting for transfers between devices: 34.1 us -> 32.7 us
    ppermute x14, waiting for transfers between devices: 12.4 us -> 11.2 us  [other(): return lax.ppermute(x, 'expert', [(i, i ^ mask) for i in range(n_expert)])]
where the time goes in v9:
time: 80.8 us; the launch traced here: 80.4 us
  waiting for transfers between devices  32.7 us (40%)
  starting transfers between devices  25.9 us (32%)
  Pallas kernels  20.9 us (26%)
  between operations  0.85 us (1%)
    pallas_call x21, Pallas kernels, call(): pl.pallas_call(body, out_shape=outs, in_specs=specs, out_specs=jax.tree.m...  20.9 us
    all_to_all x2, waiting for transfers between devices, over_slice(): lax.all_to_all(x, ('dp', 'expert'), 0, 0, axis_index_groups=slice_groups,...  13.6 us
    all_to_all x2, starting transfers between devices, over_slice(): lax.all_to_all(x, ('dp', 'expert'), 0, 0, axis_index_groups=slice_groups,...  12.3 us
    ppermute x14, waiting for transfers between devices, other(): return lax.ppermute(x, 'expert', [(i, i ^ mask) for i in range(n_expert)])  11.2 us
    ppermute x14, starting transfers between devices, other(): return lax.ppermute(x, 'expert', [(i, i ^ mask) for i in range(n_expert)])  9.32 us
    ppermute x4, waiting for transfers between devices, other_dp(): return lax.ppermute(x, 'dp', [(0, 1), (1, 0)])  7.94 us
    ppermute x4, starting transfers between devices, other_dp(): return lax.ppermute(x, 'dp', [(0, 1), (1, 0)])  4.31 us
  transfers between devices with their start and end apart: 20, of which 16 were waited for; matrix products, arithmetic and copies ran while one was open for 0% of the time, Pallas kernels for 16%

profile of v9, /device:TPU:0, one launch (start us, length us, event | category | flops | bytes accessed | tf_op | source)
XLA Modules:
  0.0 80.4 jit_solution(9109532299355660472)
XLA Ops:
  0.6 2.7 %route.1 = (bf16[1024,128]{1,0:T(8,128)(2,1)}, bf16[16,128]{1,0:T(8,128)(2,1)S(1)}) custom-call(s32[2,128]{1,0:T(2,128)} %bitcast.10, f32[2,128]{1,0:T(2,128)} %bitcast.11, bf16[128,4096]{1,0:T(8,128)(2,1)} %tokens_hbm.1, bf16[128,4096]{1,0:T(8,128)(2,1)} %target_hbm.1), custom_call_target="tpu_custom_call" | custom-call | tf_op jit(solution)/shard_map/route/pallas_call | solution.py:54
  3.3 8.3 %all-to-all-start = ((bf16[16,64,128]{2,1,0:T(8,128)(2,1)}), bf16[16,64,128]{2,1,0:T(8,128)(2,1)S(1)}, u32[]{:S(2)}, u32[]{:S(2)}) async-start(bf16[16,64,128]{2,1,0:T(8,128)(2,1)} %bitcast.3), calls=%async_computation | async-start | bytes 524288 | tf_op jit(solution)/shard_map/all_to_all | solution.py:451
  11.7 1.6 %load_weights.2 = (f32[8,128]{1,0:T(8,128)S(1)}, bf16[2048,256]{1,0:T(8,128)(2,1)S(1)}, bf16[2048,256]{1,0:T(8,128)(2,1)S(1)}) custom-call(bf16[2048,896]{1,0:T(8,128)(2,1)} %gate_w.3, bf16[2048,896]{1,0:T(8,128)(2,1)} %up_w.3), custom_call_target="tpu_custom_call" | custom-call | flops 1000000000 | bytes 4194304 | tf_op jit(solution)/shard_map/load_weights/pallas_call | solution.py:54
  13.2 8.3 %all-to-all-done = bf16[16,64,128]{2,1,0:T(8,128)(2,1)S(1)} async-done(((bf16[16,64,128]{2,1,0:T(8,128)(2,1)}), bf16[16,64,128]{2,1,0:T(8,128)(2,1)S(1)}, u32[]{:S(2)}, u32[]{:S(2)}) %all-to-all-start) | async-done | bytes 262176 | tf_op jit(solution)/shard_map/all_to_all | solution.py:451
  21.5 1.6 %load_weights.3 = (bf16[2048,256]{1,0:T(8,128)(2,1)S(1)}, bf16[2048,256]{1,0:T(8,128)(2,1)S(1)}, bf16[48,2048]{1,0:T(8,128)(2,1)S(1)}, f32[48,128]{1,0:T(8,128)S(1)}, f32[48,128]{1,0:T(8,128)S(1)}) custom-call(s32[1]{0:T(128)} %bitcast.2.place_ref, bf16[1024,128]{1,0:T(8,128)(2,1)S(1)} %bitcast.8, bf16[2048,896]{1,0:T(8,128)(2,1)} %gate_w.3, ...), custom_call_target="tpu_custom_call" | custom-call | flops 1000000000 | bytes 4194304 | tf_op jit(solution)/shard_map/load_weights/pallas_call | solution.py:54
  23.1 1.1 %pre_activations.2 = (bf16[96,2048]{1,0:T(8,128)(2,1)S(1)}, f32[96,128]{1,0:T(8,128)S(1)}, f32[96,128]{1,0:T(8,128)S(1)}, f32[2,96,512]{2,1,0:T(8,128)S(1)}, bf16[2,96,512]{2,1,0:T(8,128)(2,1)S(1)}) custom-call(s32[1]{0:T(128)} %bitcast.2.place_ref, f32[8,128]{1,0:T(8,128)S(1)} %get-tuple-element.55.loaded_ref, ...), custom_call_target="tpu_custom_call" | custom-call | flops 805306368 | bytes 4194304 | tf_op jit(solution)/shard_map/pre_activations/pallas_call | solution.py:54
  24.2 1.2 %collective-permute-start.2 = (bf16[2,96,512]{2,1,0:T(8,128)(2,1)S(1)}, bf16[2,96,512]{2,1,0:T(8,128)(2,1)S(1)}, u32[]{:S(2)}, u32[]{:S(2)}) collective-permute-start(bf16[2,96,512]{2,1,0:T(8,128)(2,1)S(1)} %get-tuple-element.68), channel_id=1, source_target_pairs={{0,16},{16,0},{1,17},{17,1},{2,18},{18,2},{3,19},{19,3},{4,20},{20... | collective-permute-start | bytes 589832 | tf_op jit(solution)/shard_map/ppermute | solution.py:448
  25.4 2.8 %pre_activations.3 = (bf16[2048,96]{1,0:T(8,128)(2,1)S(1)}, f32[2,96,384]{2,1,0:T(8,128)S(1)}, bf16[2,96,384]{2,1,0:T(8,128)(2,1)S(1)}) custom-call(bf16[96,2048]{1,0:T(8,128)(2,1)S(1)} %get-tuple-element.64.rows_ref, bf16[2048,896]{1,0:T(8,128)(2,1)} %gate_w.3, bf16[2048,896]{1,0:T(8,128)(2,1)} %up_w.3), custom_call_target="tpu_custom_call" | custom-call | flops 603979776 | bytes 3145728 | tf_op jit(solution)/shard_map/pre_activations/pallas_call | solution.py:54
  28.1 1.0 %collective-permute-start.1 = (bf16[2,96,384]{2,1,0:T(8,128)(2,1)S(1)}, bf16[2,96,384]{2,1,0:T(8,128)(2,1)S(1)}, u32[]{:S(2)}, u32[]{:S(2)}) collective-permute-start(bf16[2,96,384]{2,1,0:T(8,128)(2,1)S(1)} %get-tuple-element.66), channel_id=1, source_target_pairs={{0,16},{16,0},{1,17},{17,1},{2,18},{18,2},{3,19},{19,3},{4,20},{20... | collective-permute-start | bytes 442376 | tf_op jit(solution)/shard_map/ppermute | solution.py:448
  29.1 2.8 %collective-permute-done.2.got_ref = bf16[2,96,512]{2,1,0:T(8,128)(2,1)S(1)} collective-permute-done((bf16[2,96,512]{2,1,0:T(8,128)(2,1)S(1)}, bf16[2,96,512]{2,1,0:T(8,128)(2,1)S(1)}, u32[]{:S(2)}, u32[]{:S(2)}) %collective-permute-start.2) | collective-permute-done | bytes 196640 | tf_op jit(solution)/shard_map/ppermute | solution.py:448
  32.0 0.5 down.1
  32.5 2.2 %collective-permute-done.1.got_ref = bf16[2,96,384]{2,1,0:T(8,128)(2,1)S(1)} collective-permute-done((bf16[2,96,384]{2,1,0:T(8,128)(2,1)S(1)}, bf16[2,96,384]{2,1,0:T(8,128)(2,1)S(1)}, u32[]{:S(2)}, u32[]{:S(2)}) %collective-permute-start.1) | collective-permute-done | bytes 147488 | tf_op jit(solution)/shard_map/ppermute | solution.py:448
  34.7 0.3 down_send.1
  35.2 0.3 down_keep.1.own_ref
  35.5 1.1 %collective-permute-done.3.got_ref = bf16[768,128]{1,0:T(8,128)(2,1)S(1)} collective-permute-done((bf16[768,128]{1,0:T(8,128)(2,1)S(1)}, bf16[768,128]{1,0:T(8,128)(2,1)S(1)}, u32[]{:S(2)}, u32[]{:S(2)}) %collective-permute-start.3) | collective-permute-done | bytes 196640 | tf_op jit(solution)/shard_map/ppermute | solution.py:442
  36.7 1.0 %collective-permute-start.4 = (bf16[192,128]{1,0:T(8,128)(2,1)S(1)}, bf16[192,128]{1,0:T(8,128)(2,1)S(1)}, u32[]{:S(2)}, u32[]{:S(2)}) collective-permute-start(bf16[192,128]{1,0:T(8,128)(2,1)S(1)} %get-tuple-element.73), channel_id=1, source_target_pairs={{0,6},{1,7},{2,4},{3,5},{4,2},{5,3},{6,0},{7,1},{8,14},{9,15},{10,... | collective-permute-start | bytes 147464 | tf_op jit(solution)/shard_map/ppermute | solution.py:442
  37.6 1.5 %collective-permute-start.5 = (bf16[192,128]{1,0:T(8,128)(2,1)S(1)}, bf16[192,128]{1,0:T(8,128)(2,1)S(1)}, u32[]{:S(2)}, u32[]{:S(2)}) collective-permute-start(bf16[192,128]{1,0:T(8,128)(2,1)S(1)} %get-tuple-element.74), channel_id=1, source_target_pairs={{0,2},{1,3},{2,0},{3,1},{4,6},{5,7},{6,4},{7,5},{8,10},{9,11},{10,... | collective-permute-start | bytes 147464 | tf_op jit(solution)/shard_map/ppermute | solution.py:442
  39.1 1.1 %collective-permute-start.6 = (bf16[192,128]{1,0:T(8,128)(2,1)S(1)}, bf16[192,128]{1,0:T(8,128)(2,1)S(1)}, u32[]{:S(2)}, u32[]{:S(2)}) collective-permute-start(bf16[192,128]{1,0:T(8,128)(2,1)S(1)} %get-tuple-element.75), channel_id=1, source_target_pairs={{0,4},{1,5},{2,6},{3,7},{4,0},{5,1},{6,2},{7,3},{8,12},{9,13},{10,... | collective-permute-start | bytes 147464 | tf_op jit(solution)/shard_map/ppermute | solution.py:442
  40.2 1.9 %collective-permute-done.4.first_ref = bf16[192,128]{1,0:T(8,128)(2,1)S(1)} collective-permute-done((bf16[192,128]{1,0:T(8,128)(2,1)S(1)}, bf16[192,128]{1,0:T(8,128)(2,1)S(1)}, u32[]{:S(2)}, u32[]{:S(2)}) %collective-permute-start.4) | collective-permute-done | bytes 49184 | tf_op jit(solution)/shard_map/ppermute | solution.py:442
  42.2 0.1 collective-permute-done.5.second_ref
  42.2 0.9 %collective-permute-done.6.third_ref = bf16[192,128]{1,0:T(8,128)(2,1)S(1)} collective-permute-done((bf16[192,128]{1,0:T(8,128)(2,1)S(1)}, bf16[192,128]{1,0:T(8,128)(2,1)S(1)}, u32[]{:S(2)}, u32[]{:S(2)}) %collective-permute-start.6) | collective-permute-done | bytes 49184 | tf_op jit(solution)/shard_map/ppermute | solution.py:442
  43.2 1.7 %collective-permute-start.7 = (bf16[192,128]{1,0:T(8,128)(2,1)S(1)}, bf16[192,128]{1,0:T(8,128)(2,1)S(1)}, u32[]{:S(2)}, u32[]{:S(2)}) collective-permute-start(bf16[192,128]{1,0:T(8,128)(2,1)S(1)} %get-tuple-element.79), channel_id=1, source_target_pairs={{0,8},{1,9},{2,10},{3,11},{4,12},{5,13},{6,14},{7,15},{8,0},{9,1},... | collective-permute-start | bytes 147464 | tf_op jit(solution)/shard_map/ppermute | solution.py:442
  44.9 3.4 %collective-permute-done.7.got_ref = bf16[192,128]{1,0:T(8,128)(2,1)S(1)} collective-permute-done((bf16[192,128]{1,0:T(8,128)(2,1)S(1)}, bf16[192,128]{1,0:T(8,128)(2,1)S(1)}, u32[]{:S(2)}, u32[]{:S(2)}) %collective-permute-start.7) | collective-permute-done | bytes 49184 | tf_op jit(solution)/shard_map/ppermute | solution.py:442
  48.4 1.4 %collective-permute-start.12 = (bf16[192,128]{1,0:T(8,128)(2,1)S(1)}, bf16[192,128]{1,0:T(8,128)(2,1)S(1)}, u32[]{:S(2)}, u32[]{:S(2)}) collective-permute-start(bf16[192,128]{1,0:T(8,128)(2,1)S(1)} %cotangent.1.refs_0_), channel_id=1, source_target_pairs={{0,6},{1,7},{2,4},{3,5},{4,2},{5,3},{6,0},{7,1},{8,14},{9,15},{10,... | collective-permute-start | bytes 147464 | tf_op jit(solution)/shard_map/ppermute | solution.py:442
  49.8 0.7 collective-permute-start.10
  50.5 1.5 %collective-permute-start.8 = (bf16[192,128]{1,0:T(8,128)(2,1)S(1)}, bf16[192,128]{1,0:T(8,128)(2,1)S(1)}, u32[]{:S(2)}, u32[]{:S(2)}) collective-permute-start(bf16[192,128]{1,0:T(8,128)(2,1)S(1)} %cotangent.1.refs_0_), channel_id=1, source_target_pairs={{0,2},{1,3},{2,0},{3,1},{4,6},{5,7},{6,4},{7,5},{8,10},{9,11},{10,... | collective-permute-start | bytes 147464 | tf_op jit(solution)/shard_map/ppermute | solution.py:442
  51.9 0.3 grad_hidden_near.3.refs_1_
  52.2 0.3 grad_hidden_near.4.refs_3_
  52.5 1.1 %collective-permute-done.12.refs_2_ = bf16[192,128]{1,0:T(8,128)(2,1)S(1)} collective-permute-done((bf16[192,128]{1,0:T(8,128)(2,1)S(1)}, bf16[192,128]{1,0:T(8,128)(2,1)S(1)}, u32[]{:S(2)}, u32[]{:S(2)}) %collective-permute-start.12) | collective-permute-done | bytes 49184 | tf_op jit(solution)/shard_map/ppermute | solution.py:442
  53.6 0.2 collective-permute-done.10.refs_1_
  53.9 0.3 collective-permute-start.11
  54.2 0.4 collective-permute-done.8.refs_0_
  54.6 0.6 grad_hidden_near.5.total_ref
  55.2 0.6 collective-permute-done.9.first_ref
  55.8 0.3 grad_hidden.2
  56.1 1.0 %collective-permute-start.16 = (bf16[96,384]{1,0:T(8,128)(2,1)S(1)}, bf16[96,384]{1,0:T(8,128)(2,1)S(1)}, u32[]{:S(2)}, u32[]{:S(2)}) collective-permute-start(bf16[96,384]{1,0:T(8,128)(2,1)S(1)} %get-tuple-element.88), channel_id=1, source_target_pairs={{0,16},{16,0},{1,17},{17,1},{2,18},{18,2},{3,19},{19,3},{4,20},{20... | collective-permute-start | bytes 221192 | tf_op jit(solution)/shard_map/ppermute | solution.py:448
  57.1 0.4 grad_hidden.3
  57.5 1.2 %collective-permute-start.15 = (bf16[96,512]{1,0:T(8,128)(2,1)S(1)}, bf16[96,512]{1,0:T(8,128)(2,1)S(1)}, u32[]{:S(2)}, u32[]{:S(2)}) collective-permute-start(bf16[96,512]{1,0:T(8,128)(2,1)S(1)} %get-tuple-element.84), channel_id=1, source_target_pairs={{0,16},{16,0},{1,17},{17,1},{2,18},{18,2},{3,19},{19,3},{4,20},{20... | collective-permute-start | bytes 294920 | tf_op jit(solution)/shard_map/ppermute | solution.py:448
  58.7 2.4 %collective-permute-done.16.got_ref = bf16[96,384]{1,0:T(8,128)(2,1)S(1)} collective-permute-done((bf16[96,384]{1,0:T(8,128)(2,1)S(1)}, bf16[96,384]{1,0:T(8,128)(2,1)S(1)}, u32[]{:S(2)}, u32[]{:S(2)}) %collective-permute-start.16) | collective-permute-done | bytes 73760 | tf_op jit(solution)/shard_map/ppermute | solution.py:448
  61.0 1.1 %row_grad.2 = (bf16[96,384]{1,0:T(8,128)(2,1)S(1)}, bf16[96,384]{1,0:T(8,128)(2,1)S(1)}, f32[96,2048]{1,0:T(8,128)S(1)}) custom-call(s32[1]{0:T(128)} %bitcast.2.place_ref, f32[96,384]{1,0:T(8,128)S(1)} %get-tuple-element.87.own_ref, bf16[96,384]{1,0:T(8,128)(2,1)S(1)} %collective-permute-done.16.got_ref, f32[96,384]{1,0:T(8,128)S(1)} %get-tuple-element.89.up_deriv, ...), custom_call_target="tpu_custom_call" | custom-call | flops 603979776 | bytes 3145728 | tf_op jit(solution)/shard_map/row_grad/pallas_call | solution.py:54
  62.1 0.5 collective-permute-done.15.got_ref
  62.6 1.6 %row_grad.3 = (bf16[96,512]{1,0:T(8,128)(2,1)S(1)}, bf16[96,512]{1,0:T(8,128)(2,1)S(1)}, f32[768,128]{1,0:T(8,128)S(1)}, bf16[768,128]{1,0:T(8,128)(2,1)S(1)}) custom-call(s32[1]{0:T(128)} %bitcast.2.place_ref, f32[96,512]{1,0:T(8,128)S(1)} %get-tuple-element.83.own_ref, bf16[96,512]{1,0:T(8,128)(2,1)S(1)} %collective-permute-done.15.got_ref, ...), custom_call_target="tpu_custom_call" | custom-call | flops 805306368 | bytes 4194304 | tf_op jit(solution)/shard_map/row_grad/pallas_call | solution.py:54
  64.3 1.4 %collective-permute-done.17.got_ref = bf16[768,128]{1,0:T(8,128)(2,1)S(1)} collective-permute-done((bf16[768,128]{1,0:T(8,128)(2,1)S(1)}, bf16[768,128]{1,0:T(8,128)(2,1)S(1)}, u32[]{:S(2)}, u32[]{:S(2)}) %collective-permute-start.17) | collective-permute-done | bytes 196640 | tf_op jit(solution)/shard_map/ppermute | solution.py:442
  65.7 0.7 add_cores.1
  66.5 4.0 %all-to-all-start.1 = ((bf16[16,48,128]{2,1,0:T(8,128)(2,1)}), bf16[16,48,128]{2,1,0:T(8,128)(2,1)S(1)}, u32[]{:S(2)}, u32[]{:S(2)}) async-start(bf16[16,48,128]{2,1,0:T(8,128)(2,1)} %bitcast.5), calls=%async_computation.1 | async-start | bytes 393216 | tf_op jit(solution)/shard_map/all_to_all | solution.py:451
  70.4 3.4 %weight_grads.1 = (bf16[2048,896]{1,0:T(8,128)(2,1)}, bf16[2048,896]{1,0:T(8,128)(2,1)}) custom-call(bf16[2048,96]{1,0:T(8,128)(2,1)S(1)} %get-tuple-element.94.turned_ref, bf16[96,512]{1,0:T(8,128)(2,1)S(1)} %get-tuple-element.95.refs_0_, bf16[96,384]{1,0:T(8,128)(2,1)S(1)} %get-tuple-element.96.refs_1_, bf16[96,512]{1,0:T(8,128)(2,1)S(1)} %get-tuple-element.97.refs_2_, ...), custom_call_target="tpu_custom_call" | custom-call | flops 704643072 | bytes 7340032 | tf_op jit(solution)/shard_map/weight_grads/pallas_call | solution.py:54
  73.8 5.3 %all-to-all-done.1 = bf16[16,48,128]{2,1,0:T(8,128)(2,1)S(1)} async-done(((bf16[16,48,128]{2,1,0:T(8,128)(2,1)}), bf16[16,48,128]{2,1,0:T(8,128)(2,1)S(1)}, u32[]{:S(2)}, u32[]{:S(2)}) %all-to-all-start.1) | async-done | bytes 196640 | tf_op jit(solution)/shard_map/all_to_all | solution.py:451
  79.1 1.3 %token_grad.1 = bf16[128,4096]{1,0:T(8,128)(2,1)} custom-call(bf16[16,128]{1,0:T(8,128)(2,1)S(1)} %get-tuple-element.52.pick_ref, bf16[768,128]{1,0:T(8,128)(2,1)S(1)} %bitcast.9), custom_call_target="tpu_custom_call" | custom-call | tf_op jit(solution)/shard_map/token_grad/pallas_call | solution.py:54
  (19 shorter events, 0.4 us)
Async XLA Ops:
  3.3 18.2 %all-to-all-start = ((bf16[16,64,128]{2,1,0:T(8,128)(2,1)}), bf16[16,64,128]{2,1,0:T(8,128)(2,1)S(1)}, u32[]{:S(2)}, u32[]{:S(2)}) async-start(bf16[16,64,128]{2,1,0:T(8,128)(2,1)} %bitcast.3), calls=%async_computation | async-start | bytes 524288 | tf_op jit(solution)/shard_map/all_to_all | solution.py:451
  21.5 1.6 %collective-permute-start = (bf16[1024,128]{1,0:T(8,128)(2,1)S(1)}, bf16[1024,128]{1,0:T(8,128)(2,1)S(1)}, u32[]{:S(2)}, u32[]{:S(2)}) collective-permute-start(bf16[1024,128]{1,0:T(8,128)(2,1)S(1)} %bitcast.7), channel_id=1, source_target_pairs={{0,1},{1,0},{2,3},{3,2},{4,5},{5,4},{6,7},{7,6},{8,9},{9,8},{10,11... | collective-permute-start | bytes 786440 | tf_op jit(solution)/shard_map/ppermute | solution.py:442
  24.2 7.8 %collective-permute-start.2 = (bf16[2,96,512]{2,1,0:T(8,128)(2,1)S(1)}, bf16[2,96,512]{2,1,0:T(8,128)(2,1)S(1)}, u32[]{:S(2)}, u32[]{:S(2)}) collective-permute-start(bf16[2,96,512]{2,1,0:T(8,128)(2,1)S(1)} %get-tuple-element.68), channel_id=1, source_target_pairs={{0,16},{16,0},{1,17},{17,1},{2,18},{18,2},{3,19},{19,3},{4,20},{20... | collective-permute-start | bytes 589832 | tf_op jit(solution)/shard_map/ppermute | solution.py:448
  25.4 6.6 %copy-start = (bf16[896,2048]{1,0:T(8,128)(2,1)S(1)}, bf16[896,2048]{1,0:T(8,128)(2,1)}, u32[]{:S(2)}) copy-start(bf16[896,2048]{1,0:T(8,128)(2,1)} %down_w.15) | copy-start | bytes 11010052
  28.1 6.6 %collective-permute-start.1 = (bf16[2,96,384]{2,1,0:T(8,128)(2,1)S(1)}, bf16[2,96,384]{2,1,0:T(8,128)(2,1)S(1)}, u32[]{:S(2)}, u32[]{:S(2)}) collective-permute-start(bf16[2,96,384]{2,1,0:T(8,128)(2,1)S(1)} %get-tuple-element.66), channel_id=1, source_target_pairs={{0,16},{16,0},{1,17},{17,1},{2,18},{18,2},{3,19},{19,3},{4,20},{20... | collective-permute-start | bytes 442376 | tf_op jit(solution)/shard_map/ppermute | solution.py:448
  35.1 1.5 %collective-permute-start.3 = (bf16[768,128]{1,0:T(8,128)(2,1)S(1)}, bf16[768,128]{1,0:T(8,128)(2,1)S(1)}, u32[]{:S(2)}, u32[]{:S(2)}) collective-permute-start(bf16[768,128]{1,0:T(8,128)(2,1)S(1)} %get-tuple-element.71), channel_id=1, source_target_pairs={{0,1},{1,0},{2,3},{3,2},{4,5},{5,4},{6,7},{7,6},{8,9},{9,8},{10,11... | collective-permute-start | bytes 589832 | tf_op jit(solution)/shard_map/ppermute | solution.py:442
  36.7 5.5 %collective-permute-start.4 = (bf16[192,128]{1,0:T(8,128)(2,1)S(1)}, bf16[192,128]{1,0:T(8,128)(2,1)S(1)}, u32[]{:S(2)}, u32[]{:S(2)}) collective-permute-start(bf16[192,128]{1,0:T(8,128)(2,1)S(1)} %get-tuple-element.73), channel_id=1, source_target_pairs={{0,6},{1,7},{2,4},{3,5},{4,2},{5,3},{6,0},{7,1},{8,14},{9,15},{10,... | collective-permute-start | bytes 147464 | tf_op jit(solution)/shard_map/ppermute | solution.py:442
  37.6 4.6 %collective-permute-start.5 = (bf16[192,128]{1,0:T(8,128)(2,1)S(1)}, bf16[192,128]{1,0:T(8,128)(2,1)S(1)}, u32[]{:S(2)}, u32[]{:S(2)}) collective-permute-start(bf16[192,128]{1,0:T(8,128)(2,1)S(1)} %get-tuple-element.74), channel_id=1, source_target_pairs={{0,2},{1,3},{2,0},{3,1},{4,6},{5,7},{6,4},{7,5},{8,10},{9,11},{10,... | collective-permute-start | bytes 147464 | tf_op jit(solution)/shard_map/ppermute | solution.py:442
  39.1 4.1 %collective-permute-start.6 = (bf16[192,128]{1,0:T(8,128)(2,1)S(1)}, bf16[192,128]{1,0:T(8,128)(2,1)S(1)}, u32[]{:S(2)}, u32[]{:S(2)}) collective-permute-start(bf16[192,128]{1,0:T(8,128)(2,1)S(1)} %get-tuple-element.75), channel_id=1, source_target_pairs={{0,4},{1,5},{2,6},{3,7},{4,0},{5,1},{6,2},{7,3},{8,12},{9,13},{10,... | collective-permute-start | bytes 147464 | tf_op jit(solution)/shard_map/ppermute | solution.py:442
  43.2 5.1 %collective-permute-start.7 = (bf16[192,128]{1,0:T(8,128)(2,1)S(1)}, bf16[192,128]{1,0:T(8,128)(2,1)S(1)}, u32[]{:S(2)}, u32[]{:S(2)}) collective-permute-start(bf16[192,128]{1,0:T(8,128)(2,1)S(1)} %get-tuple-element.79), channel_id=1, source_target_pairs={{0,8},{1,9},{2,10},{3,11},{4,12},{5,13},{6,14},{7,15},{8,0},{9,1},... | collective-permute-start | bytes 147464 | tf_op jit(solution)/shard_map/ppermute | solution.py:442
  48.3 3.9 %collective-permute-start.13 = (bf16[192,128]{1,0:T(8,128)(2,1)S(1)}, bf16[192,128]{1,0:T(8,128)(2,1)S(1)}, u32[]{:S(2)}, u32[]{:S(2)}) collective-permute-start(bf16[192,128]{1,0:T(8,128)(2,1)S(1)} %cotangent.1.refs_0_), channel_id=1, source_target_pairs={{0,1},{1,0},{2,3},{3,2},{4,5},{5,4},{6,7},{7,6},{8,9},{9,8},{10,11... | collective-permute-start | bytes 147464 | tf_op jit(solution)/shard_map/ppermute | solution.py:442
  48.4 5.3 %collective-permute-start.12 = (bf16[192,128]{1,0:T(8,128)(2,1)S(1)}, bf16[192,128]{1,0:T(8,128)(2,1)S(1)}, u32[]{:S(2)}, u32[]{:S(2)}) collective-permute-start(bf16[192,128]{1,0:T(8,128)(2,1)S(1)} %cotangent.1.refs_0_), channel_id=1, source_target_pairs={{0,6},{1,7},{2,4},{3,5},{4,2},{5,3},{6,0},{7,1},{8,14},{9,15},{10,... | collective-permute-start | bytes 147464 | tf_op jit(solution)/shard_map/ppermute | solution.py:442
  49.8 4.1 %collective-permute-start.10 = (bf16[192,128]{1,0:T(8,128)(2,1)S(1)}, bf16[192,128]{1,0:T(8,128)(2,1)S(1)}, u32[]{:S(2)}, u32[]{:S(2)}) collective-permute-start(bf16[192,128]{1,0:T(8,128)(2,1)S(1)} %cotangent.1.refs_0_), channel_id=1, source_target_pairs={{0,4},{1,5},{2,6},{3,7},{4,0},{5,1},{6,2},{7,3},{8,12},{9,13},{10,... | collective-permute-start | bytes 147464 | tf_op jit(solution)/shard_map/ppermute | solution.py:442
  50.5 4.1 %collective-permute-start.8 = (bf16[192,128]{1,0:T(8,128)(2,1)S(1)}, bf16[192,128]{1,0:T(8,128)(2,1)S(1)}, u32[]{:S(2)}, u32[]{:S(2)}) collective-permute-start(bf16[192,128]{1,0:T(8,128)(2,1)S(1)} %cotangent.1.refs_0_), channel_id=1, source_target_pairs={{0,2},{1,3},{2,0},{3,1},{4,6},{5,7},{6,4},{7,5},{8,10},{9,11},{10,... | collective-permute-start | bytes 147464 | tf_op jit(solution)/shard_map/ppermute | solution.py:442
  53.6 1.5 %collective-permute-start.14 = (bf16[192,128]{1,0:T(8,128)(2,1)S(1)}, bf16[192,128]{1,0:T(8,128)(2,1)S(1)}, u32[]{:S(2)}, u32[]{:S(2)}) collective-permute-start(bf16[192,128]{1,0:T(8,128)(2,1)S(1)} %collective-permute-done.12.refs_2_), channel_id=1, source_target_pairs={{0,1},{1,0},{2,3},{3,2},{4,5},{5,4},{6,7},{7,6},{8,9},{9,8},{10,11... | collective-permute-start | bytes 147464 | tf_op jit(solution)/shard_map/ppermute | solution.py:442
  53.9 1.3 %collective-permute-start.11 = (bf16[192,128]{1,0:T(8,128)(2,1)S(1)}, bf16[192,128]{1,0:T(8,128)(2,1)S(1)}, u32[]{:S(2)}, u32[]{:S(2)}) collective-permute-start(bf16[192,128]{1,0:T(8,128)(2,1)S(1)} %collective-permute-done.10.refs_1_), channel_id=1, source_target_pairs={{0,1},{1,0},{2,3},{3,2},{4,5},{5,4},{6,7},{7,6},{8,9},{9,8},{10,11... | collective-permute-start | bytes 147464 | tf_op jit(solution)/shard_map/ppermute | solution.py:442
  54.5 1.2 %collective-permute-start.9 = (bf16[192,128]{1,0:T(8,128)(2,1)S(1)}, bf16[192,128]{1,0:T(8,128)(2,1)S(1)}, u32[]{:S(2)}, u32[]{:S(2)}) collective-permute-start(bf16[192,128]{1,0:T(8,128)(2,1)S(1)} %collective-permute-done.8.refs_0_), channel_id=1, source_target_pairs={{0,1},{1,0},{2,3},{3,2},{4,5},{5,4},{6,7},{7,6},{8,9},{9,8},{10,11... | collective-permute-start | bytes 147464 | tf_op jit(solution)/shard_map/ppermute | solution.py:442
  55.1 5.9 %copy-start.1 = (bf16[2048,896]{1,0:T(8,128)(2,1)S(1)}, bf16[2048,896]{1,0:T(8,128)(2,1)}, u32[]{:S(2)}) copy-start(bf16[2048,896]{1,0:T(8,128)(2,1)} %gate_w.3) | copy-start | bytes 11010052
  55.1 5.9 %copy-start.2 = (bf16[2048,896]{1,0:T(8,128)(2,1)S(1)}, bf16[2048,896]{1,0:T(8,128)(2,1)}, u32[]{:S(2)}) copy-start(bf16[2048,896]{1,0:T(8,128)(2,1)} %up_w.3) | copy-start | bytes 11010052
  56.1 4.9 %collective-permute-start.16 = (bf16[96,384]{1,0:T(8,128)(2,1)S(1)}, bf16[96,384]{1,0:T(8,128)(2,1)S(1)}, u32[]{:S(2)}, u32[]{:S(2)}) collective-permute-start(bf16[96,384]{1,0:T(8,128)(2,1)S(1)} %get-tuple-element.88), channel_id=1, source_target_pairs={{0,16},{16,0},{1,17},{17,1},{2,18},{18,2},{3,19},{19,3},{4,20},{20... | collective-permute-start | bytes 221192 | tf_op jit(solution)/shard_map/ppermute | solution.py:448
  57.5 5.1 %collective-permute-start.15 = (bf16[96,512]{1,0:T(8,128)(2,1)S(1)}, bf16[96,512]{1,0:T(8,128)(2,1)S(1)}, u32[]{:S(2)}, u32[]{:S(2)}) collective-permute-start(bf16[96,512]{1,0:T(8,128)(2,1)S(1)} %get-tuple-element.84), channel_id=1, source_target_pairs={{0,16},{16,0},{1,17},{17,1},{2,18},{18,2},{3,19},{19,3},{4,20},{20... | collective-permute-start | bytes 294920 | tf_op jit(solution)/shard_map/ppermute | solution.py:448
  64.2 1.5 %collective-permute-start.17 = (bf16[768,128]{1,0:T(8,128)(2,1)S(1)}, bf16[768,128]{1,0:T(8,128)(2,1)S(1)}, u32[]{:S(2)}, u32[]{:S(2)}) collective-permute-start(bf16[768,128]{1,0:T(8,128)(2,1)S(1)} %get-tuple-element.93), channel_id=1, source_target_pairs={{0,1},{1,0},{2,3},{3,2},{4,5},{5,4},{6,7},{7,6},{8,9},{9,8},{10,11... | collective-permute-start | bytes 589832 | tf_op jit(solution)/shard_map/ppermute | solution.py:442
  66.5 12.7 %all-to-all-start.1 = ((bf16[16,48,128]{2,1,0:T(8,128)(2,1)}), bf16[16,48,128]{2,1,0:T(8,128)(2,1)S(1)}, u32[]{:S(2)}, u32[]{:S(2)}) async-start(bf16[16,48,128]{2,1,0:T(8,128)(2,1)} %bitcast.5), calls=%async_computation.1 | async-start | bytes 393216 | tf_op jit(solution)/shard_map/all_to_all | solution.py:451

commit v10 on v9

--- a/solution.py
+++ b/solution.py
@@ -360,8 +360,8 @@
 
     def column(j, _):
         at = pl.ds(pl.multiple_of(j * 2 * LANES, 2 * LANES), 2 * LANES)
-        value = dot_nt(gate_out[...], gate_w[at, start : start + hid])
-        value = value + dot_nt(up_out[...], up_w[at, start : start + hid])
+        value = dot_nt(gate_w[at, start : start + hid], gate_out[...])
+        value = (value + dot_nt(up_w[at, start : start + hid], up_out[...])).T
         if total_ref is not None:
             value = value + total_ref[:, at]
         if not last:

time: 80.8 us -> 80.7 us (level)
  no operation moved by 1% of the time
where the time goes in v10:
time: 80.7 us; the launch traced here: 80.3 us
  waiting for transfers between devices  32.7 us (41%)
  starting transfers between devices  25.9 us (32%)
  Pallas kernels  20.7 us (26%)
  between operations  0.85 us (1%)
    pallas_call x21, Pallas kernels, call(): pl.pallas_call(body, out_shape=outs, in_specs=specs, out_specs=jax.tree.m...  20.7 us
    all_to_all x2, waiting for transfers between devices, over_slice(): lax.all_to_all(x, ('dp', 'expert'), 0, 0, axis_index_groups=slice_groups,...  13.6 us
    all_to_all x2, starting transfers between devices, over_slice(): lax.all_to_all(x, ('dp', 'expert'), 0, 0, axis_index_groups=slice_groups,...  12.3 us
    ppermute x14, waiting for transfers between devices, other(): return lax.ppermute(x, 'expert', [(i, i ^ mask) for i in range(n_expert)])  11.2 us
    ppermute x14, starting transfers between devices, other(): return lax.ppermute(x, 'expert', [(i, i ^ mask) for i in range(n_expert)])  9.32 us
    ppermute x4, waiting for transfers between devices, other_dp(): return lax.ppermute(x, 'dp', [(0, 1), (1, 0)])  7.96 us
    ppermute x4, starting transfers between devices, other_dp(): return lax.ppermute(x, 'dp', [(0, 1), (1, 0)])  4.31 us
  transfers between devices with their start and end apart: 20, of which 16 were waited for; matrix products, arithmetic and copies ran while one was open for 0% of the time, Pallas kernels for 16%

profile of v10, /device:TPU:0, one launch (start us, length us, event | category | flops | bytes accessed | tf_op | source)
XLA Modules:
  0.0 80.3 jit_solution(7662975100396051287)
XLA Ops:
  0.6 2.7 %route.1 = (bf16[1024,128]{1,0:T(8,128)(2,1)}, bf16[16,128]{1,0:T(8,128)(2,1)S(1)}) custom-call(s32[2,128]{1,0:T(2,128)} %bitcast.10, f32[2,128]{1,0:T(2,128)} %bitcast.11, bf16[128,4096]{1,0:T(8,128)(2,1)} %tokens_hbm.1, bf16[128,4096]{1,0:T(8,128)(2,1)} %target_hbm.1), custom_call_target="tpu_custom_call" | custom-call | tf_op jit(solution)/shard_map/route/pallas_call | solution.py:54
  3.3 8.3 %all-to-all-start = ((bf16[16,64,128]{2,1,0:T(8,128)(2,1)}), bf16[16,64,128]{2,1,0:T(8,128)(2,1)S(1)}, u32[]{:S(2)}, u32[]{:S(2)}) async-start(bf16[16,64,128]{2,1,0:T(8,128)(2,1)} %bitcast.3), calls=%async_computation | async-start | bytes 524288 | tf_op jit(solution)/shard_map/all_to_all | solution.py:451
  11.7 1.6 %load_weights.2 = (f32[8,128]{1,0:T(8,128)S(1)}, bf16[2048,256]{1,0:T(8,128)(2,1)S(1)}, bf16[2048,256]{1,0:T(8,128)(2,1)S(1)}) custom-call(bf16[2048,896]{1,0:T(8,128)(2,1)} %gate_w.3, bf16[2048,896]{1,0:T(8,128)(2,1)} %up_w.3), custom_call_target="tpu_custom_call" | custom-call | flops 1000000000 | bytes 4194304 | tf_op jit(solution)/shard_map/load_weights/pallas_call | solution.py:54
  13.2 8.3 %all-to-all-done = bf16[16,64,128]{2,1,0:T(8,128)(2,1)S(1)} async-done(((bf16[16,64,128]{2,1,0:T(8,128)(2,1)}), bf16[16,64,128]{2,1,0:T(8,128)(2,1)S(1)}, u32[]{:S(2)}, u32[]{:S(2)}) %all-to-all-start) | async-done | bytes 262176 | tf_op jit(solution)/shard_map/all_to_all | solution.py:451
  21.5 1.6 %load_weights.3 = (bf16[2048,256]{1,0:T(8,128)(2,1)S(1)}, bf16[2048,256]{1,0:T(8,128)(2,1)S(1)}, bf16[48,2048]{1,0:T(8,128)(2,1)S(1)}, f32[48,128]{1,0:T(8,128)S(1)}, f32[48,128]{1,0:T(8,128)S(1)}) custom-call(s32[1]{0:T(128)} %bitcast.2.place_ref, bf16[1024,128]{1,0:T(8,128)(2,1)S(1)} %bitcast.8, bf16[2048,896]{1,0:T(8,128)(2,1)} %gate_w.3, ...), custom_call_target="tpu_custom_call" | custom-call | flops 1000000000 | bytes 4194304 | tf_op jit(solution)/shard_map/load_weights/pallas_call | solution.py:54
  23.1 1.1 %pre_activations.2 = (bf16[96,2048]{1,0:T(8,128)(2,1)S(1)}, f32[96,128]{1,0:T(8,128)S(1)}, f32[96,128]{1,0:T(8,128)S(1)}, f32[2,96,512]{2,1,0:T(8,128)S(1)}, bf16[2,96,512]{2,1,0:T(8,128)(2,1)S(1)}) custom-call(s32[1]{0:T(128)} %bitcast.2.place_ref, f32[8,128]{1,0:T(8,128)S(1)} %get-tuple-element.55.loaded_ref, ...), custom_call_target="tpu_custom_call" | custom-call | flops 805306368 | bytes 4194304 | tf_op jit(solution)/shard_map/pre_activations/pallas_call | solution.py:54
  24.2 1.2 %collective-permute-start.2 = (bf16[2,96,512]{2,1,0:T(8,128)(2,1)S(1)}, bf16[2,96,512]{2,1,0:T(8,128)(2,1)S(1)}, u32[]{:S(2)}, u32[]{:S(2)}) collective-permute-start(bf16[2,96,512]{2,1,0:T(8,128)(2,1)S(1)} %get-tuple-element.68), channel_id=1, source_target_pairs={{0,16},{16,0},{1,17},{17,1},{2,18},{18,2},{3,19},{19,3},{4,20},{20... | collective-permute-start | bytes 589832 | tf_op jit(solution)/shard_map/ppermute | solution.py:448
  25.4 2.8 %pre_activations.3 = (bf16[2048,96]{1,0:T(8,128)(2,1)S(1)}, f32[2,96,384]{2,1,0:T(8,128)S(1)}, bf16[2,96,384]{2,1,0:T(8,128)(2,1)S(1)}) custom-call(bf16[96,2048]{1,0:T(8,128)(2,1)S(1)} %get-tuple-element.64.rows_ref, bf16[2048,896]{1,0:T(8,128)(2,1)} %gate_w.3, bf16[2048,896]{1,0:T(8,128)(2,1)} %up_w.3), custom_call_target="tpu_custom_call" | custom-call | flops 603979776 | bytes 3145728 | tf_op jit(solution)/shard_map/pre_activations/pallas_call | solution.py:54
  28.1 1.0 %collective-permute-start.1 = (bf16[2,96,384]{2,1,0:T(8,128)(2,1)S(1)}, bf16[2,96,384]{2,1,0:T(8,128)(2,1)S(1)}, u32[]{:S(2)}, u32[]{:S(2)}) collective-permute-start(bf16[2,96,384]{2,1,0:T(8,128)(2,1)S(1)} %get-tuple-element.66), channel_id=1, source_target_pairs={{0,16},{16,0},{1,17},{17,1},{2,18},{18,2},{3,19},{19,3},{4,20},{20... | collective-permute-start | bytes 442376 | tf_op jit(solution)/shard_map/ppermute | solution.py:448
  29.1 2.8 %collective-permute-done.2.got_ref = bf16[2,96,512]{2,1,0:T(8,128)(2,1)S(1)} collective-permute-done((bf16[2,96,512]{2,1,0:T(8,128)(2,1)S(1)}, bf16[2,96,512]{2,1,0:T(8,128)(2,1)S(1)}, u32[]{:S(2)}, u32[]{:S(2)}) %collective-permute-start.2) | collective-permute-done | bytes 196640 | tf_op jit(solution)/shard_map/ppermute | solution.py:448
  32.0 0.5 down.1
  32.5 2.2 %collective-permute-done.1.got_ref = bf16[2,96,384]{2,1,0:T(8,128)(2,1)S(1)} collective-permute-done((bf16[2,96,384]{2,1,0:T(8,128)(2,1)S(1)}, bf16[2,96,384]{2,1,0:T(8,128)(2,1)S(1)}, u32[]{:S(2)}, u32[]{:S(2)}) %collective-permute-start.1) | collective-permute-done | bytes 147488 | tf_op jit(solution)/shard_map/ppermute | solution.py:448
  34.7 0.3 down_send.1
  35.2 0.3 down_keep.1.own_ref
  35.5 1.1 %collective-permute-done.3.got_ref = bf16[768,128]{1,0:T(8,128)(2,1)S(1)} collective-permute-done((bf16[768,128]{1,0:T(8,128)(2,1)S(1)}, bf16[768,128]{1,0:T(8,128)(2,1)S(1)}, u32[]{:S(2)}, u32[]{:S(2)}) %collective-permute-start.3) | collective-permute-done | bytes 196640 | tf_op jit(solution)/shard_map/ppermute | solution.py:442
  36.7 1.0 %collective-permute-start.4 = (bf16[192,128]{1,0:T(8,128)(2,1)S(1)}, bf16[192,128]{1,0:T(8,128)(2,1)S(1)}, u32[]{:S(2)}, u32[]{:S(2)}) collective-permute-start(bf16[192,128]{1,0:T(8,128)(2,1)S(1)} %get-tuple-element.73), channel_id=1, source_target_pairs={{0,6},{1,7},{2,4},{3,5},{4,2},{5,3},{6,0},{7,1},{8,14},{9,15},{10,... | collective-permute-start | bytes 147464 | tf_op jit(solution)/shard_map/ppermute | solution.py:442
  37.6 1.5 %collective-permute-start.5 = (bf16[192,128]{1,0:T(8,128)(2,1)S(1)}, bf16[192,128]{1,0:T(8,128)(2,1)S(1)}, u32[]{:S(2)}, u32[]{:S(2)}) collective-permute-start(bf16[192,128]{1,0:T(8,128)(2,1)S(1)} %get-tuple-element.74), channel_id=1, source_target_pairs={{0,2},{1,3},{2,0},{3,1},{4,6},{5,7},{6,4},{7,5},{8,10},{9,11},{10,... | collective-permute-start | bytes 147464 | tf_op jit(solution)/shard_map/ppermute | solution.py:442
  39.1 1.1 %collective-permute-start.6 = (bf16[192,128]{1,0:T(8,128)(2,1)S(1)}, bf16[192,128]{1,0:T(8,128)(2,1)S(1)}, u32[]{:S(2)}, u32[]{:S(2)}) collective-permute-start(bf16[192,128]{1,0:T(8,128)(2,1)S(1)} %get-tuple-element.75), channel_id=1, source_target_pairs={{0,4},{1,5},{2,6},{3,7},{4,0},{5,1},{6,2},{7,3},{8,12},{9,13},{10,... | collective-permute-start | bytes 147464 | tf_op jit(solution)/shard_map/ppermute | solution.py:442
  40.2 1.9 %collective-permute-done.4.first_ref = bf16[192,128]{1,0:T(8,128)(2,1)S(1)} collective-permute-done((bf16[192,128]{1,0:T(8,128)(2,1)S(1)}, bf16[192,128]{1,0:T(8,128)(2,1)S(1)}, u32[]{:S(2)}, u32[]{:S(2)}) %collective-permute-start.4) | collective-permute-done | bytes 49184 | tf_op jit(solution)/shard_map/ppermute | solution.py:442
  42.2 0.1 collective-permute-done.5.second_ref
  42.2 0.9 %collective-permute-done.6.third_ref = bf16[192,128]{1,0:T(8,128)(2,1)S(1)} collective-permute-done((bf16[192,128]{1,0:T(8,128)(2,1)S(1)}, bf16[192,128]{1,0:T(8,128)(2,1)S(1)}, u32[]{:S(2)}, u32[]{:S(2)}) %collective-permute-start.6) | collective-permute-done | bytes 49184 | tf_op jit(solution)/shard_map/ppermute | solution.py:442
  43.2 1.7 %collective-permute-start.7 = (bf16[192,128]{1,0:T(8,128)(2,1)S(1)}, bf16[192,128]{1,0:T(8,128)(2,1)S(1)}, u32[]{:S(2)}, u32[]{:S(2)}) collective-permute-start(bf16[192,128]{1,0:T(8,128)(2,1)S(1)} %get-tuple-element.79), channel_id=1, source_target_pairs={{0,8},{1,9},{2,10},{3,11},{4,12},{5,13},{6,14},{7,15},{8,0},{9,1},... | collective-permute-start | bytes 147464 | tf_op jit(solution)/shard_map/ppermute | solution.py:442
  44.9 3.4 %collective-permute-done.7.got_ref = bf16[192,128]{1,0:T(8,128)(2,1)S(1)} collective-permute-done((bf16[192,128]{1,0:T(8,128)(2,1)S(1)}, bf16[192,128]{1,0:T(8,128)(2,1)S(1)}, u32[]{:S(2)}, u32[]{:S(2)}) %collective-permute-start.7) | collective-permute-done | bytes 49184 | tf_op jit(solution)/shard_map/ppermute | solution.py:442
  48.4 1.4 %collective-permute-start.12 = (bf16[192,128]{1,0:T(8,128)(2,1)S(1)}, bf16[192,128]{1,0:T(8,128)(2,1)S(1)}, u32[]{:S(2)}, u32[]{:S(2)}) collective-permute-start(bf16[192,128]{1,0:T(8,128)(2,1)S(1)} %cotangent.1.refs_0_), channel_id=1, source_target_pairs={{0,6},{1,7},{2,4},{3,5},{4,2},{5,3},{6,0},{7,1},{8,14},{9,15},{10,... | collective-permute-start | bytes 147464 | tf_op jit(solution)/shard_map/ppermute | solution.py:442
  49.8 0.7 collective-permute-start.10
  50.5 1.5 %collective-permute-start.8 = (bf16[192,128]{1,0:T(8,128)(2,1)S(1)}, bf16[192,128]{1,0:T(8,128)(2,1)S(1)}, u32[]{:S(2)}, u32[]{:S(2)}) collective-permute-start(bf16[192,128]{1,0:T(8,128)(2,1)S(1)} %cotangent.1.refs_0_), channel_id=1, source_target_pairs={{0,2},{1,3},{2,0},{3,1},{4,6},{5,7},{6,4},{7,5},{8,10},{9,11},{10,... | collective-permute-start | bytes 147464 | tf_op jit(solution)/shard_map/ppermute | solution.py:442
  51.9 0.3 grad_hidden_near.3.refs_1_
  52.2 0.3 grad_hidden_near.4.refs_3_
  52.5 1.1 %collective-permute-done.12.refs_2_ = bf16[192,128]{1,0:T(8,128)(2,1)S(1)} collective-permute-done((bf16[192,128]{1,0:T(8,128)(2,1)S(1)}, bf16[192,128]{1,0:T(8,128)(2,1)S(1)}, u32[]{:S(2)}, u32[]{:S(2)}) %collective-permute-start.12) | collective-permute-done | bytes 49184 | tf_op jit(solution)/shard_map/ppermute | solution.py:442
  53.6 0.2 collective-permute-done.10.refs_1_
  53.9 0.3 collective-permute-start.11
  54.2 0.4 collective-permute-done.8.refs_0_
  54.6 0.6 grad_hidden_near.5.total_ref
  55.2 0.6 collective-permute-done.9.first_ref
  55.8 0.3 grad_hidden.2
  56.1 1.0 %collective-permute-start.16 = (bf16[96,384]{1,0:T(8,128)(2,1)S(1)}, bf16[96,384]{1,0:T(8,128)(2,1)S(1)}, u32[]{:S(2)}, u32[]{:S(2)}) collective-permute-start(bf16[96,384]{1,0:T(8,128)(2,1)S(1)} %get-tuple-element.88), channel_id=1, source_target_pairs={{0,16},{16,0},{1,17},{17,1},{2,18},{18,2},{3,19},{19,3},{4,20},{20... | collective-permute-start | bytes 221192 | tf_op jit(solution)/shard_map/ppermute | solution.py:448
  57.1 0.4 grad_hidden.3
  57.5 1.2 %collective-permute-start.15 = (bf16[96,512]{1,0:T(8,128)(2,1)S(1)}, bf16[96,512]{1,0:T(8,128)(2,1)S(1)}, u32[]{:S(2)}, u32[]{:S(2)}) collective-permute-start(bf16[96,512]{1,0:T(8,128)(2,1)S(1)} %get-tuple-element.84), channel_id=1, source_target_pairs={{0,16},{16,0},{1,17},{17,1},{2,18},{18,2},{3,19},{19,3},{4,20},{20... | collective-permute-start | bytes 294920 | tf_op jit(solution)/shard_map/ppermute | solution.py:448
  58.7 2.4 %collective-permute-done.16.got_ref = bf16[96,384]{1,0:T(8,128)(2,1)S(1)} collective-permute-done((bf16[96,384]{1,0:T(8,128)(2,1)S(1)}, bf16[96,384]{1,0:T(8,128)(2,1)S(1)}, u32[]{:S(2)}, u32[]{:S(2)}) %collective-permute-start.16) | collective-permute-done | bytes 73760 | tf_op jit(solution)/shard_map/ppermute | solution.py:448
  61.0 1.1 %row_grad.2 = (bf16[96,384]{1,0:T(8,128)(2,1)S(1)}, bf16[96,384]{1,0:T(8,128)(2,1)S(1)}, f32[96,2048]{1,0:T(8,128)S(1)}) custom-call(s32[1]{0:T(128)} %bitcast.2.place_ref, f32[96,384]{1,0:T(8,128)S(1)} %get-tuple-element.87.own_ref, bf16[96,384]{1,0:T(8,128)(2,1)S(1)} %collective-permute-done.16.got_ref, f32[96,384]{1,0:T(8,128)S(1)} %get-tuple-element.89.up_deriv, ...), custom_call_target="tpu_custom_call" | custom-call | flops 603979776 | bytes 3145728 | tf_op jit(solution)/shard_map/row_grad/pallas_call | solution.py:54
  62.1 0.5 collective-permute-done.15.got_ref
  62.6 1.4 %row_grad.3 = (bf16[96,512]{1,0:T(8,128)(2,1)S(1)}, bf16[96,512]{1,0:T(8,128)(2,1)S(1)}, f32[768,128]{1,0:T(8,128)S(1)}, bf16[768,128]{1,0:T(8,128)(2,1)S(1)}) custom-call(s32[1]{0:T(128)} %bitcast.2.place_ref, f32[96,512]{1,0:T(8,128)S(1)} %get-tuple-element.83.own_ref, bf16[96,512]{1,0:T(8,128)(2,1)S(1)} %collective-permute-done.15.got_ref, ...), custom_call_target="tpu_custom_call" | custom-call | flops 805306368 | bytes 4194304 | tf_op jit(solution)/shard_map/row_grad/pallas_call | solution.py:54
  64.2 1.4 %collective-permute-done.17.got_ref = bf16[768,128]{1,0:T(8,128)(2,1)S(1)} collective-permute-done((bf16[768,128]{1,0:T(8,128)(2,1)S(1)}, bf16[768,128]{1,0:T(8,128)(2,1)S(1)}, u32[]{:S(2)}, u32[]{:S(2)}) %collective-permute-start.17) | collective-permute-done | bytes 196640 | tf_op jit(solution)/shard_map/ppermute | solution.py:442
  65.6 0.7 add_cores.1
  66.3 4.0 %all-to-all-start.1 = ((bf16[16,48,128]{2,1,0:T(8,128)(2,1)}), bf16[16,48,128]{2,1,0:T(8,128)(2,1)S(1)}, u32[]{:S(2)}, u32[]{:S(2)}) async-start(bf16[16,48,128]{2,1,0:T(8,128)(2,1)} %bitcast.5), calls=%async_computation.1 | async-start | bytes 393216 | tf_op jit(solution)/shard_map/all_to_all | solution.py:451
  70.3 3.4 %weight_grads.1 = (bf16[2048,896]{1,0:T(8,128)(2,1)}, bf16[2048,896]{1,0:T(8,128)(2,1)}) custom-call(bf16[2048,96]{1,0:T(8,128)(2,1)S(1)} %get-tuple-element.94.turned_ref, bf16[96,512]{1,0:T(8,128)(2,1)S(1)} %get-tuple-element.95.refs_0_, bf16[96,384]{1,0:T(8,128)(2,1)S(1)} %get-tuple-element.96.refs_1_, bf16[96,512]{1,0:T(8,128)(2,1)S(1)} %get-tuple-element.97.refs_2_, ...), custom_call_target="tpu_custom_call" | custom-call | flops 704643072 | bytes 7340032 | tf_op jit(solution)/shard_map/weight_grads/pallas_call | solution.py:54
  73.7 5.3 %all-to-all-done.1 = bf16[16,48,128]{2,1,0:T(8,128)(2,1)S(1)} async-done(((bf16[16,48,128]{2,1,0:T(8,128)(2,1)}), bf16[16,48,128]{2,1,0:T(8,128)(2,1)S(1)}, u32[]{:S(2)}, u32[]{:S(2)}) %all-to-all-start.1) | async-done | bytes 196640 | tf_op jit(solution)/shard_map/all_to_all | solution.py:451
  79.0 1.3 %token_grad.1 = bf16[128,4096]{1,0:T(8,128)(2,1)} custom-call(bf16[16,128]{1,0:T(8,128)(2,1)S(1)} %get-tuple-element.52.pick_ref, bf16[768,128]{1,0:T(8,128)(2,1)S(1)} %bitcast.9), custom_call_target="tpu_custom_call" | custom-call | tf_op jit(solution)/shard_map/token_grad/pallas_call | solution.py:54
  (19 shorter events, 0.4 us)
Async XLA Ops:
  3.3 18.2 %all-to-all-start = ((bf16[16,64,128]{2,1,0:T(8,128)(2,1)}), bf16[16,64,128]{2,1,0:T(8,128)(2,1)S(1)}, u32[]{:S(2)}, u32[]{:S(2)}) async-start(bf16[16,64,128]{2,1,0:T(8,128)(2,1)} %bitcast.3), calls=%async_computation | async-start | bytes 524288 | tf_op jit(solution)/shard_map/all_to_all | solution.py:451
  21.5 1.6 %collective-permute-start = (bf16[1024,128]{1,0:T(8,128)(2,1)S(1)}, bf16[1024,128]{1,0:T(8,128)(2,1)S(1)}, u32[]{:S(2)}, u32[]{:S(2)}) collective-permute-start(bf16[1024,128]{1,0:T(8,128)(2,1)S(1)} %bitcast.7), channel_id=1, source_target_pairs={{0,1},{1,0},{2,3},{3,2},{4,5},{5,4},{6,7},{7,6},{8,9},{9,8},{10,11... | collective-permute-start | bytes 786440 | tf_op jit(solution)/shard_map/ppermute | solution.py:442
  24.2 7.8 %collective-permute-start.2 = (bf16[2,96,512]{2,1,0:T(8,128)(2,1)S(1)}, bf16[2,96,512]{2,1,0:T(8,128)(2,1)S(1)}, u32[]{:S(2)}, u32[]{:S(2)}) collective-permute-start(bf16[2,96,512]{2,1,0:T(8,128)(2,1)S(1)} %get-tuple-element.68), channel_id=1, source_target_pairs={{0,16},{16,0},{1,17},{17,1},{2,18},{18,2},{3,19},{19,3},{4,20},{20... | collective-permute-start | bytes 589832 | tf_op jit(solution)/shard_map/ppermute | solution.py:448
  25.4 6.6 %copy-start = (bf16[896,2048]{1,0:T(8,128)(2,1)S(1)}, bf16[896,2048]{1,0:T(8,128)(2,1)}, u32[]{:S(2)}) copy-start(bf16[896,2048]{1,0:T(8,128)(2,1)} %down_w.15) | copy-start | bytes 11010052
  28.1 6.6 %collective-permute-start.1 = (bf16[2,96,384]{2,1,0:T(8,128)(2,1)S(1)}, bf16[2,96,384]{2,1,0:T(8,128)(2,1)S(1)}, u32[]{:S(2)}, u32[]{:S(2)}) collective-permute-start(bf16[2,96,384]{2,1,0:T(8,128)(2,1)S(1)} %get-tuple-element.66), channel_id=1, source_target_pairs={{0,16},{16,0},{1,17},{17,1},{2,18},{18,2},{3,19},{19,3},{4,20},{20... | collective-permute-start | bytes 442376 | tf_op jit(solution)/shard_map/ppermute | solution.py:448
  35.1 1.5 %collective-permute-start.3 = (bf16[768,128]{1,0:T(8,128)(2,1)S(1)}, bf16[768,128]{1,0:T(8,128)(2,1)S(1)}, u32[]{:S(2)}, u32[]{:S(2)}) collective-permute-start(bf16[768,128]{1,0:T(8,128)(2,1)S(1)} %get-tuple-element.71), channel_id=1, source_target_pairs={{0,1},{1,0},{2,3},{3,2},{4,5},{5,4},{6,7},{7,6},{8,9},{9,8},{10,11... | collective-permute-start | bytes 589832 | tf_op jit(solution)/shard_map/ppermute | solution.py:442
  36.7 5.5 %collective-permute-start.4 = (bf16[192,128]{1,0:T(8,128)(2,1)S(1)}, bf16[192,128]{1,0:T(8,128)(2,1)S(1)}, u32[]{:S(2)}, u32[]{:S(2)}) collective-permute-start(bf16[192,128]{1,0:T(8,128)(2,1)S(1)} %get-tuple-element.73), channel_id=1, source_target_pairs={{0,6},{1,7},{2,4},{3,5},{4,2},{5,3},{6,0},{7,1},{8,14},{9,15},{10,... | collective-permute-start | bytes 147464 | tf_op jit(solution)/shard_map/ppermute | solution.py:442
  37.6 4.6 %collective-permute-start.5 = (bf16[192,128]{1,0:T(8,128)(2,1)S(1)}, bf16[192,128]{1,0:T(8,128)(2,1)S(1)}, u32[]{:S(2)}, u32[]{:S(2)}) collective-permute-start(bf16[192,128]{1,0:T(8,128)(2,1)S(1)} %get-tuple-element.74), channel_id=1, source_target_pairs={{0,2},{1,3},{2,0},{3,1},{4,6},{5,7},{6,4},{7,5},{8,10},{9,11},{10,... | collective-permute-start | bytes 147464 | tf_op jit(solution)/shard_map/ppermute | solution.py:442
  39.1 4.1 %collective-permute-start.6 = (bf16[192,128]{1,0:T(8,128)(2,1)S(1)}, bf16[192,128]{1,0:T(8,128)(2,1)S(1)}, u32[]{:S(2)}, u32[]{:S(2)}) collective-permute-start(bf16[192,128]{1,0:T(8,128)(2,1)S(1)} %get-tuple-element.75), channel_id=1, source_target_pairs={{0,4},{1,5},{2,6},{3,7},{4,0},{5,1},{6,2},{7,3},{8,12},{9,13},{10,... | collective-permute-start | bytes 147464 | tf_op jit(solution)/shard_map/ppermute | solution.py:442
  43.2 5.1 %collective-permute-start.7 = (bf16[192,128]{1,0:T(8,128)(2,1)S(1)}, bf16[192,128]{1,0:T(8,128)(2,1)S(1)}, u32[]{:S(2)}, u32[]{:S(2)}) collective-permute-start(bf16[192,128]{1,0:T(8,128)(2,1)S(1)} %get-tuple-element.79), channel_id=1, source_target_pairs={{0,8},{1,9},{2,10},{3,11},{4,12},{5,13},{6,14},{7,15},{8,0},{9,1},... | collective-permute-start | bytes 147464 | tf_op jit(solution)/shard_map/ppermute | solution.py:442
  48.3 3.9 %collective-permute-start.13 = (bf16[192,128]{1,0:T(8,128)(2,1)S(1)}, bf16[192,128]{1,0:T(8,128)(2,1)S(1)}, u32[]{:S(2)}, u32[]{:S(2)}) collective-permute-start(bf16[192,128]{1,0:T(8,128)(2,1)S(1)} %cotangent.1.refs_0_), channel_id=1, source_target_pairs={{0,1},{1,0},{2,3},{3,2},{4,5},{5,4},{6,7},{7,6},{8,9},{9,8},{10,11... | collective-permute-start | bytes 147464 | tf_op jit(solution)/shard_map/ppermute | solution.py:442
  48.4 5.3 %collective-permute-start.12 = (bf16[192,128]{1,0:T(8,128)(2,1)S(1)}, bf16[192,128]{1,0:T(8,128)(2,1)S(1)}, u32[]{:S(2)}, u32[]{:S(2)}) collective-permute-start(bf16[192,128]{1,0:T(8,128)(2,1)S(1)} %cotangent.1.refs_0_), channel_id=1, source_target_pairs={{0,6},{1,7},{2,4},{3,5},{4,2},{5,3},{6,0},{7,1},{8,14},{9,15},{10,... | collective-permute-start | bytes 147464 | tf_op jit(solution)/shard_map/ppermute | solution.py:442
  49.8 4.1 %collective-permute-start.10 = (bf16[192,128]{1,0:T(8,128)(2,1)S(1)}, bf16[192,128]{1,0:T(8,128)(2,1)S(1)}, u32[]{:S(2)}, u32[]{:S(2)}) collective-permute-start(bf16[192,128]{1,0:T(8,128)(2,1)S(1)} %cotangent.1.refs_0_), channel_id=1, source_target_pairs={{0,4},{1,5},{2,6},{3,7},{4,0},{5,1},{6,2},{7,3},{8,12},{9,13},{10,... | collective-permute-start | bytes 147464 | tf_op jit(solution)/shard_map/ppermute | solution.py:442
  50.5 4.1 %collective-permute-start.8 = (bf16[192,128]{1,0:T(8,128)(2,1)S(1)}, bf16[192,128]{1,0:T(8,128)(2,1)S(1)}, u32[]{:S(2)}, u32[]{:S(2)}) collective-permute-start(bf16[192,128]{1,0:T(8,128)(2,1)S(1)} %cotangent.1.refs_0_), channel_id=1, source_target_pairs={{0,2},{1,3},{2,0},{3,1},{4,6},{5,7},{6,4},{7,5},{8,10},{9,11},{10,... | collective-permute-start | bytes 147464 | tf_op jit(solution)/shard_map/ppermute | solution.py:442
  53.6 1.5 %collective-permute-start.14 = (bf16[192,128]{1,0:T(8,128)(2,1)S(1)}, bf16[192,128]{1,0:T(8,128)(2,1)S(1)}, u32[]{:S(2)}, u32[]{:S(2)}) collective-permute-start(bf16[192,128]{1,0:T(8,128)(2,1)S(1)} %collective-permute-done.12.refs_2_), channel_id=1, source_target_pairs={{0,1},{1,0},{2,3},{3,2},{4,5},{5,4},{6,7},{7,6},{8,9},{9,8},{10,11... | collective-permute-start | bytes 147464 | tf_op jit(solution)/shard_map/ppermute | solution.py:442
  53.9 1.3 %collective-permute-start.11 = (bf16[192,128]{1,0:T(8,128)(2,1)S(1)}, bf16[192,128]{1,0:T(8,128)(2,1)S(1)}, u32[]{:S(2)}, u32[]{:S(2)}) collective-permute-start(bf16[192,128]{1,0:T(8,128)(2,1)S(1)} %collective-permute-done.10.refs_1_), channel_id=1, source_target_pairs={{0,1},{1,0},{2,3},{3,2},{4,5},{5,4},{6,7},{7,6},{8,9},{9,8},{10,11... | collective-permute-start | bytes 147464 | tf_op jit(solution)/shard_map/ppermute | solution.py:442
  54.5 1.2 %collective-permute-start.9 = (bf16[192,128]{1,0:T(8,128)(2,1)S(1)}, bf16[192,128]{1,0:T(8,128)(2,1)S(1)}, u32[]{:S(2)}, u32[]{:S(2)}) collective-permute-start(bf16[192,128]{1,0:T(8,128)(2,1)S(1)} %collective-permute-done.8.refs_0_), channel_id=1, source_target_pairs={{0,1},{1,0},{2,3},{3,2},{4,5},{5,4},{6,7},{7,6},{8,9},{9,8},{10,11... | collective-permute-start | bytes 147464 | tf_op jit(solution)/shard_map/ppermute | solution.py:442
  55.1 5.9 %copy-start.1 = (bf16[2048,896]{1,0:T(8,128)(2,1)S(1)}, bf16[2048,896]{1,0:T(8,128)(2,1)}, u32[]{:S(2)}) copy-start(bf16[2048,896]{1,0:T(8,128)(2,1)} %gate_w.3) | copy-start | bytes 11010052
  55.1 5.9 %copy-start.2 = (bf16[2048,896]{1,0:T(8,128)(2,1)S(1)}, bf16[2048,896]{1,0:T(8,128)(2,1)}, u32[]{:S(2)}) copy-start(bf16[2048,896]{1,0:T(8,128)(2,1)} %up_w.3) | copy-start | bytes 11010052
  56.1 4.9 %collective-permute-start.16 = (bf16[96,384]{1,0:T(8,128)(2,1)S(1)}, bf16[96,384]{1,0:T(8,128)(2,1)S(1)}, u32[]{:S(2)}, u32[]{:S(2)}) collective-permute-start(bf16[96,384]{1,0:T(8,128)(2,1)S(1)} %get-tuple-element.88), channel_id=1, source_target_pairs={{0,16},{16,0},{1,17},{17,1},{2,18},{18,2},{3,19},{19,3},{4,20},{20... | collective-permute-start | bytes 221192 | tf_op jit(solution)/shard_map/ppermute | solution.py:448
  57.5 5.1 %collective-permute-start.15 = (bf16[96,512]{1,0:T(8,128)(2,1)S(1)}, bf16[96,512]{1,0:T(8,128)(2,1)S(1)}, u32[]{:S(2)}, u32[]{:S(2)}) collective-permute-start(bf16[96,512]{1,0:T(8,128)(2,1)S(1)} %get-tuple-element.84), channel_id=1, source_target_pairs={{0,16},{16,0},{1,17},{17,1},{2,18},{18,2},{3,19},{19,3},{4,20},{20... | collective-permute-start | bytes 294920 | tf_op jit(solution)/shard_map/ppermute | solution.py:448
  64.1 1.5 %collective-permute-start.17 = (bf16[768,128]{1,0:T(8,128)(2,1)S(1)}, bf16[768,128]{1,0:T(8,128)(2,1)S(1)}, u32[]{:S(2)}, u32[]{:S(2)}) collective-permute-start(bf16[768,128]{1,0:T(8,128)(2,1)S(1)} %get-tuple-element.93), channel_id=1, source_target_pairs={{0,1},{1,0},{2,3},{3,2},{4,5},{5,4},{6,7},{7,6},{8,9},{9,8},{10,11... | collective-permute-start | bytes 589832 | tf_op jit(solution)/shard_map/ppermute | solution.py:442
  66.3 12.7 %all-to-all-start.1 = ((bf16[16,48,128]{2,1,0:T(8,128)(2,1)}), bf16[16,48,128]{2,1,0:T(8,128)(2,1)S(1)}, u32[]{:S(2)}, u32[]{:S(2)}) async-start(bf16[16,48,128]{2,1,0:T(8,128)(2,1)} %bitcast.5), calls=%async_computation.1 | async-start | bytes 393216 | tf_op jit(solution)/shard_map/all_to_all | solution.py:451

commit v11 on v10

--- a/solution.py
+++ b/solution.py
@@ -412,12 +412,14 @@
         for h in range(1, half):
             base = (d * half + h) * size
             total = total + got_ref[base : base + size, :].astype(F32)
-        for q in range(blocks):
-            rows[0:cap, q * LANES : (q + 1) * LANES] = total[q * cap : (q + 1) * cap, :]
-        cols = slice(d * width, (d + 1) * width)
-        out[:, cols] = dot_tn(pick, rows[...].astype(BF)).astype(out.dtype)
-        copies.append(pltpu.make_async_copy(out.at[:, cols], out_hbm.at[:, cols], sems.at[d]))
-        copies[-1].start()
+        for k in range(4):
+            here = slice(k * width // 4, (k + 1) * width // 4)
+            for q in range(k * blocks // 4, (k + 1) * blocks // 4):
+                rows[0:cap, q * LANES : (q + 1) * LANES] = total[q * cap : (q + 1) * cap, :]
+            cols = slice(d * width + here.start, d * width + here.stop)
+            out[:, cols] = dot_tn(pick, rows[:, here].astype(BF)).astype(out.dtype)
+            copies.append(pltpu.make_async_copy(out.at[:, cols], out_hbm.at[:, cols], sems.at[d, k]))
+            copies[-1].start()
     for copy in copies:
         copy.wait()
 
@@ -685,7 +687,7 @@
         [
             pltpu.VMEM((16, width), F32),
             pltpu.VMEM((tok_rows, features), tokens.dtype),
-            pltpu.SemaphoreType.DMA((n_dp,)),
+            pltpu.SemaphoreType.DMA((n_dp, 4)),
         ],
         out_spec=HBM,
         name="token_grad",

time: 80.7 us -> 80.6 us (level)
  no operation moved by 1% of the time
where the time goes in v11:
time: 80.6 us; the launch traced here: 80.2 us
  waiting for transfers between devices  32.7 us (41%)
  starting transfers between devices  25.9 us (32%)
  Pallas kernels  20.7 us (26%)
  between operations  0.85 us (1%)
    pallas_call x21, Pallas kernels, call(): pl.pallas_call(body, out_shape=outs, in_specs=specs, out_specs=jax.tree.m...  20.7 us
    all_to_all x2, waiting for transfers between devices, over_slice(): lax.all_to_all(x, ('dp', 'expert'), 0, 0, axis_index_groups=slice_groups,...  13.6 us
    all_to_all x2, starting transfers between devices, over_slice(): lax.all_to_all(x, ('dp', 'expert'), 0, 0, axis_index_groups=slice_groups,...  12.3 us
    ppermute x14, waiting for transfers between devices, other(): return lax.ppermute(x, 'expert', [(i, i ^ mask) for i in range(n_expert)])  11.2 us
    ppermute x14, starting transfers between devices, other(): return lax.ppermute(x, 'expert', [(i, i ^ mask) for i in range(n_expert)])  9.32 us
    ppermute x4, waiting for transfers between devices, other_dp(): return lax.ppermute(x, 'dp', [(0, 1), (1, 0)])  7.96 us
    ppermute x4, starting transfers between devices, other_dp(): return lax.ppermute(x, 'dp', [(0, 1), (1, 0)])  4.31 us
  transfers between devices with their start and end apart: 20, of which 16 were waited for; matrix products, arithmetic and copies ran while one was open for 0% of the time, Pallas kernels for 16%

profile of v11, /device:TPU:0, one launch (start us, length us, event | category | flops | bytes accessed | tf_op | source)
XLA Modules:
  0.0 80.2 jit_solution(8117657490957401237)
XLA Ops:
  0.6 2.7 %route.1 = (bf16[1024,128]{1,0:T(8,128)(2,1)}, bf16[16,128]{1,0:T(8,128)(2,1)S(1)}) custom-call(s32[2,128]{1,0:T(2,128)} %bitcast.10, f32[2,128]{1,0:T(2,128)} %bitcast.11, bf16[128,4096]{1,0:T(8,128)(2,1)} %tokens_hbm.1, bf16[128,4096]{1,0:T(8,128)(2,1)} %target_hbm.1), custom_call_target="tpu_custom_call" | custom-call | tf_op jit(solution)/shard_map/route/pallas_call | solution.py:54
  3.3 8.3 %all-to-all-start = ((bf16[16,64,128]{2,1,0:T(8,128)(2,1)}), bf16[16,64,128]{2,1,0:T(8,128)(2,1)S(1)}, u32[]{:S(2)}, u32[]{:S(2)}) async-start(bf16[16,64,128]{2,1,0:T(8,128)(2,1)} %bitcast.3), calls=%async_computation | async-start | bytes 524288 | tf_op jit(solution)/shard_map/all_to_all | solution.py:453
  11.7 1.6 %load_weights.2 = (f32[8,128]{1,0:T(8,128)S(1)}, bf16[2048,256]{1,0:T(8,128)(2,1)S(1)}, bf16[2048,256]{1,0:T(8,128)(2,1)S(1)}) custom-call(bf16[2048,896]{1,0:T(8,128)(2,1)} %gate_w.3, bf16[2048,896]{1,0:T(8,128)(2,1)} %up_w.3), custom_call_target="tpu_custom_call" | custom-call | flops 1000000000 | bytes 4194304 | tf_op jit(solution)/shard_map/load_weights/pallas_call | solution.py:54
  13.2 8.3 %all-to-all-done = bf16[16,64,128]{2,1,0:T(8,128)(2,1)S(1)} async-done(((bf16[16,64,128]{2,1,0:T(8,128)(2,1)}), bf16[16,64,128]{2,1,0:T(8,128)(2,1)S(1)}, u32[]{:S(2)}, u32[]{:S(2)}) %all-to-all-start) | async-done | bytes 262176 | tf_op jit(solution)/shard_map/all_to_all | solution.py:453
  21.5 1.6 %load_weights.3 = (bf16[2048,256]{1,0:T(8,128)(2,1)S(1)}, bf16[2048,256]{1,0:T(8,128)(2,1)S(1)}, bf16[48,2048]{1,0:T(8,128)(2,1)S(1)}, f32[48,128]{1,0:T(8,128)S(1)}, f32[48,128]{1,0:T(8,128)S(1)}) custom-call(s32[1]{0:T(128)} %bitcast.2.place_ref, bf16[1024,128]{1,0:T(8,128)(2,1)S(1)} %bitcast.8, bf16[2048,896]{1,0:T(8,128)(2,1)} %gate_w.3, ...), custom_call_target="tpu_custom_call" | custom-call | flops 1000000000 | bytes 4194304 | tf_op jit(solution)/shard_map/load_weights/pallas_call | solution.py:54
  23.1 1.1 %pre_activations.2 = (bf16[96,2048]{1,0:T(8,128)(2,1)S(1)}, f32[96,128]{1,0:T(8,128)S(1)}, f32[96,128]{1,0:T(8,128)S(1)}, f32[2,96,512]{2,1,0:T(8,128)S(1)}, bf16[2,96,512]{2,1,0:T(8,128)(2,1)S(1)}) custom-call(s32[1]{0:T(128)} %bitcast.2.place_ref, f32[8,128]{1,0:T(8,128)S(1)} %get-tuple-element.55.loaded_ref, ...), custom_call_target="tpu_custom_call" | custom-call | flops 805306368 | bytes 4194304 | tf_op jit(solution)/shard_map/pre_activations/pallas_call | solution.py:54
  24.2 1.2 %collective-permute-start.2 = (bf16[2,96,512]{2,1,0:T(8,128)(2,1)S(1)}, bf16[2,96,512]{2,1,0:T(8,128)(2,1)S(1)}, u32[]{:S(2)}, u32[]{:S(2)}) collective-permute-start(bf16[2,96,512]{2,1,0:T(8,128)(2,1)S(1)} %get-tuple-element.68), channel_id=1, source_target_pairs={{0,16},{16,0},{1,17},{17,1},{2,18},{18,2},{3,19},{19,3},{4,20},{20... | collective-permute-start | bytes 589832 | tf_op jit(solution)/shard_map/ppermute | solution.py:450
  25.4 2.8 %pre_activations.3 = (bf16[2048,96]{1,0:T(8,128)(2,1)S(1)}, f32[2,96,384]{2,1,0:T(8,128)S(1)}, bf16[2,96,384]{2,1,0:T(8,128)(2,1)S(1)}) custom-call(bf16[96,2048]{1,0:T(8,128)(2,1)S(1)} %get-tuple-element.64.rows_ref, bf16[2048,896]{1,0:T(8,128)(2,1)} %gate_w.3, bf16[2048,896]{1,0:T(8,128)(2,1)} %up_w.3), custom_call_target="tpu_custom_call" | custom-call | flops 603979776 | bytes 3145728 | tf_op jit(solution)/shard_map/pre_activations/pallas_call | solution.py:54
  28.1 1.0 %collective-permute-start.1 = (bf16[2,96,384]{2,1,0:T(8,128)(2,1)S(1)}, bf16[2,96,384]{2,1,0:T(8,128)(2,1)S(1)}, u32[]{:S(2)}, u32[]{:S(2)}) collective-permute-start(bf16[2,96,384]{2,1,0:T(8,128)(2,1)S(1)} %get-tuple-element.66), channel_id=1, source_target_pairs={{0,16},{16,0},{1,17},{17,1},{2,18},{18,2},{3,19},{19,3},{4,20},{20... | collective-permute-start | bytes 442376 | tf_op jit(solution)/shard_map/ppermute | solution.py:450
  29.1 2.8 %collective-permute-done.2.got_ref = bf16[2,96,512]{2,1,0:T(8,128)(2,1)S(1)} collective-permute-done((bf16[2,96,512]{2,1,0:T(8,128)(2,1)S(1)}, bf16[2,96,512]{2,1,0:T(8,128)(2,1)S(1)}, u32[]{:S(2)}, u32[]{:S(2)}) %collective-permute-start.2) | collective-permute-done | bytes 196640 | tf_op jit(solution)/shard_map/ppermute | solution.py:450
  32.0 0.5 down.1
  32.5 2.2 %collective-permute-done.1.got_ref = bf16[2,96,384]{2,1,0:T(8,128)(2,1)S(1)} collective-permute-done((bf16[2,96,384]{2,1,0:T(8,128)(2,1)S(1)}, bf16[2,96,384]{2,1,0:T(8,128)(2,1)S(1)}, u32[]{:S(2)}, u32[]{:S(2)}) %collective-permute-start.1) | collective-permute-done | bytes 147488 | tf_op jit(solution)/shard_map/ppermute | solution.py:450
  34.7 0.3 down_send.1
  35.2 0.3 down_keep.1.own_ref
  35.5 1.1 %collective-permute-done.3.got_ref = bf16[768,128]{1,0:T(8,128)(2,1)S(1)} collective-permute-done((bf16[768,128]{1,0:T(8,128)(2,1)S(1)}, bf16[768,128]{1,0:T(8,128)(2,1)S(1)}, u32[]{:S(2)}, u32[]{:S(2)}) %collective-permute-start.3) | collective-permute-done | bytes 196640 | tf_op jit(solution)/shard_map/ppermute | solution.py:444
  36.7 1.0 %collective-permute-start.4 = (bf16[192,128]{1,0:T(8,128)(2,1)S(1)}, bf16[192,128]{1,0:T(8,128)(2,1)S(1)}, u32[]{:S(2)}, u32[]{:S(2)}) collective-permute-start(bf16[192,128]{1,0:T(8,128)(2,1)S(1)} %get-tuple-element.73), channel_id=1, source_target_pairs={{0,6},{1,7},{2,4},{3,5},{4,2},{5,3},{6,0},{7,1},{8,14},{9,15},{10,... | collective-permute-start | bytes 147464 | tf_op jit(solution)/shard_map/ppermute | solution.py:444
  37.6 1.5 %collective-permute-start.5 = (bf16[192,128]{1,0:T(8,128)(2,1)S(1)}, bf16[192,128]{1,0:T(8,128)(2,1)S(1)}, u32[]{:S(2)}, u32[]{:S(2)}) collective-permute-start(bf16[192,128]{1,0:T(8,128)(2,1)S(1)} %get-tuple-element.74), channel_id=1, source_target_pairs={{0,2},{1,3},{2,0},{3,1},{4,6},{5,7},{6,4},{7,5},{8,10},{9,11},{10,... | collective-permute-start | bytes 147464 | tf_op jit(solution)/shard_map/ppermute | solution.py:444
  39.1 1.1 %collective-permute-start.6 = (bf16[192,128]{1,0:T(8,128)(2,1)S(1)}, bf16[192,128]{1,0:T(8,128)(2,1)S(1)}, u32[]{:S(2)}, u32[]{:S(2)}) collective-permute-start(bf16[192,128]{1,0:T(8,128)(2,1)S(1)} %get-tuple-element.75), channel_id=1, source_target_pairs={{0,4},{1,5},{2,6},{3,7},{4,0},{5,1},{6,2},{7,3},{8,12},{9,13},{10,... | collective-permute-start | bytes 147464 | tf_op jit(solution)/shard_map/ppermute | solution.py:444
  40.2 1.9 %collective-permute-done.4.first_ref = bf16[192,128]{1,0:T(8,128)(2,1)S(1)} collective-permute-done((bf16[192,128]{1,0:T(8,128)(2,1)S(1)}, bf16[192,128]{1,0:T(8,128)(2,1)S(1)}, u32[]{:S(2)}, u32[]{:S(2)}) %collective-permute-start.4) | collective-permute-done | bytes 49184 | tf_op jit(solution)/shard_map/ppermute | solution.py:444
  42.2 0.1 collective-permute-done.5.second_ref
  42.2 0.9 %collective-permute-done.6.third_ref = bf16[192,128]{1,0:T(8,128)(2,1)S(1)} collective-permute-done((bf16[192,128]{1,0:T(8,128)(2,1)S(1)}, bf16[192,128]{1,0:T(8,128)(2,1)S(1)}, u32[]{:S(2)}, u32[]{:S(2)}) %collective-permute-start.6) | collective-permute-done | bytes 49184 | tf_op jit(solution)/shard_map/ppermute | solution.py:444
  43.2 1.7 %collective-permute-start.7 = (bf16[192,128]{1,0:T(8,128)(2,1)S(1)}, bf16[192,128]{1,0:T(8,128)(2,1)S(1)}, u32[]{:S(2)}, u32[]{:S(2)}) collective-permute-start(bf16[192,128]{1,0:T(8,128)(2,1)S(1)} %get-tuple-element.79), channel_id=1, source_target_pairs={{0,8},{1,9},{2,10},{3,11},{4,12},{5,13},{6,14},{7,15},{8,0},{9,1},... | collective-permute-start | bytes 147464 | tf_op jit(solution)/shard_map/ppermute | solution.py:444
  44.9 3.4 %collective-permute-done.7.got_ref = bf16[192,128]{1,0:T(8,128)(2,1)S(1)} collective-permute-done((bf16[192,128]{1,0:T(8,128)(2,1)S(1)}, bf16[192,128]{1,0:T(8,128)(2,1)S(1)}, u32[]{:S(2)}, u32[]{:S(2)}) %collective-permute-start.7) | collective-permute-done | bytes 49184 | tf_op jit(solution)/shard_map/ppermute | solution.py:444
  48.4 1.4 %collective-permute-start.12 = (bf16[192,128]{1,0:T(8,128)(2,1)S(1)}, bf16[192,128]{1,0:T(8,128)(2,1)S(1)}, u32[]{:S(2)}, u32[]{:S(2)}) collective-permute-start(bf16[192,128]{1,0:T(8,128)(2,1)S(1)} %cotangent.1.refs_0_), channel_id=1, source_target_pairs={{0,6},{1,7},{2,4},{3,5},{4,2},{5,3},{6,0},{7,1},{8,14},{9,15},{10,... | collective-permute-start | bytes 147464 | tf_op jit(solution)/shard_map/ppermute | solution.py:444
  49.8 0.7 collective-permute-start.10
  50.5 1.5 %collective-permute-start.8 = (bf16[192,128]{1,0:T(8,128)(2,1)S(1)}, bf16[192,128]{1,0:T(8,128)(2,1)S(1)}, u32[]{:S(2)}, u32[]{:S(2)}) collective-permute-start(bf16[192,128]{1,0:T(8,128)(2,1)S(1)} %cotangent.1.refs_0_), channel_id=1, source_target_pairs={{0,2},{1,3},{2,0},{3,1},{4,6},{5,7},{6,4},{7,5},{8,10},{9,11},{10,... | collective-permute-start | bytes 147464 | tf_op jit(solution)/shard_map/ppermute | solution.py:444
  51.9 0.3 grad_hidden_near.3.refs_1_
  52.2 0.3 grad_hidden_near.4.refs_3_
  52.5 1.1 %collective-permute-done.12.refs_2_ = bf16[192,128]{1,0:T(8,128)(2,1)S(1)} collective-permute-done((bf16[192,128]{1,0:T(8,128)(2,1)S(1)}, bf16[192,128]{1,0:T(8,128)(2,1)S(1)}, u32[]{:S(2)}, u32[]{:S(2)}) %collective-permute-start.12) | collective-permute-done | bytes 49184 | tf_op jit(solution)/shard_map/ppermute | solution.py:444
  53.6 0.2 collective-permute-done.10.refs_1_
  53.9 0.3 collective-permute-start.11
  54.2 0.4 collective-permute-done.8.refs_0_
  54.6 0.6 grad_hidden_near.5.total_ref
  55.2 0.6 collective-permute-done.9.first_ref
  55.8 0.3 grad_hidden.2
  56.1 1.0 %collective-permute-start.16 = (bf16[96,384]{1,0:T(8,128)(2,1)S(1)}, bf16[96,384]{1,0:T(8,128)(2,1)S(1)}, u32[]{:S(2)}, u32[]{:S(2)}) collective-permute-start(bf16[96,384]{1,0:T(8,128)(2,1)S(1)} %get-tuple-element.88), channel_id=1, source_target_pairs={{0,16},{16,0},{1,17},{17,1},{2,18},{18,2},{3,19},{19,3},{4,20},{20... | collective-permute-start | bytes 221192 | tf_op jit(solution)/shard_map/ppermute | solution.py:450
  57.1 0.4 grad_hidden.3
  57.5 1.2 %collective-permute-start.15 = (bf16[96,512]{1,0:T(8,128)(2,1)S(1)}, bf16[96,512]{1,0:T(8,128)(2,1)S(1)}, u32[]{:S(2)}, u32[]{:S(2)}) collective-permute-start(bf16[96,512]{1,0:T(8,128)(2,1)S(1)} %get-tuple-element.84), channel_id=1, source_target_pairs={{0,16},{16,0},{1,17},{17,1},{2,18},{18,2},{3,19},{19,3},{4,20},{20... | collective-permute-start | bytes 294920 | tf_op jit(solution)/shard_map/ppermute | solution.py:450
  58.7 2.4 %collective-permute-done.16.got_ref = bf16[96,384]{1,0:T(8,128)(2,1)S(1)} collective-permute-done((bf16[96,384]{1,0:T(8,128)(2,1)S(1)}, bf16[96,384]{1,0:T(8,128)(2,1)S(1)}, u32[]{:S(2)}, u32[]{:S(2)}) %collective-permute-start.16) | collective-permute-done | bytes 73760 | tf_op jit(solution)/shard_map/ppermute | solution.py:450
  61.0 1.1 %row_grad.2 = (bf16[96,384]{1,0:T(8,128)(2,1)S(1)}, bf16[96,384]{1,0:T(8,128)(2,1)S(1)}, f32[96,2048]{1,0:T(8,128)S(1)}) custom-call(s32[1]{0:T(128)} %bitcast.2.place_ref, f32[96,384]{1,0:T(8,128)S(1)} %get-tuple-element.87.own_ref, bf16[96,384]{1,0:T(8,128)(2,1)S(1)} %collective-permute-done.16.got_ref, f32[96,384]{1,0:T(8,128)S(1)} %get-tuple-element.89.up_deriv, ...), custom_call_target="tpu_custom_call" | custom-call | flops 603979776 | bytes 3145728 | tf_op jit(solution)/shard_map/row_grad/pallas_call | solution.py:54
  62.1 0.5 collective-permute-done.15.got_ref
  62.6 1.4 %row_grad.3 = (bf16[96,512]{1,0:T(8,128)(2,1)S(1)}, bf16[96,512]{1,0:T(8,128)(2,1)S(1)}, f32[768,128]{1,0:T(8,128)S(1)}, bf16[768,128]{1,0:T(8,128)(2,1)S(1)}) custom-call(s32[1]{0:T(128)} %bitcast.2.place_ref, f32[96,512]{1,0:T(8,128)S(1)} %get-tuple-element.83.own_ref, bf16[96,512]{1,0:T(8,128)(2,1)S(1)} %collective-permute-done.15.got_ref, ...), custom_call_target="tpu_custom_call" | custom-call | flops 805306368 | bytes 4194304 | tf_op jit(solution)/shard_map/row_grad/pallas_call | solution.py:54
  64.2 1.4 %collective-permute-done.17.got_ref = bf16[768,128]{1,0:T(8,128)(2,1)S(1)} collective-permute-done((bf16[768,128]{1,0:T(8,128)(2,1)S(1)}, bf16[768,128]{1,0:T(8,128)(2,1)S(1)}, u32[]{:S(2)}, u32[]{:S(2)}) %collective-permute-start.17) | collective-permute-done | bytes 196640 | tf_op jit(solution)/shard_map/ppermute | solution.py:444
  65.6 0.7 add_cores.1
  66.3 4.0 %all-to-all-start.1 = ((bf16[16,48,128]{2,1,0:T(8,128)(2,1)}), bf16[16,48,128]{2,1,0:T(8,128)(2,1)S(1)}, u32[]{:S(2)}, u32[]{:S(2)}) async-start(bf16[16,48,128]{2,1,0:T(8,128)(2,1)} %bitcast.5), calls=%async_computation.1 | async-start | bytes 393216 | tf_op jit(solution)/shard_map/all_to_all | solution.py:453
  70.3 3.4 %weight_grads.1 = (bf16[2048,896]{1,0:T(8,128)(2,1)}, bf16[2048,896]{1,0:T(8,128)(2,1)}) custom-call(bf16[2048,96]{1,0:T(8,128)(2,1)S(1)} %get-tuple-element.94.turned_ref, bf16[96,512]{1,0:T(8,128)(2,1)S(1)} %get-tuple-element.95.refs_0_, bf16[96,384]{1,0:T(8,128)(2,1)S(1)} %get-tuple-element.96.refs_1_, bf16[96,512]{1,0:T(8,128)(2,1)S(1)} %get-tuple-element.97.refs_2_, ...), custom_call_target="tpu_custom_call" | custom-call | flops 704643072 | bytes 7340032 | tf_op jit(solution)/shard_map/weight_grads/pallas_call | solution.py:54
  73.7 5.3 %all-to-all-done.1 = bf16[16,48,128]{2,1,0:T(8,128)(2,1)S(1)} async-done(((bf16[16,48,128]{2,1,0:T(8,128)(2,1)}), bf16[16,48,128]{2,1,0:T(8,128)(2,1)S(1)}, u32[]{:S(2)}, u32[]{:S(2)}) %all-to-all-start.1) | async-done | bytes 196640 | tf_op jit(solution)/shard_map/all_to_all | solution.py:453
  79.0 1.2 %token_grad.1 = bf16[128,4096]{1,0:T(8,128)(2,1)} custom-call(bf16[16,128]{1,0:T(8,128)(2,1)S(1)} %get-tuple-element.52.pick_ref, bf16[768,128]{1,0:T(8,128)(2,1)S(1)} %bitcast.9), custom_call_target="tpu_custom_call" | custom-call | tf_op jit(solution)/shard_map/token_grad/pallas_call | solution.py:54
  (19 shorter events, 0.4 us)
Async XLA Ops:
  3.3 18.2 %all-to-all-start = ((bf16[16,64,128]{2,1,0:T(8,128)(2,1)}), bf16[16,64,128]{2,1,0:T(8,128)(2,1)S(1)}, u32[]{:S(2)}, u32[]{:S(2)}) async-start(bf16[16,64,128]{2,1,0:T(8,128)(2,1)} %bitcast.3), calls=%async_computation | async-start | bytes 524288 | tf_op jit(solution)/shard_map/all_to_all | solution.py:453
  21.5 1.6 %collective-permute-start = (bf16[1024,128]{1,0:T(8,128)(2,1)S(1)}, bf16[1024,128]{1,0:T(8,128)(2,1)S(1)}, u32[]{:S(2)}, u32[]{:S(2)}) collective-permute-start(bf16[1024,128]{1,0:T(8,128)(2,1)S(1)} %bitcast.7), channel_id=1, source_target_pairs={{0,1},{1,0},{2,3},{3,2},{4,5},{5,4},{6,7},{7,6},{8,9},{9,8},{10,11... | collective-permute-start | bytes 786440 | tf_op jit(solution)/shard_map/ppermute | solution.py:444
  24.2 7.8 %collective-permute-start.2 = (bf16[2,96,512]{2,1,0:T(8,128)(2,1)S(1)}, bf16[2,96,512]{2,1,0:T(8,128)(2,1)S(1)}, u32[]{:S(2)}, u32[]{:S(2)}) collective-permute-start(bf16[2,96,512]{2,1,0:T(8,128)(2,1)S(1)} %get-tuple-element.68), channel_id=1, source_target_pairs={{0,16},{16,0},{1,17},{17,1},{2,18},{18,2},{3,19},{19,3},{4,20},{20... | collective-permute-start | bytes 589832 | tf_op jit(solution)/shard_map/ppermute | solution.py:450
  25.4 6.6 %copy-start = (bf16[896,2048]{1,0:T(8,128)(2,1)S(1)}, bf16[896,2048]{1,0:T(8,128)(2,1)}, u32[]{:S(2)}) copy-start(bf16[896,2048]{1,0:T(8,128)(2,1)} %down_w.15) | copy-start | bytes 11010052
  28.1 6.6 %collective-permute-start.1 = (bf16[2,96,384]{2,1,0:T(8,128)(2,1)S(1)}, bf16[2,96,384]{2,1,0:T(8,128)(2,1)S(1)}, u32[]{:S(2)}, u32[]{:S(2)}) collective-permute-start(bf16[2,96,384]{2,1,0:T(8,128)(2,1)S(1)} %get-tuple-element.66), channel_id=1, source_target_pairs={{0,16},{16,0},{1,17},{17,1},{2,18},{18,2},{3,19},{19,3},{4,20},{20... | collective-permute-start | bytes 442376 | tf_op jit(solution)/shard_map/ppermute | solution.py:450
  35.1 1.5 %collective-permute-start.3 = (bf16[768,128]{1,0:T(8,128)(2,1)S(1)}, bf16[768,128]{1,0:T(8,128)(2,1)S(1)}, u32[]{:S(2)}, u32[]{:S(2)}) collective-permute-start(bf16[768,128]{1,0:T(8,128)(2,1)S(1)} %get-tuple-element.71), channel_id=1, source_target_pairs={{0,1},{1,0},{2,3},{3,2},{4,5},{5,4},{6,7},{7,6},{8,9},{9,8},{10,11... | collective-permute-start | bytes 589832 | tf_op jit(solution)/shard_map/ppermute | solution.py:444
  36.7 5.5 %collective-permute-start.4 = (bf16[192,128]{1,0:T(8,128)(2,1)S(1)}, bf16[192,128]{1,0:T(8,128)(2,1)S(1)}, u32[]{:S(2)}, u32[]{:S(2)}) collective-permute-start(bf16[192,128]{1,0:T(8,128)(2,1)S(1)} %get-tuple-element.73), channel_id=1, source_target_pairs={{0,6},{1,7},{2,4},{3,5},{4,2},{5,3},{6,0},{7,1},{8,14},{9,15},{10,... | collective-permute-start | bytes 147464 | tf_op jit(solution)/shard_map/ppermute | solution.py:444
  37.6 4.6 %collective-permute-start.5 = (bf16[192,128]{1,0:T(8,128)(2,1)S(1)}, bf16[192,128]{1,0:T(8,128)(2,1)S(1)}, u32[]{:S(2)}, u32[]{:S(2)}) collective-permute-start(bf16[192,128]{1,0:T(8,128)(2,1)S(1)} %get-tuple-element.74), channel_id=1, source_target_pairs={{0,2},{1,3},{2,0},{3,1},{4,6},{5,7},{6,4},{7,5},{8,10},{9,11},{10,... | collective-permute-start | bytes 147464 | tf_op jit(solution)/shard_map/ppermute | solution.py:444
  39.1 4.1 %collective-permute-start.6 = (bf16[192,128]{1,0:T(8,128)(2,1)S(1)}, bf16[192,128]{1,0:T(8,128)(2,1)S(1)}, u32[]{:S(2)}, u32[]{:S(2)}) collective-permute-start(bf16[192,128]{1,0:T(8,128)(2,1)S(1)} %get-tuple-element.75), channel_id=1, source_target_pairs={{0,4},{1,5},{2,6},{3,7},{4,0},{5,1},{6,2},{7,3},{8,12},{9,13},{10,... | collective-permute-start | bytes 147464 | tf_op jit(solution)/shard_map/ppermute | solution.py:444
  43.2 5.1 %collective-permute-start.7 = (bf16[192,128]{1,0:T(8,128)(2,1)S(1)}, bf16[192,128]{1,0:T(8,128)(2,1)S(1)}, u32[]{:S(2)}, u32[]{:S(2)}) collective-permute-start(bf16[192,128]{1,0:T(8,128)(2,1)S(1)} %get-tuple-element.79), channel_id=1, source_target_pairs={{0,8},{1,9},{2,10},{3,11},{4,12},{5,13},{6,14},{7,15},{8,0},{9,1},... | collective-permute-start | bytes 147464 | tf_op jit(solution)/shard_map/ppermute | solution.py:444
  48.3 3.9 %collective-permute-start.13 = (bf16[192,128]{1,0:T(8,128)(2,1)S(1)}, bf16[192,128]{1,0:T(8,128)(2,1)S(1)}, u32[]{:S(2)}, u32[]{:S(2)}) collective-permute-start(bf16[192,128]{1,0:T(8,128)(2,1)S(1)} %cotangent.1.refs_0_), channel_id=1, source_target_pairs={{0,1},{1,0},{2,3},{3,2},{4,5},{5,4},{6,7},{7,6},{8,9},{9,8},{10,11... | collective-permute-start | bytes 147464 | tf_op jit(solution)/shard_map/ppermute | solution.py:444
  48.4 5.3 %collective-permute-start.12 = (bf16[192,128]{1,0:T(8,128)(2,1)S(1)}, bf16[192,128]{1,0:T(8,128)(2,1)S(1)}, u32[]{:S(2)}, u32[]{:S(2)}) collective-permute-start(bf16[192,128]{1,0:T(8,128)(2,1)S(1)} %cotangent.1.refs_0_), channel_id=1, source_target_pairs={{0,6},{1,7},{2,4},{3,5},{4,2},{5,3},{6,0},{7,1},{8,14},{9,15},{10,... | collective-permute-start | bytes 147464 | tf_op jit(solution)/shard_map/ppermute | solution.py:444
  49.8 4.1 %collective-permute-start.10 = (bf16[192,128]{1,0:T(8,128)(2,1)S(1)}, bf16[192,128]{1,0:T(8,128)(2,1)S(1)}, u32[]{:S(2)}, u32[]{:S(2)}) collective-permute-start(bf16[192,128]{1,0:T(8,128)(2,1)S(1)} %cotangent.1.refs_0_), channel_id=1, source_target_pairs={{0,4},{1,5},{2,6},{3,7},{4,0},{5,1},{6,2},{7,3},{8,12},{9,13},{10,... | collective-permute-start | bytes 147464 | tf_op jit(solution)/shard_map/ppermute | solution.py:444
  50.5 4.1 %collective-permute-start.8 = (bf16[192,128]{1,0:T(8,128)(2,1)S(1)}, bf16[192,128]{1,0:T(8,128)(2,1)S(1)}, u32[]{:S(2)}, u32[]{:S(2)}) collective-permute-start(bf16[192,128]{1,0:T(8,128)(2,1)S(1)} %cotangent.1.refs_0_), channel_id=1, source_target_pairs={{0,2},{1,3},{2,0},{3,1},{4,6},{5,7},{6,4},{7,5},{8,10},{9,11},{10,... | collective-permute-start | bytes 147464 | tf_op jit(solution)/shard_map/ppermute | solution.py:444
  53.6 1.5 %collective-permute-start.14 = (bf16[192,128]{1,0:T(8,128)(2,1)S(1)}, bf16[192,128]{1,0:T(8,128)(2,1)S(1)}, u32[]{:S(2)}, u32[]{:S(2)}) collective-permute-start(bf16[192,128]{1,0:T(8,128)(2,1)S(1)} %collective-permute-done.12.refs_2_), channel_id=1, source_target_pairs={{0,1},{1,0},{2,3},{3,2},{4,5},{5,4},{6,7},{7,6},{8,9},{9,8},{10,11... | collective-permute-start | bytes 147464 | tf_op jit(solution)/shard_map/ppermute | solution.py:444
  53.9 1.3 %collective-permute-start.11 = (bf16[192,128]{1,0:T(8,128)(2,1)S(1)}, bf16[192,128]{1,0:T(8,128)(2,1)S(1)}, u32[]{:S(2)}, u32[]{:S(2)}) collective-permute-start(bf16[192,128]{1,0:T(8,128)(2,1)S(1)} %collective-permute-done.10.refs_1_), channel_id=1, source_target_pairs={{0,1},{1,0},{2,3},{3,2},{4,5},{5,4},{6,7},{7,6},{8,9},{9,8},{10,11... | collective-permute-start | bytes 147464 | tf_op jit(solution)/shard_map/ppermute | solution.py:444
  54.5 1.2 %collective-permute-start.9 = (bf16[192,128]{1,0:T(8,128)(2,1)S(1)}, bf16[192,128]{1,0:T(8,128)(2,1)S(1)}, u32[]{:S(2)}, u32[]{:S(2)}) collective-permute-start(bf16[192,128]{1,0:T(8,128)(2,1)S(1)} %collective-permute-done.8.refs_0_), channel_id=1, source_target_pairs={{0,1},{1,0},{2,3},{3,2},{4,5},{5,4},{6,7},{7,6},{8,9},{9,8},{10,11... | collective-permute-start | bytes 147464 | tf_op jit(solution)/shard_map/ppermute | solution.py:444
  55.1 5.9 %copy-start.1 = (bf16[2048,896]{1,0:T(8,128)(2,1)S(1)}, bf16[2048,896]{1,0:T(8,128)(2,1)}, u32[]{:S(2)}) copy-start(bf16[2048,896]{1,0:T(8,128)(2,1)} %gate_w.3) | copy-start | bytes 11010052
  55.1 5.9 %copy-start.2 = (bf16[2048,896]{1,0:T(8,128)(2,1)S(1)}, bf16[2048,896]{1,0:T(8,128)(2,1)}, u32[]{:S(2)}) copy-start(bf16[2048,896]{1,0:T(8,128)(2,1)} %up_w.3) | copy-start | bytes 11010052
  56.1 4.9 %collective-permute-start.16 = (bf16[96,384]{1,0:T(8,128)(2,1)S(1)}, bf16[96,384]{1,0:T(8,128)(2,1)S(1)}, u32[]{:S(2)}, u32[]{:S(2)}) collective-permute-start(bf16[96,384]{1,0:T(8,128)(2,1)S(1)} %get-tuple-element.88), channel_id=1, source_target_pairs={{0,16},{16,0},{1,17},{17,1},{2,18},{18,2},{3,19},{19,3},{4,20},{20... | collective-permute-start | bytes 221192 | tf_op jit(solution)/shard_map/ppermute | solution.py:450
  57.5 5.1 %collective-permute-start.15 = (bf16[96,512]{1,0:T(8,128)(2,1)S(1)}, bf16[96,512]{1,0:T(8,128)(2,1)S(1)}, u32[]{:S(2)}, u32[]{:S(2)}) collective-permute-start(bf16[96,512]{1,0:T(8,128)(2,1)S(1)} %get-tuple-element.84), channel_id=1, source_target_pairs={{0,16},{16,0},{1,17},{17,1},{2,18},{18,2},{3,19},{19,3},{4,20},{20... | collective-permute-start | bytes 294920 | tf_op jit(solution)/shard_map/ppermute | solution.py:450
  64.1 1.5 %collective-permute-start.17 = (bf16[768,128]{1,0:T(8,128)(2,1)S(1)}, bf16[768,128]{1,0:T(8,128)(2,1)S(1)}, u32[]{:S(2)}, u32[]{:S(2)}) collective-permute-start(bf16[768,128]{1,0:T(8,128)(2,1)S(1)} %get-tuple-element.93), channel_id=1, source_target_pairs={{0,1},{1,0},{2,3},{3,2},{4,5},{5,4},{6,7},{7,6},{8,9},{9,8},{10,11... | collective-permute-start | bytes 589832 | tf_op jit(solution)/shard_map/ppermute | solution.py:444
  66.3 12.7 %all-to-all-start.1 = ((bf16[16,48,128]{2,1,0:T(8,128)(2,1)}), bf16[16,48,128]{2,1,0:T(8,128)(2,1)S(1)}, u32[]{:S(2)}, u32[]{:S(2)}) async-start(bf16[16,48,128]{2,1,0:T(8,128)(2,1)} %bitcast.5), calls=%async_computation.1 | async-start | bytes 393216 | tf_op jit(solution)/shard_map/all_to_all | solution.py:453
